TPU v7x, 32 devices: a whole 2x2x4 slice. The times are simulated.
32 devices in a mesh: replica: 2 (over x), fsdp: 16 (over z, y, core).
Axes of the slice: x: 2, y: 2, z: 4, core: 2. Of those that a mesh axis runs over, the one named last changes fastest.
Arguments:
- tokens: bfloat16 [16384, 1536], P(('replica', 'fsdp')), may hold values from -6 to 6
- cotangent: bfloat16 [16384, 1536], P(('replica', 'fsdp')), may hold values from -6 to 6
- needle_mask: int32 [16384], P(('replica', 'fsdp')), may hold values from 0 to 1
- segment_ids: int32 [32, 512], P(('replica', 'fsdp')), may hold values from 0 to 2, never falling along the last dimension, each value on 1 to 256 neighbouring positions
- attn_weight: float32 [1536, 6144], P('fsdp'), may hold values from -0.15625 to 0.15625
- ffn_weight: float32 [1536, 12288], P('fsdp'), may hold values from -0.15625 to 0.15625
- vector_params: float32 [3456], replicated
- attn_error: float32 [2, 1536, 6144], P('replica', 'fsdp'), may hold values from -160 to 160
- ffn_error: float32 [2, 1536, 12288], P('replica', 'fsdp'), may hold values from -160 to 160
- attn_momentum: float32 [1536, 6144], P('fsdp'), may hold values from -16 to 16
- ffn_momentum: float32 [1536, 12288], P('fsdp'), may hold values from -16 to 16
- attn_start: float32 [16, 8, 6144], P('fsdp'), may hold values from -6 to 6
- ffn_start: float32 [16, 8, 12288], P('fsdp'), may hold values from -6 to 6
- vector_momentum: float32 [3456], replicated, may hold values from -24 to 24
Outputs:
- mixed: bfloat16 [16384, 1536], P(('replica', 'fsdp'))
- grad_tokens: float32 [16384, 1536], P(('replica', 'fsdp'))
- grad_attn: float32 [2, 1536, 6144], P('replica', 'fsdp')
- grad_ffn: float32 [2, 1536, 12288], P('replica', 'fsdp')
- left_attn: float32 [8, 1536], P(None, 'fsdp')
- left_ffn: float32 [8, 1536], P(None, 'fsdp')
- right_attn: float32 [16, 8, 6144], P('fsdp')
- right_ffn: float32 [16, 8, 12288], P('fsdp')
- attn_error_new: float32 [2, 1536, 6144], P('replica', 'fsdp')
- ffn_error_new: float32 [2, 1536, 12288], P('replica', 'fsdp')
- attn_momentum_new: float32 [1536, 6144], P('fsdp')
- ffn_momentum_new: float32 [1536, 12288], P('fsdp')
- attn_weight_new: float32 [1536, 6144], P('fsdp')
- ffn_weight_new: float32 [1536, 12288], P('fsdp')
- vector_momentum_new: float32 [3456], replicated
- vector_new: float32 [3456], replicated
Inputs may be any that keep to these rules, and one draw needn't show every extreme that they name: `segment_ids`: within each row the document numbers never fall.
All inputs are finite; a program needn't handle non-finite values.
Results may differ from a plain program's by a relative error of at most 0.022.
The roundings to bfloat16 on the way count: a program that leaves them out, or rounds other values in their place, can miss the bound.
Values may be sent and summed in bfloat16 or wider, within the bound.
No kernel may reach another device: no remote copies, remote signals or barrier semaphores. Data moves between devices by JAX's collectives and lax.ppermute only.
A program may use at most 448 MiB of HBM per device.

v0:
```python
import jax
import jax.numpy as jnp
from jax import lax
from jax.sharding import PartitionSpec as P

D = 1536
HEADS = 12
HD = 64
FF = 4096


NEEDLE = 3.0
LAMBDA_INIT = 0.2
DECAY_ERROR = 0.5
MOMENTUM = 0.9
RATE_MATRIX = 0.005
RATE_VECTOR = 0.02
MASKED = -1e30
HIGHEST = lax.Precision.HIGHEST


def rms_scale(values, epsilon):
    return lax.rsqrt(jnp.mean(values * values, -1, keepdims=True) + epsilon)


def norm_back(grad_normed, normed, scale):
    return scale * (grad_normed - normed * jnp.mean(grad_normed * normed, -1, keepdims=True))


def contract_rows(left, right):
    return lax.dot_general(
        left, right, (((0,), (0,)), ((), ())), preferred_element_type=jnp.float32
    )


def contract_cols(left, right):
    return lax.dot_general(
        left, right, (((1,), (1,)), ((), ())), preferred_element_type=jnp.float32
    )


def orthonormal(left):
    columns = []
    for number in range(left.shape[-1]):
        column = left[..., number]
        for earlier in columns:
            column = column - jnp.sum(earlier * column, -1, keepdims=True) * earlier
        column = column * lax.rsqrt(jnp.sum(column * column, -1, keepdims=True))
        columns.append(column)
    return jnp.stack(columns, -1)


def local(
    tokens,
    cotangent,
    needle_mask,
    segment_ids,
    attn_weight,
    ffn_weight,
    vector_params,
    attn_error,
    ffn_error,
    attn_momentum,
    ffn_momentum,
    attn_start,
    ffn_start,
    vector_momentum,
):
    length = tokens.shape[0]
    gain_in = vector_params[0:D]
    gain_mid = vector_params[D : 2 * D]
    gain_head = vector_params[2 * D : 2 * D + 2 * HD]
    lambda_q_one = vector_params[2 * D + 2 * HD : 2 * D + 3 * HD]
    lambda_k_one = vector_params[2 * D + 3 * HD : 2 * D + 4 * HD]
    lambda_q_two = vector_params[2 * D + 4 * HD : 2 * D + 5 * HD]
    lambda_k_two = vector_params[2 * D + 5 * HD : 2 * D + 6 * HD]
    score_scale = HD ** (-0.5)
    attn_low = attn_weight.astype(jnp.bfloat16)
    ffn_low = ffn_weight.astype(jnp.bfloat16)
    attn_full = lax.all_gather(attn_low, "fsdp", axis=0, tiled=True)
    residual_in = tokens.astype(jnp.float32)
    scale_in = rms_scale(residual_in, 1e-06)
    normed_in = residual_in * scale_in
    normed_low = (normed_in * gain_in).astype(jnp.bfloat16)
    qkv_proj = jnp.dot(
        normed_low, attn_full[:, 0 : 3 * D], preferred_element_type=jnp.float32
    ).astype(jnp.bfloat16)
    queries = qkv_proj[:, 0:D].reshape(length, HEADS, 2, HD)
    keys_all = qkv_proj[:, D : 2 * D].reshape(length, HEADS, 2, HD)
    values = qkv_proj[:, 2 * D : 3 * D].reshape(length, HEADS, 2 * HD)
    query_one = queries[:, :, 0]
    query_two = queries[:, :, 1]
    key_one = keys_all[:, :, 0]
    key_two = keys_all[:, :, 1]
    exp_one = jnp.exp(jnp.sum(lambda_q_one * lambda_k_one))
    exp_two = jnp.exp(jnp.sum(lambda_q_two * lambda_k_two))
    lambda_value = exp_one - exp_two + LAMBDA_INIT
    segments = segment_ids[0]
    positions = jnp.arange(length, dtype=jnp.int32)
    block_rows = min(512, length)
    block_count = length // block_rows

    def block_scores(block_index):
        row_start = block_index * block_rows
        allowed = (positions[None, :] <= positions[:, None]) & (
            segments[None, :] == segments[:, None]
        )
        score_one = (
            jnp.einsum("ihd,thd->hit", query_one, key_one, preferred_element_type=jnp.float32)
            * score_scale
        )
        score_two = (
            jnp.einsum("ihd,thd->hit", query_two, key_two, preferred_element_type=jnp.float32)
            * score_scale
        )
        score_one = jnp.where(allowed[None], score_one, MASKED)
        score_two = jnp.where(allowed[None], score_two, MASKED)
        return (row_start, query_one, query_two, score_one, score_two)

    def forward_block(block_index):
        row_start, q_one, q_two, score_one, score_two = block_scores(block_index)
        top_one = jnp.max(score_one, -1, keepdims=True)
        top_two = jnp.max(score_two, -1, keepdims=True)
        expo_one = jnp.exp(score_one - top_one)
        expo_two = jnp.exp(score_two - top_two)
        total_one = jnp.sum(expo_one, -1, keepdims=True)
        total_two = jnp.sum(expo_two, -1, keepdims=True)
        mixture = (expo_one / total_one - lambda_value * (expo_two / total_two)).astype(
            jnp.bfloat16
        )
        block_out = jnp.einsum("hit,the->ihe", mixture, values, preferred_element_type=jnp.float32)
        return (
            block_out,
            (top_one + jnp.log(total_one))[..., 0],
            (top_two + jnp.log(total_two))[..., 0],
        )

    block_outs, lse_one, lse_two = lax.map(forward_block, jnp.arange(block_count))
    heads_out = block_outs.reshape(length, HEADS, 2 * HD)
    scale_head = rms_scale(heads_out, 1e-05)
    normed_head = heads_out * scale_head
    heads_low = (
        (normed_head * gain_head * (1.0 - LAMBDA_INIT)).reshape(length, D).astype(jnp.bfloat16)
    )
    residual_mid = residual_in + jnp.dot(
        heads_low, attn_full[:, 3 * D : 4 * D], preferred_element_type=jnp.float32
    )
    scale_mid = rms_scale(residual_mid, 1e-06)
    normed_mid = residual_mid * scale_mid
    mid_low = (normed_mid * gain_mid).astype(jnp.bfloat16)
    ffn_full = lax.all_gather(ffn_low, "fsdp", axis=0, tiled=True)
    gate_up = jnp.dot(mid_low, ffn_full[:, 0 : 2 * FF], preferred_element_type=jnp.float32)
    gate_proj = gate_up[:, 0:FF]
    up_proj = gate_up[:, FF : 2 * FF]
    sigmoid_gate = jax.nn.sigmoid(gate_proj)
    activated = gate_proj * sigmoid_gate
    hidden = (activated * up_proj).astype(jnp.bfloat16)
    ffn_out = contract_cols(hidden, ffn_full[:, 2 * FF : 3 * FF])
    mixed = (residual_mid + ffn_out).astype(jnp.bfloat16)
    loss_weights = 1.0 + NEEDLE * needle_mask.astype(jnp.float32)
    weight_total = lax.psum(jnp.sum(loss_weights), ("replica", "fsdp"))
    everyone = length * lax.axis_size(("replica", "fsdp"))
    grad_out = cotangent.astype(jnp.float32) * (loss_weights * (everyone / weight_total))[:, None]
    ffn_back = lax.all_gather(ffn_low, "fsdp", axis=0, tiled=True)
    attn_back = None
    grad_ffn_low = grad_out.astype(jnp.bfloat16)
    grad_hidden = jnp.dot(
        grad_ffn_low, ffn_back[:, 2 * FF : 3 * FF], preferred_element_type=jnp.float32
    )
    grad_gate = grad_hidden * up_proj * (sigmoid_gate * (1.0 + gate_proj * (1.0 - sigmoid_gate)))
    grad_up = grad_hidden * activated
    grad_gu = jnp.concatenate([grad_gate, grad_up], 1).astype(jnp.bfloat16)
    grad_mid_low = contract_cols(grad_gu, ffn_back[:, 0 : 2 * FF])
    ffn_grad = lax.psum_scatter(
        jnp.concatenate([contract_rows(mid_low, grad_gu), contract_rows(grad_ffn_low, hidden)], 1),
        "fsdp",
        scatter_dimension=0,
        tiled=True,
    )
    grad_gain_mid = jnp.sum(grad_mid_low * normed_mid, 0)
    grad_mid = grad_out + norm_back(grad_mid_low * gain_mid, normed_mid, scale_mid)
    attn_back = lax.all_gather(attn_low, "fsdp", axis=0, tiled=True)
    grad_attn_low = grad_mid.astype(jnp.bfloat16)
    grad_heads = contract_cols(grad_attn_low, attn_back[:, 3 * D : 4 * D]).reshape(
        length, HEADS, 2 * HD
    )
    grad_gain_head = jnp.sum(grad_heads * normed_head * (1.0 - LAMBDA_INIT), (0, 1))
    grad_normed_head = grad_heads * gain_head * (1.0 - LAMBDA_INIT)
    grad_head_out = norm_back(grad_normed_head, normed_head, scale_head).astype(jnp.bfloat16)

    def backward_block(totals, block_index):
        row_start, q_one, q_two, score_one, score_two = block_scores(block_index)
        prob_one = jnp.exp(score_one - lse_one[block_index][..., None])
        prob_two = jnp.exp(score_two - lse_two[block_index][..., None])
        mixture = (prob_one - lambda_value * prob_two).astype(jnp.bfloat16)
        grad_values_part = jnp.einsum(
            "hit,ihe->the", mixture, grad_head_out, preferred_element_type=jnp.float32
        )
        grad_mix = jnp.einsum(
            "ihe,the->hit", grad_head_out, values, preferred_element_type=jnp.float32
        )
        grad_lambda_part = -jnp.sum(grad_mix * prob_two)
        grad_score_one = prob_one * (grad_mix - jnp.sum(grad_mix * prob_one, -1, keepdims=True))
        minus_mix = -lambda_value * grad_mix
        grad_score_two = prob_two * (minus_mix - jnp.sum(minus_mix * prob_two, -1, keepdims=True))
        low_one = grad_score_one.astype(jnp.bfloat16)
        low_two = grad_score_two.astype(jnp.bfloat16)
        grad_q_one = (
            jnp.einsum("hit,thd->ihd", low_one, key_one, preferred_element_type=jnp.float32)
            * score_scale
        )
        grad_q_two = (
            jnp.einsum("hit,thd->ihd", low_two, key_two, preferred_element_type=jnp.float32)
            * score_scale
        )
        grad_k_one = (
            jnp.einsum("hit,ihd->thd", low_one, q_one, preferred_element_type=jnp.float32)
            * score_scale
        )
        grad_k_two = (
            jnp.einsum("hit,ihd->thd", low_two, q_two, preferred_element_type=jnp.float32)
            * score_scale
        )
        new_totals = (
            totals[0] + grad_k_one,
            totals[1] + grad_k_two,
            totals[2] + grad_values_part,
            totals[3] + grad_lambda_part,
        )
        return (new_totals, (grad_q_one, grad_q_two))

    start_totals = (
        jnp.zeros((length, HEADS, HD), jnp.float32),
        jnp.zeros((length, HEADS, HD), jnp.float32),
        jnp.zeros((length, HEADS, 2 * HD), jnp.float32),
        jnp.zeros((), jnp.float32),
    )
    totals, query_grads = lax.scan(backward_block, start_totals, jnp.arange(block_count))
    grad_key_one, grad_key_two, grad_values, grad_lambda = totals
    grad_query = jnp.stack(
        [query_grads[0].reshape(length, HEADS, HD), query_grads[1].reshape(length, HEADS, HD)], 2
    )
    grad_keys = jnp.stack([grad_key_one, grad_key_two], 2)
    grad_qkv = jnp.concatenate(
        [
            grad_query.reshape(length, D),
            grad_keys.reshape(length, D),
            grad_values.reshape(length, D),
        ],
        1,
    ).astype(jnp.bfloat16)
    grad_in_low = contract_cols(grad_qkv, attn_back[:, 0 : 3 * D])
    attn_grad = lax.psum_scatter(
        jnp.concatenate(
            [contract_rows(normed_low, grad_qkv), contract_rows(heads_low, grad_attn_low)], 1
        ),
        "fsdp",
        scatter_dimension=0,
        tiled=True,
    )
    grad_gain_in = jnp.sum(grad_in_low * normed_in, 0)
    grad_tokens = grad_mid + norm_back(grad_in_low * gain_in, normed_in, scale_in)
    vector_local = jnp.concatenate(
        [
            grad_gain_in,
            grad_gain_mid,
            grad_gain_head,
            grad_lambda * exp_one * lambda_k_one,
            grad_lambda * exp_one * lambda_q_one,
            -grad_lambda * exp_two * lambda_k_two,
            -grad_lambda * exp_two * lambda_q_two,
        ]
    )
    merged_attn = attn_grad + DECAY_ERROR * attn_error[0]
    merged_ffn = ffn_grad + DECAY_ERROR * ffn_error[0]
    left_attn = lax.dot_general(
        merged_attn, attn_start[0], (((1,), (1,)), ((), ())), precision=HIGHEST
    )
    left_ffn = lax.dot_general(
        merged_ffn, ffn_start[0], (((1,), (1,)), ((), ())), precision=HIGHEST
    )
    vector_grad = lax.psum(vector_local, ("replica", "fsdp"))
    left_attn_sum, left_ffn_sum = lax.psum((left_attn, left_ffn), "replica")
    ortho_attn = orthonormal(left_attn_sum)
    ortho_ffn = orthonormal(left_ffn_sum)
    right_attn = lax.dot_general(
        ortho_attn, merged_attn, (((0,), (0,)), ((), ())), precision=HIGHEST
    )
    right_ffn = lax.dot_general(ortho_ffn, merged_ffn, (((0,), (0,)), ((), ())), precision=HIGHEST)
    right_attn_sum, right_ffn_sum = (
        lax.psum(right_attn.astype(jnp.bfloat16), "replica").astype(jnp.float32),
        lax.psum(right_ffn.astype(jnp.bfloat16), "replica").astype(jnp.float32),
    )
    copies = lax.axis_size("replica")
    right_attn_mean = right_attn_sum / copies
    right_ffn_mean = right_ffn_sum / copies
    approx_attn = jnp.dot(ortho_attn, right_attn_mean, precision=HIGHEST)
    approx_ffn = jnp.dot(ortho_ffn, right_ffn_mean, precision=HIGHEST)
    attn_error_new = merged_attn - approx_attn
    ffn_error_new = merged_ffn - approx_ffn
    attn_momentum_new = MOMENTUM * attn_momentum + (1.0 - MOMENTUM) * approx_attn
    ffn_momentum_new = MOMENTUM * ffn_momentum + (1.0 - MOMENTUM) * approx_ffn
    attn_weight_new = attn_weight - RATE_MATRIX * attn_momentum_new
    ffn_weight_new = ffn_weight - RATE_MATRIX * ffn_momentum_new
    vector_momentum_new = MOMENTUM * vector_momentum + (1.0 - MOMENTUM) * vector_grad
    vector_new = vector_params - RATE_VECTOR * vector_momentum_new
    return (
        mixed,
        grad_tokens,
        attn_grad[None],
        ffn_grad[None],
        ortho_attn.T,
        ortho_ffn.T,
        right_attn_mean[None],
        right_ffn_mean[None],
        attn_error_new[None],
        ffn_error_new[None],
        attn_momentum_new,
        ffn_momentum_new,
        attn_weight_new,
        ffn_weight_new,
        vector_momentum_new,
        vector_new,
    )


def solution(mesh):
    in_specs = (
        P(("replica", "fsdp"), None),
        P(("replica", "fsdp"), None),
        P(("replica", "fsdp")),
        P(("replica", "fsdp"), None),
        P("fsdp", None),
        P("fsdp", None),
        P(),
        P("replica", "fsdp", None),
        P("replica", "fsdp", None),
        P("fsdp", None),
        P("fsdp", None),
        P("fsdp", None, None),
        P("fsdp", None, None),
        P(),
    )
    out_specs = (
        P(("replica", "fsdp"), None),
        P(("replica", "fsdp"), None),
        P("replica", "fsdp", None),
        P("replica", "fsdp", None),
        P(None, "fsdp"),
        P(None, "fsdp"),
        P("fsdp", None, None),
        P("fsdp", None, None),
        P("replica", "fsdp", None),
        P("replica", "fsdp", None),
        P("fsdp", None),
        P("fsdp", None),
        P("fsdp", None),
        P("fsdp", None),
        P(),
        P(),
    )
    return jax.shard_map(local, mesh=mesh, in_specs=in_specs, out_specs=out_specs, check_vma=False)
```

profile of v0, /device:TPU:0, one launch (start us, length us, event | category | flops | bytes accessed | tf_op | source)
XLA Modules:
  0.0 1764.5 jit_solution(14240966462571077443)
XLA Ops:
  7.2 2.9 convert_element_type.77
  10.2 4.1 convert_element_type.83
  15.0 43.4 %psum.42 = f32[]{:T(128)} all-reduce(f32[]{:T(128)} %fusion.78), channel_id=1, replica_groups=mesh['replica'=2,'fsdp'=16] {'replica','fsdp'}, use_global_device_ids=true, to_apply=%region_10.11 | all-reduce | flops 1 | bytes 8 | tf_op jit(solution)/shard_map/psum | solution.py:161
  62.5 50.6 %all-gather.3.cloned.1.call-done = bf16[1536,6144]{1,0:T(8,128)(2,1)} async-done(((bf16[96,6144]{1,0:T(8,128)(2,1)}), bf16[1536,6144]{1,0:T(8,128)(2,1)}) %all-gather.3.cloned.1.call-update) | async-done | bytes 18874384 | tf_op jit(solution)/shard_map/all_gather | solution.py:80
  113.1 11.0 fusion.16
  127.9 2.3 copy.46
  130.2 3.3 fusion.28
  133.6 9.2 fusion.8
  142.8 7.5 fusion.9
  150.3 10.4 fusion.43
  162.2 7.3 multiply_reduce_fusion.7
  170.2 133.0 %all-gather.5.cloned.1.call-done = bf16[1536,12288]{1,0:T(8,128)(2,1)} async-done(((bf16[96,12288]{1,0:T(8,128)(2,1)}), bf16[1536,12288]{1,0:T(8,128)(2,1)}) %all-gather.5.cloned.1.call-update) | async-done | bytes 37748752 | tf_op jit(solution)/shard_map/all_gather | solution.py:151
  303.2 22.2 %fusion.2 = f32[512,8192]{1,0:T(8,128)} fusion(bf16[1536,12288]{1,0:T(8,128)(2,1)} %all-gather.5.cloned.1.call-done, f32[512,1536]{1,0:T(8,128)} %get-tuple-element.273, f32[1536]{0:T(1024)S(1)} %get-tuple-element.265, f32[512]{0:T(512)S(1)} %add_rsqrt_fusion.1), kind=kOutput, calls=%fused_computation.4 | convolution fusion | flops 12887261184 | bytes 45096960 | tf_op jit(solution)/shard_map/dot_general | solution.py:152
  325.4 19.6 %multiply_convert_fusion.3 = (bf16[512,4096]{1,0:T(8,128)(2,1)}, bf16[512,4096]{1,0:T(8,128)(2,1)}, bf16[512,4096]{1,0:T(8,128)(2,1)}) fusion(f32[512,8192]{1,0:T(8,128)} %fusion.2, bf16[1536,12288]{1,0:T(8,128)(2,1)} %all-gather.5.cloned.1.call-done, bf16[512,1536]{1,0:T(8,128)(2,1)} %param.15, f32[512]{0:T(512)S(1)} %fusion.77), kind=kOutput, calls=%fused_computation.32 | convolution fusion | flops 6476267520 | bytes 43517952 | tf_op jit(solution)/shard_map/dot_general | solution.py:167
  344.9 21.7 %multiply_reduce_fusion.4 = (f32[1536]{0:T(1024)}, f32[512]{0:T(512)}, f32[512,1536]{1,0:T(8,128)}) fusion(f32[512,1536]{1,0:T(8,128)} %get-tuple-element.273, f32[512]{0:T(512)S(1)} %add_rsqrt_fusion.1, f32[1536]{0:T(1024)S(1)} %get-tuple-element.265, bf16[1536,12288]{1,0:T(8,128)(2,1)} %all-gather.5.cloned.1.call-done, ...), kind=kOutput, calls=%fused_computation.73 | convolution fusion | flops 12906395648 | bytes 39862272 | tf_op jit(solution)/shard_map/dot_general | solution.py:37
  367.3 4.2 multiply_add_fusion.1
  371.6 5.9 fusion.29
  377.6 1.8 multiply_reduce_fusion.3
  379.4 2.2 multiply_convert_fusion.5
  381.6 10.4 fusion.51
  392.0 17.5 multiply_reduce_fusion
  409.5 14.7 multiply_convert_fusion.1
  424.3 2.0 fusion.55
  427.4 2.0 fusion.54
  431.8 5.1 fusion.57
  440.1 16.6 fusion.50
  456.6 24.9 %pad_maximum_fusion.1 = f32[1536,6144]{1,0:T(8,128)} fusion(f32[1536,1536]{1,0:T(8,128)} %fusion.57, f32[1536,4608]{1,0:T(8,128)} %fusion.50), kind=kLoop, calls=%fused_computation.1 | loop fusion | flops 9437184 | bytes 75497472 | tf_op jit(solution)/shard_map/concatenate | solution.py:254
  481.6 20.0 %fusion.62 = f32[1536,4096]{1,0:T(8,128)} fusion(bf16[512,4096]{1,0:T(8,128)(2,1)} %get-tuple-element.253, bf16[512,1536]{1,0:T(8,128)(2,1)} %param.15, f32[512]{0:T(512)} %copy-done.42), kind=kOutput, calls=%fused_computation.112 | convolution fusion | flops 6444810240 | bytes 30935040 | tf_op jit(solution)/shard_map/dot_general | solution.py:31
  501.7 34.8 %fusion.23 = f32[1536,8192]{1,0:T(8,128)} fusion(bf16[512,4096]{1,0:T(8,128)(2,1)} %get-tuple-element.252, bf16[512,4096]{1,0:T(8,128)(2,1)} %get-tuple-element.251, f32[512,1536]{1,0:T(8,128)S(1)} %copy-done.9, f32[1536]{0:T(1024)S(1)} %get-tuple-element.265, f32[512]{0:T(512)S(1)} %add_rsqrt_fusion.1), kind=kOutput, calls=%fused_computation.43 | convolution fusion | flops 12904038400 | bytes 61874176 | tf_op jit(solution)/shard_map/dot_general | solution.py:31
  536.5 50.2 %pad_maximum_fusion = f32[1536,12288]{1,0:T(8,128)} fusion(f32[1536,4096]{1,0:T(8,128)} %fusion.62, f32[1536,8192]{1,0:T(8,128)} %fusion.23), kind=kLoop, calls=%fused_computation | loop fusion | flops 18874368 | bytes 150994944 | tf_op jit(solution)/shard_map/concatenate | solution.py:175
  588.2 17.4 fusion.41
  606.4 5.0 fusion.40
  611.9 10.9 fusion.47
  622.8 226.7 %reduce-scatter.3.cloned.1.call-done = f32[96,6144]{1,0:T(8,128)} async-done(((f32[1536,6144]{1,0:T(8,128)}), f32[96,6144]{1,0:T(8,128)}) %reduce-scatter.3.cloned.1.call-update) | async-done | bytes 2359312 | tf_op jit(solution)/shard_map/reduce_scatter | solution.py:253
  849.6 3.6 fusion.71
  853.2 704.3 %reduce-scatter.5.cloned.1.call-done = f32[96,12288]{1,0:T(8,128)} async-done(((f32[1536,12288]{1,0:T(8,128)}), f32[96,12288]{1,0:T(8,128)}) %reduce-scatter.5.cloned.1.call-update) | async-done | bytes 4718608 | tf_op jit(solution)/shard_map/reduce_scatter | solution.py:174
  1557.5 6.3 fusion.67
  1563.7 5.0 all-reduce
  1572.6 1.9 multiply_reduce_fusion.63
  1574.5 4.6 multiply_reduce_fusion.43
  1579.7 4.5 multiply_reduce_fusion.42
  1584.3 1.9 multiply_reduce_fusion.59
  1588.5 5.1 multiply_reduce_fusion.41
  1594.2 3.2 multiply_reduce_fusion.40
  1597.4 1.8 multiply_reduce_fusion.50
  1599.9 3.2 multiply_reduce_fusion.39
  1606.3 1.8 multiply_reduce_fusion.37
  1608.7 17.7 %subtract_multiply_fusion.7 = (f32[96,1]{0,1:T(1,128)S(1)}, f32[96,1]{0,1:T(1,128)S(1)}, f32[96,1]{0,1:T(1,128)S(1)}, f32[96,1]{0,1:T(1,128)S(1)}, f32[96,1]{0,1...) fusion(f32[96,1]{0,1:T(1,128)S(1)} %get-tuple-element.250, f32[]{:T(128)S(6)} %rsqrt.98, ...), kind=kLoop, calls=%fused_computation.251 | loop fusion | flops 6048 | bytes 5900 | tf_op jit(solution)/shard_map/mul | solution.py:48
  1630.2 1.9 multiply_reduce_fusion.34
  1632.1 4.6 multiply_reduce_fusion.14
  1637.4 4.5 multiply_reduce_fusion.13
  1641.9 1.9 multiply_reduce_fusion.30
  1646.1 5.1 multiply_reduce_fusion.12
  1651.9 3.2 multiply_reduce_fusion.11
  1655.0 1.8 multiply_reduce_fusion.21
  1657.5 3.2 multiply_reduce_fusion.10
  1663.9 1.8 multiply_reduce_fusion.8
  1666.4 17.7 %subtract_multiply_fusion = (f32[96,1]{0,1:T(1,128)S(1)}, f32[96,1]{0,1:T(1,128)S(1)}, f32[96,1]{0,1:T(1,128)S(1)}, f32[96,1]{0,1:T(1,128)S(1)}, f32[96,1]{0,1:T...) fusion(f32[96,1]{0,1:T(1,128)S(1)} %get-tuple-element.216, f32[]{:T(128)S(6)} %rsqrt.106, ...), kind=kLoop, calls=%fused_computation.195 | loop fusion | flops 6048 | bytes 5900 | tf_op jit(solution)/shard_map/mul | solution.py:48
  1684.1 3.8 convolution_convert_fusion.1
  1688.0 5.8 convolution_convert_fusion
  1694.0 39.8 %psum.47 = f32[3456]{0:T(1024)S(1)} all-reduce(f32[3456]{0:T(1024)S(1)} %concatenate.21), channel_id=1, replica_groups=mesh['replica'=2,'fsdp'=16] {'replica','fsdp'}, use_global_device_ids=true, to_apply=%region_98.99 | all-reduce | flops 3456 | bytes 27648 | tf_op jit(solution)/shard_map/psum | solution.py:282
  1736.0 1.8 fusion.70
  1737.8 8.9 multiply_subtract_fusion.1
  1746.8 10.8 multiply_subtract_fusion
  (172 shorter events, 33.4 us)
Async XLA Ops:
  7.2 1550.3 %copy-start = (f32[1,8,12288]{2,1,0:T(8,128)S(1)}, f32[1,8,12288]{2,1,0:T(8,128)}, u32[]{:S(2)}) copy-start(f32[1,8,12288]{2,1,0:T(8,128)} %param.26) | copy-start | bytes 1179652
  7.2 105.9 %all-gather.3.cloned.1.call-start = ((), (), s32[]{:S(2)}) async-start(), calls=%async_computation.2 | async-start | bytes 20054016 | tf_op jit(solution)/shard_map/all_gather | solution.py:80
  10.1 4.3 copy-start.45
  10.1 48.2 %copy-start.30 = (f32[3456]{0:T(1024)S(1)}, f32[3456]{0:T(1024)}, u32[]{:S(2)}) copy-start(f32[3456]{0:T(1024)} %param.20) | copy-start | bytes 41476
  10.1 51.0 %copy-start.15 = (bf16[512,1536]{1,0:T(8,128)(2,1)S(1)}, bf16[512,1536]{1,0:T(8,128)(2,1)}, u32[]{:S(2)}) copy-start(bf16[512,1536]{1,0:T(8,128)(2,1)} %param.14) | copy-start | bytes 4718596
  10.2 51.5 %copy-start.39 = (s32[1,512]{1,0:T(1,128)S(1)}, s32[1,512]{1,0:T(1,128)}, u32[]{:S(2)}) copy-start(s32[1,512]{1,0:T(1,128)} %param.17) | copy-start | bytes 6148
  10.2 293.0 %all-gather.5.cloned.1.call-start = ((), (), s32[]{:S(2)}) async-start(), calls=%async_computation.3 | async-start | bytes 40108032 | tf_op jit(solution)/shard_map/all_gather | solution.py:151
  14.4 835.2 %reduce-scatter.3.cloned.1.call-start = ((), (), s32[]{:S(2)}) async-start(), calls=%async_computation.4 | async-start | bytes 40108032 | tf_op jit(solution)/shard_map/reduce_scatter | solution.py:253
  58.4 102.4 %copy-start.46 = (f32[128]{0:T(128)}, f32[128]{0:T(128)S(1)}, u32[]{:S(2)}) copy-start(f32[128]{0:T(128)S(1)} %slice.125) | copy-start | bytes 1540
  61.5 51.6 %copy-start.40 = (f32[512]{0:T(512)}, f32[512]{0:T(512)S(1)}, u32[]{:S(2)}) copy-start(f32[512]{0:T(512)S(1)} %add_rsqrt_fusion.2) | copy-start | bytes 6148
  61.6 305.7 %copy-start.42 = (f32[512]{0:T(512)}, f32[512]{0:T(512)S(1)}, u32[]{:S(2)}) copy-start(f32[512]{0:T(512)S(1)} %fusion.77) | copy-start | bytes 6148
  61.6 51.5 %copy-start.35 = (f32[1536]{0:T(1024)}, f32[1536]{0:T(1024)S(1)}, u32[]{:S(2)}) copy-start(f32[1536]{0:T(1024)S(1)} %get-tuple-element.266) | copy-start | bytes 18436
  127.9 5.6 copy-start.7
  130.2 3.3 copy-start.11
  130.2 3.3 copy-start.18
  133.5 16.8 copy-start.1
  160.8 1.4 copy-start.16
  160.8 0.6 copy-start.25
  162.0 7.5 copy-start.13
  162.2 7.3 copy-start.34
  371.5 6.0 copy-start.3
  371.6 6.0 copy-start.26
  371.6 6.0 copy-start.47
  371.6 10.0 slice-start
  371.6 10.0 slice-start.1
  377.5 4.0 slice-start.2
  379.4 2.2 copy-start.19
  381.6 10.5 copy-start.21
  381.6 10.4 copy-start.28
  381.6 10.4 copy-start.29
  392.0 17.5 copy-start.20
  409.5 14.7 copy-start.12
  424.2 2.0 copy-start.8
  429.4 1.9 copy-start.4
  429.4 2.4 copy-start.14
  437.0 2.1 copy-start.17
  437.0 2.1 copy-start.36
  437.0 2.1 copy-start.41
  437.0 3.0 copy-start.49
  437.2 19.5 %copy-start.22 = (bf16[512,12,2,64]{0,3,2,1:T(8,128)(2,1)}, bf16[512,12,2,64]{0,3,2,1:T(8,128)(2,1)S(1)}, u32[]{:S(2)}) copy-start(bf16[512,12,2,64]{0,3,2,1:T(8,128)(2,1)S(1)} %copy.61) | copy-start | bytes 4718596
  437.4 19.2 %copy-start.23 = (bf16[512,12,2,64]{0,3,2,1:T(8,128)(2,1)}, bf16[512,12,2,64]{0,3,2,1:T(8,128)(2,1)S(1)}, u32[]{:S(2)}) copy-start(bf16[512,12,2,64]{0,3,2,1:T(8,128)(2,1)S(1)} %copy.58) | copy-start | bytes 4718596
  481.6 1075.9 %reduce-scatter.5.cloned.1.call-start = ((), (), s32[]{:S(2)}) async-start(), calls=%async_computation.5 | async-start | bytes 80216064 | tf_op jit(solution)/shard_map/reduce_scatter | solution.py:174
  481.6 20.0 %copy-start.9 = (f32[512,1536]{1,0:T(8,128)S(1)}, f32[512,1536]{1,0:T(8,128)}, u32[]{:S(2)}) copy-start(f32[512,1536]{1,0:T(8,128)} %get-tuple-element.273) | copy-start | bytes 9437188
  586.7 1.5 copy-start.37
  586.7 1147.7 %all-reduce.4.cloned.1.call-start = ((), (), s32[]{:S(2)}) async-start(), calls=%async_computation.6 | async-start | bytes 589824 | tf_op jit(solution)/shard_map/psum | solution.py:291
  588.2 18.1 %copy-start.5 = (f32[512,1536]{1,0:T(8,128)S(1)}, f32[512,1536]{1,0:T(8,128)}, u32[]{:S(2)}) copy-start(f32[512,1536]{1,0:T(8,128)} %copy-done.3) | copy-start | bytes 9437188
  606.4 5.0 copy-start.10
  606.4 5.5 copy-start.50
  611.9 237.7 %copy-start.6 = (f32[1,96,6144]{2,1,0:T(8,128)S(1)}, f32[1,96,6144]{2,1,0:T(8,128)}, u32[]{:S(2)}) copy-start(f32[1,96,6144]{2,1,0:T(8,128)} %param.21) | copy-start | bytes 7077892
  611.9 237.7 %copy-start.27 = (f32[1,8,6144]{2,1,0:T(8,128)S(1)}, f32[1,8,6144]{2,1,0:T(8,128)}, u32[]{:S(2)}) copy-start(f32[1,8,6144]{2,1,0:T(8,128)} %param.25) | copy-start | bytes 589828
  1684.1 53.7 %copy-start.33 = (f32[96,8]{0,1:T(8,128)}, f32[96,8]{0,1:T(8,128)S(1)}, u32[]{:S(2)}) copy-start(f32[96,8]{0,1:T(8,128)S(1)} %stack.20) | copy-start | bytes 9220
  1684.1 62.6 %copy-start.32 = (f32[96,8]{0,1:T(8,128)}, f32[96,8]{0,1:T(8,128)S(1)}, u32[]{:S(2)}) copy-start(f32[96,8]{0,1:T(8,128)S(1)} %stack.21) | copy-start | bytes 9220
  1684.1 3.8 copy-start.2
  1687.9 5.9 copy-start.31
  1687.9 5.9 copy-start.43
  1687.9 5.9 copy-start.44
  1688.0 5.9 copy-start.48
  1688.0 45.8 %copy-start.38 = (f32[3456]{0:T(1024)S(1)}, f32[3456]{0:T(1024)}, u32[]{:S(2)}) copy-start(f32[3456]{0:T(1024)} %param.27) | copy-start | bytes 41476
  1688.0 58.8 %slice-start.3 = ((s8[4718592]{0:T(1024)(128)(4,1)}), s8[524288]{0:T(1024)(128)(4,1)S(1)}, s32[]{:S(2)}) async-start(s8[4718592]{0:T(1024)(128)(4,1)} %bitcast.292), calls=%async_computation.10 | async-start | bytes 1048576
  1736.0 10.8 slice-start.5
  1737.8 8.9 slice-start.4
  1737.8 8.9 slice-start.6
  1737.8 8.9 copy-start.24
Sparse Core Ops, SparseCore 0:
  10.2 102.8 all-gather.2
  115.3 187.8 all-gather.4
  481.7 367.8 reduce-scatter.2
  854.2 703.2 reduce-scatter.4
  1693.9 23.0 all-reduce.3
where the time goes:
time: 1770 us; the launch traced here: 1760 us
  waiting for transfers between devices  1110 us (63%)
  matrix products  289 us (16%)
  other arithmetic  232 us (13%)
  blocking collectives  88.1 us (5%)
  between operations  28.9 us (2%)
    reduce_scatter x1, waiting for transfers between devices, local(): lax.psum_scatter(jnp.concatenate([contract_rows(mid_low, grad_gu), contra...  704 us
    reduce_scatter x1, waiting for transfers between devices, local(): lax.psum_scatter(jnp.concatenate([contract_rows(normed_low, grad_qkv), co...  227 us
    all_gather x1, waiting for transfers between devices, local(): ffn_full = lax.all_gather(ffn_low, 'fsdp', axis=0, tiled=True)  133 us
    dot_general x4, matrix products, contract_rows(): lax.dot_general(left, right, (((0,), (0,)), ((), ())), preferred_element_...  76.5 us
    dot_general x4, matrix products, contract_cols(): lax.dot_general(left, right, (((1,), (1,)), ((), ())), preferred_element_...  55.9 us
    reduce_sum x20, other arithmetic, orthonormal(): column = column - jnp.sum(earlier * column, -1, keepdims=True) * earlier  54.5 us
    all_gather x1, waiting for transfers between devices, local(): attn_full = lax.all_gather(attn_low, 'fsdp', axis=0, tiled=True)  50.6 us
    concatenate x1, other arithmetic, local(): jnp.concatenate([contract_rows(mid_low, grad_gu), contract_rows(grad_ffn_...  50.2 us
  transfers between devices with their start and end apart: 5, of which 4 were waited for; matrix products, arithmetic and copies ran while one was open for 12% of the time, Pallas kernels for 0%

commit v1 on v0

v1 whole, which is shorter than its diff:
```python
from functools import partial

import jax
import jax.numpy as jnp
from jax import lax
from jax.experimental import pallas as pl
from jax.experimental.pallas import tpu as pltpu
from jax.sharding import PartitionSpec as P

D = 1536
HEADS = 12
HD = 64
FF = 4096

NEEDLE = 3.0
LAMBDA_INIT = 0.2
KEEP = 1.0 - LAMBDA_INIT
DECAY_ERROR = 0.5
MOMENTUM = 0.9
RATE_MATRIX = 0.005
RATE_VECTOR = 0.02
MASKED = -1e30
HIGHEST = lax.Precision.HIGHEST
BF16 = jnp.bfloat16
F32 = jnp.float32

GROUP = 4
BLOCK = 128
REACH = 256
WIDTH = 2 * HD
OWN_HEADS = HEADS // GROUP
ATTN_Q = D // GROUP
FF_Q = FF // GROUP


def rms_scale(values, epsilon):
    return lax.rsqrt(jnp.mean(values * values, -1, keepdims=True) + epsilon)


def norm_back(grad_normed, normed, scale):
    return scale * (grad_normed - normed * jnp.mean(grad_normed * normed, -1, keepdims=True))


def dot(left, right, left_dim=1, right_dim=0, **kinds):
    return lax.dot_general(
        left, right, (((left_dim,), (right_dim,)), ((), ())), preferred_element_type=F32, **kinds
    )


def score_parts(qkv_ref, head, block, reach, lam, bias):
    rows = pl.ds(block * BLOCK, BLOCK)
    lane = lax.broadcasted_iota(jnp.int32, (1, WIDTH), 1)
    first = lane < HD
    query = qkv_ref[rows, head * WIDTH : (head + 1) * WIDTH] * BF16(HD**-0.5)
    key = qkv_ref[reach, ATTN_Q + head * WIDTH : ATTN_Q + (head + 1) * WIDTH]
    value = qkv_ref[reach, 2 * ATTN_Q + head * WIDTH : 2 * ATTN_Q + (head + 1) * WIDTH]
    zero = jnp.zeros((), BF16)
    query_one = jnp.where(first, query, zero)
    query_two = jnp.where(first, zero, query)
    probs = []
    for half in (query_one, query_two):
        score = dot(half, key, 1, 1) + bias
        expo = jnp.exp(score - jnp.max(score, -1, keepdims=True))
        probs.append(expo * (1.0 / jnp.sum(expo, -1, keepdims=True)))
    mixture = (probs[0] - lam * probs[1]).astype(BF16)
    return query_one, query_two, key, value, probs[0], probs[1], mixture


def block_bias(seg_q_ref, seg_k_ref, block, low, high):
    rows = lax.broadcasted_iota(jnp.int32, (BLOCK, high - low), 0) + block * BLOCK
    cols = lax.broadcasted_iota(jnp.int32, (BLOCK, high - low), 1) + low
    same = seg_q_ref[0, block * BLOCK : (block + 1) * BLOCK, :] == seg_k_ref[0, :, low:high]
    return jnp.where((cols <= rows) & same, 0.0, MASKED)


def reach_of(block):
    return max(0, block - REACH // BLOCK) * BLOCK, (block + 1) * BLOCK


def attend_kernel(lam_ref, qkv_ref, seg_q_ref, seg_k_ref, gain_ref, heads_ref):
    lam = lam_ref[0]
    gain = gain_ref[...] * KEEP
    for block in range(qkv_ref.shape[0] // BLOCK):
        low, high = reach_of(block)
        bias = block_bias(seg_q_ref, seg_k_ref, block, low, high)
        for head in range(OWN_HEADS):
            parts = score_parts(qkv_ref, head, block, pl.ds(low, high - low), lam, bias)
            out = dot(parts[6], parts[3])
            normed = out * rms_scale(out, 1e-05)
            heads_ref[pl.ds(block * BLOCK, BLOCK), head * WIDTH : (head + 1) * WIDTH] = (
                normed * gain
            ).astype(BF16)


def attend_back_kernel(
    lam_ref, qkv_ref, seg_q_ref, seg_k_ref, gain_ref, grad_ref, out_ref, stat_ref, dk_ref, dv_ref
):
    lam = lam_ref[0]
    gain = gain_ref[...] * KEEP
    blocks = qkv_ref.shape[0] // BLOCK
    first = lax.broadcasted_iota(jnp.int32, (1, WIDTH), 1) < HD
    zero = jnp.zeros((), BF16)
    gain_total = jnp.zeros((1, WIDTH), F32)
    lam_total = jnp.zeros((1, 1), F32)
    biases = [block_bias(seg_q_ref, seg_k_ref, b, *reach_of(b)) for b in range(blocks)]
    for head in range(OWN_HEADS):
        lanes = slice(head * WIDTH, (head + 1) * WIDTH)
        dk_ref[...] = jnp.zeros_like(dk_ref)
        dv_ref[...] = jnp.zeros_like(dv_ref)
        for block in range(blocks):
            low, high = reach_of(block)
            rows, reach = pl.ds(block * BLOCK, BLOCK), pl.ds(low, high - low)
            query_one, query_two, key, value, prob_one, prob_two, mixture = score_parts(
                qkv_ref, head, block, reach, lam, biases[block]
            )
            out = dot(mixture, value)
            scale = rms_scale(out, 1e-05)
            normed = out * scale
            grad = grad_ref[rows, lanes].astype(F32)
            gain_total = gain_total + jnp.sum(grad * normed, 0, keepdims=True)
            grad_out = norm_back(grad * gain, normed, scale).astype(BF16)
            grad_mix = dot(grad_out, value, 1, 1)
            mean_one = jnp.sum(grad_mix * prob_one, -1, keepdims=True)
            mean_two = jnp.sum(grad_mix * prob_two, -1, keepdims=True)
            lam_total = lam_total - jnp.sum(mean_two, 0, keepdims=True)
            low_one = (prob_one * (grad_mix - mean_one)).astype(BF16)
            low_two = (prob_two * (-lam * (grad_mix - mean_two))).astype(BF16)
            dv_ref[reach, :] += dot(mixture, grad_out, 0, 0)
            dk_ref[reach, :] += dot(low_one, query_one, 0, 0) + dot(low_two, query_two, 0, 0)
            grad_query = dot(low_one, jnp.where(first, key, zero)) + dot(
                low_two, jnp.where(first, zero, key)
            )
            out_ref[rows, lanes] = (grad_query * HD**-0.5).astype(BF16)
        out_ref[:, ATTN_Q + head * WIDTH : ATTN_Q + (head + 1) * WIDTH] = dk_ref[...].astype(BF16)
        out_ref[:, 2 * ATTN_Q + head * WIDTH : 2 * ATTN_Q + (head + 1) * WIDTH] = dv_ref[
            ...
        ].astype(BF16)
    stat_ref[0, 0:1, :] = gain_total * KEEP
    stat_ref[0, 1:2, :] = jnp.broadcast_to(lam_total, (1, WIDTH))
    stat_ref[0, 2:8, :] = jnp.zeros((6, WIDTH), F32)


def attention_specs(length):
    return [
        pl.BlockSpec(memory_space=pltpu.SMEM),
        pl.BlockSpec((length, 3 * ATTN_Q), lambda i: (i, 0)),
        pl.BlockSpec((1, length, 1), lambda i: (i, 0, 0)),
        pl.BlockSpec((1, 1, length), lambda i: (i, 0, 0)),
        pl.BlockSpec((1, WIDTH), lambda i: (0, 0)),
    ]


def attend(lam, qkv, segments, gain):
    length = segments.shape[1]
    return pl.pallas_call(
        attend_kernel,
        grid=(GROUP,),
        in_specs=attention_specs(length),
        out_specs=pl.BlockSpec((length, ATTN_Q), lambda i: (i, 0)),
        out_shape=jax.ShapeDtypeStruct((GROUP * length, ATTN_Q), BF16),
        compiler_params=pltpu.CompilerParams(vmem_limit_bytes=32 * 2**20),
        cost_estimate=pl.CostEstimate(
            flops=GROUP * OWN_HEADS * 2 * 4 * length * 320 * WIDTH,
            bytes_accessed=GROUP * length * 8 * ATTN_Q,
            transcendentals=GROUP * OWN_HEADS * 2 * length * 320,
        ),
        name="attend",
    )(lam, qkv, segments[:, :, None], segments[:, None, :], gain)


def attend_back(lam, qkv, segments, gain, grad):
    length = segments.shape[1]
    return pl.pallas_call(
        attend_back_kernel,
        grid=(GROUP,),
        in_specs=attention_specs(length)
        + [pl.BlockSpec((length, ATTN_Q), lambda i: (i, 0))],
        out_specs=[
            pl.BlockSpec((length, 3 * ATTN_Q), lambda i: (i, 0)),
            pl.BlockSpec((1, 8, WIDTH), lambda i: (i, 0, 0)),
        ],
        out_shape=[
            jax.ShapeDtypeStruct((GROUP * length, 3 * ATTN_Q), BF16),
            jax.ShapeDtypeStruct((GROUP, 8, WIDTH), F32),
        ],
        scratch_shapes=[pltpu.VMEM((length, WIDTH), F32), pltpu.VMEM((length, WIDTH), F32)],
        compiler_params=pltpu.CompilerParams(vmem_limit_bytes=32 * 2**20),
        cost_estimate=pl.CostEstimate(
            flops=GROUP * OWN_HEADS * 2 * 10 * length * 320 * WIDTH,
            bytes_accessed=GROUP * length * 14 * ATTN_Q,
            transcendentals=GROUP * OWN_HEADS * 2 * length * 320,
        ),
        name="attend_back",
    )(lam, qkv, segments[:, :, None], segments[:, None, :], gain, grad)


def orthonormal_kernel(attn_ref, ffn_ref, attn_out_ref, ffn_out_ref):
    for source, target in ((attn_ref, attn_out_ref), (ffn_ref, ffn_out_ref)):
        left = source[...]
        number = lax.broadcasted_iota(jnp.int32, (left.shape[0], 1), 0)
        for step in range(left.shape[0]):
            row = left[step : step + 1]
            row = row * lax.rsqrt(jnp.sum(row * row, -1, keepdims=True))
            share = jnp.sum(left * row, -1, keepdims=True)
            left = jnp.where(
                number > step, left - share * row, jnp.where(number == step, row, left)
            )
        target[...] = left


def orthonormal(attn, ffn):
    kind = jax.ShapeDtypeStruct(attn.shape, F32)
    return pl.pallas_call(orthonormal_kernel, out_shape=[kind, kind], name="orthonormal")(attn, ffn)


def swap(value, bits, shards):
    return lax.ppermute(value, "fsdp", [(f, f ^ bits) for f in range(shards)])


def hop(value, low, high, step):
    pairs = [
        (GROUP * z + j, GROUP * (z + step) + j) for z in range(low, high + 1) for j in range(GROUP)
    ]
    return lax.ppermute(value, "fsdp", pairs)


def cross(value, low, high, shards, copies):
    pairs = [
        (r * shards + GROUP * z + j, (r + 1) % copies * shards + GROUP * z + j)
        for r in range(copies)
        for z in range(low, high + 1)
        for j in range(GROUP)
    ]
    return lax.ppermute(value, ("replica", "fsdp"), pairs)


def arrange(items, member):
    low, high = (member & 1) == 1, (member & 2) == 2
    pairs = [jnp.where(low, items[t ^ 1], items[t]) for t in range(GROUP)]
    return [jnp.where(high, pairs[t ^ 2], pairs[t]) for t in range(GROUP)]


def share_out(items, member, shards):
    mine = arrange(items, member)
    return [mine[0]] + [swap(mine[k], k, shards) for k in range(1, GROUP)]


def gather_group(value, shards):
    beside = swap(value, 1, shards)
    across = swap(value, 2, shards)
    return [value, beside, across, swap(across, 1, shards)]


def gather_rows(block, layer, copy, layers, shards, copies):
    half, cols = block.shape[0] // 2, block.shape[1]
    mine = lax.dynamic_index_in_dim(block.reshape(2, half, cols), copy, 0, False)
    ups, downs = [None], [None]
    up = down = mine
    for step in range(1, layers):
        up = hop(up, step - 1, layers - 2, 1)
        down = hop(down, 1, layers - step, -1)
        ups.append((up, cross(up, step, layers - 1, shards, copies)))
        downs.append((down, cross(down, 0, layers - 1 - step, shards, copies)))
    whole = jnp.zeros((layers, 2, half, cols), block.dtype)
    whole = lax.dynamic_update_slice(
        whole, block.reshape(1, 2, half, cols), (layer, 0, 0, 0)
    )
    for shift in range(1, layers):
        below = layer >= shift
        source = jnp.where(below, layer - shift, layer - shift + layers)
        for part, owner in ((0, copy), (1, 1 - copy)):
            piece = jnp.where(below, ups[shift][part], downs[layers - shift][part])
            whole = lax.dynamic_update_slice(whole, piece[None, None], (source, owner, 0, 0))
    return whole.reshape(layers * 2 * half, cols)


def scatter_rows(partials, layer, layers):
    blocks = partials.reshape(layers, partials.shape[0] // layers, partials.shape[1])

    def block_of(number):
        number = jnp.where(number < 0, number + layers, number)
        number = jnp.where(number >= layers, number - layers, number)
        return lax.dynamic_index_in_dim(blocks, number, 0, False).astype(F32)

    up = down = None
    for step in range(1, layers):
        send_up, send_down = block_of(layer - step), block_of(layer + step)
        if step > 1:
            send_up = send_up + up.astype(F32)
            send_down = send_down + down.astype(F32)
        up = hop(send_up.astype(BF16), 0, min(step - 1, layers - 2), 1)
        down = hop(send_down.astype(BF16), max(layers - step, 1), layers - 1, -1)
    total = block_of(layer)
    if layers > 1:
        total = total + up.astype(F32) + down.astype(F32)
    return total


def own_rows(total, member, shards):
    rows = total.shape[0] // GROUP
    parts = share_out(
        [total[t * rows : (t + 1) * rows].astype(BF16) for t in range(GROUP)], member, shards
    )
    return arrange(parts, member)


def sum_everywhere(value, shards, copies):
    bits = 1
    while bits < shards:
        value = value + swap(value, bits, shards)
        bits *= 2
    return value + cross_all(value, copies)


def cross_all(value, copies):
    return lax.ppermute(value, "replica", [(r, (r + 1) % copies) for r in range(copies)])


def local(
    shards,
    copies,
    tokens,
    cotangent,
    needle_mask,
    segment_ids,
    attn_weight,
    ffn_weight,
    vector_params,
    attn_error,
    ffn_error,
    attn_momentum,
    ffn_momentum,
    attn_start,
    ffn_start,
    vector_momentum,
):
    length = tokens.shape[0]
    layers = shards // GROUP
    place = lax.axis_index("fsdp")
    copy = lax.axis_index("replica")
    layer, member = place // GROUP, place % GROUP

    gain_in = vector_params[0:D]
    gain_mid = vector_params[D : 2 * D]
    gain_head = vector_params[2 * D : 2 * D + 2 * HD]
    lambda_q_one = vector_params[2 * D + 2 * HD : 2 * D + 3 * HD]
    lambda_k_one = vector_params[2 * D + 3 * HD : 2 * D + 4 * HD]
    lambda_q_two = vector_params[2 * D + 4 * HD : 2 * D + 5 * HD]
    lambda_k_two = vector_params[2 * D + 5 * HD : 2 * D + 6 * HD]
    exp_one = jnp.exp(jnp.sum(lambda_q_one * lambda_k_one))
    exp_two = jnp.exp(jnp.sum(lambda_q_two * lambda_k_two))
    lam = (exp_one - exp_two + LAMBDA_INIT).reshape(1)

    gather = partial(
        gather_rows, layer=layer, copy=copy, layers=layers, shards=shards, copies=copies
    )

    def layer_block(weight, sections, width):
        quarters = [
            jnp.concatenate(
                [
                    weight[:, s * GROUP * width + t * width : s * GROUP * width + (t + 1) * width]
                    for s in sections
                ],
                1,
            ).astype(BF16)
            for t in range(GROUP)
        ]
        return jnp.concatenate(arrange(share_out(quarters, member, shards), member), 0)

    qkv_weight = gather(layer_block(attn_weight, (0, 1, 2), ATTN_Q))
    residual_in = tokens.astype(F32)
    scale_in = rms_scale(residual_in, 1e-06)
    normed_in = residual_in * scale_in
    normed_all = jnp.concatenate(gather_group((normed_in * gain_in).astype(BF16), shards), 0)
    segments = jnp.concatenate(gather_group(segment_ids, shards), 0)
    out_weight = lax.all_gather(attn_weight[:, 3 * D :].astype(BF16), "fsdp", axis=0, tiled=True)
    up_weight = gather(layer_block(ffn_weight, (0, 1), FF_Q))
    down_weight = gather(layer_block(ffn_weight, (2,), FF_Q))

    qkv = dot(normed_all, qkv_weight).astype(BF16)
    heads_part = attend(lam, qkv, segments, gain_head[None])
    heads_shares = [heads_part[k * length : (k + 1) * length] for k in range(GROUP)]
    heads_got = [heads_shares[0]] + [swap(heads_shares[k], k, shards) for k in range(1, GROUP)]
    heads_low = jnp.concatenate(arrange(heads_got, member), 1)
    residual_mid = residual_in + dot(heads_low, out_weight)
    scale_mid = rms_scale(residual_mid, 1e-06)
    normed_mid = residual_mid * scale_mid
    mid_all = jnp.concatenate(gather_group((normed_mid * gain_mid).astype(BF16), shards), 0)

    loss_weights = 1.0 + NEEDLE * needle_mask.astype(F32)
    weight_total = sum_everywhere(
        jnp.broadcast_to(jnp.sum(loss_weights), (8, 128)), shards, copies
    )[0, 0]
    everyone = length * shards * copies
    grad_out = cotangent.astype(F32) * (loss_weights * (everyone / weight_total))[:, None]
    grad_out_all = jnp.concatenate(gather_group(grad_out.astype(BF16), shards), 0)

    gate_up = dot(mid_all, up_weight)
    gate_proj, up_proj = gate_up[:, :FF_Q], gate_up[:, FF_Q:]
    sigmoid_gate = jax.nn.sigmoid(gate_proj)
    activated = gate_proj * sigmoid_gate
    hidden = (activated * up_proj).astype(BF16)
    grad_hidden = dot(grad_out_all, down_weight)
    grad_gate = grad_hidden * up_proj * (sigmoid_gate * (1.0 + gate_proj * (1.0 - sigmoid_gate)))
    grad_up = grad_hidden * activated
    grad_gu = jnp.concatenate([grad_gate, grad_up], 1).astype(BF16)

    def sum_group(parts):
        got = [swap(parts[k], 1, shards) for k in (3, 1)]
        across = parts[2].astype(F32) + got[0].astype(F32)
        across = swap(across.astype(BF16), 2, shards)
        return parts[0].astype(F32) + got[1].astype(F32) + across.astype(F32)

    def token_parts(values):
        return [values[k * length : (k + 1) * length] for k in range(GROUP)]

    grad_mid_low = sum_group(token_parts(dot(grad_gu, up_weight, 1, 1).astype(BF16)))
    ffn_out = sum_group(token_parts(dot(hidden, down_weight, 1, 1).astype(BF16)))
    mixed = (residual_mid + ffn_out).astype(BF16)

    down_grad = scatter_rows(dot(grad_out_all, hidden, 0, 0).astype(BF16), layer, layers)
    up_partials = dot(mid_all, grad_gu, 0, 0).astype(BF16)
    gate_grad = scatter_rows(up_partials[:, :FF_Q], layer, layers)
    up_grad = scatter_rows(up_partials[:, FF_Q:], layer, layers)
    ffn_grad = jnp.concatenate(
        sum([own_rows(part, member, shards) for part in (gate_grad, up_grad, down_grad)], []), 1
    ).astype(F32)

    grad_gain_mid = jnp.sum(grad_mid_low * normed_mid, 0)
    grad_mid = grad_out + norm_back(grad_mid_low * gain_mid, normed_mid, scale_mid)
    grad_attn_low = grad_mid.astype(BF16)
    grad_heads = dot(grad_attn_low, out_weight, 1, 1).astype(BF16)
    grad_heads_all = jnp.concatenate(
        share_out(
            [grad_heads[:, t * ATTN_Q : (t + 1) * ATTN_Q] for t in range(GROUP)], member, shards
        ),
        0,
    )
    grad_qkv, stats = attend_back(lam, qkv, segments, gain_head[None], grad_heads_all)
    stats = jnp.sum(stats, 0)
    grad_gain_head, grad_lambda = stats[0], stats[1, 0]

    heads_all = jnp.concatenate(gather_group(heads_low, shards), 0)
    grad_attn_all = jnp.concatenate(
        share_out(
            [grad_attn_low[:, t * ATTN_Q : (t + 1) * ATTN_Q] for t in range(GROUP)], member, shards
        ),
        0,
    )
    out_grad = scatter_rows(dot(heads_all, grad_attn_all, 0, 0).astype(BF16), layer, layers)
    qkv_grad = scatter_rows(dot(normed_all, grad_qkv, 0, 0).astype(BF16), layer, layers)
    qkv_rows = own_rows(qkv_grad, member, shards)
    attn_grad = jnp.concatenate(
        [part[:, s * ATTN_Q : (s + 1) * ATTN_Q] for s in range(3) for part in qkv_rows]
        + own_rows(out_grad, member, shards),
        1,
    ).astype(F32)

    grad_in_low = sum_group(token_parts(dot(grad_qkv, qkv_weight, 1, 1).astype(BF16)))
    grad_gain_in = jnp.sum(grad_in_low * normed_in, 0)
    grad_tokens = grad_mid + norm_back(grad_in_low * gain_in, normed_in, scale_in)

    vector_local = jnp.concatenate(
        [
            grad_gain_in,
            grad_gain_mid,
            grad_gain_head,
            grad_lambda * exp_one * lambda_k_one,
            grad_lambda * exp_one * lambda_q_one,
            -grad_lambda * exp_two * lambda_k_two,
            -grad_lambda * exp_two * lambda_q_two,
        ]
    )
    vector_grad = sum_everywhere(vector_local, shards, copies)

    merged_attn = attn_grad + DECAY_ERROR * attn_error[0]
    merged_ffn = ffn_grad + DECAY_ERROR * ffn_error[0]
    left_attn = dot(attn_start[0], merged_attn, 1, 1, precision=HIGHEST)
    left_ffn = dot(ffn_start[0], merged_ffn, 1, 1, precision=HIGHEST)
    left_attn = left_attn + cross_all(left_attn, copies)
    left_ffn = left_ffn + cross_all(left_ffn, copies)
    ortho_attn, ortho_ffn = orthonormal(left_attn, left_ffn)

    def update(ortho, merged, momentum, weight):
        right = dot(ortho, merged, 1, 0, precision=HIGHEST).astype(BF16)
        other = cross_all(right, copies)
        right = (right.astype(F32) + other.astype(F32)) / copies
        approx = dot(ortho, right, 0, 0, precision=HIGHEST)
        momentum_new = MOMENTUM * momentum + (1.0 - MOMENTUM) * approx
        return right, merged - approx, momentum_new, weight - RATE_MATRIX * momentum_new

    right_ffn, ffn_error_new, ffn_momentum_new, ffn_weight_new = update(
        ortho_ffn, merged_ffn, ffn_momentum, ffn_weight
    )
    right_attn, attn_error_new, attn_momentum_new, attn_weight_new = update(
        ortho_attn, merged_attn, attn_momentum, attn_weight
    )
    vector_momentum_new = MOMENTUM * vector_momentum + (1.0 - MOMENTUM) * vector_grad
    vector_new = vector_params - RATE_VECTOR * vector_momentum_new
    return (
        mixed,
        grad_tokens,
        attn_grad[None],
        ffn_grad[None],
        ortho_attn,
        ortho_ffn,
        right_attn[None],
        right_ffn[None],
        attn_error_new[None],
        ffn_error_new[None],
        attn_momentum_new,
        ffn_momentum_new,
        attn_weight_new,
        ffn_weight_new,
        vector_momentum_new,
        vector_new,
    )


def solution(mesh):
    in_specs = (
        P(("replica", "fsdp"), None),
        P(("replica", "fsdp"), None),
        P(("replica", "fsdp")),
        P(("replica", "fsdp"), None),
        P("fsdp", None),
        P("fsdp", None),
        P(),
        P("replica", "fsdp", None),
        P("replica", "fsdp", None),
        P("fsdp", None),
        P("fsdp", None),
        P("fsdp", None, None),
        P("fsdp", None, None),
        P(),
    )
    out_specs = (
        P(("replica", "fsdp"), None),
        P(("replica", "fsdp"), None),
        P("replica", "fsdp", None),
        P("replica", "fsdp", None),
        P(None, "fsdp"),
        P(None, "fsdp"),
        P("fsdp", None, None),
        P("fsdp", None, None),
        P("replica", "fsdp", None),
        P("replica", "fsdp", None),
        P("fsdp", None),
        P("fsdp", None),
        P("fsdp", None),
        P("fsdp", None),
        P(),
        P(),
    )
    step = partial(local, mesh.shape["fsdp"], mesh.shape["replica"])
    return jax.shard_map(step, mesh=mesh, in_specs=in_specs, out_specs=out_specs, check_vma=False)
```

time: 1770 us -> 964 us (0.54)
  waiting for transfers between devices: 1110 us -> 336 us
  starting transfers between devices: 0.38 us -> 195 us
  other arithmetic: 232 us -> 115 us
  matrix products: 289 us -> 184 us
  blocking collectives: 88.1 us -> 0 us
  Pallas kernels: 0 us -> 68.4 us
  local copies, waits for them, and re-layouts: 11.8 us -> 34.6 us
    reduce_scatter x2 -> x0, waiting for transfers between devices: 931 us -> none  [the longest x1 704 us: local(): lax.psum_scatter(jnp.concatenate([contract_rows(mid_low, grad_gu), contra...]
    ppermute x0 -> x137, waiting for transfers between devices: none -> 336 us  [the longest x48 178 us: hop(): return lax.ppermute(value, 'fsdp', pairs)]
    ppermute x0 -> x137, starting transfers between devices: none -> 195 us  [the longest x48 106 us: hop(): return lax.ppermute(value, 'fsdp', pairs)]
    all_gather x2 -> x1, waiting for transfers between devices: 184 us -> 0.01 us  [local(): lax.all_gather(attn_weight[:, 3 * D:].astype(BF16), 'fsdp', axis=0, tiled...]
    dot_general x27 -> x18, matrix products: 289 us -> 184 us  [dot(): lax.dot_general(left, right, (((left_dim,), (right_dim,)), ((), ())), pre...]
    psum x3 -> x0, blocking collectives: 88.1 us -> none  [the longest x1 43.4 us: local(): weight_total = lax.psum(jnp.sum(loss_weights), ('replica', 'fsdp'))]
    concatenate x2 -> x10, other arithmetic: 75.1 us -> 2.53 us  [the longest x1 1.27 us: local(): heads_low = jnp.concatenate(arrange(heads_got, member), 1)]
    reduce_sum x33 -> x4, other arithmetic: 79.3 us -> 7.48 us  [the longest x1 3.68 us: local(): grad_gain_in = jnp.sum(grad_in_low * normed_in, 0)]
  transfers between devices with their start and end apart: 5 -> 138, of which waited for: 4 -> 53; matrix products, arithmetic and copies ran while one was open for 12% -> 29% of each run, Pallas kernels for 0% -> 7%
where the time goes in v1:
time: 964 us; the launch traced here: 954 us
  waiting for transfers between devices  336 us (35%)
  starting transfers between devices  195 us (20%)
  matrix products  184 us (19%)
  other arithmetic  115 us (12%)
  Pallas kernels  68.4 us (7%)
  local copies, waits for them, and re-layouts  34.6 us (4%)
  between operations  20.3 us (2%)
    dot_general x18, matrix products, dot(): lax.dot_general(left, right, (((left_dim,), (right_dim,)), ((), ())), pre...  184 us
    ppermute x48, waiting for transfers between devices, hop(): return lax.ppermute(value, 'fsdp', pairs)  178 us
    ppermute x48, starting transfers between devices, hop(): return lax.ppermute(value, 'fsdp', pairs)  106 us
    ppermute x65, waiting for transfers between devices, swap(): return lax.ppermute(value, 'fsdp', [(f, f ^ bits) for f in range(shards)])  104 us
    ppermute x18, waiting for transfers between devices, cross(): return lax.ppermute(value, ('replica', 'fsdp'), pairs)  48.9 us
    pallas_call x1, Pallas kernels, attend_back(): pl.pallas_call(attend_back_kernel, grid=(GROUP,), in_specs=attention_spec...  47.9 us
    ppermute x65, starting transfers between devices, swap(): return lax.ppermute(value, 'fsdp', [(f, f ^ bits) for f in range(shards)])  47.6 us
    ppermute x18, starting transfers between devices, cross(): return lax.ppermute(value, ('replica', 'fsdp'), pairs)  30.6 us
  transfers between devices with their start and end apart: 138, of which 53 were waited for; matrix products, arithmetic and copies ran while one was open for 29% of the time, Pallas kernels for 7%

profile of v1, /device:TPU:0, one launch (start us, length us, event | category | flops | bytes accessed | tf_op | source)
XLA Modules:
  0.0 953.7 jit_solution(882155776714872570)
XLA Ops:
  14.5 4.8 collective-permute-start.43
  61.8 17.4 %collective-permute-done.4 = bf16[96,1152]{1,0:T(8,128)(2,1)S(1)} collective-permute-done((bf16[96,1152]{1,0:T(8,128)(2,1)S(1)}, bf16[96,1152]{1,0:T(8,128)(2,1)S(1)}, u32[]{:S(2)}, u32[]{:S(2)}) %collective-permute-start.4) | collective-permute-done | bytes 221216 | tf_op jit(solution)/shard_map/ppermute | solution.py:217
  85.9 4.6 collective-permute-start.45
  92.1 4.2 collective-permute-start.6
  100.1 6.9 collective-permute-done.7
  108.4 7.1 collective-permute-done.47
  117.8 7.1 collective-permute-done.8
  127.8 5.5 collective-permute-done.48
  134.9 7.5 collective-permute-done.9
  149.8 7.5 collective-permute-done.11
  158.9 6.6 collective-permute-done.14
  169.2 9.1 collective-permute-done.17
  183.5 12.8 %convolution_convert_fusion.4.qkv_ref = bf16[2048,1152]{1,0:T(8,128)(2,1)S(1)} fusion(bf16[1536,1152]{1,0:T(8,128)(2,1)S(1)} %bitcast.316, bf16[512,1536]{1,0:T(8,128)(2,1)S(1)} %collective-permute-done.2, bf16[512,1536]{1,0:T(8,128)(2,1)S(1)} %collective-permute-done.1, bf16[512,1536]{1,0:T(8,128)(2,1)S(1)} %collective-permute-done, ...), kind=kOutput, calls=%fused_computation.10 | convolution fusion | flops 7275282432 | bytes 14548992 | tf_op jit(solution)/shard_map/dot_general | solution.py:45
  196.3 18.0 %attend.1 = bf16[2048,384]{1,0:T(8,128)(2,1)S(1)} custom-call(f32[1]{0:T(128)} %bitcast.lam_ref, bf16[2048,1152]{1,0:T(8,128)(2,1)S(1)} %convolution_convert_fusion.4.qkv_ref, s32[4,512,1]{2,1,0:T(8,128)S(1)} %copy.30.seg_q_ref, s32[4,1,512]{2,1,0:T(1,128)S(1)} %broadcast_in_dim.109.seg_k_ref, f32[1,128]{1,0:T(1,128)S(1)} %slice_bitcast_fusion.1.gain_ref), custom_call_target="tpu_custom_call" | custom-call | flops 2013265920 | bytes 6291456 | tf_op jit(solution)/shard_map/attend/pallas_call | solution.py:155
  226.9 7.5 collective-permute-done.22
  238.9 5.5 multiply_reduce_fusion.2
  245.9 12.8 %collective-permute-done.32 = bf16[192,2048]{1,0:T(8,128)(2,1)} collective-permute-done((bf16[192,2048]{1,0:T(8,128)(2,1)}, bf16[192,2048]{1,0:T(8,128)(2,1)}, u32[]{:S(2)}, u32[]{:S(2)}) %collective-permute-start.32) | collective-permute-done | bytes 786464 | tf_op jit(solution)/shard_map/ppermute | solution.py:224
  265.3 14.8 %collective-permute-done.33 = bf16[192,2048]{1,0:T(8,128)(2,1)S(1)} collective-permute-done((bf16[192,2048]{1,0:T(8,128)(2,1)}, bf16[192,2048]{1,0:T(8,128)(2,1)S(1)}, u32[]{:S(2)}, u32[]{:S(2)}) %collective-permute-start.33) | collective-permute-done | bytes 786464 | tf_op jit(solution)/shard_map/ppermute | solution.py:224
  292.3 10.1 %collective-permute-done.35 = bf16[192,2048]{1,0:T(8,128)(2,1)S(1)} collective-permute-done((bf16[192,2048]{1,0:T(8,128)(2,1)S(1)}, bf16[192,2048]{1,0:T(8,128)(2,1)S(1)}, u32[]{:S(2)}, u32[]{:S(2)}) %collective-permute-start.35) | collective-permute-done | bytes 786464 | tf_op jit(solution)/shard_map/ppermute | solution.py:234
  307.2 10.0 %collective-permute-done.38 = bf16[192,2048]{1,0:T(8,128)(2,1)S(1)} collective-permute-done((bf16[192,2048]{1,0:T(8,128)(2,1)}, bf16[192,2048]{1,0:T(8,128)(2,1)S(1)}, u32[]{:S(2)}, u32[]{:S(2)}) %collective-permute-start.38) | collective-permute-done | bytes 786464 | tf_op jit(solution)/shard_map/ppermute | solution.py:234
  323.7 7.6 collective-permute-done.66
  331.3 5.6 collective-permute-done.41
  340.3 21.2 %fusion.79 = f32[2048,2048]{0,1:T(8,128)} fusion(bf16[1536,2048]{1,0:T(8,128)(2,1)} %bitcast.303, bf16[512,1536]{1,0:T(8,128)(2,1)} %copy-done.87, bf16[512,1536]{1,0:T(8,128)(2,1)} %copy-done.85, bf16[512,1536]{1,0:T(8,128)(2,1)} %copy-done.86, bf16[512,1536]{1,0:T(8,128)(2,1)} %copy-done.40), kind=kOutput, calls=%fused_computation.137 | convolution fusion | flops 12910067712 | bytes 29360128 | tf_op jit(solution)/shard_map/dot_general | solution.py:45
  361.6 18.3 %multiply_convert_fusion.1 = (bf16[2048,1024]{0,1:T(8,128)(2,1)}, bf16[2048,1024]{0,1:T(8,128)(2,1)}, bf16[2048,1024]{0,1:T(8,128)(2,1)S(1)}) fusion(f32[2048,2048]{0,1:T(8,128)} %fusion.79, bf16[1536,1024]{1,0:T(8,128)(2,1)} %bitcast.32, bf16[512,1536]{1,0:T(8,128)(2,1)} %collective-permute-done.67, bf16[512,1536]{1,0:T(8,128)(2,1)} %collective-permute-done.66, ...), kind=kOutput, calls=%fused_computation.3 | convolution fusion | flops 6499074048 | bytes 38797312 | tf_op jit(solution)/shard_map/dot_general | solution.py:45
  379.9 10.3 %convolution_convert_fusion.3 = bf16[2048,1536]{1,0:T(8,128)(2,1)S(1)} fusion(bf16[2048,1024]{0,1:T(8,128)(2,1)S(1)} %get-tuple-element.76, bf16[1536,1024]{1,0:T(8,128)(2,1)} %bitcast.32), kind=kOutput, calls=%fused_computation.9 | convolution fusion | flops 6445596672 | bytes 13631488 | tf_op jit(solution)/shard_map/dot_general | solution.py:45
  394.4 17.3 %convolution_convert_fusion.6 = bf16[2048,1536]{1,0:T(8,128)(2,1)} fusion(bf16[1536,2048]{1,0:T(8,128)(2,1)S(1)} %bitcast.306, bf16[2048,1024]{0,1:T(8,128)(2,1)} %get-tuple-element.75, bf16[2048,1024]{0,1:T(8,128)(2,1)} %get-tuple-element.74), kind=kOutput, calls=%fused_computation.12 | convolution fusion | flops 12904824832 | bytes 20971520 | tf_op jit(solution)/shard_map/dot_general | solution.py:45
  411.6 19.6 %convolution_convert_fusion.5 = bf16[1536,2048]{1,0:T(8,128)(2,1)} fusion(bf16[2048,1024]{0,1:T(8,128)(2,1)} %get-tuple-element.75, bf16[2048,1024]{0,1:T(8,128)(2,1)} %get-tuple-element.74, bf16[512,1536]{1,0:T(8,128)(2,1)} %copy-done.87, bf16[512,1536]{1,0:T(8,128)(2,1)} %copy-done.85, bf16[512,1536]{1,0:T(8,128)(2,1)} %copy-done.86, ...), kind=kOutput, calls=%fused_computation.11 | convolution fusion | flops 12929990656 | bytes 20971520 | tf_op jit(solution)/shard_map/dot_general | solution.py:45
  439.2 10.4 %convolution_convert_fusion.8 = bf16[1536,1024]{1,0:T(8,128)(2,1)S(1)} fusion(bf16[2048,1024]{0,1:T(8,128)(2,1)} %copy-done.88, bf16[512,1536]{1,0:T(8,128)(2,1)} %collective-permute-done.67, bf16[512,1536]{1,0:T(8,128)(2,1)} %collective-permute-done.66, bf16[512,1536]{1,0:T(8,128)(2,1)} %collective-permute-done.65, bf16[512,1536]{1,0:T(8,128)(2,1)} %fusion.30), kind=kOutput, calls=%fused_computation.46 | convolution fusion | flops 6469189632 | bytes 13631488 | tf_op jit(solution)/shard_map/dot_general | solution.py:45
  457.6 4.5 collective-permute-start.111
  463.9 8.2 collective-permute-done.119
  474.8 14.3 %collective-permute-done.101 = bf16[384,1024]{1,0:T(8,128)(2,1)} collective-permute-done((bf16[384,1024]{1,0:T(8,128)(2,1)}, bf16[384,1024]{1,0:T(8,128)(2,1)}, u32[]{:S(2)}, u32[]{:S(2)}) %collective-permute-start.101) | collective-permute-done | bytes 786464 | tf_op jit(solution)/shard_map/ppermute | solution.py:224
  489.1 4.4 collective-permute-start.120
  494.9 11.1 %collective-permute-done.111 = bf16[384,1024]{1,0:T(8,128)(2,1)} collective-permute-done((bf16[384,1024]{1,0:T(8,128)(2,1)}, bf16[384,1024]{1,0:T(8,128)(2,1)}, u32[]{:S(2)}, u32[]{:S(2)}) %collective-permute-start.111) | collective-permute-done | bytes 786464 | tf_op jit(solution)/shard_map/ppermute | solution.py:224
  511.8 10.3 %collective-permute-done.120 = bf16[384,1024]{1,0:T(8,128)(2,1)S(1)} collective-permute-done((bf16[384,1024]{1,0:T(8,128)(2,1)S(1)}, bf16[384,1024]{1,0:T(8,128)(2,1)S(1)}, u32[]{:S(2)}, u32[]{:S(2)}) %collective-permute-start.120) | collective-permute-done | bytes 786464 | tf_op jit(solution)/shard_map/ppermute | solution.py:224
  522.1 4.4 collective-permute-start.102
  535.0 8.1 collective-permute-done.102
  546.7 6.4 collective-permute-start.112
  559.8 9.4 collective-permute-done.112
  569.3 7.5 collective-permute-start.121
  578.1 4.6 collective-permute-done.70
  587.5 6.6 collective-permute-done.121
  594.1 14.9 %collective-permute-done.115 = bf16[384,1024]{1,0:T(8,128)(2,1)S(1)} collective-permute-done((bf16[384,1024]{1,0:T(8,128)(2,1)S(1)}, bf16[384,1024]{1,0:T(8,128)(2,1)S(1)}, u32[]{:S(2)}, u32[]{:S(2)}) %collective-permute-start.115) | collective-permute-done | bytes 786464 | tf_op jit(solution)/shard_map/ppermute | solution.py:224
  609.1 14.9 %collective-permute-done.124 = bf16[384,1024]{1,0:T(8,128)(2,1)S(1)} collective-permute-done((bf16[384,1024]{1,0:T(8,128)(2,1)S(1)}, bf16[384,1024]{1,0:T(8,128)(2,1)S(1)}, u32[]{:S(2)}, u32[]{:S(2)}) %collective-permute-start.124) | collective-permute-done | bytes 786464 | tf_op jit(solution)/shard_map/ppermute | solution.py:224
  624.0 3.8 collective-permute-start.103
  631.0 5.5 fusion.112
  642.6 5.6 collective-permute-done.106
  650.7 5.1 collective-permute-done.107
  681.8 3.9 fusion.76
  688.7 5.9 collective-permute-done.73
  696.8 47.9 %attend_back.1 = (bf16[2048,1152]{1,0:T(8,128)(2,1)S(1)}, f32[4,8,128]{2,1,0:T(8,128)S(1)}) custom-call(f32[1]{0:T(128)} %bitcast.lam_ref, bf16[2048,1152]{1,0:T(8,128)(2,1)S(1)} %bitcast.272, s32[4,512,1]{2,1,0:T(8,128)S(1)} %copy.30.seg_q_ref, s32[4,1,512]{2,1,0:T(1,128)S(1)} %copy-done.2, f32[1,128]{1,0:T(1,128)S(1)} %copy-done.4, ...), custom_call_target="tpu_custom_call" | custom-call | flops 5033164800 | bytes 11010048 | tf_op jit(solution)/shard_map/attend_back/pallas_call | solution.py:173
  744.7 9.0 convolution_convert_fusion.2
  753.7 12.3 %convolution_convert_fusion.1 = bf16[1536,1152]{1,0:T(8,128)(2,1)S(1)} fusion(bf16[2048,1152]{1,0:T(8,128)(2,1)S(1)} %get-tuple-element.20, bf16[512,1536]{1,0:T(8,128)(2,1)} %copy-done.84, bf16[512,1536]{1,0:T(8,128)(2,1)} %copy-done.82, bf16[512,1536]{1,0:T(8,128)(2,1)} %copy-done.83, bf16[512,1536]{1,0:T(8,128)(2,1)S(1)} %copy-done.38), kind=kOutput, calls=%fused_computation.7 | convolution fusion | flops 7274692608 | bytes 14548992 | tf_op jit(solution)/shard_map/dot_general | solution.py:45
  773.3 13.4 %fusion.31 = bf16[1536,384]{1,0:T(8,128)(2,1)S(1)} fusion(bf16[512,1536]{1,0:T(8,128)(2,1)} %collective-permute-done.88, bf16[512,1536]{1,0:T(8,128)(2,1)} %collective-permute-done.87, bf16[512,1536]{1,0:T(8,128)(2,1)} %collective-permute-done.86, bf16[512,384]{1,0:T(8,128)(2,1)S(1)} %copy-done.48, bf16[512,384]{1,0:T(8,128)(2,1)S(1)} %copy-done.46, ...), kind=kOutput, calls=%fused_computation.68 | convolution fusion | flops 2466840576 | bytes 9043968 | tf_op jit(solution)/shard_map/dot_general | solution.py:45
  793.7 4.7 collective-permute-done.92
  800.1 4.4 collective-permute-start.93
  818.5 8.9 collective-permute-start.94
  838.7 10.2 %collective-permute-done.76 = bf16[512,1536]{1,0:T(8,128)(2,1)} collective-permute-done((bf16[512,1536]{1,0:T(8,128)(2,1)}, bf16[512,1536]{1,0:T(8,128)(2,1)}, u32[]{:S(2)}, u32[]{:S(2)}) %collective-permute-start.76) | collective-permute-done | bytes 1572896 | tf_op jit(solution)/shard_map/ppermute | solution.py:217
  862.1 19.9 %collective-permute-done.134 = f32[3456]{0:T(1024)S(1)} collective-permute-done((f32[3456]{0:T(1024)S(1)}, f32[3456]{0:T(1024)S(1)}, u32[]{:S(2)}, u32[]{:S(2)}) %collective-permute-start.134) | collective-permute-done | bytes 13856 | tf_op jit(solution)/shard_map/ppermute | solution.py:217
  882.2 5.3 fusion.27
  893.2 5.2 collective-permute-done.83
  918.8 5.9 convolution_convert_fusion
  924.7 3.9 collective-permute-start.131
  929.4 5.8 multiply_subtract_fusion.1
  936.5 10.2 %multiply_subtract_fusion = (f32[96,12288]{1,0:T(8,128)}, f32[96,12288]{1,0:T(8,128)}, f32[1,96,12288]{2,1,0:T(8,128)}) fusion(f32[96,12288]{1,0:T(8,128)S(1)} %bitcast.288, f32[96,12288]{1,0:T(8,128)} %param.24, f32[1,96,12288]{2,1,0:T(8,128)S(1)} %bitcast.276, bf16[96,12288]{1,0:T(8,128)(2,1)} %constant_dynamic-update-slice_fusion.32, ...), kind=kOutput, calls=%fused_computation.41 | convolution fusion | flops 124256256 | bytes 31067136 | tf_op jit(solution)/shard_map/dot_general | solution.py:45
  (633 shorter events, 316.9 us)
Async XLA Ops:
  7.2 231.7 %all-gather.2.cloned.1.call-start = ((), (), s32[]{:S(2)}) async-start(), calls=%async_computation | async-start | bytes 5013504 | tf_op jit(solution)/shard_map/all_gather | solution.py:377
  7.2 36.4 %collective-permute-start.19 = (s32[1,512]{1,0:T(1,128)}, s32[1,512]{1,0:T(1,128)S(1)}, u32[]{:S(2)}, u32[]{:S(2)}) collective-permute-start(s32[1,512]{1,0:T(1,128)} %param.17), channel_id=1, source_target_pairs={{0,2},{1,3},{2,0},{3,1},{4,6},{5,7},{6,4},{7,5},{8,10},{9,11},{10,... | collective-permute-start | bytes 6152 | tf_op jit(solution)/shard_map/ppermute | solution.py:217
  10.3 36.5 %collective-permute-start.18 = (s32[1,512]{1,0:T(1,128)}, s32[1,512]{1,0:T(1,128)S(1)}, u32[]{:S(2)}, u32[]{:S(2)}) collective-permute-start(s32[1,512]{1,0:T(1,128)} %param.17), channel_id=1, source_target_pairs={{0,1},{1,0},{2,3},{3,2},{4,5},{5,4},{6,7},{7,6},{8,9},{9,8},{10,11... | collective-permute-start | bytes 6152 | tf_op jit(solution)/shard_map/ppermute | solution.py:217
  14.5 40.7 %collective-permute-start.43 = (bf16[96,1024]{1,0:T(8,128)(2,1)}, bf16[96,1024]{1,0:T(8,128)(2,1)}, u32[]{:S(2)}, u32[]{:S(2)}) collective-permute-start(bf16[96,1024]{1,0:T(8,128)(2,1)} %get-tuple-element.117), channel_id=1, source_target_pairs={{0,2},{1,3},{2,0},{3,1},{4,6},{5,7},{6,4},{7,5},{8,10},{9,11},{10,... | collective-permute-start | bytes 589832 | tf_op jit(solution)/shard_map/ppermute | solution.py:217
  19.3 37.2 %collective-permute-start.44 = (bf16[96,1024]{1,0:T(8,128)(2,1)}, bf16[96,1024]{1,0:T(8,128)(2,1)}, u32[]{:S(2)}, u32[]{:S(2)}) collective-permute-start(bf16[96,1024]{1,0:T(8,128)(2,1)} %get-tuple-element.108), channel_id=1, source_target_pairs={{0,1},{1,0},{2,3},{3,2},{4,5},{5,4},{6,7},{7,6},{8,9},{9,8},{10,11... | collective-permute-start | bytes 589832 | tf_op jit(solution)/shard_map/ppermute | solution.py:217
  46.7 39.1 %collective-permute-start.28 = (bf16[96,2048]{1,0:T(8,128)(2,1)}, bf16[96,2048]{1,0:T(8,128)(2,1)}, u32[]{:S(2)}, u32[]{:S(2)}) collective-permute-start(bf16[96,2048]{1,0:T(8,128)(2,1)} %get-tuple-element.68), channel_id=1, source_target_pairs={{0,2},{1,3},{2,0},{3,1},{4,6},{5,7},{6,4},{7,5},{8,10},{9,11},{10,... | collective-permute-start | bytes 1179656 | tf_op jit(solution)/shard_map/ppermute | solution.py:217
  51.1 39.3 %collective-permute-start.29 = (bf16[96,2048]{1,0:T(8,128)(2,1)}, bf16[96,2048]{1,0:T(8,128)(2,1)S(1)}, u32[]{:S(2)}, u32[]{:S(2)}) collective-permute-start(bf16[96,2048]{1,0:T(8,128)(2,1)} %get-tuple-element.132), channel_id=1, source_target_pairs={{0,1},{1,0},{2,3},{3,2},{4,5},{5,4},{6,7},{7,6},{8,9},{9,8},{10,11... | collective-permute-start | bytes 1179656 | tf_op jit(solution)/shard_map/ppermute | solution.py:217
  55.2 24.0 %collective-permute-start.4 = (bf16[96,1152]{1,0:T(8,128)(2,1)S(1)}, bf16[96,1152]{1,0:T(8,128)(2,1)S(1)}, u32[]{:S(2)}, u32[]{:S(2)}) collective-permute-start(bf16[96,1152]{1,0:T(8,128)(2,1)S(1)} %copy-done.63), channel_id=1, source_target_pairs={{0,2},{1,3},{2,0},{3,1},{4,6},{5,7},{6,4},{7,5},{8,10},{9,11},{10,... | collective-permute-start | bytes 663560 | tf_op jit(solution)/shard_map/ppermute | solution.py:217
  56.5 23.6 %collective-permute-start.5 = (bf16[96,1152]{1,0:T(8,128)(2,1)S(1)}, bf16[96,1152]{1,0:T(8,128)(2,1)S(1)}, u32[]{:S(2)}, u32[]{:S(2)}) collective-permute-start(bf16[96,1152]{1,0:T(8,128)(2,1)S(1)} %copy-done.61), channel_id=1, source_target_pairs={{0,1},{1,0},{2,3},{3,2},{4,5},{5,4},{6,7},{7,6},{8,9},{9,8},{10,11... | collective-permute-start | bytes 663560 | tf_op jit(solution)/shard_map/ppermute | solution.py:217
  56.7 27.0 %collective-permute-start.3 = (bf16[96,1152]{1,0:T(8,128)(2,1)S(1)}, bf16[96,1152]{1,0:T(8,128)(2,1)S(1)}, u32[]{:S(2)}, u32[]{:S(2)}) collective-permute-start(bf16[96,1152]{1,0:T(8,128)(2,1)S(1)} %copy-done.62), channel_id=1, source_target_pairs={{0,3},{1,2},{2,1},{3,0},{4,7},{5,6},{6,5},{7,4},{8,11},{9,10},{10,... | collective-permute-start | bytes 663560 | tf_op jit(solution)/shard_map/ppermute | solution.py:217
  80.1 69.0 %collective-permute-start.1 = (bf16[512,1536]{1,0:T(8,128)(2,1)S(1)}, bf16[512,1536]{1,0:T(8,128)(2,1)S(1)}, u32[]{:S(2)}, u32[]{:S(2)}) collective-permute-start(bf16[512,1536]{1,0:T(8,128)(2,1)S(1)} %copy-done.37), channel_id=1, source_target_pairs={{0,2},{1,3},{2,0},{3,1},{4,6},{5,7},{6,4},{7,5},{8,10},{9,11},{10,... | collective-permute-start | bytes 4718600 | tf_op jit(solution)/shard_map/ppermute | solution.py:217
  85.9 41.2 %collective-permute-start.45 = (bf16[192,1024]{1,0:T(8,128)(2,1)S(1)}, bf16[192,1024]{1,0:T(8,128)(2,1)S(1)}, u32[]{:S(2)}, u32[]{:S(2)}) collective-permute-start(bf16[192,1024]{1,0:T(8,128)(2,1)S(1)} %dynamic-slice_bitcast_fusion.10), channel_id=1, source_target_pairs={{0,4},{1,5},{2,6},{3,7},{4,8},{5,9},{6,10},{7,11},{8,12},{9,13},{1... | collective-permute-start | bytes 1179656 | tf_op jit(solution)/shard_map/ppermute | solution.py:224
  92.1 35.0 %collective-permute-start.6 = (bf16[192,1152]{1,0:T(8,128)(2,1)S(1)}, bf16[192,1152]{1,0:T(8,128)(2,1)S(1)}, u32[]{:S(2)}, u32[]{:S(2)}) collective-permute-start(bf16[192,1152]{1,0:T(8,128)(2,1)S(1)} %dynamic-slice_bitcast_fusion.9), channel_id=1, source_target_pairs={{0,4},{1,5},{2,6},{3,7},{4,8},{5,9},{6,10},{7,11},{8,12},{9,13},{1... | collective-permute-start | bytes 1327112 | tf_op jit(solution)/shard_map/ppermute | solution.py:224
  127.1 53.5 %collective-permute-start = (bf16[512,1536]{1,0:T(8,128)(2,1)S(1)}, bf16[512,1536]{1,0:T(8,128)(2,1)S(1)}, u32[]{:S(2)}, u32[]{:S(2)}) collective-permute-start(bf16[512,1536]{1,0:T(8,128)(2,1)S(1)} %copy-done.37), channel_id=1, source_target_pairs={{0,1},{1,0},{2,3},{3,2},{4,5},{5,4},{6,7},{7,6},{8,9},{9,8},{10,11... | collective-permute-start | bytes 4718600 | tf_op jit(solution)/shard_map/ppermute | solution.py:217
  157.3 26.1 %collective-permute-start.2 = (bf16[512,1536]{1,0:T(8,128)(2,1)S(1)}, bf16[512,1536]{1,0:T(8,128)(2,1)S(1)}, u32[]{:S(2)}, u32[]{:S(2)}) collective-permute-start(bf16[512,1536]{1,0:T(8,128)(2,1)S(1)} %collective-permute-done.1), channel_id=1, source_target_pairs={{0,1},{1,0},{2,3},{3,2},{4,5},{5,4},{6,7},{7,6},{8,9},{9,8},{10,11... | collective-permute-start | bytes 4718600 | tf_op jit(solution)/shard_map/ppermute | solution.py:217
  157.6 64.1 %collective-permute-start.31 = (bf16[192,2048]{1,0:T(8,128)(2,1)}, bf16[192,2048]{1,0:T(8,128)(2,1)}, u32[]{:S(2)}, u32[]{:S(2)}) collective-permute-start(bf16[192,2048]{1,0:T(8,128)(2,1)} %dynamic-slice_bitcast_fusion.8), channel_id=1, source_target_pairs={{4,0},{5,1},{6,2},{7,3},{8,4},{9,5},{10,6},{11,7},{12,8},{13,9},{1... | collective-permute-start | bytes 2359304 | tf_op jit(solution)/shard_map/ppermute | solution.py:224
  178.3 36.2 %collective-permute-start.49 = (bf16[192,1024]{1,0:T(8,128)(2,1)S(1)}, bf16[192,1024]{1,0:T(8,128)(2,1)S(1)}, u32[]{:S(2)}, u32[]{:S(2)}) collective-permute-start(bf16[192,1024]{1,0:T(8,128)(2,1)S(1)} %collective-permute-done.45), channel_id=1, source_target_pairs={{4,20},{5,21},{6,22},{7,23},{8,24},{9,25},{10,26},{11,27},{12,28},... | collective-permute-start | bytes 1179656 | tf_op jit(solution)/shard_map/ppermute | solution.py:234
  179.0 38.6 %collective-permute-start.51 = (bf16[192,1024]{1,0:T(8,128)(2,1)S(1)}, bf16[192,1024]{1,0:T(8,128)(2,1)}, u32[]{:S(2)}, u32[]{:S(2)}) collective-permute-start(bf16[192,1024]{1,0:T(8,128)(2,1)S(1)} %collective-permute-done.45), channel_id=1, source_target_pairs={{4,8},{5,9},{6,10},{7,11},{8,12},{9,13},{10,14},{11,15},{20,24},{2... | collective-permute-start | bytes 1179656 | tf_op jit(solution)/shard_map/ppermute | solution.py:224
  180.6 36.0 %collective-permute-start.50 = (bf16[192,1024]{1,0:T(8,128)(2,1)S(1)}, bf16[192,1024]{1,0:T(8,128)(2,1)S(1)}, u32[]{:S(2)}, u32[]{:S(2)}) collective-permute-start(bf16[192,1024]{1,0:T(8,128)(2,1)S(1)} %collective-permute-done.48), channel_id=1, source_target_pairs={{0,16},{1,17},{2,18},{3,19},{16,0},{17,1},{18,2},{19,3}} | collective-permute-start | bytes 1179656 | tf_op jit(solution)/shard_map/ppermute | solution.py:234
  217.6 26.9 %collective-permute-start.30 = (bf16[192,2048]{1,0:T(8,128)(2,1)}, bf16[192,2048]{1,0:T(8,128)(2,1)}, u32[]{:S(2)}, u32[]{:S(2)}) collective-permute-start(bf16[192,2048]{1,0:T(8,128)(2,1)} %dynamic-slice_bitcast_fusion.8), channel_id=1, source_target_pairs={{0,4},{1,5},{2,6},{3,7},{4,8},{5,9},{6,10},{7,11},{8,12},{9,13},{1... | collective-permute-start | bytes 2359304 | tf_op jit(solution)/shard_map/ppermute | solution.py:224
  221.7 42.9 %collective-permute-start.56 = (bf16[192,1024]{1,0:T(8,128)(2,1)}, bf16[192,1024]{1,0:T(8,128)(2,1)}, u32[]{:S(2)}, u32[]{:S(2)}) collective-permute-start(bf16[192,1024]{1,0:T(8,128)(2,1)} %collective-permute-done.46), channel_id=1, source_target_pairs={{0,16},{1,17},{2,18},{3,19},{4,20},{5,21},{6,22},{7,23},{8,24},{9,... | collective-permute-start | bytes 1179656 | tf_op jit(solution)/shard_map/ppermute | solution.py:234
  234.4 26.9 %collective-permute-start.53 = (bf16[192,1024]{1,0:T(8,128)(2,1)}, bf16[192,1024]{1,0:T(8,128)(2,1)}, u32[]{:S(2)}, u32[]{:S(2)}) collective-permute-start(bf16[192,1024]{1,0:T(8,128)(2,1)} %collective-permute-done.47), channel_id=1, source_target_pairs={{0,16},{1,17},{2,18},{3,19},{4,20},{5,21},{6,22},{7,23},{16,0},{17... | collective-permute-start | bytes 1179656 | tf_op jit(solution)/shard_map/ppermute | solution.py:234
  245.2 42.2 %collective-permute-start.36 = (bf16[192,2048]{1,0:T(8,128)(2,1)}, bf16[192,2048]{1,0:T(8,128)(2,1)S(1)}, u32[]{:S(2)}, u32[]{:S(2)}) collective-permute-start(bf16[192,2048]{1,0:T(8,128)(2,1)} %collective-permute-done.30), channel_id=1, source_target_pairs={{4,8},{5,9},{6,10},{7,11},{8,12},{9,13},{10,14},{11,15},{20,24},{2... | collective-permute-start | bytes 2359304 | tf_op jit(solution)/shard_map/ppermute | solution.py:224
  260.6 23.3 %collective-permute-start.55 = (bf16[192,1024]{1,0:T(8,128)(2,1)S(1)}, bf16[192,1024]{1,0:T(8,128)(2,1)S(1)}, u32[]{:S(2)}, u32[]{:S(2)}) collective-permute-start(bf16[192,1024]{1,0:T(8,128)(2,1)S(1)} %collective-permute-done.54), channel_id=1, source_target_pairs={{12,28},{13,29},{14,30},{15,31},{28,12},{29,13},{30,14},{31,15}} | collective-permute-start | bytes 1179656 | tf_op jit(solution)/shard_map/ppermute | solution.py:234
  261.3 43.1 %collective-permute-start.25 = (bf16[512,1536]{1,0:T(8,128)(2,1)S(1)}, bf16[512,1536]{1,0:T(8,128)(2,1)S(1)}, u32[]{:S(2)}, u32[]{:S(2)}) collective-permute-start(bf16[512,1536]{1,0:T(8,128)(2,1)S(1)} %multiply_convert_fusion.3), channel_id=1, source_target_pairs={{0,2},{1,3},{2,0},{3,1},{4,6},{5,7},{6,4},{7,5},{8,10},{9,11},{10,... | collective-permute-start | bytes 4718600 | tf_op jit(solution)/shard_map/ppermute | solution.py:217
  264.6 24.7 %collective-permute-start.34 = (bf16[192,2048]{1,0:T(8,128)(2,1)}, bf16[192,2048]{1,0:T(8,128)(2,1)S(1)}, u32[]{:S(2)}, u32[]{:S(2)}) collective-permute-start(bf16[192,2048]{1,0:T(8,128)(2,1)} %collective-permute-done.30), channel_id=1, source_target_pairs={{4,20},{5,21},{6,22},{7,23},{8,24},{9,25},{10,26},{11,27},{12,28},... | collective-permute-start | bytes 2359304 | tf_op jit(solution)/shard_map/ppermute | solution.py:234
  283.9 47.4 %collective-permute-start.66 = (bf16[512,1536]{1,0:T(8,128)(2,1)}, bf16[512,1536]{1,0:T(8,128)(2,1)}, u32[]{:S(2)}, u32[]{:S(2)}) collective-permute-start(bf16[512,1536]{1,0:T(8,128)(2,1)} %fusion.30), channel_id=1, source_target_pairs={{0,2},{1,3},{2,0},{3,1},{4,6},{5,7},{6,4},{7,5},{8,10},{9,11},{10,... | collective-permute-start | bytes 4718600 | tf_op jit(solution)/shard_map/ppermute | solution.py:217
  289.3 27.9 %collective-permute-start.38 = (bf16[192,2048]{1,0:T(8,128)(2,1)}, bf16[192,2048]{1,0:T(8,128)(2,1)S(1)}, u32[]{:S(2)}, u32[]{:S(2)}) collective-permute-start(bf16[192,2048]{1,0:T(8,128)(2,1)} %collective-permute-done.32), channel_id=1, source_target_pairs={{0,16},{1,17},{2,18},{3,19},{4,20},{5,21},{6,22},{7,23},{16,0},{17... | collective-permute-start | bytes 2359304 | tf_op jit(solution)/shard_map/ppermute | solution.py:234
  304.3 33.7 %collective-permute-start.24 = (bf16[512,1536]{1,0:T(8,128)(2,1)S(1)}, bf16[512,1536]{1,0:T(8,128)(2,1)S(1)}, u32[]{:S(2)}, u32[]{:S(2)}) collective-permute-start(bf16[512,1536]{1,0:T(8,128)(2,1)S(1)} %multiply_convert_fusion.3), channel_id=1, source_target_pairs={{0,1},{1,0},{2,3},{3,2},{4,5},{5,4},{6,7},{7,6},{8,9},{9,8},{10,11... | collective-permute-start | bytes 4718600 | tf_op jit(solution)/shard_map/ppermute | solution.py:217
  304.4 33.7 %collective-permute-start.26 = (bf16[512,1536]{1,0:T(8,128)(2,1)S(1)}, bf16[512,1536]{1,0:T(8,128)(2,1)S(1)}, u32[]{:S(2)}, u32[]{:S(2)}) collective-permute-start(bf16[512,1536]{1,0:T(8,128)(2,1)S(1)} %collective-permute-done.25), channel_id=1, source_target_pairs={{0,1},{1,0},{2,3},{3,2},{4,5},{5,4},{6,7},{7,6},{8,9},{9,8},{10,11... | collective-permute-start | bytes 4718600 | tf_op jit(solution)/shard_map/ppermute | solution.py:217
  331.3 30.3 %collective-permute-start.65 = (bf16[512,1536]{1,0:T(8,128)(2,1)}, bf16[512,1536]{1,0:T(8,128)(2,1)}, u32[]{:S(2)}, u32[]{:S(2)}) collective-permute-start(bf16[512,1536]{1,0:T(8,128)(2,1)} %fusion.30), channel_id=1, source_target_pairs={{0,1},{1,0},{2,3},{3,2},{4,5},{5,4},{6,7},{7,6},{8,9},{9,8},{10,11... | collective-permute-start | bytes 4718600 | tf_op jit(solution)/shard_map/ppermute | solution.py:217
  336.9 24.7 %collective-permute-start.67 = (bf16[512,1536]{1,0:T(8,128)(2,1)}, bf16[512,1536]{1,0:T(8,128)(2,1)}, u32[]{:S(2)}, u32[]{:S(2)}) collective-permute-start(bf16[512,1536]{1,0:T(8,128)(2,1)} %collective-permute-done.66), channel_id=1, source_target_pairs={{0,1},{1,0},{2,3},{3,2},{4,5},{5,4},{6,7},{7,6},{8,9},{9,8},{10,11... | collective-permute-start | bytes 4718600 | tf_op jit(solution)/shard_map/ppermute | solution.py:217
  393.9 134.6 %collective-permute-start.58 = (bf16[512,1536]{1,0:T(8,128)(2,1)}, bf16[512,1536]{1,0:T(8,128)(2,1)}, u32[]{:S(2)}, u32[]{:S(2)}) collective-permute-start(bf16[512,1536]{1,0:T(8,128)(2,1)} %get-tuple-element.84), channel_id=1, source_target_pairs={{0,1},{1,0},{2,3},{3,2},{4,5},{5,4},{6,7},{7,6},{8,9},{9,8},{10,11... | collective-permute-start | bytes 4718600 | tf_op jit(solution)/shard_map/ppermute | solution.py:217
  437.5 36.4 %collective-permute-start.113 = (bf16[384,1024]{1,0:T(8,128)(2,1)}, bf16[384,1024]{1,0:T(8,128)(2,1)}, u32[]{:S(2)}, u32[]{:S(2)}) collective-permute-start(bf16[384,1024]{1,0:T(8,128)(2,1)} %get-tuple-element.97), channel_id=1, source_target_pairs={{12,8},{13,9},{14,10},{15,11},{28,24},{29,25},{30,26},{31,27}} | collective-permute-start | bytes 2359304 | tf_op jit(solution)/shard_map/ppermute | solution.py:224
  454.2 34.9 %collective-permute-start.101 = (bf16[384,1024]{1,0:T(8,128)(2,1)}, bf16[384,1024]{1,0:T(8,128)(2,1)}, u32[]{:S(2)}, u32[]{:S(2)}) collective-permute-start(bf16[384,1024]{1,0:T(8,128)(2,1)} %get-tuple-element.100), channel_id=1, source_target_pairs={{0,4},{1,5},{2,6},{3,7},{16,20},{17,21},{18,22},{19,23}} | collective-permute-start | bytes 2359304 | tf_op jit(solution)/shard_map/ppermute | solution.py:224
  457.6 48.4 %collective-permute-start.111 = (bf16[384,1024]{1,0:T(8,128)(2,1)}, bf16[384,1024]{1,0:T(8,128)(2,1)}, u32[]{:S(2)}, u32[]{:S(2)}) collective-permute-start(bf16[384,1024]{1,0:T(8,128)(2,1)} %fusion.61), channel_id=1, source_target_pairs={{0,4},{1,5},{2,6},{3,7},{4,8},{5,9},{6,10},{7,11},{16,20},{17,21},... | collective-permute-start | bytes 2359304 | tf_op jit(solution)/shard_map/ppermute | solution.py:224
  472.2 57.8 %collective-permute-start.69 = (bf16[512,1536]{1,0:T(8,128)(2,1)}, bf16[512,1536]{1,0:T(8,128)(2,1)}, u32[]{:S(2)}, u32[]{:S(2)}) collective-permute-start(bf16[512,1536]{1,0:T(8,128)(2,1)} %get-tuple-element.82), channel_id=1, source_target_pairs={{0,1},{1,0},{2,3},{3,2},{4,5},{5,4},{6,7},{7,6},{8,9},{9,8},{10,11... | collective-permute-start | bytes 4718600 | tf_op jit(solution)/shard_map/ppermute | solution.py:217
  474.0 37.8 %collective-permute-start.122 = (bf16[384,1024]{1,0:T(8,128)(2,1)}, bf16[384,1024]{1,0:T(8,128)(2,1)S(1)}, u32[]{:S(2)}, u32[]{:S(2)}) collective-permute-start(bf16[384,1024]{1,0:T(8,128)(2,1)} %get-tuple-element.93), channel_id=1, source_target_pairs={{12,8},{13,9},{14,10},{15,11},{28,24},{29,25},{30,26},{31,27}} | collective-permute-start | bytes 2359304 | tf_op jit(solution)/shard_map/ppermute | solution.py:224
  489.1 33.0 %collective-permute-start.120 = (bf16[384,1024]{1,0:T(8,128)(2,1)S(1)}, bf16[384,1024]{1,0:T(8,128)(2,1)S(1)}, u32[]{:S(2)}, u32[]{:S(2)}) collective-permute-start(bf16[384,1024]{1,0:T(8,128)(2,1)S(1)} %fusion.55), channel_id=1, source_target_pairs={{0,4},{1,5},{2,6},{3,7},{4,8},{5,9},{6,10},{7,11},{16,20},{17,21},... | collective-permute-start | bytes 2359304 | tf_op jit(solution)/shard_map/ppermute | solution.py:224
  511.8 47.8 %collective-permute-start.87 = (bf16[512,1536]{1,0:T(8,128)(2,1)}, bf16[512,1536]{1,0:T(8,128)(2,1)}, u32[]{:S(2)}, u32[]{:S(2)}) collective-permute-start(bf16[512,1536]{1,0:T(8,128)(2,1)} %pad_maximum_fusion.6), channel_id=1, source_target_pairs={{0,2},{1,3},{2,0},{3,1},{4,6},{5,7},{6,4},{7,5},{8,10},{9,11},{10,... | collective-permute-start | bytes 4718600 | tf_op jit(solution)/shard_map/ppermute | solution.py:217
  528.4 31.3 %collective-permute-start.68 = (bf16[512,1536]{1,0:T(8,128)(2,1)}, bf16[512,1536]{1,0:T(8,128)(2,1)S(1)}, u32[]{:S(2)}, u32[]{:S(2)}) collective-permute-start(bf16[512,1536]{1,0:T(8,128)(2,1)} %get-tuple-element.81), channel_id=1, source_target_pairs={{0,1},{1,0},{2,3},{3,2},{4,5},{5,4},{6,7},{7,6},{8,9},{9,8},{10,11... | collective-permute-start | bytes 4718600 | tf_op jit(solution)/shard_map/ppermute | solution.py:217
  530.0 23.0 %collective-permute-start.123 = (bf16[384,1024]{1,0:T(8,128)(2,1)}, bf16[384,1024]{1,0:T(8,128)(2,1)}, u32[]{:S(2)}, u32[]{:S(2)}) collective-permute-start(bf16[384,1024]{1,0:T(8,128)(2,1)} %get-tuple-element.91), channel_id=1, source_target_pairs={{8,4},{9,5},{10,6},{11,7},{12,8},{13,9},{14,10},{15,11},{24,20},{2... | collective-permute-start | bytes 2359304 | tf_op jit(solution)/shard_map/ppermute | solution.py:224
  543.9 38.8 %collective-permute-start.70 = (bf16[512,1536]{1,0:T(8,128)(2,1)}, bf16[512,1536]{1,0:T(8,128)(2,1)}, u32[]{:S(2)}, u32[]{:S(2)}) collective-permute-start(bf16[512,1536]{1,0:T(8,128)(2,1)} %add_convert_fusion.1), channel_id=1, source_target_pairs={{0,2},{1,3},{2,0},{3,1},{4,6},{5,7},{6,4},{7,5},{8,10},{9,11},{10,... | collective-permute-start | bytes 4718600 | tf_op jit(solution)/shard_map/ppermute | solution.py:217
  553.1 23.7 %collective-permute-start.105 = (bf16[384,1024]{1,0:T(8,128)(2,1)S(1)}, bf16[384,1024]{1,0:T(8,128)(2,1)S(1)}, u32[]{:S(2)}, u32[]{:S(2)}) collective-permute-start(bf16[384,1024]{1,0:T(8,128)(2,1)S(1)} %get-tuple-element.99), channel_id=1, source_target_pairs={{8,4},{9,5},{10,6},{11,7},{12,8},{13,9},{14,10},{15,11},{24,20},{2... | collective-permute-start | bytes 2359304 | tf_op jit(solution)/shard_map/ppermute | solution.py:224
  559.6 69.4 %collective-permute-start.57 = (bf16[512,1536]{1,0:T(8,128)(2,1)S(1)}, bf16[512,1536]{1,0:T(8,128)(2,1)S(1)}, u32[]{:S(2)}, u32[]{:S(2)}) collective-permute-start(bf16[512,1536]{1,0:T(8,128)(2,1)S(1)} %copy-done.39), channel_id=1, source_target_pairs={{0,1},{1,0},{2,3},{3,2},{4,5},{5,4},{6,7},{7,6},{8,9},{9,8},{10,11... | collective-permute-start | bytes 4718600 | tf_op jit(solution)/shard_map/ppermute | solution.py:217
  559.7 71.3 %collective-permute-start.59 = (bf16[512,1536]{1,0:T(8,128)(2,1)S(1)}, bf16[512,1536]{1,0:T(8,128)(2,1)S(1)}, u32[]{:S(2)}, u32[]{:S(2)}) collective-permute-start(bf16[512,1536]{1,0:T(8,128)(2,1)S(1)} %add_convert_fusion.3), channel_id=1, source_target_pairs={{0,2},{1,3},{2,0},{3,1},{4,6},{5,7},{6,4},{7,5},{8,10},{9,11},{10,... | collective-permute-start | bytes 4718600 | tf_op jit(solution)/shard_map/ppermute | solution.py:217
  569.3 24.9 %collective-permute-start.121 = (bf16[384,1024]{1,0:T(8,128)(2,1)S(1)}, bf16[384,1024]{1,0:T(8,128)(2,1)S(1)}, u32[]{:S(2)}, u32[]{:S(2)}) collective-permute-start(bf16[384,1024]{1,0:T(8,128)(2,1)S(1)} %copy-done.54), channel_id=1, source_target_pairs={{0,4},{1,5},{2,6},{3,7},{4,8},{5,9},{6,10},{7,11},{8,12},{9,13},{1... | collective-permute-start | bytes 2359304 | tf_op jit(solution)/shard_map/ppermute | solution.py:224
  576.8 32.3 %collective-permute-start.115 = (bf16[384,1024]{1,0:T(8,128)(2,1)S(1)}, bf16[384,1024]{1,0:T(8,128)(2,1)S(1)}, u32[]{:S(2)}, u32[]{:S(2)}) collective-permute-start(bf16[384,1024]{1,0:T(8,128)(2,1)S(1)} %fusion.60), channel_id=1, source_target_pairs={{4,0},{5,1},{6,2},{7,3},{8,4},{9,5},{10,6},{11,7},{12,8},{13,9},{1... | collective-permute-start | bytes 2359304 | tf_op jit(solution)/shard_map/ppermute | solution.py:224
  582.7 41.3 %collective-permute-start.124 = (bf16[384,1024]{1,0:T(8,128)(2,1)S(1)}, bf16[384,1024]{1,0:T(8,128)(2,1)S(1)}, u32[]{:S(2)}, u32[]{:S(2)}) collective-permute-start(bf16[384,1024]{1,0:T(8,128)(2,1)S(1)} %fusion.54), channel_id=1, source_target_pairs={{4,0},{5,1},{6,2},{7,3},{8,4},{9,5},{10,6},{11,7},{12,8},{13,9},{1... | collective-permute-start | bytes 2359304 | tf_op jit(solution)/shard_map/ppermute | solution.py:224
  594.1 176.0 %collective-permute-start.86 = (bf16[512,1536]{1,0:T(8,128)(2,1)}, bf16[512,1536]{1,0:T(8,128)(2,1)}, u32[]{:S(2)}, u32[]{:S(2)}) collective-permute-start(bf16[512,1536]{1,0:T(8,128)(2,1)} %pad_maximum_fusion.6), channel_id=1, source_target_pairs={{0,1},{1,0},{2,3},{3,2},{4,5},{5,4},{6,7},{7,6},{8,9},{9,8},{10,11... | collective-permute-start | bytes 4718600 | tf_op jit(solution)/shard_map/ppermute | solution.py:217
  609.1 161.1 %collective-permute-start.88 = (bf16[512,1536]{1,0:T(8,128)(2,1)}, bf16[512,1536]{1,0:T(8,128)(2,1)}, u32[]{:S(2)}, u32[]{:S(2)}) collective-permute-start(bf16[512,1536]{1,0:T(8,128)(2,1)} %collective-permute-done.87), channel_id=1, source_target_pairs={{0,1},{1,0},{2,3},{3,2},{4,5},{5,4},{6,7},{7,6},{8,9},{9,8},{10,11... | collective-permute-start | bytes 4718600 | tf_op jit(solution)/shard_map/ppermute | solution.py:217
  685.7 87.6 %collective-permute-start.89 = (bf16[512,384]{1,0:T(8,128)(2,1)S(1)}, bf16[512,384]{1,0:T(8,128)(2,1)S(1)}, u32[]{:S(2)}, u32[]{:S(2)}) collective-permute-start(bf16[512,384]{1,0:T(8,128)(2,1)S(1)} %get-tuple-element.125), channel_id=1, source_target_pairs={{0,1},{1,0},{2,3},{3,2},{4,5},{5,4},{6,7},{7,6},{8,9},{9,8},{10,11... | collective-permute-start | bytes 1179656 | tf_op jit(solution)/shard_map/ppermute | solution.py:217
  688.0 85.3 %collective-permute-start.90 = (bf16[512,384]{1,0:T(8,128)(2,1)S(1)}, bf16[512,384]{1,0:T(8,128)(2,1)S(1)}, u32[]{:S(2)}, u32[]{:S(2)}) collective-permute-start(bf16[512,384]{1,0:T(8,128)(2,1)S(1)} %get-tuple-element.126), channel_id=1, source_target_pairs={{0,2},{1,3},{2,0},{3,1},{4,6},{5,7},{6,4},{7,5},{8,10},{9,11},{10,... | collective-permute-start | bytes 1179656 | tf_op jit(solution)/shard_map/ppermute | solution.py:217
  694.7 78.6 %collective-permute-start.91 = (bf16[512,384]{1,0:T(8,128)(2,1)S(1)}, bf16[512,384]{1,0:T(8,128)(2,1)S(1)}, u32[]{:S(2)}, u32[]{:S(2)}) collective-permute-start(bf16[512,384]{1,0:T(8,128)(2,1)S(1)} %get-tuple-element.127), channel_id=1, source_target_pairs={{0,3},{1,2},{2,1},{3,0},{4,7},{5,6},{6,5},{7,4},{8,11},{9,10},{10,... | collective-permute-start | bytes 1179656 | tf_op jit(solution)/shard_map/ppermute | solution.py:217
  770.2 36.0 %collective-permute-start.75 = (bf16[512,1536]{1,0:T(8,128)(2,1)}, bf16[512,1536]{1,0:T(8,128)(2,1)}, u32[]{:S(2)}, u32[]{:S(2)}) collective-permute-start(bf16[512,1536]{1,0:T(8,128)(2,1)} %get-tuple-element.80), channel_id=1, source_target_pairs={{0,1},{1,0},{2,3},{3,2},{4,5},{5,4},{6,7},{7,6},{8,9},{9,8},{10,11... | collective-permute-start | bytes 4718600 | tf_op jit(solution)/shard_map/ppermute | solution.py:217
  770.2 29.9 %collective-permute-start.77 = (bf16[384,1152]{1,0:T(8,128)(2,1)}, bf16[384,1152]{1,0:T(8,128)(2,1)}, u32[]{:S(2)}, u32[]{:S(2)}) collective-permute-start(bf16[384,1152]{1,0:T(8,128)(2,1)} %get-tuple-element.88), channel_id=1, source_target_pairs={{0,4},{1,5},{2,6},{3,7},{16,20},{17,21},{18,22},{19,23}} | collective-permute-start | bytes 2654216 | tf_op jit(solution)/shard_map/ppermute | solution.py:224
  793.0 45.6 %collective-permute-start.74 = (bf16[512,1536]{1,0:T(8,128)(2,1)}, bf16[512,1536]{1,0:T(8,128)(2,1)}, u32[]{:S(2)}, u32[]{:S(2)}) collective-permute-start(bf16[512,1536]{1,0:T(8,128)(2,1)} %get-tuple-element.79), channel_id=1, source_target_pairs={{0,1},{1,0},{2,3},{3,2},{4,5},{5,4},{6,7},{7,6},{8,9},{9,8},{10,11... | collective-permute-start | bytes 4718600 | tf_op jit(solution)/shard_map/ppermute | solution.py:217
  798.4 29.1 %collective-permute-start.80 = (bf16[384,1152]{1,0:T(8,128)(2,1)}, bf16[384,1152]{1,0:T(8,128)(2,1)}, u32[]{:S(2)}, u32[]{:S(2)}) collective-permute-start(bf16[384,1152]{1,0:T(8,128)(2,1)} %get-tuple-element.89), channel_id=1, source_target_pairs={{12,8},{13,9},{14,10},{15,11},{28,24},{29,25},{30,26},{31,27}} | collective-permute-start | bytes 2654216 | tf_op jit(solution)/shard_map/ppermute | solution.py:224
  806.2 24.7 %collective-permute-start.78 = (bf16[384,1152]{1,0:T(8,128)(2,1)S(1)}, bf16[384,1152]{1,0:T(8,128)(2,1)}, u32[]{:S(2)}, u32[]{:S(2)}) collective-permute-start(bf16[384,1152]{1,0:T(8,128)(2,1)S(1)} %fusion.42), channel_id=1, source_target_pairs={{0,4},{1,5},{2,6},{3,7},{4,8},{5,9},{6,10},{7,11},{16,20},{17,21},... | collective-permute-start | bytes 2654216 | tf_op jit(solution)/shard_map/ppermute | solution.py:224
  812.8 36.1 %collective-permute-start.76 = (bf16[512,1536]{1,0:T(8,128)(2,1)}, bf16[512,1536]{1,0:T(8,128)(2,1)}, u32[]{:S(2)}, u32[]{:S(2)}) collective-permute-start(bf16[512,1536]{1,0:T(8,128)(2,1)} %add_convert_fusion), channel_id=1, source_target_pairs={{0,2},{1,3},{2,0},{3,1},{4,6},{5,7},{6,4},{7,5},{8,10},{9,11},{10,... | collective-permute-start | bytes 4718600 | tf_op jit(solution)/shard_map/ppermute | solution.py:217
  852.7 50.0 %collective-permute-start.100 = (bf16[96,384]{1,0:T(8,128)(2,1)S(1)}, bf16[96,384]{1,0:T(8,128)(2,1)S(1)}, u32[]{:S(2)}, u32[]{:S(2)}) collective-permute-start(bf16[96,384]{1,0:T(8,128)(2,1)S(1)} %get-tuple-element.179), channel_id=1, source_target_pairs={{0,1},{1,0},{2,3},{3,2},{4,5},{5,4},{6,7},{7,6},{8,9},{9,8},{10,11... | collective-permute-start | bytes 221192 | tf_op jit(solution)/shard_map/ppermute | solution.py:217
  853.3 49.5 %collective-permute-start.98 = (bf16[96,384]{1,0:T(8,128)(2,1)S(1)}, bf16[96,384]{1,0:T(8,128)(2,1)S(1)}, u32[]{:S(2)}, u32[]{:S(2)}) collective-permute-start(bf16[96,384]{1,0:T(8,128)(2,1)S(1)} %get-tuple-element.180), channel_id=1, source_target_pairs={{0,3},{1,2},{2,1},{3,0},{4,7},{5,6},{6,5},{7,4},{8,11},{9,10},{10,... | collective-permute-start | bytes 221192 | tf_op jit(solution)/shard_map/ppermute | solution.py:217
  854.2 34.7 %collective-permute-start.79 = (bf16[384,1152]{1,0:T(8,128)(2,1)}, bf16[384,1152]{1,0:T(8,128)(2,1)S(1)}, u32[]{:S(2)}, u32[]{:S(2)}) collective-permute-start(bf16[384,1152]{1,0:T(8,128)(2,1)} %get-tuple-element.86), channel_id=1, source_target_pairs={{0,4},{1,5},{2,6},{3,7},{4,8},{5,9},{6,10},{7,11},{8,12},{9,13},{1... | collective-permute-start | bytes 2654216 | tf_op jit(solution)/shard_map/ppermute | solution.py:224
  858.1 30.9 %collective-permute-start.82 = (bf16[384,1152]{1,0:T(8,128)(2,1)S(1)}, bf16[384,1152]{1,0:T(8,128)(2,1)S(1)}, u32[]{:S(2)}, u32[]{:S(2)}) collective-permute-start(bf16[384,1152]{1,0:T(8,128)(2,1)S(1)} %fusion.41), channel_id=1, source_target_pairs={{4,0},{5,1},{6,2},{7,3},{8,4},{9,5},{10,6},{11,7},{12,8},{13,9},{1... | collective-permute-start | bytes 2654216 | tf_op jit(solution)/shard_map/ppermute | solution.py:224
  (177 other events, 3667.3 us)
Sparse Core Ops, SparseCore 0:
  21.7 67.5 all-gather.1

commit v2 on v1

v2 whole, which is shorter than its diff:
```python
from functools import partial

import jax
import jax.numpy as jnp
from jax import lax
from jax.experimental import pallas as pl
from jax.experimental.pallas import tpu as pltpu
from jax.sharding import PartitionSpec as P

D = 1536
HEADS = 12
HD = 64
FF = 4096

NEEDLE = 3.0
LAMBDA_INIT = 0.2
KEEP = 1.0 - LAMBDA_INIT
DECAY_ERROR = 0.5
MOMENTUM = 0.9
RATE_MATRIX = 0.005
RATE_VECTOR = 0.02
MASKED = -1e30
HIGHEST = lax.Precision.HIGHEST
BF16 = jnp.bfloat16
F32 = jnp.float32

GROUP = 4
BLOCK = 128
REACH = 256
WIDTH = 2 * HD
OWN_HEADS = HEADS // GROUP
ATTN_Q = D // GROUP
FF_Q = FF // GROUP


def rms_scale(values, epsilon):
    return lax.rsqrt(jnp.mean(values * values, -1, keepdims=True) + epsilon)


def norm_back(grad_normed, normed, scale):
    return scale * (grad_normed - normed * jnp.mean(grad_normed * normed, -1, keepdims=True))


def dot(left, right, left_dim=1, right_dim=0, **kinds):
    return lax.dot_general(
        left, right, (((left_dim,), (right_dim,)), ((), ())), preferred_element_type=F32, **kinds
    )


def score_parts(qkv_ref, head, block, reach, lam, bias):
    rows = pl.ds(block * BLOCK, BLOCK)
    lane = lax.broadcasted_iota(jnp.int32, (1, WIDTH), 1)
    first = lane < HD
    query = qkv_ref[rows, head * WIDTH : (head + 1) * WIDTH] * BF16(HD**-0.5)
    key = qkv_ref[reach, ATTN_Q + head * WIDTH : ATTN_Q + (head + 1) * WIDTH]
    value = qkv_ref[reach, 2 * ATTN_Q + head * WIDTH : 2 * ATTN_Q + (head + 1) * WIDTH]
    zero = jnp.zeros((), BF16)
    query_one = jnp.where(first, query, zero)
    query_two = jnp.where(first, zero, query)
    probs = []
    for half in (query_one, query_two):
        score = dot(half, key, 1, 1) + bias
        expo = jnp.exp(score - jnp.max(score, -1, keepdims=True))
        probs.append(expo * (1.0 / jnp.sum(expo, -1, keepdims=True)))
    mixture = (probs[0] - lam * probs[1]).astype(BF16)
    return query_one, query_two, key, value, probs[0], probs[1], mixture


def block_bias(seg_q_ref, seg_k_ref, block, low, high):
    rows = lax.broadcasted_iota(jnp.int32, (BLOCK, high - low), 0) + block * BLOCK
    cols = lax.broadcasted_iota(jnp.int32, (BLOCK, high - low), 1) + low
    same = seg_q_ref[block * BLOCK : (block + 1) * BLOCK, :] == seg_k_ref[:, low:high]
    return jnp.where((cols <= rows) & same, 0.0, MASKED)


def reach_of(block):
    return max(0, block - REACH // BLOCK) * BLOCK, (block + 1) * BLOCK


def attend_kernel(lam_ref, qkv_ref, seg_q_ref, seg_k_ref, gain_ref, heads_ref):
    lam = lam_ref[0]
    gain = gain_ref[...] * KEEP
    for block in range(qkv_ref.shape[0] // BLOCK):
        low, high = reach_of(block)
        bias = block_bias(seg_q_ref, seg_k_ref, block, low, high)
        for head in range(OWN_HEADS):
            parts = score_parts(qkv_ref, head, block, pl.ds(low, high - low), lam, bias)
            out = dot(parts[6], parts[3])
            normed = out * rms_scale(out, 1e-05)
            heads_ref[pl.ds(block * BLOCK, BLOCK), head * WIDTH : (head + 1) * WIDTH] = (
                normed * gain
            ).astype(BF16)


def attend_back_kernel(
    lam_ref, qkv_ref, seg_q_ref, seg_k_ref, gain_ref, grad_ref, out_ref, stat_ref, dk_ref, dv_ref
):
    lam = lam_ref[0]
    gain = gain_ref[...] * KEEP
    blocks = qkv_ref.shape[0] // BLOCK
    first = lax.broadcasted_iota(jnp.int32, (1, WIDTH), 1) < HD
    zero = jnp.zeros((), BF16)
    gain_total = jnp.zeros((1, WIDTH), F32)
    lam_total = jnp.zeros((1, 1), F32)
    biases = [block_bias(seg_q_ref, seg_k_ref, b, *reach_of(b)) for b in range(blocks)]
    for head in range(OWN_HEADS):
        lanes = slice(head * WIDTH, (head + 1) * WIDTH)
        dk_ref[...] = jnp.zeros_like(dk_ref)
        dv_ref[...] = jnp.zeros_like(dv_ref)
        for block in range(blocks):
            low, high = reach_of(block)
            rows, reach = pl.ds(block * BLOCK, BLOCK), pl.ds(low, high - low)
            query_one, query_two, key, value, prob_one, prob_two, mixture = score_parts(
                qkv_ref, head, block, reach, lam, biases[block]
            )
            out = dot(mixture, value)
            scale = rms_scale(out, 1e-05)
            normed = out * scale
            grad = grad_ref[rows, lanes].astype(F32)
            gain_total = gain_total + jnp.sum(grad * normed, 0, keepdims=True)
            grad_out = norm_back(grad * gain, normed, scale).astype(BF16)
            grad_mix = dot(grad_out, value, 1, 1)
            mean_one = jnp.sum(grad_mix * prob_one, -1, keepdims=True)
            mean_two = jnp.sum(grad_mix * prob_two, -1, keepdims=True)
            lam_total = lam_total - jnp.sum(mean_two, 0, keepdims=True)
            low_one = (prob_one * (grad_mix - mean_one)).astype(BF16)
            low_two = (prob_two * (-lam * (grad_mix - mean_two))).astype(BF16)
            dv_ref[reach, :] += dot(mixture, grad_out, 0, 0)
            dk_ref[reach, :] += dot(low_one, query_one, 0, 0) + dot(low_two, query_two, 0, 0)
            grad_query = dot(low_one, jnp.where(first, key, zero)) + dot(
                low_two, jnp.where(first, zero, key)
            )
            out_ref[rows, lanes] = (grad_query * HD**-0.5).astype(BF16)
        out_ref[:, ATTN_Q + head * WIDTH : ATTN_Q + (head + 1) * WIDTH] = dk_ref[...].astype(BF16)
        out_ref[:, 2 * ATTN_Q + head * WIDTH : 2 * ATTN_Q + (head + 1) * WIDTH] = dv_ref[
            ...
        ].astype(BF16)
    stat_ref[0:1, :] = gain_total * KEEP
    stat_ref[1:2, :] = jnp.broadcast_to(lam_total, (1, WIDTH))
    stat_ref[2:8, :] = jnp.zeros((6, WIDTH), F32)


def attention_specs(length):
    return [
        pl.BlockSpec(memory_space=pltpu.SMEM),
        pl.BlockSpec((length, 3 * ATTN_Q), lambda i: (0, 0)),
        pl.BlockSpec((length, 1), lambda i: (0, 0)),
        pl.BlockSpec((1, length), lambda i: (0, 0)),
        pl.BlockSpec((1, WIDTH), lambda i: (0, 0)),
    ]


def attend(lam, qkv, segments, gain):
    length = segments.shape[0]
    return pl.pallas_call(
        attend_kernel,
        grid=(1,),
        in_specs=attention_specs(length),
        out_specs=pl.BlockSpec((length, ATTN_Q), lambda i: (0, 0)),
        out_shape=jax.ShapeDtypeStruct((length, ATTN_Q), BF16),
        compiler_params=pltpu.CompilerParams(vmem_limit_bytes=32 * 2**20),
        cost_estimate=pl.CostEstimate(
            flops=OWN_HEADS * 2 * 4 * length * 320 * WIDTH,
            bytes_accessed=length * 8 * ATTN_Q,
            transcendentals=OWN_HEADS * 2 * length * 320,
        ),
        name="attend",
    )(lam, qkv, segments[:, None], segments[None, :], gain)


def attend_back(lam, qkv, segments, gain, grad):
    length = segments.shape[0]
    return pl.pallas_call(
        attend_back_kernel,
        grid=(1,),
        in_specs=attention_specs(length) + [pl.BlockSpec((length, ATTN_Q), lambda i: (0, 0))],
        out_specs=[
            pl.BlockSpec((length, 3 * ATTN_Q), lambda i: (0, 0)),
            pl.BlockSpec((8, WIDTH), lambda i: (0, 0)),
        ],
        out_shape=[
            jax.ShapeDtypeStruct((length, 3 * ATTN_Q), BF16),
            jax.ShapeDtypeStruct((8, WIDTH), F32),
        ],
        scratch_shapes=[pltpu.VMEM((length, WIDTH), F32), pltpu.VMEM((length, WIDTH), F32)],
        compiler_params=pltpu.CompilerParams(vmem_limit_bytes=32 * 2**20),
        cost_estimate=pl.CostEstimate(
            flops=OWN_HEADS * 2 * 10 * length * 320 * WIDTH,
            bytes_accessed=length * 14 * ATTN_Q,
            transcendentals=OWN_HEADS * 2 * length * 320,
        ),
        name="attend_back",
    )(lam, qkv, segments[:, None], segments[None, :], gain, grad)


def quarter_kernel(member_ref, *refs):
    for source, target in zip(refs[:GROUP], refs[GROUP:]):
        target[...] = source[...].astype(BF16)


def quarters(member, weight, sections, width):
    rows = weight.shape[0]

    def columns(bits):
        return lambda i, member: (0, i * GROUP + (member[0] ^ bits))

    kind = jax.ShapeDtypeStruct((rows, sections * width), BF16)
    return pl.pallas_call(
        quarter_kernel,
        grid_spec=pltpu.PrefetchScalarGridSpec(
            num_scalar_prefetch=1,
            grid=(sections,),
            in_specs=[pl.BlockSpec((rows, width), columns(bits)) for bits in range(GROUP)],
            out_specs=[pl.BlockSpec((rows, width), lambda i, member: (0, i))] * GROUP,
        ),
        out_shape=[kind] * GROUP,
        compiler_params=pltpu.CompilerParams(vmem_limit_bytes=32 * 2**20),
        cost_estimate=pl.CostEstimate(flops=0, bytes_accessed=rows * width, transcendentals=0),
        name="quarters",
    )(member.reshape(1), *[weight] * GROUP)


def back_kernel(pairs, *refs):
    total = None
    for left, right in zip(refs[:pairs], refs[pairs : 2 * pairs]):
        part = dot(left[...], right[...], 1, 1)
        total = part if total is None else total + part
    if len(refs) > 2 * pairs + 1:
        total = total + refs[2 * pairs][...].astype(F32)
    refs[-1][...] = total.astype(refs[-1].dtype)


def back_product(lefts, right, got=None, kind=BF16, tile=512, first=0, share=32):
    pairs, (length, depth) = len(lefts), lefts[0].shape
    width = right.shape[0]
    specs = [pl.BlockSpec((length, depth), lambda i: (0, 0))] * pairs
    for number in range(pairs):
        specs.append(pl.BlockSpec((tile, depth), lambda i, s=first + number: (i, s)))
    out_spec = pl.BlockSpec((length, tile), lambda i: (0, i))
    operands = list(lefts) + [right] * pairs
    if got is not None:
        specs.append(out_spec)
        operands.append(got)
    return pl.pallas_call(
        partial(back_kernel, pairs),
        grid=(width // tile,),
        in_specs=specs,
        out_specs=out_spec,
        out_shape=jax.ShapeDtypeStruct((length, width), kind),
        compiler_params=pltpu.CompilerParams(vmem_limit_bytes=48 * 2**20),
        cost_estimate=pl.CostEstimate(
            flops=2 * pairs * length * depth * width // share,
            bytes_accessed=2 * pairs * (length + width) * depth // share,
            transcendentals=0,
        ),
        name="back_product",
    )(*operands)


def weight_kernel(*refs):
    out_ref = refs[-1]
    total = None
    for left, right in zip(refs[:GROUP], refs[GROUP : 2 * GROUP]):
        part = dot(left[...], right[...], 0, 0)
        total = part if total is None else total + part
    out_ref[...] = total.astype(BF16)


def weight_product(lefts, rights, columns, place, into=None, rows=512):
    length, depth = lefts[0].shape
    width = rights[0].shape[1]
    specs = [pl.BlockSpec((length, rows), lambda i: (0, i))] * GROUP
    specs += [pl.BlockSpec((length, width), lambda i: (0, 0))] * GROUP
    operands = [*lefts, *rights]
    if into is not None:
        specs.append(pl.BlockSpec(memory_space=pl.ANY))
        operands.append(into)
    return pl.pallas_call(
        weight_kernel,
        grid=(depth // rows,),
        in_specs=specs,
        out_specs=pl.BlockSpec((rows, width), lambda i: (i, place)),
        out_shape=jax.ShapeDtypeStruct((depth, columns), BF16),
        input_output_aliases={} if into is None else {2 * GROUP: 0},
        compiler_params=pltpu.CompilerParams(vmem_limit_bytes=48 * 2**20),
        cost_estimate=pl.CostEstimate(
            flops=GROUP * length * depth * width // 32,
            bytes_accessed=GROUP * length * (depth + width) // 32,
            transcendentals=0,
        ),
        name="weight_product",
    )(*operands)


def project_kernel(left_ref, right_ref, out_ref):
    out_ref[...] = dot(left_ref[...], right_ref[...]).astype(BF16)


def project(left, right, tile=384):
    (length, depth), width = left.shape, right.shape[1]
    return pl.pallas_call(
        project_kernel,
        grid=(width // tile,),
        in_specs=[
            pl.BlockSpec((length, depth), lambda i: (0, 0)),
            pl.BlockSpec((depth, tile), lambda i: (0, i)),
        ],
        out_specs=pl.BlockSpec((length, tile), lambda i: (0, i)),
        out_shape=jax.ShapeDtypeStruct((length, width), BF16),
        compiler_params=pltpu.CompilerParams(vmem_limit_bytes=48 * 2**20),
        cost_estimate=pl.CostEstimate(flops=0, bytes_accessed=length * depth, transcendentals=0),
        name="project",
    )(left, right)


def raise_kernel(*refs):
    mids, (gate_ref, up_ref), outs = refs[:GROUP], refs[GROUP : GROUP + 2], refs[GROUP + 2 :]
    for k, mid_ref in enumerate(mids):
        gate = dot(mid_ref[...], gate_ref[...])
        up = dot(mid_ref[...], up_ref[...])
        outs[k][...] = (gate * jax.nn.sigmoid(gate) * up).astype(BF16)
        outs[GROUP + k][...] = gate
        outs[2 * GROUP + k][...] = up


def raise_up(mids, weight, tile=256):
    length, depth = mids[0].shape
    count = FF_Q // tile
    out_spec = pl.BlockSpec((length, tile), lambda i: (0, i))
    low = jax.ShapeDtypeStruct((length, FF_Q), BF16)
    high = jax.ShapeDtypeStruct((length, FF_Q), F32)
    outs = pl.pallas_call(
        raise_kernel,
        grid=(count,),
        in_specs=[pl.BlockSpec((length, depth), lambda i: (0, 0))] * GROUP
        + [
            pl.BlockSpec((depth, tile), lambda i: (0, i)),
            pl.BlockSpec((depth, tile), lambda i: (0, i + count)),
        ],
        out_specs=[out_spec] * (3 * GROUP),
        out_shape=[low] * GROUP + [high] * (2 * GROUP),
        compiler_params=pltpu.CompilerParams(vmem_limit_bytes=48 * 2**20),
        cost_estimate=pl.CostEstimate(flops=0, bytes_accessed=length * depth, transcendentals=0),
        name="raise_up",
    )(*mids, weight, weight)
    return outs[:GROUP], outs[GROUP : 2 * GROUP], outs[2 * GROUP :]


def raise_back_kernel(*refs):
    grads, down_ref, gates = refs[:GROUP], refs[GROUP], refs[GROUP + 1 : 2 * GROUP + 1]
    ups, outs = refs[2 * GROUP + 1 : 3 * GROUP + 1], refs[3 * GROUP + 1 :]
    for k in range(GROUP):
        grad_hidden = dot(grads[k][...], down_ref[...])
        gate = gates[k][...]
        sigmoid = jax.nn.sigmoid(gate)
        slope = sigmoid * (1.0 + gate * (1.0 - sigmoid))
        outs[k][...] = (grad_hidden * ups[k][...] * slope).astype(BF16)
        outs[GROUP + k][...] = (grad_hidden * gate * sigmoid).astype(BF16)


def raise_back(grads, weight, gates, ups, tile=256):
    length, depth = grads[0].shape
    count = FF_Q // tile
    spec = pl.BlockSpec((length, tile), lambda i: (0, i))
    kind = jax.ShapeDtypeStruct((length, FF_Q), BF16)
    outs = pl.pallas_call(
        raise_back_kernel,
        grid=(count,),
        in_specs=[pl.BlockSpec((length, depth), lambda i: (0, 0))] * GROUP
        + [pl.BlockSpec((depth, tile), lambda i: (0, i + 2 * count))]
        + [spec] * (2 * GROUP),
        out_specs=[spec] * (2 * GROUP),
        out_shape=[kind] * (2 * GROUP),
        compiler_params=pltpu.CompilerParams(vmem_limit_bytes=48 * 2**20),
        cost_estimate=pl.CostEstimate(flops=0, bytes_accessed=length * depth, transcendentals=0),
        name="raise_back",
    )(*grads, weight, *gates, *ups)
    return outs[:GROUP], outs[GROUP:]


def assemble_kernel(place_ref, *refs):
    out_ref = refs[-1]
    number = pl.program_id(0)
    for step, ref in enumerate(refs[:-1]):

        @pl.when(number == step)
        def _():
            out_ref[0, 0] = ref[...]


def assemble(layer, copy, layers, pieces):
    rows, cols = pieces[0].shape

    def target(i, place):
        step, part = i // 2, i % 2
        source = place[0] - step
        source = jnp.where(source < 0, source + layers, source)
        part = jnp.where(step == 0, part, jnp.where(part == 0, place[1], 1 - place[1]))
        return source, part, 0, 0

    return pl.pallas_call(
        assemble_kernel,
        grid_spec=pltpu.PrefetchScalarGridSpec(
            num_scalar_prefetch=1,
            grid=(2 * layers,),
            in_specs=[pl.BlockSpec((rows, cols), lambda i, place: (0, 0))] * (2 * layers),
            out_specs=pl.BlockSpec((1, 1, rows, cols), target),
        ),
        out_shape=jax.ShapeDtypeStruct((layers, 2, rows, cols), pieces[0].dtype),
        compiler_params=pltpu.CompilerParams(vmem_limit_bytes=48 * 2**20),
        cost_estimate=pl.CostEstimate(flops=0, bytes_accessed=rows * cols, transcendentals=0),
        name="assemble",
    )(jnp.stack([layer, copy]), *pieces)


def interleave_kernel(core_ref, own_ref, other_ref, out_ref):
    rows = own_ref.shape[0]
    first = core_ref[0] == 0
    own, other = own_ref[...], other_ref[...]
    out_ref[0:rows] = jnp.where(first, own, other)
    out_ref[rows : 2 * rows] = jnp.where(first, other, own)


def interleave(core, own, other, rows):
    total, cols = own.shape
    spec = pl.BlockSpec((rows, cols), lambda i: (i, 0))
    return pl.pallas_call(
        interleave_kernel,
        grid=(total // rows,),
        in_specs=[pl.BlockSpec(memory_space=pltpu.SMEM), spec, spec],
        out_specs=pl.BlockSpec((2 * rows, cols), lambda i: (i, 0)),
        out_shape=jax.ShapeDtypeStruct((2 * total, cols), own.dtype),
        cost_estimate=pl.CostEstimate(
            flops=0, bytes_accessed=8 * total * cols, transcendentals=0
        ),
        name="interleave",
    )(core.reshape(1), own, other)


def orthonormal_kernel(source, target):
    left = source[...]
    number = lax.broadcasted_iota(jnp.int32, (left.shape[0], 1), 0)
    for step in range(left.shape[0]):
        row = left[step : step + 1]
        row = row * lax.rsqrt(jnp.sum(row * row, -1, keepdims=True))
        share = jnp.sum(left * row, -1, keepdims=True)
        left = jnp.where(
            number > step, left - share * row, jnp.where(number == step, row, left)
        )
    target[...] = left


def orthonormal(left):
    kind = jax.ShapeDtypeStruct(left.shape, F32)
    return pl.pallas_call(orthonormal_kernel, out_shape=kind, name="orthonormal")(left)


def after(value, *earlier):
    return lax.optimization_barrier((value, *earlier))[0]


def swap(value, bits):
    return lax.ppermute(value, "member", [(j, j ^ bits) for j in range(GROUP)])


def swap_layers(value, bits, layers):
    return lax.ppermute(value, "layer", [(z, z ^ bits) for z in range(layers)])


def ring(value, layers):
    return lax.ppermute(value, "layer", [(z, (z + 1) % layers) for z in range(layers)])


def cross(value, copies):
    return lax.ppermute(value, "replica", [(r, (r + 1) % copies) for r in range(copies)])


def sum_layers(partials):
    return lax.psum_scatter(partials, "layer", scatter_dimension=0, tiled=True)


def arrange(items, member):
    low, high = (member & 1) == 1, (member & 2) == 2
    pairs = [jnp.where(low, items[t ^ 1], items[t]) for t in range(GROUP)]
    return [jnp.where(high, pairs[t ^ 2], pairs[t]) for t in range(GROUP)]


class Line:
    def __init__(self, token):
        self.token = token

    def __call__(self, value):
        value, self.token = lax.optimization_barrier((value, self.token))
        return value

    def run(self, step, first, *others):
        return self(step(self(first), *others))


class Gather:
    def __init__(self, line, halves, layer, copy, layers, copies):
        self.line, self.layer, self.copy = line, layer, copy
        self.layers, self.copies = layers, copies
        self.halves = halves
        self.got = jnp.where(copy == 0, halves[0], halves[1])
        self.way, self.over_way, self.pieces, self.over = None, [], [], []

    def hop(self):
        self.way = ring(self.line(self.got), self.layers)

    def land(self):
        self.got = self.line(self.way)
        self.pieces.append(self.got)
        self.over_way.append(cross(self.got, self.copies))

    def land_over(self):
        self.over.append(self.line(self.over_way[len(self.over)]))

    def finish(self):
        while len(self.over) < self.layers - 1:
            if len(self.pieces) < self.layers - 1 and len(self.pieces) == len(self.over):
                self.hop()
                self.land()
            self.land_over()
        pieces = list(self.halves)
        for own, other in zip(self.pieces, self.over):
            pieces += [own, other]
        whole = assemble(self.layer, self.copy, self.layers, pieces)
        return whole.reshape(-1, whole.shape[-1])


def local(
    layers,
    copies,
    tokens,
    cotangent,
    needle_mask,
    segment_ids,
    attn_weight,
    ffn_weight,
    vector_params,
    attn_error,
    ffn_error,
    attn_momentum,
    ffn_momentum,
    attn_start,
    ffn_start,
    vector_momentum,
):
    length = tokens.shape[0]
    copy = lax.axis_index("replica")
    layer, member = lax.axis_index("layer"), lax.axis_index("member")

    gain_in = vector_params[0:D]
    gain_mid = vector_params[D : 2 * D]
    gain_head = vector_params[2 * D : 2 * D + 2 * HD]
    lambda_q_one = vector_params[2 * D + 2 * HD : 2 * D + 3 * HD]
    lambda_k_one = vector_params[2 * D + 3 * HD : 2 * D + 4 * HD]
    lambda_q_two = vector_params[2 * D + 4 * HD : 2 * D + 5 * HD]
    lambda_k_two = vector_params[2 * D + 5 * HD : 2 * D + 6 * HD]
    exp_one = jnp.exp(jnp.sum(lambda_q_one * lambda_k_one))
    exp_two = jnp.exp(jnp.sum(lambda_q_two * lambda_k_two))
    lam = (exp_one - exp_two + LAMBDA_INIT).reshape(1)

    line = Line(jnp.zeros((8, 128), F32))

    def gather(halves):
        return Gather(line, halves, layer, copy, layers, copies)

    def halves_of(block):
        rows = block.shape[0] // 2
        return block[:rows], block[rows:]

    def columns(values, width):
        return [values[:, t * width : (t + 1) * width] for t in range(GROUP)]

    def layer_block(parts):
        return jnp.concatenate(arrange(parts, member), 0)

    needles = jnp.broadcast_to(jnp.sum(needle_mask).astype(F32), (8, 128))
    needles_other = cross(needles, copies)
    qkv_parts = quarters(member, attn_weight, 3, ATTN_Q)
    qkv_got = [swap(qkv_parts[k], k) for k in (2, 3, 1)]
    needles = needles + line(needles_other)
    bits = 1
    while bits < layers:
        needles = needles + line(swap_layers(needles, bits, layers))
        bits *= 2
    qkv_got = [line(got) for got in qkv_got]
    qkv_block = layer_block([qkv_parts[0], qkv_got[2], qkv_got[0], qkv_got[1]])
    qkv_gather = gather(halves_of(qkv_block))
    qkv_gather.hop()
    ffn_parts = quarters(member, line(ffn_weight), 3, FF_Q)
    ffn_got = [swap(line(ffn_parts[k]), k) for k in (2, 3, 1)]
    out_own = line(attn_weight)[:, 3 * D :].astype(BF16)
    out_across = swap(out_own, 2)
    qkv_gather.land()
    qkv_gather.hop()
    residual_in = line(tokens).astype(F32)
    scale_in = rms_scale(residual_in, 1e-06)
    normed_in = residual_in * scale_in
    normed_low = line((normed_in * gain_in).astype(BF16))
    qkv_gather.land()
    qkv_gather.hop()
    lines = length // 128
    marks = segment_ids.reshape(lines, 128) + GROUP * needle_mask.reshape(lines, 128)
    small = jnp.concatenate([marks.astype(F32), needles[: 8 - lines % 8]])
    rows = small.shape[0]
    small_pair = jnp.concatenate([small, line(swap(line(small), 1))])
    out_across = swap(line(out_own), 2)
    qkv_gather.land()
    ffn_got = [line(got) for got in ffn_got]
    normed_across = swap(line(normed_low), 2)
    small_across = swap(small_pair, 2)
    normed_beside = swap(normed_low, 1)
    ffn_half = layer_block([ffn_parts[0], ffn_got[2], ffn_got[0], ffn_got[1]])
    ffn_half = ffn_half.reshape(2, -1, ffn_half.shape[1])
    ffn_half = line(lax.dynamic_index_in_dim(ffn_half, copy, 0, False))
    out_across = line(out_across)
    side = (member // 2) == 0
    out_gather = gather(
        (jnp.where(side, out_own, out_across), jnp.where(side, out_across, out_own))
    )
    out_gather.hop()
    qkv_gather.land_over()
    qkv_gather.land_over()
    out_gather.land()
    out_gather.hop()
    qkv_gather.land_over()
    ffn_weight_low = lax.all_gather(line(ffn_half), ("layer", "replica"), axis=0, tiled=True)
    out_gather.land()
    out_gather.hop()
    normed_across = line(normed_across)
    small_across = line(small_across)
    normed_opposite = swap(normed_across, 1)
    cotangent_across = swap(line(cotangent), 2)
    qkv_weight = qkv_gather.finish()
    normed_beside = line(normed_beside)

    def heads_of(qkv, segments):
        return attend(lam, qkv, segments, gain_head[None])

    qkv = [None] * GROUP
    heads = [None] * GROUP
    qkv[0] = line.run(project, normed_low, qkv_weight)
    qkv[1] = line.run(project, normed_beside, qkv_weight)
    small_beside, small_own = small_pair[rows:], small_pair[:rows]

    def marks_of(part):
        marks = part[:lines].reshape(length)
        mask = (marks >= GROUP).astype(F32)
        return marks - GROUP * mask, mask

    segments, masks = [None] * GROUP, [None] * GROUP
    segments[0], masks[0] = marks_of(small_own)
    segments[1], masks[1] = marks_of(small_beside)
    heads[0] = line.run(heads_of, qkv[0], segments[0])
    heads[1] = line.run(heads_of, qkv[1], segments[1])
    heads_beside = swap(heads[1], 1)
    segments[2], masks[2] = marks_of(small_across[:rows])
    segments[3], masks[3] = marks_of(small_across[rows:])
    out_gather.land()
    qkv[2] = line.run(project, normed_across, qkv_weight)
    heads[2] = line.run(heads_of, qkv[2], segments[2])
    heads_across = swap(heads[2], 2)
    normed_opposite = line(normed_opposite)
    cotangent_across = line(cotangent_across)
    cotangent_near = swap(line(cotangent), 1)
    cotangent_far = swap(cotangent_across, 1)
    normed_all = [normed_low, normed_beside, normed_across, normed_opposite]
    qkv[3] = line.run(project, normed_opposite, qkv_weight)
    heads[3] = line.run(heads_of, qkv[3], segments[3])
    heads_opposite = swap(heads[3], 3)
    out_mine = out_gather.finish()
    out_rest = swap(out_mine, 1)
    heads_beside, heads_across = line(heads_beside), line(heads_across)
    out_rest = line(out_rest)
    out_weight = interleave(member % 2, out_mine, out_rest, D // (layers * GROUP))
    heads_opposite = line(heads_opposite)
    heads_low = jnp.concatenate(
        arrange([heads[0], heads_beside, heads_across, heads_opposite], member), 1
    )
    residual_mid = line.run(lambda x: residual_in + dot(x, out_weight), heads_low)
    scale_mid = rms_scale(residual_mid, 1e-06)
    normed_mid = residual_mid * scale_mid
    mid_low = line((normed_mid * gain_mid).astype(BF16))
    mid_across = swap(mid_low, 2)
    mid_beside = swap(mid_low, 1)
    mid_across = line(mid_across)
    mid_opposite = swap(mid_across, 1)
    heads_across_all = swap(line(heads_low), 2)
    small = jnp.concatenate([small_pair, small_across])
    needles = sum([small[k * rows + lines, 0] for k in range(GROUP)])
    everyone = length * layers * GROUP * copies
    weight_total = everyone + NEEDLE * needles

    def grad_of(cotangent, k):
        loss_weights = 1.0 + NEEDLE * masks[k]
        return cotangent.astype(F32) * (loss_weights * (everyone / weight_total))[:, None]

    mid_beside, mid_opposite = line(mid_beside), line(mid_opposite)
    cotangents = [cotangent, line(cotangent_near), cotangent_across, line(cotangent_far)]
    grad_out = grad_of(cotangent, 0)
    grad_out_all = [line(grad_of(one, k).astype(BF16)) for k, one in enumerate(cotangents)]
    ffn_weight_low = line(ffn_weight_low)

    def product(lefts, rights, columns, place, into=None):
        return line.run(
            lambda x: weight_product([x, *lefts[1:]], rights, columns, place, into), lefts[0]
        )

    mid_all = [mid_low, mid_beside, mid_across, mid_opposite]
    hidden, gate_proj, up_proj = line.run(
        lambda x: raise_up([x, *mid_all[1:]], ffn_weight_low), mid_low
    )
    grad_gate, grad_up = line.run(
        lambda x: raise_back([x, *grad_out_all[1:]], ffn_weight_low, gate_proj, up_proj),
        grad_out_all[0],
    )
    ffn_partial = product(grad_out_all, hidden, 3 * FF_Q, 2)
    ffn_partial = product(mid_all, grad_gate, 3 * FF_Q, 0, ffn_partial)
    heads_across_all = line(heads_across_all)
    heads_beside_all = swap(line(heads_low), 1)
    heads_opposite_all = swap(heads_across_all, 1)
    ffn_partial = product(mid_all, grad_up, 3 * FF_Q, 1, ffn_partial)
    ffn_total = sum_layers(ffn_partial)

    def lower(k, got=None, kind=BF16):
        return line.run(
            lambda x: back_product([x, grad_up[k]], ffn_weight_low, got, kind), grad_gate[k]
        )

    def lower_hidden(k, got=None, kind=BF16):
        return line.run(
            lambda x: back_product([x], ffn_weight_low, got, kind, first=2), hidden[k]
        )

    opposite_got = swap(lower(3), 1)
    beside_got = swap(lower(1), 1)
    opposite_got = line(opposite_got)
    beside_got = line(beside_got)
    mid_sum = swap(lower(2, opposite_got), 2)
    grad_mid_own = lower(0, beside_got, F32)
    ffn_opposite_got = swap(lower_hidden(3), 1)
    ffn_beside_got = swap(lower_hidden(1), 1)
    mid_sum = line(mid_sum)

    grad_mid_low = grad_mid_own + mid_sum.astype(F32)
    grad_gain_mid = jnp.sum(grad_mid_low * normed_mid, 0)
    grad_mid = grad_out + norm_back(grad_mid_low * gain_mid, normed_mid, scale_mid)
    grad_attn_low = grad_mid.astype(BF16)
    grad_heads = line.run(lambda x: dot(x, out_weight, 1, 1).astype(BF16), grad_attn_low)
    grad_heads = arrange(columns(grad_heads, ATTN_Q), member)
    grad_heads_got = [swap(grad_heads[k], k) for k in (2, 3, 1)]
    grad_attn = arrange(columns(grad_attn_low, ATTN_Q), member)

    def back(grad, k):
        return attend_back(lam, qkv[k], segments[k], gain_head[None], grad)

    grad_qkv, stats = [None] * GROUP, [None] * GROUP
    grad_qkv[0], stats[0] = line.run(back, grad_heads[0], 0)
    grad_qkv[1], stats[1] = line.run(back, line(grad_heads_got[2]), 1)
    grad_heads_across, grad_heads_opposite = line(grad_heads_got[0]), line(grad_heads_got[1])
    grad_attn_got = [swap(line(grad_attn[k]), k) for k in (2, 3, 1)]
    grad_qkv[2], stats[2] = line.run(back, grad_heads_across, 2)
    grad_attn_got = [line(got) for got in grad_attn_got]
    heads_all = [heads_low, line(heads_beside_all), heads_across_all, line(heads_opposite_all)]
    grad_attn_all = [grad_attn[0], grad_attn_got[2], grad_attn_got[0], grad_attn_got[1]]
    ffn_opposite_got = line(ffn_opposite_got)
    ffn_sum = swap(lower_hidden(2, ffn_opposite_got), 2)
    attn_partial = product(heads_all, grad_attn_all, 4 * ATTN_Q, 3)
    grad_qkv[3], stats[3] = line.run(back, grad_heads_opposite, 3)
    attn_partial = product(normed_all, grad_qkv, 4 * ATTN_Q, 0, attn_partial)
    attn_total = sum_layers(attn_partial)
    ffn_sum = line(ffn_sum)
    stats = sum(stats)
    grad_gain_head, grad_lambda = stats[0], stats[1, 0]

    def lower_in(k, got=None, kind=BF16):
        return line.run(
            lambda x: back_product([x], qkv_weight, got, kind, share=1), grad_qkv[k]
        )

    def rows_of(total):
        size = total.shape[0] // GROUP
        return arrange([total[t * size : (t + 1) * size] for t in range(GROUP)], member)

    def share(parts):
        return [parts[0]] + [swap(line(parts[k]), k) for k in range(1, GROUP)]

    def landed(parts):
        return arrange([parts[0]] + [line(part) for part in parts[1:]], member)

    def left_of(grad, error, start):
        merged = grad + DECAY_ERROR * error[0]
        left = line.run(lambda x: dot(start[0], x, 1, 1, precision=HIGHEST), merged)
        return merged, left, cross(left, copies)

    def right_of(merged, left, other):
        ortho = orthonormal(left + line(other))
        right = line(dot(ortho, merged, 1, 0, precision=HIGHEST).astype(BF16))
        return ortho, right, cross(right, copies)

    def update(ortho, merged, right, other, momentum, weight):
        right = (right.astype(F32) + line(other).astype(F32)) / copies
        approx = dot(ortho, right, 0, 0, precision=HIGHEST)
        momentum_new = MOMENTUM * momentum + (1.0 - MOMENTUM) * approx
        weight_new = line(weight - RATE_MATRIX * momentum_new)
        return right, merged - approx, momentum_new, weight_new

    in_opposite_got = swap(lower_in(3), 1)
    in_beside_got = swap(lower_in(1), 1)
    ffn_shares = share(rows_of(line(ffn_total)))
    in_opposite_got = line(in_opposite_got)
    in_sent = lower_in(2, in_opposite_got)
    in_beside_got = line(in_beside_got)
    in_own = lower_in(0, in_beside_got, F32)
    ffn_own = lower_hidden(0, line(ffn_beside_got), F32)
    mixed = line((residual_mid + ffn_own + ffn_sum.astype(F32)).astype(BF16))
    ffn_rows = landed(ffn_shares)
    in_sum = swap(line(in_sent), 2)
    ffn_grad = jnp.concatenate(
        [part[:, s * FF_Q : (s + 1) * FF_Q] for s in range(3) for part in ffn_rows], 1
    ).astype(F32)
    merged_ffn, left_ffn, left_ffn_other = left_of(ffn_grad, ffn_error, ffn_start)
    ortho_ffn, right_ffn, right_ffn_other = right_of(merged_ffn, left_ffn, left_ffn_other)
    right_ffn, ffn_error_new, ffn_momentum_new, ffn_weight_new = update(
        ortho_ffn, merged_ffn, right_ffn, right_ffn_other, ffn_momentum, ffn_weight
    )
    in_sum = line(in_sum)
    grad_in_low = in_own + in_sum.astype(F32)
    grad_gain_in = line(jnp.sum(grad_in_low * normed_in, 0))
    vector_grad = jnp.concatenate(
        [
            grad_gain_in,
            grad_gain_mid,
            grad_gain_head,
            grad_lambda * exp_one * lambda_k_one,
            grad_lambda * exp_one * lambda_q_one,
            -grad_lambda * exp_two * lambda_k_two,
            -grad_lambda * exp_two * lambda_q_two,
        ]
    ).reshape(-1, 128)
    attn_shares = share(rows_of(line(attn_total)))
    attn_rows = landed(attn_shares)
    attn_grad = jnp.concatenate(
        [part[:, s * ATTN_Q : (s + 1) * ATTN_Q] for s in range(4) for part in attn_rows],
        1,
    ).astype(F32)
    merged_attn, left_attn, left_attn_other = left_of(attn_grad, attn_error, attn_start)
    vector_other = cross(line(vector_grad), copies)
    ortho_attn, right_attn, right_attn_other = right_of(merged_attn, left_attn, left_attn_other)
    vector_grad = vector_grad + line(vector_other)
    vector_other = swap(vector_grad, 1)
    grad_tokens = line(grad_mid + norm_back(grad_in_low * gain_in, normed_in, scale_in))
    right_attn, attn_error_new, attn_momentum_new, attn_weight_new = update(
        ortho_attn, merged_attn, right_attn, right_attn_other, attn_momentum, attn_weight
    )
    vector_grad = vector_grad + line(vector_other)
    bits = 1
    while bits < layers:
        vector_grad = vector_grad + line(swap_layers(vector_grad, bits, layers))
        bits *= 2
    vector_grad = (vector_grad + line(swap(vector_grad, 2))).reshape(-1)
    vector_grad = vector_grad + line.token[0, 0]
    vector_momentum_new = MOMENTUM * vector_momentum + (1.0 - MOMENTUM) * vector_grad
    vector_new = vector_params - RATE_VECTOR * vector_momentum_new
    return (
        mixed,
        grad_tokens,
        attn_grad[None],
        ffn_grad[None],
        ortho_attn,
        ortho_ffn,
        right_attn[None],
        right_ffn[None],
        attn_error_new[None],
        ffn_error_new[None],
        attn_momentum_new,
        ffn_momentum_new,
        attn_weight_new,
        ffn_weight_new,
        vector_momentum_new,
        vector_new,
    )


def solution(mesh):
    copies, shards = mesh.shape["replica"], mesh.shape["fsdp"]
    layers = shards // GROUP
    mesh = jax.sharding.Mesh(
        mesh.devices.reshape(copies, layers, GROUP), ("replica", "layer", "member")
    )
    fsdp = ("layer", "member")
    everywhere = ("replica", *fsdp)
    in_specs = (
        P(everywhere, None),
        P(everywhere, None),
        P(everywhere),
        P(everywhere, None),
        P(fsdp, None),
        P(fsdp, None),
        P(),
        P("replica", fsdp, None),
        P("replica", fsdp, None),
        P(fsdp, None),
        P(fsdp, None),
        P(fsdp, None, None),
        P(fsdp, None, None),
        P(),
    )
    out_specs = (
        P(everywhere, None),
        P(everywhere, None),
        P("replica", fsdp, None),
        P("replica", fsdp, None),
        P(None, fsdp),
        P(None, fsdp),
        P(fsdp, None, None),
        P(fsdp, None, None),
        P("replica", fsdp, None),
        P("replica", fsdp, None),
        P(fsdp, None),
        P(fsdp, None),
        P(fsdp, None),
        P(fsdp, None),
        P(),
        P(),
    )
    step = partial(local, layers, copies)
    return jax.shard_map(step, mesh=mesh, in_specs=in_specs, out_specs=out_specs, check_vma=False)
```

time: 964 us -> 694 us (0.72)
  Pallas kernels: 68.4 us -> 261 us
  matrix products: 184 us -> 41 us
  starting transfers between devices: 195 us -> 55.9 us
  waiting for transfers between devices: 336 us -> 200 us
  other arithmetic: 115 us -> 65.3 us
    pallas_call x3 -> x38, Pallas kernels: 68.4 us -> 261 us  [the longest x12 65.1 us: back_product(): pl.pallas_call(partial(back_kernel, pairs), grid=(width // tile,), in_spe...]
    dot_general x18 -> x8, matrix products: 184 us -> 41 us  [dot(): lax.dot_general(left, right, (((left_dim,), (right_dim,)), ((), ())), pre...]
    ppermute x137 -> x70, starting transfers between devices: 195 us -> 55.8 us  [the longest x48 29.3 us: swap(): return lax.ppermute(value, 'member', [(j, j ^ bits) for j in range(GROUP)])]
    ppermute x137 -> x70, waiting for transfers between devices: 336 us -> 200 us  [the longest x48 149 us: swap(): return lax.ppermute(value, 'member', [(j, j ^ bits) for j in range(GROUP)])]
    convert_element_type x22 -> x9, other arithmetic: 39.3 us -> 17.2 us  [the longest x4 8.74 us: local(): grad_of(one, k).astype(BF16)]
    dynamic_update_slice x18 -> x0, other arithmetic: 19.6 us -> none  [gather_rows(): lax.dynamic_update_slice(whole, piece[None, None], (source, owner, 0, 0))]
    unnamed x230 -> x300, local copies, waits for them, and re-layouts: 11.7 us -> 27.4 us
    unnamed x35 -> x3, other arithmetic: 10.3 us -> 0.01 us
  transfers between devices with their start and end apart: 138 -> 73, of which waited for: 53 -> 31; matrix products, arithmetic and copies ran while one was open for 29% -> 16% of each run, Pallas kernels for 7% -> 37%
where the time goes in v2:
time: 694 us; the launch traced here: 688 us
  Pallas kernels  261 us (38%)
  waiting for transfers between devices  200 us (29%)
  other arithmetic  65.3 us (9%)
  starting transfers between devices  55.9 us (8%)
  local copies, waits for them, and re-layouts  42.5 us (6%)
  matrix products  41 us (6%)
  between operations  21.9 us (3%)
    ppermute x48, waiting for transfers between devices, swap(): return lax.ppermute(value, 'member', [(j, j ^ bits) for j in range(GROUP)])  149 us
    pallas_call x12, Pallas kernels, back_product(): pl.pallas_call(partial(back_kernel, pairs), grid=(width // tile,), in_spe...  65.1 us
    pallas_call x4, Pallas kernels, attend_back(): pl.pallas_call(attend_back_kernel, grid=(1,), in_specs=attention_specs(le...  48.2 us
    pallas_call x5, Pallas kernels, weight_product(): pl.pallas_call(weight_kernel, grid=(depth // rows,), in_specs=specs, out_...  47.9 us
    dot_general x8, matrix products, dot(): lax.dot_general(left, right, (((left_dim,), (right_dim,)), ((), ())), pre...  41 us
    ppermute x6, waiting for transfers between devices, ring(): lax.ppermute(value, 'layer', [(z, (z + 1) % layers) for z in range(layers)])  36.9 us
    ppermute x48, starting transfers between devices, swap(): return lax.ppermute(value, 'member', [(j, j ^ bits) for j in range(GROUP)])  29.3 us
    unnamed x300, local copies, waits for them, and re-layouts  27.4 us
  transfers between devices with their start and end apart: 73, of which 31 were waited for; matrix products, arithmetic and copies ran while one was open for 16% of the time, Pallas kernels for 37%

profile of v2, /device:TPU:0, one launch (start us, length us, event | category | flops | bytes accessed | tf_op | source)
XLA Modules:
  0.0 687.6 jit_solution(16080328828015283298)
XLA Ops:
  36.6 7.2 %collective-permute-done.6.refs_2_ = bf16[192,1152]{1,0:T(8,128)(2,1)S(1)} collective-permute-done((bf16[192,1152]{1,0:T(8,128)(2,1)S(1)}, bf16[192,1152]{1,0:T(8,128)(2,1)S(1)}, u32[]{:S(2)}, u32[]{:S(2)}) %collective-permute-start.6) | collective-permute-done | bytes 442400 | tf_op jit(solution)/shard_map/ppermute | solution.py:471
  44.7 13.4 %collective-permute-done.10.refs_4_ = bf16[192,1152]{1,0:T(8,128)(2,1)S(1)} collective-permute-done((bf16[192,1152]{1,0:T(8,128)(2,1)S(1)}, bf16[192,1152]{1,0:T(8,128)(2,1)S(1)}, u32[]{:S(2)}, u32[]{:S(2)}) %collective-permute-start.10) | collective-permute-done | bytes 442400 | tf_op jit(solution)/shard_map/ppermute | solution.py:471
  61.7 9.6 %collective-permute-done.11.refs_6_ = bf16[192,1152]{1,0:T(8,128)(2,1)} collective-permute-done((bf16[192,1152]{1,0:T(8,128)(2,1)S(1)}, bf16[192,1152]{1,0:T(8,128)(2,1)}, u32[]{:S(2)}, u32[]{:S(2)}) %collective-permute-start.11) | collective-permute-done | bytes 442400 | tf_op jit(solution)/shard_map/ppermute | solution.py:471
  76.8 3.2 collective-permute-done.14
  84.4 6.7 collective-permute-done.15.refs_2_
  109.9 5.3 assemble.2
  116.1 11.0 %collective-permute-done.13.left_ref.refs_2_ = bf16[512,1536]{1,0:T(8,128)(2,1)S(1)} collective-permute-done((bf16[512,1536]{1,0:T(8,128)(2,1)S(1)}, bf16[512,1536]{1,0:T(8,128)(2,1)S(1)}, u32[]{:S(2)}, u32[]{:S(2)}) %collective-permute-start.13) | collective-permute-done | bytes 1572896 | tf_op jit(solution)/shard_map/ppermute | solution.py:463
  134.8 4.6 project.4.qkv_ref
  139.4 5.5 project.5.qkv_ref
  146.2 4.5 attend.4
  154.8 5.2 attend.5
  160.1 4.6 project.6.qkv_ref
  165.3 5.2 attend.6
  171.9 5.6 project.7.qkv_ref
  177.5 5.2 attend.7
  190.4 7.9 %collective-permute-done.30 = bf16[512,384]{1,0:T(8,128)(2,1)} collective-permute-done((bf16[512,384]{1,0:T(8,128)(2,1)}, bf16[512,384]{1,0:T(8,128)(2,1)}, u32[]{:S(2)}, u32[]{:S(2)}) %collective-permute-start.30) | collective-permute-done | bytes 393248 | tf_op jit(solution)/shard_map/ppermute | solution.py:463
  198.2 6.7 collective-permute-done.25
  207.6 7.0 %interleave.1 = bf16[1536,1536]{1,0:T(8,128)(2,1)} custom-call(s32[1]{0:T(128)} %bitcast.20.core_ref, bf16[768,1536]{1,0:T(8,128)(2,1)} %bitcast.137, bf16[768,1536]{1,0:T(8,128)(2,1)} %collective-permute-done.29.other_ref), custom_call_target="tpu_custom_call" | custom-call | bytes 9437184 | tf_op jit(solution)/shard_map/interleave/pallas_call | solution.py:427
  214.7 4.7 convert_add_fusion
  222.8 35.5 %collective-permute-done.34.refs_2_ = bf16[512,1536]{1,0:T(8,128)(2,1)S(1)} collective-permute-done((bf16[512,1536]{1,0:T(8,128)(2,1)S(1)}, bf16[512,1536]{1,0:T(8,128)(2,1)S(1)}, u32[]{:S(2)}, u32[]{:S(2)}) %collective-permute-start.34) | collective-permute-done | bytes 1572896 | tf_op jit(solution)/shard_map/ppermute | solution.py:463
  270.6 19.4 %raise_up.1 = (bf16[512,1024]{1,0:T(8,128)(2,1)S(1)}, bf16[512,1024]{1,0:T(8,128)(2,1)S(1)}, bf16[512,1024]{1,0:T(8,128)(2,1)S(1)}, bf16[512,1024]{1,0:T(8,128)(...) custom-call(bf16[512,1536]{1,0:T(8,128)(2,1)S(1)} %multiply_convert_, ...), custom_call_target="tpu_custom_call" | custom-call | bytes 786432 | tf_op jit(solution)/shard_map/raise_up/pallas_call | solution.py:332
  290.1 17.3 %raise_back.1 = (bf16[512,1024]{1,0:T(8,128)(2,1)S(1)}, bf16[512,1024]{1,0:T(8,128)(2,1)S(1)}, bf16[512,1024]{1,0:T(8,128)(2,1)S(1)}, bf16[512,1024]{1,0:T(8,128...) custom-call(bf16[512,1536]{1,0:T(8,128)(2,1)} %fusion.11.refs_0_, ...), custom_call_target="tpu_custom_call" | custom-call | bytes 786432 | tf_op jit(solution)/shard_map/raise_back/pallas_call | solution.py:366
  307.5 11.0 %weight_product.5.refs_8_ = bf16[1536,3072]{1,0:T(8,128)(2,1)} custom-call(bf16[512,1536]{1,0:T(8,128)(2,1)S(1)} %copy-done.7, bf16[512,1536]{1,0:T(8,128)(2,1)} %multiply_convert_fusion.refs_1_, bf16[512,1536]{1,0:T(8,128)(2,1)} %multiply_convert_fusion.1.refs_2_, bf16[512,1536]{1,0:T(8,128)(2,1)} %multiply_convert_fusion.2.refs_3_, ...), custom_call_target="tpu_custom_call" | custom-call | flops 100663296 | bytes 163840 | tf_op jit(solution)/shard_map/weight_product/pallas_call | solution.py:278
  318.5 9.8 %weight_product.6.refs_8_ = bf16[1536,3072]{1,0:T(8,128)(2,1)} custom-call(bf16[512,1536]{1,0:T(8,128)(2,1)S(1)} %multiply_convert_fusion.3.refs_0_, bf16[512,1536]{1,0:T(8,128)(2,1)} %copy-done.82, bf16[512,1536]{1,0:T(8,128)(2,1)} %copy-done.81, bf16[512,1536]{1,0:T(8,128)(2,1)} %copy-done.83, ...), custom_call_target="tpu_custom_call", output_to_operand_aliasing={{}: (8, {})} | custom-call | flops 100663296 | bytes 163840 | tf_op jit(solution)/shard_map/weight_product/pallas_call | solution.py:278
  328.4 9.6 %weight_product.7 = bf16[1536,3072]{1,0:T(8,128)(2,1)} custom-call(bf16[512,1536]{1,0:T(8,128)(2,1)S(1)} %multiply_convert_fusion.3.refs_0_, bf16[512,1536]{1,0:T(8,128)(2,1)} %copy-done.82, bf16[512,1536]{1,0:T(8,128)(2,1)} %copy-done.81, bf16[512,1536]{1,0:T(8,128)(2,1)} %copy-done.83, ...), custom_call_target="tpu_custom_call", output_to_operand_aliasing={{}: (8, {})} | custom-call | flops 100663296 | bytes 163840 | tf_op jit(solution)/shard_map/weight_product/pallas_call | solution.py:278
  340.6 5.8 back_product.12
  346.6 6.2 back_product.13
  353.4 3.0 collective-permute-done.38.refs_4_
  356.5 5.8 back_product.14
  363.9 7.0 %back_product.15 = f32[512,1536]{1,0:T(8,128)} custom-call(bf16[512,1024]{1,0:T(8,128)(2,1)S(1)} %copy-done.19, bf16[512,1024]{1,0:T(8,128)(2,1)S(1)} %copy-done.21, bf16[1536,3072]{1,0:T(8,128)(2,1)} %all-gather.2.cloned.1.call-done.refs_4_.refs_5_.refs_2_.refs_3_.refs_1_, ...), custom_call_target="tpu_custom_call" | custom-call | flops 100663296 | bytes 262144 | tf_op jit(solution)/shard_map/back_product/pallas_call | solution.py:244
  370.9 4.1 back_product.16
  375.0 5.3 back_product.17
  380.3 18.6 %collective-permute-done.41 = bf16[512,1536]{1,0:T(8,128)(2,1)S(1)} collective-permute-done((bf16[512,1536]{1,0:T(8,128)(2,1)S(1)}, bf16[512,1536]{1,0:T(8,128)(2,1)S(1)}, u32[]{:S(2)}, u32[]{:S(2)}) %collective-permute-start.41) | collective-permute-done | bytes 1572896 | tf_op jit(solution)/shard_map/ppermute | solution.py:463
  399.0 3.6 multiply_reduce_fusion
  402.6 4.2 fusion.26
  412.8 11.9 %attend_back.4 = (bf16[512,1152]{1,0:T(8,128)(2,1)S(1)}, f32[8,128]{1,0:T(8,128)S(1)}) custom-call(f32[1]{0:T(128)} %bitcast.1.lam_ref, bf16[512,1152]{1,0:T(8,128)(2,1)S(1)} %copy-done.51, f32[512,1]{1,0:T(8,128)S(1)} %copy-done.63, f32[1,512]{1,0:T(1,128)S(1)} %bitcast.140, f32[1,128]{1,0:T(1,128)S(1)} %copy-done.71, ...), custom_call_target="tpu_custom_call" | custom-call | flops 1258291200 | bytes 2752512 | tf_op jit(solution)/shard_map/attend_back/pallas_call | solution.py:173
  426.1 12.3 %attend_back.5 = (bf16[512,1152]{1,0:T(8,128)(2,1)S(1)}, f32[8,128]{1,0:T(8,128)S(1)}) custom-call(f32[1]{0:T(128)} %bitcast.1.lam_ref, bf16[512,1152]{1,0:T(8,128)(2,1)S(1)} %copy-done.49, f32[512,1]{1,0:T(8,128)S(1)} %copy-done.65, f32[1,512]{1,0:T(1,128)S(1)} %fusion.20.seg_k_ref, f32[1,128]{1,0:T(1,128)S(1)} %copy-done.71, ...), custom_call_target="tpu_custom_call" | custom-call | flops 1258291200 | bytes 2752512 | tf_op jit(solution)/shard_map/attend_back/pallas_call | solution.py:173
  440.3 10.1 %collective-permute-done.50.refs_6_ = bf16[512,384]{1,0:T(8,128)(2,1)S(1)} collective-permute-done((bf16[512,384]{1,0:T(8,128)(2,1)S(1)}, bf16[512,384]{1,0:T(8,128)(2,1)S(1)}, u32[]{:S(2)}, u32[]{:S(2)}) %collective-permute-start.50) | collective-permute-done | bytes 393248 | tf_op jit(solution)/shard_map/ppermute | solution.py:463
  450.4 12.1 %attend_back.6 = (bf16[512,1152]{1,0:T(8,128)(2,1)S(1)}, f32[8,128]{1,0:T(8,128)S(1)}) custom-call(f32[1]{0:T(128)} %bitcast.1.lam_ref, bf16[512,1152]{1,0:T(8,128)(2,1)S(1)} %copy-done.47, f32[512,1]{1,0:T(8,128)S(1)} %copy-done.61, f32[1,512]{1,0:T(1,128)S(1)} %copy-done.67, f32[1,128]{1,0:T(1,128)S(1)} %copy-done.71, ...), custom_call_target="tpu_custom_call" | custom-call | flops 1258291200 | bytes 2752512 | tf_op jit(solution)/shard_map/attend_back/pallas_call | solution.py:173
  462.5 5.3 back_product.18
  469.1 6.1 weight_product.8.refs_8_
  475.2 11.9 %attend_back.7 = (bf16[512,1152]{1,0:T(8,128)(2,1)S(1)}, f32[8,128]{1,0:T(8,128)S(1)}) custom-call(f32[1]{0:T(128)} %bitcast.1.lam_ref, bf16[512,1152]{1,0:T(8,128)(2,1)S(1)} %copy-done.45, f32[512,1]{1,0:T(8,128)S(1)} %copy-done.59, f32[1,512]{1,0:T(1,128)S(1)} %fusion.22.seg_k_ref, f32[1,128]{1,0:T(1,128)S(1)} %copy-done.71, ...), custom_call_target="tpu_custom_call" | custom-call | flops 1258291200 | bytes 2752512 | tf_op jit(solution)/shard_map/attend_back/pallas_call | solution.py:173
  487.1 11.4 %weight_product.9 = bf16[1536,1536]{1,0:T(8,128)(2,1)} custom-call(bf16[512,1536]{1,0:T(8,128)(2,1)} %copy-done.8, bf16[512,1536]{1,0:T(8,128)(2,1)} %collective-permute-done.22.left_ref.refs_1_, bf16[512,1536]{1,0:T(8,128)(2,1)} %copy-done.10, bf16[512,1536]{1,0:T(8,128)(2,1)} %collective-permute-done.20.left_ref.refs_3_, ...), custom_call_target="tpu_custom_call", output_to_operand_aliasing={{}: (8, {})} | custom-call | flops 113246208 | bytes 172032 | tf_op jit(solution)/shard_map/weight_product/pallas_call | solution.py:278
  498.5 6.4 collective-permute-done.51
  504.9 5.5 back_product.19
  510.4 5.3 back_product.20
  522.1 5.5 back_product.21
  527.6 4.8 back_product.22
  534.1 4.6 back_product.23
  540.6 3.4 add_convert_fusion
  544.0 10.9 %collective-permute-done.55 = bf16[96,3072]{1,0:T(8,128)(2,1)S(1)} collective-permute-done((bf16[96,3072]{1,0:T(8,128)(2,1)S(1)}, bf16[96,3072]{1,0:T(8,128)(2,1)S(1)}, u32[]{:S(2)}, u32[]{:S(2)}) %collective-permute-start.55) | collective-permute-done | bytes 589856 | tf_op jit(solution)/shard_map/ppermute | solution.py:463
  554.9 11.7 %collective-permute-done.54 = bf16[96,3072]{1,0:T(8,128)(2,1)S(1)} collective-permute-done((bf16[96,3072]{1,0:T(8,128)(2,1)S(1)}, bf16[96,3072]{1,0:T(8,128)(2,1)S(1)}, u32[]{:S(2)}, u32[]{:S(2)}) %collective-permute-start.54) | collective-permute-done | bytes 589856 | tf_op jit(solution)/shard_map/ppermute | solution.py:463
  571.7 3.8 convolution_bitcast_fusion
  583.0 4.8 convolution_convert_fusion
  589.4 4.3 convert_element_type.135
  594.9 10.7 %multiply_subtract_fusion = (f32[96,12288]{1,0:T(8,128)}, f32[96,12288]{1,0:T(8,128)}, f32[1,96,12288]{2,1,0:T(8,128)}) fusion(f32[96,12288]{1,0:T(8,128)S(1)} %bitcast.135, f32[96,12288]{1,0:T(8,128)} %param.24, f32[96,12288]{1,0:T(8,128)} %copy-done.75, f32[8,96]{1,0:T(8,128)S(1)} %copy-done.98, bf16[8,12288]{1,0:T(8,128)(2,1)S(1)} %collective-permute-done.59, ...), kind=kOutput, calls=%fused_computation.11 | convolution fusion | flops 120717312 | bytes 28707840 | tf_op jit(solution)/shard_map/dot_general | solution.py:45
  606.4 7.7 %collective-permute-done.57 = bf16[512,1536]{1,0:T(8,128)(2,1)} collective-permute-done((bf16[512,1536]{1,0:T(8,128)(2,1)}, bf16[512,1536]{1,0:T(8,128)(2,1)}, u32[]{:S(2)}, u32[]{:S(2)}) %collective-permute-start.57) | collective-permute-done | bytes 1572896 | tf_op jit(solution)/shard_map/ppermute | solution.py:463
  614.2 3.2 fusion.9
  622.1 5.1 fusion.8
  627.9 7.6 %collective-permute-done.61 = bf16[96,1536]{1,0:T(8,128)(2,1)} collective-permute-done((bf16[96,1536]{1,0:T(8,128)(2,1)}, bf16[96,1536]{1,0:T(8,128)(2,1)}, u32[]{:S(2)}, u32[]{:S(2)}) %collective-permute-start.61) | collective-permute-done | bytes 294944 | tf_op jit(solution)/shard_map/ppermute | solution.py:463
  639.2 3.6 convolution_bitcast_fusion.1
  653.0 4.1 collective-permute-done.65
  657.1 7.9 %multiply_subtract_fusion.1 = (f32[96,6144]{1,0:T(8,128)}, f32[96,6144]{1,0:T(8,128)}, f32[1,96,6144]{2,1,0:T(8,128)}) fusion(f32[96,6144]{1,0:T(8,128)S(1)} %copy-done.3, f32[96,6144]{1,0:T(8,128)} %param.23, f32[96,6144]{1,0:T(8,128)} %bitcast_add_fusion.1, f32[8,96]{1,0:T(8,128)S(1)} %copy-done.97, bf16[8,6144]{1,0:T(8,128)(2,1)S(1)} %collective-permute-done.65, ...), kind=kOutput, calls=%fused_computation.36 | convolution fusion | flops 60358656 | bytes 14355456 | tf_op jit(solution)/shard_map/dot_general | solution.py:45
  668.9 4.4 collective-permute-start.68
  (519 shorter events, 170.0 us)
Async XLA Ops:
  7.2 263.4 %all-gather.2.cloned.1.call-start = ((), (), s32[]{:S(2)}) async-start(), calls=%async_computation.2 | async-start | bytes 10616832 | tf_op jit(solution)/shard_map/all_gather | solution.py:630
  13.9 6.5 collective-permute-start.3
  18.2 7.4 %collective-permute-start.1 = (bf16[96,1152]{1,0:T(8,128)(2,1)S(1)}, bf16[96,1152]{1,0:T(8,128)(2,1)S(1)}, u32[]{:S(2)}, u32[]{:S(2)}) collective-permute-start(bf16[96,1152]{1,0:T(8,128)(2,1)S(1)} %get-tuple-element.443), channel_id=1, source_target_pairs={{0,2},{1,3},{2,0},{3,1},{4,6},{5,7},{6,4},{7,5},{8,10},{9,11},{10,... | collective-permute-start | bytes 663560 | tf_op jit(solution)/shard_map/ppermute | solution.py:463
  19.8 8.1 %collective-permute-start = (bf16[96,1152]{1,0:T(8,128)(2,1)S(1)}, bf16[96,1152]{1,0:T(8,128)(2,1)S(1)}, u32[]{:S(2)}, u32[]{:S(2)}) collective-permute-start(bf16[96,1152]{1,0:T(8,128)(2,1)S(1)} %get-tuple-element.442), channel_id=1, source_target_pairs={{0,3},{1,2},{2,1},{3,0},{4,7},{5,6},{6,5},{7,4},{8,11},{9,10},{10,... | collective-permute-start | bytes 663560 | tf_op jit(solution)/shard_map/ppermute | solution.py:463
  19.8 8.1 %collective-permute-start.5 = (bf16[96,1152]{1,0:T(8,128)(2,1)S(1)}, bf16[96,1152]{1,0:T(8,128)(2,1)S(1)}, u32[]{:S(2)}, u32[]{:S(2)}) collective-permute-start(bf16[96,1152]{1,0:T(8,128)(2,1)S(1)} %get-tuple-element.452), channel_id=1, source_target_pairs={{0,1},{1,0},{2,3},{3,2},{4,5},{5,4},{6,7},{7,6},{8,9},{9,8},{10,11... | collective-permute-start | bytes 663560 | tf_op jit(solution)/shard_map/ppermute | solution.py:463
  29.1 14.7 %collective-permute-start.6 = (bf16[192,1152]{1,0:T(8,128)(2,1)S(1)}, bf16[192,1152]{1,0:T(8,128)(2,1)S(1)}, u32[]{:S(2)}, u32[]{:S(2)}) collective-permute-start(bf16[192,1152]{1,0:T(8,128)(2,1)S(1)} %get-tuple-element.457), channel_id=1, source_target_pairs={{0,4},{4,8},{8,12},{12,0},{1,5},{5,9},{9,13},{13,1},{2,6},{6,10},{... | collective-permute-start | bytes 1327112 | tf_op jit(solution)/shard_map/ppermute | solution.py:471
  34.4 38.3 %collective-permute-start.9 = (bf16[96,3072]{1,0:T(8,128)(2,1)}, bf16[96,3072]{1,0:T(8,128)(2,1)}, u32[]{:S(2)}, u32[]{:S(2)}) collective-permute-start(bf16[96,3072]{1,0:T(8,128)(2,1)} %get-tuple-element.474), channel_id=1, source_target_pairs={{0,2},{1,3},{2,0},{3,1},{4,6},{5,7},{6,4},{7,5},{8,10},{9,11},{10,... | collective-permute-start | bytes 1769480 | tf_op jit(solution)/shard_map/ppermute | solution.py:463
  34.7 39.1 %collective-permute-start.8 = (bf16[96,3072]{1,0:T(8,128)(2,1)}, bf16[96,3072]{1,0:T(8,128)(2,1)}, u32[]{:S(2)}, u32[]{:S(2)}) collective-permute-start(bf16[96,3072]{1,0:T(8,128)(2,1)} %get-tuple-element.473), channel_id=1, source_target_pairs={{0,3},{1,2},{2,1},{3,0},{4,7},{5,6},{6,5},{7,4},{8,11},{9,10},{10,... | collective-permute-start | bytes 1769480 | tf_op jit(solution)/shard_map/ppermute | solution.py:463
  36.3 37.6 %collective-permute-start.7 = (bf16[96,3072]{1,0:T(8,128)(2,1)}, bf16[96,3072]{1,0:T(8,128)(2,1)}, u32[]{:S(2)}, u32[]{:S(2)}) collective-permute-start(bf16[96,3072]{1,0:T(8,128)(2,1)} %get-tuple-element.472), channel_id=1, source_target_pairs={{0,1},{1,0},{2,3},{3,2},{4,5},{5,4},{6,7},{7,6},{8,9},{9,8},{10,11... | collective-permute-start | bytes 1769480 | tf_op jit(solution)/shard_map/ppermute | solution.py:463
  44.2 13.9 %collective-permute-start.10 = (bf16[192,1152]{1,0:T(8,128)(2,1)S(1)}, bf16[192,1152]{1,0:T(8,128)(2,1)S(1)}, u32[]{:S(2)}, u32[]{:S(2)}) collective-permute-start(bf16[192,1152]{1,0:T(8,128)(2,1)S(1)} %collective-permute-done.6.refs_2_), channel_id=1, source_target_pairs={{0,4},{4,8},{8,12},{12,0},{1,5},{5,9},{9,13},{13,1},{2,6},{6,10},{... | collective-permute-start | bytes 1327112 | tf_op jit(solution)/shard_map/ppermute | solution.py:471
  58.1 13.1 %collective-permute-start.11 = (bf16[192,1152]{1,0:T(8,128)(2,1)S(1)}, bf16[192,1152]{1,0:T(8,128)(2,1)}, u32[]{:S(2)}, u32[]{:S(2)}) collective-permute-start(bf16[192,1152]{1,0:T(8,128)(2,1)S(1)} %collective-permute-done.10.refs_4_), channel_id=1, source_target_pairs={{0,4},{4,8},{8,12},{12,0},{1,5},{5,9},{9,13},{13,1},{2,6},{6,10},{... | collective-permute-start | bytes 1327112 | tf_op jit(solution)/shard_map/ppermute | solution.py:471
  60.1 22.4 %collective-permute-start.17 = (bf16[192,1152]{1,0:T(8,128)(2,1)S(1)}, bf16[192,1152]{1,0:T(8,128)(2,1)}, u32[]{:S(2)}, u32[]{:S(2)}) collective-permute-start(bf16[192,1152]{1,0:T(8,128)(2,1)S(1)} %collective-permute-done.6.refs_2_), channel_id=1, source_target_pairs={{0,16},{16,0},{1,17},{17,1},{2,18},{18,2},{3,19},{19,3},{4,20},{20... | collective-permute-start | bytes 1327112 | tf_op jit(solution)/shard_map/ppermute | solution.py:475
  71.2 13.2 %collective-permute-start.16 = (bf16[192,1152]{1,0:T(8,128)(2,1)S(1)}, bf16[192,1152]{1,0:T(8,128)(2,1)}, u32[]{:S(2)}, u32[]{:S(2)}) collective-permute-start(bf16[192,1152]{1,0:T(8,128)(2,1)S(1)} %collective-permute-done.10.refs_4_), channel_id=1, source_target_pairs={{0,16},{16,0},{1,17},{17,1},{2,18},{18,2},{3,19},{19,3},{4,20},{20... | collective-permute-start | bytes 1327112 | tf_op jit(solution)/shard_map/ppermute | solution.py:475
  72.7 7.2 %collective-permute-start.14 = (bf16[96,1536]{1,0:T(8,128)(2,1)}, bf16[96,1536]{1,0:T(8,128)(2,1)}, u32[]{:S(2)}, u32[]{:S(2)}) collective-permute-start(bf16[96,1536]{1,0:T(8,128)(2,1)} %slice.493), channel_id=1, source_target_pairs={{0,2},{1,3},{2,0},{3,1},{4,6},{5,7},{6,4},{7,5},{8,10},{9,11},{10,... | collective-permute-start | bytes 884744 | tf_op jit(solution)/shard_map/ppermute | solution.py:463
  80.0 11.7 %collective-permute-start.19 = (bf16[192,1152]{1,0:T(8,128)(2,1)}, bf16[192,1152]{1,0:T(8,128)(2,1)S(1)}, u32[]{:S(2)}, u32[]{:S(2)}) collective-permute-start(bf16[192,1152]{1,0:T(8,128)(2,1)} %collective-permute-done.11.refs_6_), channel_id=1, source_target_pairs={{0,16},{16,0},{1,17},{17,1},{2,18},{18,2},{3,19},{19,3},{4,20},{20... | collective-permute-start | bytes 1327112 | tf_op jit(solution)/shard_map/ppermute | solution.py:475
  82.5 8.6 %collective-permute-start.15 = (bf16[96,1536]{1,0:T(8,128)(2,1)S(1)}, bf16[96,1536]{1,0:T(8,128)(2,1)}, u32[]{:S(2)}, u32[]{:S(2)}) collective-permute-start(bf16[96,1536]{1,0:T(8,128)(2,1)S(1)} %get-tuple-element.499), channel_id=1, source_target_pairs={{0,4},{4,8},{8,12},{12,0},{1,5},{5,9},{9,13},{13,1},{2,6},{6,10},{... | collective-permute-start | bytes 884744 | tf_op jit(solution)/shard_map/ppermute | solution.py:471
  92.5 427.6 %reduce-scatter.3.cloned.1.call-start = ((), (), s32[]{:S(2)}) async-start(), calls=%async_computation.3 | async-start | bytes 11796480 | tf_op jit(solution)/shard_map/reduce_scatter | solution.py:479
  92.5 34.5 %collective-permute-start.13 = (bf16[512,1536]{1,0:T(8,128)(2,1)S(1)}, bf16[512,1536]{1,0:T(8,128)(2,1)S(1)}, u32[]{:S(2)}, u32[]{:S(2)}) collective-permute-start(bf16[512,1536]{1,0:T(8,128)(2,1)S(1)} %fusion.4.left_ref.refs_0_), channel_id=1, source_target_pairs={{0,2},{1,3},{2,0},{3,1},{4,6},{5,7},{6,4},{7,5},{8,10},{9,11},{10,... | collective-permute-start | bytes 4718600 | tf_op jit(solution)/shard_map/ppermute | solution.py:463
  93.8 39.3 %collective-permute-start.22 = (bf16[512,1536]{1,0:T(8,128)(2,1)S(1)}, bf16[512,1536]{1,0:T(8,128)(2,1)}, u32[]{:S(2)}, u32[]{:S(2)}) collective-permute-start(bf16[512,1536]{1,0:T(8,128)(2,1)S(1)} %fusion.4.left_ref.refs_0_), channel_id=1, source_target_pairs={{0,1},{1,0},{2,3},{3,2},{4,5},{5,4},{6,7},{7,6},{8,9},{9,8},{10,11... | collective-permute-start | bytes 4718600 | tf_op jit(solution)/shard_map/ppermute | solution.py:463
  94.5 20.7 %collective-permute-start.18 = (bf16[96,1536]{1,0:T(8,128)(2,1)}, bf16[96,1536]{1,0:T(8,128)(2,1)}, u32[]{:S(2)}, u32[]{:S(2)}) collective-permute-start(bf16[96,1536]{1,0:T(8,128)(2,1)} %collective-permute-done.15.refs_2_), channel_id=1, source_target_pairs={{0,4},{4,8},{8,12},{12,0},{1,5},{5,9},{9,13},{13,1},{2,6},{6,10},{... | collective-permute-start | bytes 884744 | tf_op jit(solution)/shard_map/ppermute | solution.py:471
  97.3 29.9 %collective-permute-start.23 = (f32[16,128]{1,0:T(8,128)}, f32[16,128]{1,0:T(8,128)}, u32[]{:S(2)}, u32[]{:S(2)}) collective-permute-start(f32[16,128]{1,0:T(8,128)} %pad_maximum_fusion.4), channel_id=1, source_target_pairs={{0,2},{1,3},{2,0},{3,1},{4,6},{5,7},{6,4},{7,5},{8,10},{9,11},{10,... | collective-permute-start | bytes 24584 | tf_op jit(solution)/shard_map/ppermute | solution.py:463
  103.3 79.5 %collective-permute-start.26 = (bf16[96,1536]{1,0:T(8,128)(2,1)}, bf16[96,1536]{1,0:T(8,128)(2,1)}, u32[]{:S(2)}, u32[]{:S(2)}) collective-permute-start(bf16[96,1536]{1,0:T(8,128)(2,1)} %collective-permute-done.15.refs_2_), channel_id=1, source_target_pairs={{0,16},{16,0},{1,17},{17,1},{2,18},{18,2},{3,19},{19,3},{4,20},{20... | collective-permute-start | bytes 884744 | tf_op jit(solution)/shard_map/ppermute | solution.py:475
  115.2 44.9 %collective-permute-start.21 = (bf16[96,1536]{1,0:T(8,128)(2,1)}, bf16[96,1536]{1,0:T(8,128)(2,1)}, u32[]{:S(2)}, u32[]{:S(2)}) collective-permute-start(bf16[96,1536]{1,0:T(8,128)(2,1)} %collective-permute-done.18.refs_4_), channel_id=1, source_target_pairs={{0,4},{4,8},{8,12},{12,0},{1,5},{5,9},{9,13},{13,1},{2,6},{6,10},{... | collective-permute-start | bytes 884744 | tf_op jit(solution)/shard_map/ppermute | solution.py:471
  129.8 42.1 %collective-permute-start.20 = (bf16[512,1536]{1,0:T(8,128)(2,1)S(1)}, bf16[512,1536]{1,0:T(8,128)(2,1)}, u32[]{:S(2)}, u32[]{:S(2)}) collective-permute-start(bf16[512,1536]{1,0:T(8,128)(2,1)S(1)} %collective-permute-done.13.left_ref.refs_2_), channel_id=1, source_target_pairs={{0,1},{1,0},{2,3},{3,2},{4,5},{5,4},{6,7},{7,6},{8,9},{9,8},{10,11... | collective-permute-start | bytes 4718600 | tf_op jit(solution)/shard_map/ppermute | solution.py:463
  129.9 42.0 %collective-permute-start.24 = (bf16[512,1536]{1,0:T(8,128)(2,1)}, bf16[512,1536]{1,0:T(8,128)(2,1)}, u32[]{:S(2)}, u32[]{:S(2)}) collective-permute-start(bf16[512,1536]{1,0:T(8,128)(2,1)} %param.15), channel_id=1, source_target_pairs={{0,2},{1,3},{2,0},{3,1},{4,6},{5,7},{6,4},{7,5},{8,10},{9,11},{10,... | collective-permute-start | bytes 4718600 | tf_op jit(solution)/shard_map/ppermute | solution.py:463
  133.1 49.7 %collective-permute-start.27 = (bf16[96,1536]{1,0:T(8,128)(2,1)}, bf16[96,1536]{1,0:T(8,128)(2,1)}, u32[]{:S(2)}, u32[]{:S(2)}) collective-permute-start(bf16[96,1536]{1,0:T(8,128)(2,1)} %collective-permute-done.18.refs_4_), channel_id=1, source_target_pairs={{0,16},{16,0},{1,17},{17,1},{2,18},{18,2},{3,19},{19,3},{4,20},{20... | collective-permute-start | bytes 884744 | tf_op jit(solution)/shard_map/ppermute | solution.py:475
  164.8 18.0 %collective-permute-start.28 = (bf16[96,1536]{1,0:T(8,128)(2,1)}, bf16[96,1536]{1,0:T(8,128)(2,1)S(1)}, u32[]{:S(2)}, u32[]{:S(2)}) collective-permute-start(bf16[96,1536]{1,0:T(8,128)(2,1)} %collective-permute-done.21.refs_6_), channel_id=1, source_target_pairs={{0,16},{16,0},{1,17},{17,1},{2,18},{18,2},{3,19},{19,3},{4,20},{20... | collective-permute-start | bytes 884744 | tf_op jit(solution)/shard_map/ppermute | solution.py:475
  185.4 12.9 %collective-permute-start.29 = (bf16[768,1536]{1,0:T(8,128)(2,1)S(1)}, bf16[768,1536]{1,0:T(8,128)(2,1)}, u32[]{:S(2)}, u32[]{:S(2)}) collective-permute-start(bf16[768,1536]{1,0:T(8,128)(2,1)S(1)} %bitcast.136), channel_id=1, source_target_pairs={{0,1},{1,0},{2,3},{3,2},{4,5},{5,4},{6,7},{7,6},{8,9},{9,8},{10,11... | collective-permute-start | bytes 7077896 | tf_op jit(solution)/shard_map/ppermute | solution.py:463
  185.4 4.9 collective-permute-start.31
  185.9 12.3 %collective-permute-start.30 = (bf16[512,384]{1,0:T(8,128)(2,1)}, bf16[512,384]{1,0:T(8,128)(2,1)}, u32[]{:S(2)}, u32[]{:S(2)}) collective-permute-start(bf16[512,384]{1,0:T(8,128)(2,1)} %attend.6), channel_id=1, source_target_pairs={{0,2},{1,3},{2,0},{3,1},{4,6},{5,7},{6,4},{7,5},{8,10},{9,11},{10,... | collective-permute-start | bytes 1179656 | tf_op jit(solution)/shard_map/ppermute | solution.py:463
  186.9 18.0 %collective-permute-start.25 = (bf16[512,384]{1,0:T(8,128)(2,1)}, bf16[512,384]{1,0:T(8,128)(2,1)}, u32[]{:S(2)}, u32[]{:S(2)}) collective-permute-start(bf16[512,384]{1,0:T(8,128)(2,1)} %attend.7), channel_id=1, source_target_pairs={{0,3},{1,2},{2,1},{3,0},{4,7},{5,6},{6,5},{7,4},{8,11},{9,10},{10,... | collective-permute-start | bytes 1179656 | tf_op jit(solution)/shard_map/ppermute | solution.py:463
  221.0 37.2 %collective-permute-start.34 = (bf16[512,1536]{1,0:T(8,128)(2,1)S(1)}, bf16[512,1536]{1,0:T(8,128)(2,1)S(1)}, u32[]{:S(2)}, u32[]{:S(2)}) collective-permute-start(bf16[512,1536]{1,0:T(8,128)(2,1)S(1)} %multiply_convert_fusion.3.refs_0_), channel_id=1, source_target_pairs={{0,2},{1,3},{2,0},{3,1},{4,6},{5,7},{6,4},{7,5},{8,10},{9,11},{10,... | collective-permute-start | bytes 4718600 | tf_op jit(solution)/shard_map/ppermute | solution.py:463
  221.9 43.5 %collective-permute-start.36 = (bf16[512,1536]{1,0:T(8,128)(2,1)S(1)}, bf16[512,1536]{1,0:T(8,128)(2,1)S(1)}, u32[]{:S(2)}, u32[]{:S(2)}) collective-permute-start(bf16[512,1536]{1,0:T(8,128)(2,1)S(1)} %multiply_convert_fusion.3.refs_0_), channel_id=1, source_target_pairs={{0,1},{1,0},{2,3},{3,2},{4,5},{5,4},{6,7},{7,6},{8,9},{9,8},{10,11... | collective-permute-start | bytes 4718600 | tf_op jit(solution)/shard_map/ppermute | solution.py:463
  258.3 7.1 %collective-permute-start.35 = (bf16[512,1536]{1,0:T(8,128)(2,1)S(1)}, bf16[512,1536]{1,0:T(8,128)(2,1)S(1)}, u32[]{:S(2)}, u32[]{:S(2)}) collective-permute-start(bf16[512,1536]{1,0:T(8,128)(2,1)S(1)} %collective-permute-done.34.refs_2_), channel_id=1, source_target_pairs={{0,1},{1,0},{2,3},{3,2},{4,5},{5,4},{6,7},{7,6},{8,9},{9,8},{10,11... | collective-permute-start | bytes 4718600 | tf_op jit(solution)/shard_map/ppermute | solution.py:463
  258.3 8.2 %collective-permute-start.33 = (bf16[512,1536]{1,0:T(8,128)(2,1)}, bf16[512,1536]{1,0:T(8,128)(2,1)S(1)}, u32[]{:S(2)}, u32[]{:S(2)}) collective-permute-start(bf16[512,1536]{1,0:T(8,128)(2,1)} %param.15), channel_id=1, source_target_pairs={{0,1},{1,0},{2,3},{3,2},{4,5},{5,4},{6,7},{7,6},{8,9},{9,8},{10,11... | collective-permute-start | bytes 4718600 | tf_op jit(solution)/shard_map/ppermute | solution.py:463
  258.8 8.9 %collective-permute-start.32 = (bf16[512,1536]{1,0:T(8,128)(2,1)}, bf16[512,1536]{1,0:T(8,128)(2,1)S(1)}, u32[]{:S(2)}, u32[]{:S(2)}) collective-permute-start(bf16[512,1536]{1,0:T(8,128)(2,1)} %collective-permute-done.24), channel_id=1, source_target_pairs={{0,1},{1,0},{2,3},{3,2},{4,5},{5,4},{6,7},{7,6},{8,9},{9,8},{10,11... | collective-permute-start | bytes 4718600 | tf_op jit(solution)/shard_map/ppermute | solution.py:463
  261.7 66.6 %collective-permute-start.37 = (bf16[512,1536]{1,0:T(8,128)(2,1)S(1)}, bf16[512,1536]{1,0:T(8,128)(2,1)}, u32[]{:S(2)}, u32[]{:S(2)}) collective-permute-start(bf16[512,1536]{1,0:T(8,128)(2,1)S(1)} %copy-done.11), channel_id=1, source_target_pairs={{0,2},{1,3},{2,0},{3,1},{4,6},{5,7},{6,4},{7,5},{8,10},{9,11},{10,... | collective-permute-start | bytes 4718600 | tf_op jit(solution)/shard_map/ppermute | solution.py:463
  338.0 279.4 %reduce-scatter.5.cloned.1.call-start = ((), (), s32[]{:S(2)}) async-start(), calls=%async_computation.4 | async-start | bytes 5898240 | tf_op jit(solution)/shard_map/reduce_scatter | solution.py:479
  346.4 7.0 %collective-permute-start.39 = (bf16[512,1536]{1,0:T(8,128)(2,1)S(1)}, bf16[512,1536]{1,0:T(8,128)(2,1)S(1)}, u32[]{:S(2)}, u32[]{:S(2)}) collective-permute-start(bf16[512,1536]{1,0:T(8,128)(2,1)S(1)} %back_product.12), channel_id=1, source_target_pairs={{0,1},{1,0},{2,3},{3,2},{4,5},{5,4},{6,7},{7,6},{8,9},{9,8},{10,11... | collective-permute-start | bytes 4718600 | tf_op jit(solution)/shard_map/ppermute | solution.py:463
  362.2 36.7 %collective-permute-start.41 = (bf16[512,1536]{1,0:T(8,128)(2,1)S(1)}, bf16[512,1536]{1,0:T(8,128)(2,1)S(1)}, u32[]{:S(2)}, u32[]{:S(2)}) collective-permute-start(bf16[512,1536]{1,0:T(8,128)(2,1)S(1)} %back_product.14), channel_id=1, source_target_pairs={{0,2},{1,3},{2,0},{3,1},{4,6},{5,7},{6,4},{7,5},{8,10},{9,11},{10,... | collective-permute-start | bytes 4718600 | tf_op jit(solution)/shard_map/ppermute | solution.py:463
  409.8 52.7 %collective-permute-start.47 = (bf16[512,1536]{1,0:T(8,128)(2,1)S(1)}, bf16[512,1536]{1,0:T(8,128)(2,1)S(1)}, u32[]{:S(2)}, u32[]{:S(2)}) collective-permute-start(bf16[512,1536]{1,0:T(8,128)(2,1)S(1)} %copy-done.11), channel_id=1, source_target_pairs={{0,1},{1,0},{2,3},{3,2},{4,5},{5,4},{6,7},{7,6},{8,9},{9,8},{10,11... | collective-permute-start | bytes 4718600 | tf_op jit(solution)/shard_map/ppermute | solution.py:463
  410.2 52.3 %collective-permute-start.46 = (bf16[512,1536]{1,0:T(8,128)(2,1)}, bf16[512,1536]{1,0:T(8,128)(2,1)}, u32[]{:S(2)}, u32[]{:S(2)}) collective-permute-start(bf16[512,1536]{1,0:T(8,128)(2,1)} %collective-permute-done.37.refs_2_), channel_id=1, source_target_pairs={{0,1},{1,0},{2,3},{3,2},{4,5},{5,4},{6,7},{7,6},{8,9},{9,8},{10,11... | collective-permute-start | bytes 4718600 | tf_op jit(solution)/shard_map/ppermute | solution.py:463
  410.3 52.2 %collective-permute-start.45 = (bf16[512,1536]{1,0:T(8,128)(2,1)S(1)}, bf16[512,1536]{1,0:T(8,128)(2,1)S(1)}, u32[]{:S(2)}, u32[]{:S(2)}) collective-permute-start(bf16[512,1536]{1,0:T(8,128)(2,1)S(1)} %back_product.16), channel_id=1, source_target_pairs={{0,1},{1,0},{2,3},{3,2},{4,5},{5,4},{6,7},{7,6},{8,9},{9,8},{10,11... | collective-permute-start | bytes 4718600 | tf_op jit(solution)/shard_map/ppermute | solution.py:463
  410.8 27.6 %collective-permute-start.44 = (bf16[512,384]{1,0:T(8,128)(2,1)S(1)}, bf16[512,384]{1,0:T(8,128)(2,1)S(1)}, u32[]{:S(2)}, u32[]{:S(2)}) collective-permute-start(bf16[512,384]{1,0:T(8,128)(2,1)S(1)} %get-tuple-element.913), channel_id=1, source_target_pairs={{0,2},{1,3},{2,0},{3,1},{4,6},{5,7},{6,4},{7,5},{8,10},{9,11},{10,... | collective-permute-start | bytes 1179656 | tf_op jit(solution)/shard_map/ppermute | solution.py:463
  412.3 26.1 %collective-permute-start.43 = (bf16[512,384]{1,0:T(8,128)(2,1)S(1)}, bf16[512,384]{1,0:T(8,128)(2,1)S(1)}, u32[]{:S(2)}, u32[]{:S(2)}) collective-permute-start(bf16[512,384]{1,0:T(8,128)(2,1)S(1)} %get-tuple-element.912), channel_id=1, source_target_pairs={{0,3},{1,2},{2,1},{3,0},{4,7},{5,6},{6,5},{7,4},{8,11},{9,10},{10,... | collective-permute-start | bytes 1179656 | tf_op jit(solution)/shard_map/ppermute | solution.py:463
  438.4 12.0 %collective-permute-start.50 = (bf16[512,384]{1,0:T(8,128)(2,1)S(1)}, bf16[512,384]{1,0:T(8,128)(2,1)S(1)}, u32[]{:S(2)}, u32[]{:S(2)}) collective-permute-start(bf16[512,384]{1,0:T(8,128)(2,1)S(1)} %get-tuple-element.721), channel_id=1, source_target_pairs={{0,2},{1,3},{2,0},{3,1},{4,6},{5,7},{6,4},{7,5},{8,10},{9,11},{10,... | collective-permute-start | bytes 1179656 | tf_op jit(solution)/shard_map/ppermute | solution.py:463
  439.4 23.1 %collective-permute-start.49 = (bf16[512,384]{1,0:T(8,128)(2,1)S(1)}, bf16[512,384]{1,0:T(8,128)(2,1)S(1)}, u32[]{:S(2)}, u32[]{:S(2)}) collective-permute-start(bf16[512,384]{1,0:T(8,128)(2,1)S(1)} %get-tuple-element.720), channel_id=1, source_target_pairs={{0,3},{1,2},{2,1},{3,0},{4,7},{5,6},{6,5},{7,4},{8,11},{9,10},{10,... | collective-permute-start | bytes 1179656 | tf_op jit(solution)/shard_map/ppermute | solution.py:463
  450.4 12.1 %collective-permute-start.48 = (bf16[512,384]{1,0:T(8,128)(2,1)S(1)}, bf16[512,384]{1,0:T(8,128)(2,1)S(1)}, u32[]{:S(2)}, u32[]{:S(2)}) collective-permute-start(bf16[512,384]{1,0:T(8,128)(2,1)S(1)} %get-tuple-element.719), channel_id=1, source_target_pairs={{0,1},{1,0},{2,3},{3,2},{4,5},{5,4},{6,7},{7,6},{8,9},{9,8},{10,11... | collective-permute-start | bytes 1179656 | tf_op jit(solution)/shard_map/ppermute | solution.py:463
  467.8 37.1 %collective-permute-start.51 = (bf16[512,1536]{1,0:T(8,128)(2,1)}, bf16[512,1536]{1,0:T(8,128)(2,1)}, u32[]{:S(2)}, u32[]{:S(2)}) collective-permute-start(bf16[512,1536]{1,0:T(8,128)(2,1)} %back_product.18), channel_id=1, source_target_pairs={{0,2},{1,3},{2,0},{3,1},{4,6},{5,7},{6,4},{7,5},{8,10},{9,11},{10,... | collective-permute-start | bytes 4718600 | tf_op jit(solution)/shard_map/ppermute | solution.py:463
  469.0 65.1 %collective-permute-start.40 = (bf16[512,1536]{1,0:T(8,128)(2,1)}, bf16[512,1536]{1,0:T(8,128)(2,1)}, u32[]{:S(2)}, u32[]{:S(2)}) collective-permute-start(bf16[512,1536]{1,0:T(8,128)(2,1)} %back_product.17), channel_id=1, source_target_pairs={{0,1},{1,0},{2,3},{3,2},{4,5},{5,4},{6,7},{7,6},{8,9},{9,8},{10,11... | collective-permute-start | bytes 4718600 | tf_op jit(solution)/shard_map/ppermute | solution.py:463
  510.4 11.6 %collective-permute-start.53 = (bf16[512,1536]{1,0:T(8,128)(2,1)}, bf16[512,1536]{1,0:T(8,128)(2,1)}, u32[]{:S(2)}, u32[]{:S(2)}) collective-permute-start(bf16[512,1536]{1,0:T(8,128)(2,1)} %back_product.19), channel_id=1, source_target_pairs={{0,1},{1,0},{2,3},{3,2},{4,5},{5,4},{6,7},{7,6},{8,9},{9,8},{10,11... | collective-permute-start | bytes 4718600 | tf_op jit(solution)/shard_map/ppermute | solution.py:463
  515.7 11.9 %collective-permute-start.52 = (bf16[512,1536]{1,0:T(8,128)(2,1)}, bf16[512,1536]{1,0:T(8,128)(2,1)}, u32[]{:S(2)}, u32[]{:S(2)}) collective-permute-start(bf16[512,1536]{1,0:T(8,128)(2,1)} %back_product.20), channel_id=1, source_target_pairs={{0,1},{1,0},{2,3},{3,2},{4,5},{5,4},{6,7},{7,6},{8,9},{9,8},{10,11... | collective-permute-start | bytes 4718600 | tf_op jit(solution)/shard_map/ppermute | solution.py:463
  538.7 5.3 collective-permute-start.56
  538.7 16.2 %collective-permute-start.55 = (bf16[96,3072]{1,0:T(8,128)(2,1)S(1)}, bf16[96,3072]{1,0:T(8,128)(2,1)S(1)}, u32[]{:S(2)}, u32[]{:S(2)}) collective-permute-start(bf16[96,3072]{1,0:T(8,128)(2,1)S(1)} %get-tuple-element.796), channel_id=1, source_target_pairs={{0,2},{1,3},{2,0},{3,1},{4,6},{5,7},{6,4},{7,5},{8,10},{9,11},{10,... | collective-permute-start | bytes 1769480 | tf_op jit(solution)/shard_map/ppermute | solution.py:463
  540.0 26.6 %collective-permute-start.54 = (bf16[96,3072]{1,0:T(8,128)(2,1)S(1)}, bf16[96,3072]{1,0:T(8,128)(2,1)S(1)}, u32[]{:S(2)}, u32[]{:S(2)}) collective-permute-start(bf16[96,3072]{1,0:T(8,128)(2,1)S(1)} %get-tuple-element.795), channel_id=1, source_target_pairs={{0,3},{1,2},{2,1},{3,0},{4,7},{5,6},{6,5},{7,4},{8,11},{9,10},{10,... | collective-permute-start | bytes 1769480 | tf_op jit(solution)/shard_map/ppermute | solution.py:463
  577.1 37.0 %collective-permute-start.57 = (bf16[512,1536]{1,0:T(8,128)(2,1)}, bf16[512,1536]{1,0:T(8,128)(2,1)}, u32[]{:S(2)}, u32[]{:S(2)}) collective-permute-start(bf16[512,1536]{1,0:T(8,128)(2,1)} %back_product.21), channel_id=1, source_target_pairs={{0,2},{1,3},{2,0},{3,1},{4,6},{5,7},{6,4},{7,5},{8,10},{9,11},{10,... | collective-permute-start | bytes 4718600 | tf_op jit(solution)/shard_map/ppermute | solution.py:463
  587.8 7.0 %collective-permute-start.59 = (bf16[8,12288]{1,0:T(8,128)(2,1)S(1)}, bf16[8,12288]{1,0:T(8,128)(2,1)S(1)}, u32[]{:S(2)}, u32[]{:S(2)}) collective-permute-start(bf16[8,12288]{1,0:T(8,128)(2,1)S(1)} %convolution_convert_fusion), channel_id=1, source_target_pairs={{0,16},{16,0},{1,17},{17,1},{2,18},{18,2},{3,19},{19,3},{4,20},{20... | collective-permute-start | bytes 589832 | tf_op jit(solution)/shard_map/ppermute | solution.py:475
  619.9 15.6 %collective-permute-start.60 = (bf16[96,1536]{1,0:T(8,128)(2,1)}, bf16[96,1536]{1,0:T(8,128)(2,1)}, u32[]{:S(2)}, u32[]{:S(2)}) collective-permute-start(bf16[96,1536]{1,0:T(8,128)(2,1)} %get-tuple-element.831), channel_id=1, source_target_pairs={{0,3},{1,2},{2,1},{3,0},{4,7},{5,6},{6,5},{7,4},{8,11},{9,10},{10,... | collective-permute-start | bytes 884744 | tf_op jit(solution)/shard_map/ppermute | solution.py:463
  620.3 7.6 %collective-permute-start.62 = (bf16[96,1536]{1,0:T(8,128)(2,1)}, bf16[96,1536]{1,0:T(8,128)(2,1)}, u32[]{:S(2)}, u32[]{:S(2)}) collective-permute-start(bf16[96,1536]{1,0:T(8,128)(2,1)} %get-tuple-element.833), channel_id=1, source_target_pairs={{0,1},{1,0},{2,3},{3,2},{4,5},{5,4},{6,7},{7,6},{8,9},{9,8},{10,11... | collective-permute-start | bytes 884744 | tf_op jit(solution)/shard_map/ppermute | solution.py:463
  621.2 14.3 %collective-permute-start.61 = (bf16[96,1536]{1,0:T(8,128)(2,1)}, bf16[96,1536]{1,0:T(8,128)(2,1)}, u32[]{:S(2)}, u32[]{:S(2)}) collective-permute-start(bf16[96,1536]{1,0:T(8,128)(2,1)} %get-tuple-element.832), channel_id=1, source_target_pairs={{0,2},{1,3},{2,0},{3,1},{4,6},{5,7},{6,4},{7,5},{8,10},{9,11},{10,... | collective-permute-start | bytes 884744 | tf_op jit(solution)/shard_map/ppermute | solution.py:463
  643.3 9.7 %collective-permute-start.63 = (f32[27,128]{1,0:T(8,128)S(1)}, f32[27,128]{1,0:T(8,128)S(1)}, u32[]{:S(2)}, u32[]{:S(2)}) collective-permute-start(f32[27,128]{1,0:T(8,128)S(1)} %bitcast.154), channel_id=1, source_target_pairs={{0,16},{16,0},{1,17},{17,1},{2,18},{18,2},{3,19},{19,3},{4,20},{20... | collective-permute-start | bytes 41480 | tf_op jit(solution)/shard_map/ppermute | solution.py:475
  652.5 4.7 collective-permute-start.65
  652.9 12.1 %collective-permute-start.66 = (f32[27,128]{1,0:T(8,128)S(1)}, f32[27,128]{1,0:T(8,128)S(1)}, u32[]{:S(2)}, u32[]{:S(2)}) collective-permute-start(f32[27,128]{1,0:T(8,128)S(1)} %bitcast_add_fusion.4), channel_id=1, source_target_pairs={{0,1},{1,0},{2,3},{3,2},{4,5},{5,4},{6,7},{7,6},{8,9},{9,8},{10,11... | collective-permute-start | bytes 41480 | tf_op jit(solution)/shard_map/ppermute | solution.py:463
  668.9 6.1 collective-permute-start.68
  (133 other events, 2072.2 us)
Sparse Core Ops, SparseCore 0:
  92.6 151.0 all-gather.1
  338.1 163.5 reduce-scatter.2
  518.2 87.6 reduce-scatter.4

commit v3 on v2

--- a/solution.py
+++ b/solution.py
@@ -47,29 +47,41 @@
     )
 
 
-def score_parts(qkv_ref, head, block, reach, lam, bias):
-    rows = pl.ds(block * BLOCK, BLOCK)
-    lane = lax.broadcasted_iota(jnp.int32, (1, WIDTH), 1)
-    first = lane < HD
+def score_parts(qkv_ref, head, block, low, high, lam, bias):
+    rows, reach = pl.ds(block * BLOCK, BLOCK), pl.ds(low, high - low)
+    first = lax.broadcasted_iota(jnp.int32, (1, WIDTH), 1) < HD
     query = qkv_ref[rows, head * WIDTH : (head + 1) * WIDTH] * BF16(HD**-0.5)
     key = qkv_ref[reach, ATTN_Q + head * WIDTH : ATTN_Q + (head + 1) * WIDTH]
     value = qkv_ref[reach, 2 * ATTN_Q + head * WIDTH : 2 * ATTN_Q + (head + 1) * WIDTH]
     zero = jnp.zeros((), BF16)
-    query_one = jnp.where(first, query, zero)
-    query_two = jnp.where(first, zero, query)
-    probs = []
-    for half in (query_one, query_two):
-        score = dot(half, key, 1, 1) + bias
-        expo = jnp.exp(score - jnp.max(score, -1, keepdims=True))
-        probs.append(expo * (1.0 / jnp.sum(expo, -1, keepdims=True)))
-    mixture = (probs[0] - lam * probs[1]).astype(BF16)
-    return query_one, query_two, key, value, probs[0], probs[1], mixture
-
-
-def block_bias(seg_q_ref, seg_k_ref, block, low, high):
+    queries = jnp.concatenate(
+        [jnp.where(first, query, zero), jnp.where(first, zero, query)], 0
+    )
+    score = dot(queries, key, 1, 1) + jnp.concatenate([bias, bias], 0)
+    expo = jnp.exp(score - jnp.max(score, -1, keepdims=True))
+    probs = expo * (1.0 / jnp.sum(expo, -1, keepdims=True))
+    mixture = (probs[:BLOCK] - lam * probs[BLOCK:]).astype(BF16)
+    return queries, key, value, probs, mixture
+
+
+def column_of(row):
+    rows = lax.broadcasted_iota(jnp.int32, (BLOCK, BLOCK), 0)
+    cols = lax.broadcasted_iota(jnp.int32, (BLOCK, BLOCK), 1)
+    return jnp.sum(jnp.where(rows == cols, row, 0.0), -1, keepdims=True)
+
+
+def documents_of(marks):
+    return jnp.where(marks >= GROUP, marks - GROUP, marks)
+
+
+def block_bias(marks_ref, block, low, high):
     rows = lax.broadcasted_iota(jnp.int32, (BLOCK, high - low), 0) + block * BLOCK
     cols = lax.broadcasted_iota(jnp.int32, (BLOCK, high - low), 1) + low
-    same = seg_q_ref[block * BLOCK : (block + 1) * BLOCK, :] == seg_k_ref[:, low:high]
+    keys = jnp.concatenate(
+        [marks_ref[b : b + 1, :] for b in range(low // BLOCK, high // BLOCK)], 1
+    )
+    queries = column_of(marks_ref[block : block + 1, :])
+    same = documents_of(queries) == documents_of(keys)
     return jnp.where((cols <= rows) & same, 0.0, MASKED)
 
 
@@ -77,15 +89,15 @@
     return max(0, block - REACH // BLOCK) * BLOCK, (block + 1) * BLOCK
 
 
-def attend_kernel(lam_ref, qkv_ref, seg_q_ref, seg_k_ref, gain_ref, heads_ref):
+def attend_kernel(lam_ref, qkv_ref, marks_ref, gain_ref, heads_ref):
     lam = lam_ref[0]
     gain = gain_ref[...] * KEEP
     for block in range(qkv_ref.shape[0] // BLOCK):
         low, high = reach_of(block)
-        bias = block_bias(seg_q_ref, seg_k_ref, block, low, high)
+        bias = block_bias(marks_ref, block, low, high)
         for head in range(OWN_HEADS):
-            parts = score_parts(qkv_ref, head, block, pl.ds(low, high - low), lam, bias)
-            out = dot(parts[6], parts[3])
+            _, _, value, _, mixture = score_parts(qkv_ref, head, block, low, high, lam, bias)
+            out = dot(mixture, value)
             normed = out * rms_scale(out, 1e-05)
             heads_ref[pl.ds(block * BLOCK, BLOCK), head * WIDTH : (head + 1) * WIDTH] = (
                 normed * gain
@@ -93,16 +105,17 @@
 
 
 def attend_back_kernel(
-    lam_ref, qkv_ref, seg_q_ref, seg_k_ref, gain_ref, grad_ref, out_ref, stat_ref, dk_ref, dv_ref
+    lam_ref, qkv_ref, marks_ref, gain_ref, grad_ref, out_ref, stat_ref, dk_ref, dv_ref
 ):
     lam = lam_ref[0]
     gain = gain_ref[...] * KEEP
     blocks = qkv_ref.shape[0] // BLOCK
     first = lax.broadcasted_iota(jnp.int32, (1, WIDTH), 1) < HD
-    zero = jnp.zeros((), BF16)
+    upper = lax.broadcasted_iota(jnp.int32, (2 * BLOCK, 1), 0) < BLOCK
+    share = jnp.where(upper, 1.0, -lam)
     gain_total = jnp.zeros((1, WIDTH), F32)
     lam_total = jnp.zeros((1, 1), F32)
-    biases = [block_bias(seg_q_ref, seg_k_ref, b, *reach_of(b)) for b in range(blocks)]
+    biases = [block_bias(marks_ref, b, *reach_of(b)) for b in range(blocks)]
     for head in range(OWN_HEADS):
         lanes = slice(head * WIDTH, (head + 1) * WIDTH)
         dk_ref[...] = jnp.zeros_like(dk_ref)
@@ -110,8 +123,8 @@
         for block in range(blocks):
             low, high = reach_of(block)
             rows, reach = pl.ds(block * BLOCK, BLOCK), pl.ds(low, high - low)
-            query_one, query_two, key, value, prob_one, prob_two, mixture = score_parts(
-                qkv_ref, head, block, reach, lam, biases[block]
+            queries, key, value, probs, mixture = score_parts(
+                qkv_ref, head, block, low, high, lam, biases[block]
             )
             out = dot(mixture, value)
             scale = rms_scale(out, 1e-05)
@@ -120,16 +133,14 @@
             gain_total = gain_total + jnp.sum(grad * normed, 0, keepdims=True)
             grad_out = norm_back(grad * gain, normed, scale).astype(BF16)
             grad_mix = dot(grad_out, value, 1, 1)
-            mean_one = jnp.sum(grad_mix * prob_one, -1, keepdims=True)
-            mean_two = jnp.sum(grad_mix * prob_two, -1, keepdims=True)
-            lam_total = lam_total - jnp.sum(mean_two, 0, keepdims=True)
-            low_one = (prob_one * (grad_mix - mean_one)).astype(BF16)
-            low_two = (prob_two * (-lam * (grad_mix - mean_two))).astype(BF16)
+            grad_mix = jnp.concatenate([grad_mix, grad_mix], 0)
+            mean = jnp.sum(grad_mix * probs, -1, keepdims=True)
+            lam_total = lam_total - jnp.sum(mean[BLOCK:], 0, keepdims=True)
+            low_scores = (probs * (share * (grad_mix - mean))).astype(BF16)
             dv_ref[reach, :] += dot(mixture, grad_out, 0, 0)
-            dk_ref[reach, :] += dot(low_one, query_one, 0, 0) + dot(low_two, query_two, 0, 0)
-            grad_query = dot(low_one, jnp.where(first, key, zero)) + dot(
-                low_two, jnp.where(first, zero, key)
-            )
+            dk_ref[reach, :] += dot(low_scores, queries, 0, 0)
+            grad_query = dot(low_scores, key)
+            grad_query = jnp.where(first, grad_query[:BLOCK], grad_query[BLOCK:])
             out_ref[rows, lanes] = (grad_query * HD**-0.5).astype(BF16)
         out_ref[:, ATTN_Q + head * WIDTH : ATTN_Q + (head + 1) * WIDTH] = dk_ref[...].astype(BF16)
         out_ref[:, 2 * ATTN_Q + head * WIDTH : 2 * ATTN_Q + (head + 1) * WIDTH] = dv_ref[
@@ -140,40 +151,38 @@
     stat_ref[2:8, :] = jnp.zeros((6, WIDTH), F32)
 
 
-def attention_specs(length):
+def attention_specs(length, lines, part):
     return [
         pl.BlockSpec(memory_space=pltpu.SMEM),
         pl.BlockSpec((length, 3 * ATTN_Q), lambda i: (0, 0)),
-        pl.BlockSpec((length, 1), lambda i: (0, 0)),
-        pl.BlockSpec((1, length), lambda i: (0, 0)),
+        pl.BlockSpec((lines, BLOCK), lambda i: (part, 0)),
         pl.BlockSpec((1, WIDTH), lambda i: (0, 0)),
     ]
 
 
-def attend(lam, qkv, segments, gain):
-    length = segments.shape[0]
+def attend(lam, qkv, marks, part, lines, gain):
+    length = qkv.shape[0]
     return pl.pallas_call(
         attend_kernel,
         grid=(1,),
-        in_specs=attention_specs(length),
+        in_specs=attention_specs(length, lines, part),
         out_specs=pl.BlockSpec((length, ATTN_Q), lambda i: (0, 0)),
         out_shape=jax.ShapeDtypeStruct((length, ATTN_Q), BF16),
-        compiler_params=pltpu.CompilerParams(vmem_limit_bytes=32 * 2**20),
+        compiler_params=pltpu.CompilerParams(vmem_limit_bytes=40 * 2**20),
         cost_estimate=pl.CostEstimate(
-            flops=OWN_HEADS * 2 * 4 * length * 320 * WIDTH,
-            bytes_accessed=length * 8 * ATTN_Q,
-            transcendentals=OWN_HEADS * 2 * length * 320,
+            flops=0, bytes_accessed=length * ATTN_Q, transcendentals=0
         ),
         name="attend",
-    )(lam, qkv, segments[:, None], segments[None, :], gain)
-
-
-def attend_back(lam, qkv, segments, gain, grad):
-    length = segments.shape[0]
+    )(lam, qkv, marks, gain)
+
+
+def attend_back(lam, qkv, marks, part, lines, gain, grad):
+    length = qkv.shape[0]
     return pl.pallas_call(
         attend_back_kernel,
         grid=(1,),
-        in_specs=attention_specs(length) + [pl.BlockSpec((length, ATTN_Q), lambda i: (0, 0))],
+        in_specs=attention_specs(length, lines, part)
+        + [pl.BlockSpec((length, ATTN_Q), lambda i: (0, 0))],
         out_specs=[
             pl.BlockSpec((length, 3 * ATTN_Q), lambda i: (0, 0)),
             pl.BlockSpec((8, WIDTH), lambda i: (0, 0)),
@@ -183,14 +192,44 @@
             jax.ShapeDtypeStruct((8, WIDTH), F32),
         ],
         scratch_shapes=[pltpu.VMEM((length, WIDTH), F32), pltpu.VMEM((length, WIDTH), F32)],
-        compiler_params=pltpu.CompilerParams(vmem_limit_bytes=32 * 2**20),
+        compiler_params=pltpu.CompilerParams(vmem_limit_bytes=40 * 2**20),
         cost_estimate=pl.CostEstimate(
-            flops=OWN_HEADS * 2 * 10 * length * 320 * WIDTH,
-            bytes_accessed=length * 14 * ATTN_Q,
-            transcendentals=OWN_HEADS * 2 * length * 320,
+            flops=0, bytes_accessed=length * ATTN_Q, transcendentals=0
         ),
         name="attend_back",
-    )(lam, qkv, segments[:, None], segments[None, :], gain, grad)
+    )(lam, qkv, marks, gain, grad)
+
+
+def loss_kernel(everyone, lines, *refs):
+    cotangents, smalls, outs = refs[:GROUP], refs[GROUP : 2 * GROUP], refs[2 * GROUP :]
+    block = pl.program_id(0)
+    needles = sum([small[lines : lines + 1, :] for small in smalls])
+    scale = everyone / (everyone + NEEDLE * needles[:, 0:1])
+    for k in range(GROUP):
+        marks = column_of(smalls[k][pl.ds(block, 1), :])
+        weights = 1.0 + NEEDLE * jnp.where(marks >= GROUP, 1.0, 0.0)
+        grad = cotangents[k][...].astype(F32) * (weights * scale)
+        outs[k][...] = grad.astype(BF16)
+        if k == 0:
+            outs[GROUP][...] = grad
+
+
+def loss_gradients(everyone, lines, cotangents, smalls):
+    length, width = cotangents[0].shape
+    spec = pl.BlockSpec((BLOCK, width), lambda i: (i, 0))
+    rows = smalls[0][0].shape[0]
+    low = jax.ShapeDtypeStruct((length, width), BF16)
+    return pl.pallas_call(
+        partial(loss_kernel, everyone, lines),
+        grid=(length // BLOCK,),
+        in_specs=[spec] * GROUP
+        + [pl.BlockSpec((rows, BLOCK), lambda i, p=part: (p, 0)) for _, part in smalls],
+        out_specs=[spec] * (GROUP + 1),
+        out_shape=[low] * GROUP + [jax.ShapeDtypeStruct((length, width), F32)],
+        compiler_params=pltpu.CompilerParams(vmem_limit_bytes=40 * 2**20),
+        cost_estimate=pl.CostEstimate(flops=0, bytes_accessed=length * width, transcendentals=0),
+        name="loss_gradients",
+    )(*cotangents, *[small for small, _ in smalls])
 
 
 def quarter_kernel(member_ref, *refs):
@@ -214,7 +253,7 @@
             out_specs=[pl.BlockSpec((rows, width), lambda i, member: (0, i))] * GROUP,
         ),
         out_shape=[kind] * GROUP,
-        compiler_params=pltpu.CompilerParams(vmem_limit_bytes=32 * 2**20),
+        compiler_params=pltpu.CompilerParams(vmem_limit_bytes=40 * 2**20),
         cost_estimate=pl.CostEstimate(flops=0, bytes_accessed=rows * width, transcendentals=0),
         name="quarters",
     )(member.reshape(1), *[weight] * GROUP)
@@ -247,7 +286,7 @@
         in_specs=specs,
         out_specs=out_spec,
         out_shape=jax.ShapeDtypeStruct((length, width), kind),
-        compiler_params=pltpu.CompilerParams(vmem_limit_bytes=48 * 2**20),
+        compiler_params=pltpu.CompilerParams(vmem_limit_bytes=40 * 2**20),
         cost_estimate=pl.CostEstimate(
             flops=2 * pairs * length * depth * width // share,
             bytes_accessed=2 * pairs * (length + width) * depth // share,
@@ -282,7 +321,7 @@
         out_specs=pl.BlockSpec((rows, width), lambda i: (i, place)),
         out_shape=jax.ShapeDtypeStruct((depth, columns), BF16),
         input_output_aliases={} if into is None else {2 * GROUP: 0},
-        compiler_params=pltpu.CompilerParams(vmem_limit_bytes=48 * 2**20),
+        compiler_params=pltpu.CompilerParams(vmem_limit_bytes=40 * 2**20),
         cost_estimate=pl.CostEstimate(
             flops=GROUP * length * depth * width // 32,
             bytes_accessed=GROUP * length * (depth + width) // 32,
@@ -307,7 +346,7 @@
         ],
         out_specs=pl.BlockSpec((length, tile), lambda i: (0, i)),
         out_shape=jax.ShapeDtypeStruct((length, width), BF16),
-        compiler_params=pltpu.CompilerParams(vmem_limit_bytes=48 * 2**20),
+        compiler_params=pltpu.CompilerParams(vmem_limit_bytes=40 * 2**20),
         cost_estimate=pl.CostEstimate(flops=0, bytes_accessed=length * depth, transcendentals=0),
         name="project",
     )(left, right)
@@ -339,7 +378,7 @@
         ],
         out_specs=[out_spec] * (3 * GROUP),
         out_shape=[low] * GROUP + [high] * (2 * GROUP),
-        compiler_params=pltpu.CompilerParams(vmem_limit_bytes=48 * 2**20),
+        compiler_params=pltpu.CompilerParams(vmem_limit_bytes=40 * 2**20),
         cost_estimate=pl.CostEstimate(flops=0, bytes_accessed=length * depth, transcendentals=0),
         name="raise_up",
     )(*mids, weight, weight)
@@ -371,7 +410,7 @@
         + [spec] * (2 * GROUP),
         out_specs=[spec] * (2 * GROUP),
         out_shape=[kind] * (2 * GROUP),
-        compiler_params=pltpu.CompilerParams(vmem_limit_bytes=48 * 2**20),
+        compiler_params=pltpu.CompilerParams(vmem_limit_bytes=40 * 2**20),
         cost_estimate=pl.CostEstimate(flops=0, bytes_accessed=length * depth, transcendentals=0),
         name="raise_back",
     )(*grads, weight, *gates, *ups)
@@ -407,7 +446,7 @@
             out_specs=pl.BlockSpec((1, 1, rows, cols), target),
         ),
         out_shape=jax.ShapeDtypeStruct((layers, 2, rows, cols), pieces[0].dtype),
-        compiler_params=pltpu.CompilerParams(vmem_limit_bytes=48 * 2**20),
+        compiler_params=pltpu.CompilerParams(vmem_limit_bytes=40 * 2**20),
         cost_estimate=pl.CostEstimate(flops=0, bytes_accessed=rows * cols, transcendentals=0),
         name="assemble",
     )(jnp.stack([layer, copy]), *pieces)
@@ -437,22 +476,109 @@
     )(core.reshape(1), own, other)
 
 
-def orthonormal_kernel(source, target):
-    left = source[...]
-    number = lax.broadcasted_iota(jnp.int32, (left.shape[0], 1), 0)
-    for step in range(left.shape[0]):
-        row = left[step : step + 1]
-        row = row * lax.rsqrt(jnp.sum(row * row, -1, keepdims=True))
-        share = jnp.sum(left * row, -1, keepdims=True)
-        left = jnp.where(
-            number > step, left - share * row, jnp.where(number == step, row, left)
-        )
-    target[...] = left
-
-
-def orthonormal(left):
-    kind = jax.ShapeDtypeStruct(left.shape, F32)
-    return pl.pallas_call(orthonormal_kernel, out_shape=kind, name="orthonormal")(left)
+def merge_kernel(member_ref, *refs):
+    shares, (error_ref, start_ref), outs = refs[:GROUP], refs[GROUP : GROUP + 2], refs[GROUP + 2 :]
+    grad_ref, merged_ref, left_ref = outs
+    width = shares[0].shape[1]
+    values = arrange([share[...].astype(F32) for share in shares], member_ref[0])
+
+    @pl.when(pl.program_id(0) == 0)
+    def _():
+        left_ref[...] = jnp.zeros_like(left_ref)
+
+    for number, value in enumerate(values):
+        lanes = slice(number * width, (number + 1) * width)
+        grad_ref[:, lanes] = value
+        merged = value + DECAY_ERROR * error_ref[:, lanes]
+        merged_ref[:, lanes] = merged
+        left_ref[...] += dot(start_ref[:, lanes], merged, 1, 1, precision=HIGHEST)
+
+
+def merge(member, shares, error, start, width):
+    rows, total = error.shape
+    rank = start.shape[0]
+    wide = pl.BlockSpec((rows, GROUP * width), lambda i: (0, i))
+    kind = jax.ShapeDtypeStruct((rows, total), F32)
+    return pl.pallas_call(
+        merge_kernel,
+        grid=(total // (GROUP * width),),
+        in_specs=[pl.BlockSpec(memory_space=pltpu.SMEM)]
+        + [pl.BlockSpec((rows, width), lambda i: (0, i))] * GROUP
+        + [wide, pl.BlockSpec((rank, GROUP * width), lambda i: (0, i))],
+        out_specs=[wide, wide, pl.BlockSpec((rank, rows), lambda i: (0, 0))],
+        out_shape=[kind, kind, jax.ShapeDtypeStruct((rank, rows), F32)],
+        compiler_params=pltpu.CompilerParams(vmem_limit_bytes=40 * 2**20),
+        cost_estimate=pl.CostEstimate(flops=0, bytes_accessed=rows * total, transcendentals=0),
+        name="merge",
+    )(member.reshape(1), *shares, error, start)
+
+
+def right_kernel(own_ref, other_ref, merged_ref, ortho_ref, right_ref, left_ref):
+    @pl.when(pl.program_id(0) == 0)
+    def _():
+        left = own_ref[...] + other_ref[...]
+        number = lax.broadcasted_iota(jnp.int32, (left.shape[0], 1), 0)
+        for step in range(left.shape[0]):
+            row = left[step : step + 1]
+            row = row * lax.rsqrt(jnp.sum(row * row, -1, keepdims=True))
+            share = jnp.sum(left * row, -1, keepdims=True)
+            left = jnp.where(
+                number > step, left - share * row, jnp.where(number == step, row, left)
+            )
+        left_ref[...] = left
+        ortho_ref[...] = left
+
+    right_ref[...] = dot(left_ref[...], merged_ref[...], precision=HIGHEST).astype(BF16)
+
+
+def right_factor(own, other, merged, tile=3072):
+    rank, rows = own.shape
+    total = merged.shape[1]
+    small = pl.BlockSpec((rank, rows), lambda i: (0, 0))
+    return pl.pallas_call(
+        right_kernel,
+        grid=(total // tile,),
+        in_specs=[small, small, pl.BlockSpec((rows, tile), lambda i: (0, i))],
+        out_specs=[small, pl.BlockSpec((rank, tile), lambda i: (0, i))],
+        out_shape=[
+            jax.ShapeDtypeStruct((rank, rows), F32),
+            jax.ShapeDtypeStruct((rank, total), BF16),
+        ],
+        scratch_shapes=[pltpu.VMEM((rank, rows), F32)],
+        compiler_params=pltpu.CompilerParams(vmem_limit_bytes=40 * 2**20),
+        cost_estimate=pl.CostEstimate(flops=0, bytes_accessed=rows * total, transcendentals=0),
+        name="right_factor",
+    )(own, other, merged)
+
+
+def update_kernel(copies, ortho_ref, own_ref, other_ref, merged_ref, momentum_ref, weight_ref, *outs):
+    right_ref, error_ref, momentum_out_ref, weight_out_ref = outs
+    right = (own_ref[...].astype(F32) + other_ref[...].astype(F32)) / copies
+    approx = dot(ortho_ref[...], right, 0, 0, precision=HIGHEST)
+    momentum = MOMENTUM * momentum_ref[...] + (1.0 - MOMENTUM) * approx
+    right_ref[...] = right
+    error_ref[...] = merged_ref[...] - approx
+    momentum_out_ref[...] = momentum
+    weight_out_ref[...] = weight_ref[...] - RATE_MATRIX * momentum
+
+
+def update(copies, ortho, own, other, merged, momentum, weight, tile=3072):
+    rank, rows = ortho.shape
+    total = merged.shape[1]
+    small = pl.BlockSpec((rank, rows), lambda i: (0, 0))
+    low = pl.BlockSpec((rank, tile), lambda i: (0, i))
+    wide = pl.BlockSpec((rows, tile), lambda i: (0, i))
+    kind = jax.ShapeDtypeStruct((rows, total), F32)
+    return pl.pallas_call(
+        partial(update_kernel, copies),
+        grid=(total // tile,),
+        in_specs=[small, low, low, wide, wide, wide],
+        out_specs=[low, wide, wide, wide],
+        out_shape=[jax.ShapeDtypeStruct((rank, total), F32), kind, kind, kind],
+        compiler_params=pltpu.CompilerParams(vmem_limit_bytes=40 * 2**20),
+        cost_estimate=pl.CostEstimate(flops=0, bytes_accessed=rows * total, transcendentals=0),
+        name="update",
+    )(ortho, own, other, merged, momentum, weight)
 
 
 def after(value, *earlier):
@@ -606,7 +732,8 @@
     marks = segment_ids.reshape(lines, 128) + GROUP * needle_mask.reshape(lines, 128)
     small = jnp.concatenate([marks.astype(F32), needles[: 8 - lines % 8]])
     rows = small.shape[0]
-    small_pair = jnp.concatenate([small, line(swap(line(small), 1))])
+    small_beside = line(swap(line(small), 1))
+    small_pair = jnp.concatenate([small, small_beside])
     out_across = swap(line(out_own), 2)
     qkv_gather.land()
     ffn_got = [line(got) for got in ffn_got]
@@ -630,6 +757,9 @@
     ffn_weight_low = lax.all_gather(line(ffn_half), ("layer", "replica"), axis=0, tiled=True)
     out_gather.land()
     out_gather.hop()
+    out_gather.land_over()
+    out_gather.land()
+    out_gather.land_over()
     normed_across = line(normed_across)
     small_across = line(small_across)
     normed_opposite = swap(normed_across, 1)
@@ -637,45 +767,36 @@
     qkv_weight = qkv_gather.finish()
     normed_beside = line(normed_beside)
 
-    def heads_of(qkv, segments):
-        return attend(lam, qkv, segments, gain_head[None])
+    smalls = [(small, 0), (small_beside, 0), (small_across, 0), (small_across, 1)]
+
+    def heads_of(qkv, k):
+        return attend(lam, qkv, *smalls[k], rows, gain_head[None])
 
     qkv = [None] * GROUP
     heads = [None] * GROUP
     qkv[0] = line.run(project, normed_low, qkv_weight)
     qkv[1] = line.run(project, normed_beside, qkv_weight)
-    small_beside, small_own = small_pair[rows:], small_pair[:rows]
-
-    def marks_of(part):
-        marks = part[:lines].reshape(length)
-        mask = (marks >= GROUP).astype(F32)
-        return marks - GROUP * mask, mask
-
-    segments, masks = [None] * GROUP, [None] * GROUP
-    segments[0], masks[0] = marks_of(small_own)
-    segments[1], masks[1] = marks_of(small_beside)
-    heads[0] = line.run(heads_of, qkv[0], segments[0])
-    heads[1] = line.run(heads_of, qkv[1], segments[1])
+    heads[0] = line.run(heads_of, qkv[0], 0)
+    heads[1] = line.run(heads_of, qkv[1], 1)
     heads_beside = swap(heads[1], 1)
-    segments[2], masks[2] = marks_of(small_across[:rows])
-    segments[3], masks[3] = marks_of(small_across[rows:])
-    out_gather.land()
+    cotangent_across = line(cotangent_across)
+    out_mine = line(out_gather.finish())
+    out_rest = swap(out_mine, 1)
     qkv[2] = line.run(project, normed_across, qkv_weight)
-    heads[2] = line.run(heads_of, qkv[2], segments[2])
+    heads[2] = line.run(heads_of, qkv[2], 2)
     heads_across = swap(heads[2], 2)
     normed_opposite = line(normed_opposite)
-    cotangent_across = line(cotangent_across)
+    normed_all = [normed_low, normed_beside, normed_across, normed_opposite]
+    qkv[3] = line.run(project, normed_opposite, qkv_weight)
+    heads[3] = line.run(heads_of, qkv[3], 3)
+    heads_opposite = swap(heads[3], 3)
     cotangent_near = swap(line(cotangent), 1)
     cotangent_far = swap(cotangent_across, 1)
-    normed_all = [normed_low, normed_beside, normed_across, normed_opposite]
-    qkv[3] = line.run(project, normed_opposite, qkv_weight)
-    heads[3] = line.run(heads_of, qkv[3], segments[3])
-    heads_opposite = swap(heads[3], 3)
-    out_mine = out_gather.finish()
-    out_rest = swap(out_mine, 1)
     heads_beside, heads_across = line(heads_beside), line(heads_across)
     out_rest = line(out_rest)
-    out_weight = interleave(member % 2, out_mine, out_rest, D // (layers * GROUP))
+    out_weight = line.run(
+        lambda x: interleave(member % 2, x, out_rest, D // (layers * GROUP)), out_mine
+    )
     heads_opposite = line(heads_opposite)
     heads_low = jnp.concatenate(
         arrange([heads[0], heads_beside, heads_across, heads_opposite], member), 1
@@ -686,22 +807,17 @@
     mid_low = line((normed_mid * gain_mid).astype(BF16))
     mid_across = swap(mid_low, 2)
     mid_beside = swap(mid_low, 1)
+    cotangents = [cotangent, line(cotangent_near), cotangent_across, line(cotangent_far)]
+    *grad_out_all, grad_out = line.run(
+        lambda x: loss_gradients(
+            length * layers * GROUP * copies, lines, [x, *cotangents[1:]], smalls
+        ),
+        cotangent,
+    )
     mid_across = line(mid_across)
     mid_opposite = swap(mid_across, 1)
     heads_across_all = swap(line(heads_low), 2)
-    small = jnp.concatenate([small_pair, small_across])
-    needles = sum([small[k * rows + lines, 0] for k in range(GROUP)])
-    everyone = length * layers * GROUP * copies
-    weight_total = everyone + NEEDLE * needles
-
-    def grad_of(cotangent, k):
-        loss_weights = 1.0 + NEEDLE * masks[k]
-        return cotangent.astype(F32) * (loss_weights * (everyone / weight_total))[:, None]
-
     mid_beside, mid_opposite = line(mid_beside), line(mid_opposite)
-    cotangents = [cotangent, line(cotangent_near), cotangent_across, line(cotangent_far)]
-    grad_out = grad_of(cotangent, 0)
-    grad_out_all = [line(grad_of(one, k).astype(BF16)) for k, one in enumerate(cotangents)]
     ffn_weight_low = line(ffn_weight_low)
 
     def product(lefts, rights, columns, place, into=None):
@@ -717,13 +833,8 @@
         lambda x: raise_back([x, *grad_out_all[1:]], ffn_weight_low, gate_proj, up_proj),
         grad_out_all[0],
     )
-    ffn_partial = product(grad_out_all, hidden, 3 * FF_Q, 2)
-    ffn_partial = product(mid_all, grad_gate, 3 * FF_Q, 0, ffn_partial)
     heads_across_all = line(heads_across_all)
-    heads_beside_all = swap(line(heads_low), 1)
-    heads_opposite_all = swap(heads_across_all, 1)
-    ffn_partial = product(mid_all, grad_up, 3 * FF_Q, 1, ffn_partial)
-    ffn_total = sum_layers(ffn_partial)
+    down_total = sum_layers(product(grad_out_all, hidden, FF_Q, 0))
 
     def lower(k, got=None, kind=BF16):
         return line.run(
@@ -740,13 +851,18 @@
     opposite_got = line(opposite_got)
     beside_got = line(beside_got)
     mid_sum = swap(lower(2, opposite_got), 2)
+    up_partial = product(mid_all, grad_gate, 2 * FF_Q, 0)
     grad_mid_own = lower(0, beside_got, F32)
+    up_partial = product(mid_all, grad_up, 2 * FF_Q, 1, up_partial)
     ffn_opposite_got = swap(lower_hidden(3), 1)
     ffn_beside_got = swap(lower_hidden(1), 1)
     mid_sum = line(mid_sum)
+    down_total = line(down_total)
+    up_total = sum_layers(line(up_partial))
+    heads_beside_all = swap(line(heads_low), 1)
+    heads_opposite_all = swap(heads_across_all, 1)
 
     grad_mid_low = grad_mid_own + mid_sum.astype(F32)
-    grad_gain_mid = jnp.sum(grad_mid_low * normed_mid, 0)
     grad_mid = grad_out + norm_back(grad_mid_low * gain_mid, normed_mid, scale_mid)
     grad_attn_low = grad_mid.astype(BF16)
     grad_heads = line.run(lambda x: dot(x, out_weight, 1, 1).astype(BF16), grad_attn_low)
@@ -755,24 +871,27 @@
     grad_attn = arrange(columns(grad_attn_low, ATTN_Q), member)
 
     def back(grad, k):
-        return attend_back(lam, qkv[k], segments[k], gain_head[None], grad)
+        return attend_back(lam, qkv[k], *smalls[k], rows, gain_head[None], grad)
 
     grad_qkv, stats = [None] * GROUP, [None] * GROUP
     grad_qkv[0], stats[0] = line.run(back, grad_heads[0], 0)
+    heads_beside_all, heads_opposite_all = line(heads_beside_all), line(heads_opposite_all)
+    heads_all = [heads_low, heads_beside_all, heads_across_all, heads_opposite_all]
+    ffn_opposite_got, ffn_beside_got = line(ffn_opposite_got), line(ffn_beside_got)
     grad_qkv[1], stats[1] = line.run(back, line(grad_heads_got[2]), 1)
     grad_heads_across, grad_heads_opposite = line(grad_heads_got[0]), line(grad_heads_got[1])
     grad_attn_got = [swap(line(grad_attn[k]), k) for k in (2, 3, 1)]
     grad_qkv[2], stats[2] = line.run(back, grad_heads_across, 2)
     grad_attn_got = [line(got) for got in grad_attn_got]
-    heads_all = [heads_low, line(heads_beside_all), heads_across_all, line(heads_opposite_all)]
     grad_attn_all = [grad_attn[0], grad_attn_got[2], grad_attn_got[0], grad_attn_got[1]]
-    ffn_opposite_got = line(ffn_opposite_got)
     ffn_sum = swap(lower_hidden(2, ffn_opposite_got), 2)
+    grad_qkv[3], stats[3] = line.run(back, grad_heads_opposite, 3)
     attn_partial = product(heads_all, grad_attn_all, 4 * ATTN_Q, 3)
-    grad_qkv[3], stats[3] = line.run(back, grad_heads_opposite, 3)
+    ffn_own = lower_hidden(0, ffn_beside_got, F32)
     attn_partial = product(normed_all, grad_qkv, 4 * ATTN_Q, 0, attn_partial)
-    attn_total = sum_layers(attn_partial)
     ffn_sum = line(ffn_sum)
+    attn_total = sum_layers(line(attn_partial))
+    mixed = line((residual_mid + ffn_own + ffn_sum.astype(F32)).astype(BF16))
     stats = sum(stats)
     grad_gain_head, grad_lambda = stats[0], stats[1, 0]
 
@@ -789,43 +908,27 @@
         return [parts[0]] + [swap(line(parts[k]), k) for k in range(1, GROUP)]
 
     def landed(parts):
-        return arrange([parts[0]] + [line(part) for part in parts[1:]], member)
-
-    def left_of(grad, error, start):
-        merged = grad + DECAY_ERROR * error[0]
-        left = line.run(lambda x: dot(start[0], x, 1, 1, precision=HIGHEST), merged)
-        return merged, left, cross(left, copies)
-
-    def right_of(merged, left, other):
-        ortho = orthonormal(left + line(other))
-        right = line(dot(ortho, merged, 1, 0, precision=HIGHEST).astype(BF16))
-        return ortho, right, cross(right, copies)
-
-    def update(ortho, merged, right, other, momentum, weight):
-        right = (right.astype(F32) + line(other).astype(F32)) / copies
-        approx = dot(ortho, right, 0, 0, precision=HIGHEST)
-        momentum_new = MOMENTUM * momentum + (1.0 - MOMENTUM) * approx
-        weight_new = line(weight - RATE_MATRIX * momentum_new)
-        return right, merged - approx, momentum_new, weight_new
+        return [parts[0]] + [line(part) for part in parts[1:]]
 
     in_opposite_got = swap(lower_in(3), 1)
     in_beside_got = swap(lower_in(1), 1)
-    ffn_shares = share(rows_of(line(ffn_total)))
+    ffn_total = jnp.concatenate([line(up_total), down_total], 1)
+    ffn_shares = share(rows_of(ffn_total))
     in_opposite_got = line(in_opposite_got)
     in_sent = lower_in(2, in_opposite_got)
     in_beside_got = line(in_beside_got)
     in_own = lower_in(0, in_beside_got, F32)
-    ffn_own = lower_hidden(0, line(ffn_beside_got), F32)
-    mixed = line((residual_mid + ffn_own + ffn_sum.astype(F32)).astype(BF16))
+    grad_gain_mid = line(jnp.sum(line(grad_mid_low) * normed_mid, 0))
     ffn_rows = landed(ffn_shares)
     in_sum = swap(line(in_sent), 2)
-    ffn_grad = jnp.concatenate(
-        [part[:, s * FF_Q : (s + 1) * FF_Q] for s in range(3) for part in ffn_rows], 1
-    ).astype(F32)
-    merged_ffn, left_ffn, left_ffn_other = left_of(ffn_grad, ffn_error, ffn_start)
-    ortho_ffn, right_ffn, right_ffn_other = right_of(merged_ffn, left_ffn, left_ffn_other)
-    right_ffn, ffn_error_new, ffn_momentum_new, ffn_weight_new = update(
-        ortho_ffn, merged_ffn, right_ffn, right_ffn_other, ffn_momentum, ffn_weight
+    ffn_grad, merged_ffn, left_ffn = line.run(
+        lambda x: merge(member, [x, *ffn_rows[1:]], ffn_error[0], ffn_start[0], FF_Q), ffn_rows[0]
+    )
+    left_other = line(cross(left_ffn, copies))
+    ortho_ffn, right_ffn = line.run(right_factor, left_ffn, left_other, merged_ffn)
+    right_other = line(cross(right_ffn, copies))
+    right_ffn, ffn_error_new, ffn_momentum_new, ffn_weight_new = line.run(
+        partial(update, copies), ortho_ffn, right_ffn, right_other, merged_ffn, ffn_momentum, ffn_weight
     )
     in_sum = line(in_sum)
     grad_in_low = in_own + in_sum.astype(F32)
@@ -842,26 +945,33 @@
         ]
     ).reshape(-1, 128)
     attn_shares = share(rows_of(line(attn_total)))
-    attn_rows = landed(attn_shares)
-    attn_grad = jnp.concatenate(
-        [part[:, s * ATTN_Q : (s + 1) * ATTN_Q] for s in range(4) for part in attn_rows],
-        1,
-    ).astype(F32)
-    merged_attn, left_attn, left_attn_other = left_of(attn_grad, attn_error, attn_start)
-    vector_other = cross(line(vector_grad), copies)
-    ortho_attn, right_attn, right_attn_other = right_of(merged_attn, left_attn, left_attn_other)
-    vector_grad = vector_grad + line(vector_other)
-    vector_other = swap(vector_grad, 1)
-    grad_tokens = line(grad_mid + norm_back(grad_in_low * gain_in, normed_in, scale_in))
-    right_attn, attn_error_new, attn_momentum_new, attn_weight_new = update(
-        ortho_attn, merged_attn, right_attn, right_attn_other, attn_momentum, attn_weight
-    )
-    vector_grad = vector_grad + line(vector_other)
+    vector_grad = vector_grad + line(cross(vector_grad, copies))
+    vector_grad = vector_grad + line(swap(vector_grad, 1))
     bits = 1
     while bits < layers:
         vector_grad = vector_grad + line(swap_layers(vector_grad, bits, layers))
         bits *= 2
-    vector_grad = (vector_grad + line(swap(vector_grad, 2))).reshape(-1)
+    attn_rows = landed(attn_shares)
+    vector_other = swap(line(vector_grad), 2)
+    attn_grad, merged_attn, left_attn = line.run(
+        lambda x: merge(member, [x, *attn_rows[1:]], attn_error[0], attn_start[0], ATTN_Q),
+        attn_rows[0],
+    )
+    left_other = line(cross(left_attn, copies))
+    vector_grad = (vector_grad + line(vector_other)).reshape(-1)
+    ortho_attn, right_attn = line.run(right_factor, left_attn, left_other, merged_attn)
+    right_other = cross(right_attn, copies)
+    grad_tokens = line(grad_mid + norm_back(grad_in_low * gain_in, normed_in, scale_in))
+    right_other = line(right_other)
+    right_attn, attn_error_new, attn_momentum_new, attn_weight_new = line.run(
+        partial(update, copies),
+        ortho_attn,
+        right_attn,
+        right_other,
+        merged_attn,
+        attn_momentum,
+        attn_weight,
+    )
     vector_grad = vector_grad + line.token[0, 0]
     vector_momentum_new = MOMENTUM * vector_momentum + (1.0 - MOMENTUM) * vector_grad
     vector_new = vector_params - RATE_VECTOR * vector_momentum_new

time: 694 us -> 624 us (0.90)
  local copies, waits for them, and re-layouts: 42.5 us -> 85.6 us
  waiting for transfers between devices: 200 us -> 161 us
  matrix products: 41 us -> 6.64 us
  other arithmetic: 65.3 us -> 36.3 us
  Pallas kernels: 261 us -> 254 us
    ppermute x48, waiting for transfers between devices: 149 us -> 77.2 us  [swap(): return lax.ppermute(value, 'member', [(j, j ^ bits) for j in range(GROUP)])]
    unnamed x300 -> x341, local copies, waits for them, and re-layouts: 27.4 us -> 80.9 us
    dot_general x8 -> x2, matrix products: 41 us -> 6.64 us  [dot(): lax.dot_general(left, right, (((left_dim,), (right_dim,)), ((), ())), pre...]
    pallas_call x6 -> x11, Pallas kernels: 25.2 us -> 54.1 us  [the longest x4 18.1 us: attend(): pl.pallas_call(attend_kernel, grid=(1,), in_specs=attention_specs(length,...]
    ppermute x6, waiting for transfers between devices: 36.9 us -> 57.6 us  [ring(): lax.ppermute(value, 'layer', [(z, (z + 1) % layers) for z in range(layers)])]
    convert_element_type x6 -> x0, other arithmetic: 14.6 us -> none  [the longest x4 8.74 us: local(): grad_of(one, k).astype(BF16)]
    pallas_call x12, Pallas kernels: 65.1 us -> 50.5 us  [back_product(): pl.pallas_call(partial(back_kernel, pairs), grid=(width // tile,), in_spe...]
    pallas_call x5, Pallas kernels: 47.9 us -> 40.9 us  [weight_product(): pl.pallas_call(weight_kernel, grid=(depth // rows,), in_specs=specs, out_...]
  transfers between devices with their start and end apart: 73 -> 74, of which waited for: 31 -> 29; matrix products, arithmetic and copies ran while one was open for 16% -> 7% of each run, Pallas kernels for 37% -> 38%
where the time goes in v3:
time: 624 us; the launch traced here: 618 us
  Pallas kernels  254 us (41%)
  waiting for transfers between devices  161 us (26%)
  local copies, waits for them, and re-layouts  85.6 us (14%)
  starting transfers between devices  56.4 us (9%)
  other arithmetic  36.3 us (6%)
  between operations  18.9 us (3%)
  matrix products  6.64 us (1%)
    unnamed x341, local copies, waits for them, and re-layouts  80.9 us
    ppermute x48, waiting for transfers between devices, swap(): return lax.ppermute(value, 'member', [(j, j ^ bits) for j in range(GROUP)])  77.2 us
    ppermute x6, waiting for transfers between devices, ring(): lax.ppermute(value, 'layer', [(z, (z + 1) % layers) for z in range(layers)])  57.6 us
    pallas_call x12, Pallas kernels, back_product(): pl.pallas_call(partial(back_kernel, pairs), grid=(width // tile,), in_spe...  50.5 us
    pallas_call x4, Pallas kernels, attend_back(): pl.pallas_call(attend_back_kernel, grid=(1,), in_specs=attention_specs(le...  47.5 us
    pallas_call x5, Pallas kernels, weight_product(): pl.pallas_call(weight_kernel, grid=(depth // rows,), in_specs=specs, out_...  40.9 us
    ppermute x48, starting transfers between devices, swap(): return lax.ppermute(value, 'member', [(j, j ^ bits) for j in range(GROUP)])  30.1 us
    pallas_call x4, Pallas kernels, attend(): pl.pallas_call(attend_kernel, grid=(1,), in_specs=attention_specs(length,...  18.1 us
  transfers between devices with their start and end apart: 74, of which 29 were waited for; matrix products, arithmetic and copies ran while one was open for 7% of the time, Pallas kernels for 38%

profile of v3, /device:TPU:0, one launch (start us, length us, event | category | flops | bytes accessed | tf_op | source)
XLA Modules:
  0.0 618.3 jit_solution(8250724980575971389)
XLA Ops:
  9.2 3.0 collective-permute-start.2
  24.6 6.1 collective-permute-done.1
  39.0 6.7 %collective-permute-done.6.refs_2_ = bf16[192,1152]{1,0:T(8,128)(2,1)S(1)} collective-permute-done((bf16[192,1152]{1,0:T(8,128)(2,1)S(1)}, bf16[192,1152]{1,0:T(8,128)(2,1)S(1)}, u32[]{:S(2)}, u32[]{:S(2)}) %collective-permute-start.6) | collective-permute-done | bytes 442400 | tf_op jit(solution)/shard_map/ppermute | solution.py:597
  46.7 12.6 %collective-permute-done.10.refs_4_ = bf16[192,1152]{1,0:T(8,128)(2,1)S(1)} collective-permute-done((bf16[192,1152]{1,0:T(8,128)(2,1)S(1)}, bf16[192,1152]{1,0:T(8,128)(2,1)S(1)}, u32[]{:S(2)}, u32[]{:S(2)}) %collective-permute-start.10) | collective-permute-done | bytes 442400 | tf_op jit(solution)/shard_map/ppermute | solution.py:597
  62.7 8.8 %collective-permute-done.11.refs_6_ = bf16[192,1152]{1,0:T(8,128)(2,1)} collective-permute-done((bf16[192,1152]{1,0:T(8,128)(2,1)S(1)}, bf16[192,1152]{1,0:T(8,128)(2,1)}, u32[]{:S(2)}, u32[]{:S(2)}) %collective-permute-start.11) | collective-permute-done | bytes 442400 | tf_op jit(solution)/shard_map/ppermute | solution.py:597
  84.7 7.1 %collective-permute-done.15.refs_2_ = bf16[96,1536]{1,0:T(8,128)(2,1)} collective-permute-done((bf16[96,1536]{1,0:T(8,128)(2,1)S(1)}, bf16[96,1536]{1,0:T(8,128)(2,1)}, u32[]{:S(2)}, u32[]{:S(2)}) %collective-permute-start.15) | collective-permute-done | bytes 294944 | tf_op jit(solution)/shard_map/ppermute | solution.py:597
  95.4 9.1 %collective-permute-done.18.refs_4_ = bf16[96,1536]{1,0:T(8,128)(2,1)S(1)} collective-permute-done((bf16[96,1536]{1,0:T(8,128)(2,1)}, bf16[96,1536]{1,0:T(8,128)(2,1)S(1)}, u32[]{:S(2)}, u32[]{:S(2)}) %collective-permute-start.18) | collective-permute-done | bytes 294944 | tf_op jit(solution)/shard_map/ppermute | solution.py:597
  108.5 13.3 %collective-permute-done.21.refs_6_ = bf16[96,1536]{1,0:T(8,128)(2,1)S(1)} collective-permute-done((bf16[96,1536]{1,0:T(8,128)(2,1)S(1)}, bf16[96,1536]{1,0:T(8,128)(2,1)S(1)}, u32[]{:S(2)}, u32[]{:S(2)}) %collective-permute-start.21) | collective-permute-done | bytes 294944 | tf_op jit(solution)/shard_map/ppermute | solution.py:597
  122.5 5.6 collective-permute-done.13.left_ref.refs_2_
  138.4 2.7 assemble.2
  141.2 3.4 project.4.qkv_ref
  144.6 3.4 project.5.qkv_ref
  148.1 4.3 attend.4
  152.5 5.1 attend.5
  157.6 6.3 %collective-permute-done.26.refs_2_ = bf16[512,1536]{1,0:T(8,128)(2,1)} collective-permute-done((bf16[512,1536]{1,0:T(8,128)(2,1)}, bf16[512,1536]{1,0:T(8,128)(2,1)}, u32[]{:S(2)}, u32[]{:S(2)}) %collective-permute-start.26) | collective-permute-done | bytes 1572896 | tf_op jit(solution)/shard_map/ppermute | solution.py:589
  166.7 3.4 project.6.qkv_ref
  170.2 4.3 attend.6
  174.9 3.6 project.7.qkv_ref
  178.6 4.3 attend.7
  186.1 6.8 %interleave.1 = bf16[1536,1536]{1,0:T(8,128)(2,1)} custom-call(s32[1]{0:T(128)} %bitcast.11.core_ref, bf16[768,1536]{1,0:T(8,128)(2,1)} %bitcast.55, bf16[768,1536]{1,0:T(8,128)(2,1)} %collective-permute-done.29.other_ref), custom_call_target="tpu_custom_call" | custom-call | bytes 9437184 | tf_op jit(solution)/shard_map/interleave/pallas_call | solution.py:466
  197.9 4.0 convert_add_fusion
  205.5 4.9 loss_gradients.1
  215.0 25.3 %collective-permute-done.32.refs_2_ = bf16[512,1536]{1,0:T(8,128)(2,1)S(1)} collective-permute-done((bf16[512,1536]{1,0:T(8,128)(2,1)S(1)}, bf16[512,1536]{1,0:T(8,128)(2,1)S(1)}, u32[]{:S(2)}, u32[]{:S(2)}) %collective-permute-start.32) | collective-permute-done | bytes 1572896 | tf_op jit(solution)/shard_map/ppermute | solution.py:589
  247.7 18.0 %raise_up.1 = (bf16[512,1024]{1,0:T(8,128)(2,1)S(1)}, bf16[512,1024]{1,0:T(8,128)(2,1)S(1)}, bf16[512,1024]{1,0:T(8,128)(2,1)S(1)}, bf16[512,1024]{1,0:T(8,128)(...) custom-call(bf16[512,1536]{1,0:T(8,128)(2,1)S(1)} %multiply_convert_, ...), custom_call_target="tpu_custom_call" | custom-call | bytes 786432 | tf_op jit(solution)/shard_map/raise_up/pallas_call | solution.py:371
  268.1 14.7 %raise_back.1 = (bf16[512,1024]{1,0:T(8,128)(2,1)S(1)}, bf16[512,1024]{1,0:T(8,128)(2,1)S(1)}, bf16[512,1024]{1,0:T(8,128)(2,1)S(1)}, bf16[512,1024]{1,0:T(8,128...) custom-call(bf16[512,1536]{1,0:T(8,128)(2,1)S(1)} %copy-done.34, ...), custom_call_target="tpu_custom_call" | custom-call | bytes 786432 | tf_op jit(solution)/shard_map/raise_back/pallas_call | solution.py:405
  291.9 7.9 %weight_product.5 = bf16[1536,1024]{1,0:T(8,128)(2,1)S(1)} custom-call(bf16[512,1536]{1,0:T(8,128)(2,1)S(1)} %copy-done.34, bf16[512,1536]{1,0:T(8,128)(2,1)S(1)} %copy-done.36, bf16[512,1536]{1,0:T(8,128)(2,1)S(1)} %copy-done.38, bf16[512,1536]{1,0:T(8,128)(2,1)S(1)} %copy-done.40, bf16[512,1024]{1,0:T(8,128)(2,1)S(1)} %copy-done.79, ...), custom_call_target="tpu_custom_call" | custom-call | flops 100663296 | bytes 163840 | tf_op jit(solution)/shard_map/weight_product/pallas_call | solution.py:317
  301.6 3.7 copy-done
  307.7 5.1 back_product.12
  313.0 4.4 back_product.13
  318.9 3.2 collective-permute-done.38.refs_4_
  322.2 6.7 %back_product.14 = bf16[512,1536]{1,0:T(8,128)(2,1)} custom-call(bf16[512,1024]{1,0:T(8,128)(2,1)S(1)} %copy-done.68, bf16[512,1024]{1,0:T(8,128)(2,1)S(1)} %copy-done.59, bf16[1536,3072]{1,0:T(8,128)(2,1)} %all-gather.2.cloned.1.call-done.refs_4_.refs_5_.refs_2_.refs_3_.refs_1_, ...), custom_call_target="tpu_custom_call" | custom-call | flops 100663296 | bytes 262144 | tf_op jit(solution)/shard_map/back_product/pallas_call | solution.py:283
  330.7 8.6 %weight_product.6.refs_8_ = bf16[1536,2048]{1,0:T(8,128)(2,1)} custom-call(bf16[512,1536]{1,0:T(8,128)(2,1)S(1)} %multiply_convert_fusion.refs_0_, bf16[512,1536]{1,0:T(8,128)(2,1)S(1)} %copy-done.14, bf16[512,1536]{1,0:T(8,128)(2,1)S(1)} %collective-permute-done.32.refs_2_, bf16[512,1536]{1,0:T(8,128)(2,1)S(1)} %copy-done.17, ...), custom_call_target="tpu_custom_call" | custom-call | flops 100663296 | bytes 163840 | tf_op jit(solution)/shard_map/weight_product/pallas_call | solution.py:317
  339.3 5.9 back_product.15
  346.9 8.6 %weight_product.7 = bf16[1536,2048]{1,0:T(8,128)(2,1)} custom-call(bf16[512,1536]{1,0:T(8,128)(2,1)S(1)} %multiply_convert_fusion.refs_0_, bf16[512,1536]{1,0:T(8,128)(2,1)S(1)} %copy-done.14, bf16[512,1536]{1,0:T(8,128)(2,1)S(1)} %collective-permute-done.32.refs_2_, bf16[512,1536]{1,0:T(8,128)(2,1)S(1)} %copy-done.17, ...), custom_call_target="tpu_custom_call", output_to_operand_aliasing={{}: (8, {})} | custom-call | flops 100663296 | bytes 163840 | tf_op jit(solution)/shard_map/weight_product/pallas_call | solution.py:317
  355.4 3.7 copy-done.1
  369.7 3.8 multiply_reduce_fusion.1
  376.3 2.6 convolution_convert_fusion
  383.2 11.7 %attend_back.4 = (bf16[512,1152]{1,0:T(8,128)(2,1)S(1)}, f32[8,128]{1,0:T(8,128)S(1)}) custom-call(f32[1]{0:T(128)} %bitcast.1.lam_ref, bf16[512,1152]{1,0:T(8,128)(2,1)S(1)} %copy-done.31, f32[8,128]{1,0:T(8,128)S(1)} %pad_maximum_fusion.5.marks_ref.refs_4_, f32[1,128]{1,0:T(1,128)S(1)} %copy-done.127, bf16[512,384]{1,0:T(8,128)(2,1)S(1)} %get-tuple-element.772.grad_ref), custom_call_target="tpu_custom_call" | custom-call | bytes 196608 | tf_op jit(solution)/shard_map/attend_back/pallas_call | solution.py:181
  395.6 12.1 %attend_back.5 = (bf16[512,1152]{1,0:T(8,128)(2,1)S(1)}, f32[8,128]{1,0:T(8,128)S(1)}) custom-call(f32[1]{0:T(128)} %bitcast.1.lam_ref, bf16[512,1152]{1,0:T(8,128)(2,1)S(1)} %copy-done.27, f32[8,128]{1,0:T(8,128)S(1)} %collective-permute-done.12.marks_ref.refs_5_, f32[1,128]{1,0:T(1,128)S(1)} %copy-done.127, ...), custom_call_target="tpu_custom_call" | custom-call | bytes 196608 | tf_op jit(solution)/shard_map/attend_back/pallas_call | solution.py:181
  410.7 11.9 %attend_back.6 = (bf16[512,1152]{1,0:T(8,128)(2,1)S(1)}, f32[8,128]{1,0:T(8,128)S(1)}) custom-call(f32[1]{0:T(128)} %bitcast.1.lam_ref, bf16[512,1152]{1,0:T(8,128)(2,1)S(1)} %copy-done.29, f32[16,128]{1,0:T(8,128)S(1)} %collective-permute-done.25.marks_ref.refs_6_.refs_7_, f32[1,128]{1,0:T(1,128)S(1)} %copy-done.127, ...), custom_call_target="tpu_custom_call" | custom-call | bytes 196608 | tf_op jit(solution)/shard_map/attend_back/pallas_call | solution.py:181
  422.7 5.6 collective-permute-done.49.refs_7_
  430.5 2.7 back_product.18
  433.5 11.7 %attend_back.7 = (bf16[512,1152]{1,0:T(8,128)(2,1)S(1)}, f32[8,128]{1,0:T(8,128)S(1)}) custom-call(f32[1]{0:T(128)} %bitcast.1.lam_ref, bf16[512,1152]{1,0:T(8,128)(2,1)S(1)} %copy-done.25, f32[16,128]{1,0:T(8,128)S(1)} %collective-permute-done.25.marks_ref.refs_6_.refs_7_, f32[1,128]{1,0:T(1,128)S(1)} %copy-done.127, bf16[512,384]{1,0:T(8,128)(2,1)S(1)} %copy-done.115), custom_call_target="tpu_custom_call" | custom-call | bytes 196608 | tf_op jit(solution)/shard_map/attend_back/pallas_call | solution.py:181
  446.6 5.3 weight_product.8.refs_8_
  454.1 4.7 back_product.19
  460.5 10.5 %weight_product.9 = bf16[1536,1536]{1,0:T(8,128)(2,1)} custom-call(bf16[512,1536]{1,0:T(8,128)(2,1)S(1)} %copy-done.19, bf16[512,1536]{1,0:T(8,128)(2,1)S(1)} %copy-done.45, bf16[512,1536]{1,0:T(8,128)(2,1)S(1)} %copy-done.43, bf16[512,1536]{1,0:T(8,128)(2,1)S(1)} %copy-done.47, ...), custom_call_target="tpu_custom_call", output_to_operand_aliasing={{}: (8, {})} | custom-call | flops 113246208 | bytes 172032 | tf_op jit(solution)/shard_map/weight_product/pallas_call | solution.py:317
  471.0 5.6 add_convert_fusion
  476.7 3.5 back_product.20
  480.5 3.4 back_product.21
  488.8 4.9 back_product.22
  493.7 4.2 back_product.23
  500.4 14.7 %collective-permute-done.55.refs_2_ = bf16[96,3072]{1,0:T(8,128)(2,1)S(1)} collective-permute-done((bf16[96,3072]{1,0:T(8,128)(2,1)S(1)}, bf16[96,3072]{1,0:T(8,128)(2,1)S(1)}, u32[]{:S(2)}, u32[]{:S(2)}) %collective-permute-start.55) | collective-permute-done | bytes 589856 | tf_op jit(solution)/shard_map/ppermute | solution.py:589
  526.3 6.7 %merge.2 = (f32[96,12288]{1,0:T(8,128)}, f32[96,12288]{1,0:T(8,128)S(1)}, f32[8,96]{1,0:T(8,128)S(1)}) custom-call(s32[1]{0:T(128)} %bitcast.member_ref, bf16[96,3072]{1,0:T(8,128)(2,1)S(1)} %copy-done.83, bf16[96,3072]{1,0:T(8,128)(2,1)S(1)} %copy-done.105, bf16[96,3072]{1,0:T(8,128)(2,1)S(1)} %copy-done.103, bf16[96,3072]{1,0:T(8,128)(2,1)S(1)} %copy-done.101, ...), custom_call_target="tpu_custom_call" | custom-call | bytes 1179648 | tf_op jit(solution)/shard_map/merge/pallas_call | solution.py:502
  536.6 4.2 right_factor.2
  542.3 4.2 collective-permute-done.59.other_ref
  551.9 8.0 %update.2 = (f32[8,12288]{1,0:T(8,128)}, f32[96,12288]{1,0:T(8,128)}, f32[96,12288]{1,0:T(8,128)}, f32[96,12288]{1,0:T(8,128)}) custom-call(f32[8,96]{1,0:T(8,128)S(1)} %copy-done.133, bf16[8,12288]{1,0:T(8,128)(2,1)S(1)} %get-tuple-element.899.own_ref, bf16[8,12288]{1,0:T(8,128)(2,1)S(1)} %collective-permute-done.59.other_ref, f32[96,12288]{1,0:T(8,128)S(1)} %copy-done.11, ...), custom_call_target="tpu_custom_call" | custom-call | bytes 1179648 | tf_op jit(solution)/shard_map/update/pallas_call | solution.py:572
  562.6 6.8 %reduce-scatter.8.cloned.1.call-done = bf16[384,1536]{1,0:T(8,128)(2,1)} async-done(((bf16[1536,1536]{1,0:T(8,128)(2,1)}), bf16[384,1536]{1,0:T(8,128)(2,1)}) %reduce-scatter.8.cloned.1.call-update) | async-done | bytes 1179664 | tf_op jit(solution)/shard_map/reduce_scatter | solution.py:605
  579.2 2.9 collective-permute-start.63
  583.9 4.1 collective-permute-done.65.refs_2_
  588.0 4.4 merge.3
  594.1 2.9 collective-permute-done.68.other_ref
  597.0 2.9 right_factor.3
  600.7 4.3 fusion.8
  605.0 4.8 update.3
  (530 shorter events, 179.3 us)
Async XLA Ops:
  7.2 237.7 %all-gather.2.cloned.1.call-start = ((), (), s32[]{:S(2)}) async-start(), calls=%async_computation.3 | async-start | bytes 10616832 | tf_op jit(solution)/shard_map/all_gather | solution.py:757
  13.8 6.2 %collective-permute-start.3 = (f32[8,128]{1,0:T(8,128)S(1)}, f32[8,128]{1,0:T(8,128)S(1)}, u32[]{:S(2)}, u32[]{:S(2)}) collective-permute-start(f32[8,128]{1,0:T(8,128)S(1)} %broadcast_add_fusion), channel_id=1, source_target_pairs={{0,4},{4,0},{8,12},{12,8},{1,5},{5,1},{9,13},{13,9},{2,6},{6,2},{1... | collective-permute-start | bytes 12296 | tf_op jit(solution)/shard_map/ppermute | solution.py:593
  18.1 12.5 %collective-permute-start = (bf16[96,1152]{1,0:T(8,128)(2,1)S(1)}, bf16[96,1152]{1,0:T(8,128)(2,1)S(1)}, u32[]{:S(2)}, u32[]{:S(2)}) collective-permute-start(bf16[96,1152]{1,0:T(8,128)(2,1)S(1)} %get-tuple-element.500), channel_id=1, source_target_pairs={{0,3},{1,2},{2,1},{3,0},{4,7},{5,6},{6,5},{7,4},{8,11},{9,10},{10,... | collective-permute-start | bytes 663560 | tf_op jit(solution)/shard_map/ppermute | solution.py:589
  18.2 12.5 %collective-permute-start.1 = (bf16[96,1152]{1,0:T(8,128)(2,1)S(1)}, bf16[96,1152]{1,0:T(8,128)(2,1)S(1)}, u32[]{:S(2)}, u32[]{:S(2)}) collective-permute-start(bf16[96,1152]{1,0:T(8,128)(2,1)S(1)} %get-tuple-element.501), channel_id=1, source_target_pairs={{0,2},{1,3},{2,0},{3,1},{4,6},{5,7},{6,4},{7,5},{8,10},{9,11},{10,... | collective-permute-start | bytes 663560 | tf_op jit(solution)/shard_map/ppermute | solution.py:589
  19.8 10.9 %collective-permute-start.5 = (bf16[96,1152]{1,0:T(8,128)(2,1)S(1)}, bf16[96,1152]{1,0:T(8,128)(2,1)S(1)}, u32[]{:S(2)}, u32[]{:S(2)}) collective-permute-start(bf16[96,1152]{1,0:T(8,128)(2,1)S(1)} %get-tuple-element.510), channel_id=1, source_target_pairs={{0,1},{1,0},{2,3},{3,2},{4,5},{5,4},{6,7},{7,6},{8,9},{9,8},{10,11... | collective-permute-start | bytes 663560 | tf_op jit(solution)/shard_map/ppermute | solution.py:589
  31.8 13.9 %collective-permute-start.6 = (bf16[192,1152]{1,0:T(8,128)(2,1)S(1)}, bf16[192,1152]{1,0:T(8,128)(2,1)S(1)}, u32[]{:S(2)}, u32[]{:S(2)}) collective-permute-start(bf16[192,1152]{1,0:T(8,128)(2,1)S(1)} %get-tuple-element.515), channel_id=1, source_target_pairs={{0,4},{4,8},{8,12},{12,0},{1,5},{5,9},{9,13},{13,1},{2,6},{6,10},{... | collective-permute-start | bytes 1327112 | tf_op jit(solution)/shard_map/ppermute | solution.py:597
  36.9 38.0 %collective-permute-start.7 = (bf16[96,3072]{1,0:T(8,128)(2,1)}, bf16[96,3072]{1,0:T(8,128)(2,1)}, u32[]{:S(2)}, u32[]{:S(2)}) collective-permute-start(bf16[96,3072]{1,0:T(8,128)(2,1)} %get-tuple-element.530), channel_id=1, source_target_pairs={{0,1},{1,0},{2,3},{3,2},{4,5},{5,4},{6,7},{7,6},{8,9},{9,8},{10,11... | collective-permute-start | bytes 1769480 | tf_op jit(solution)/shard_map/ppermute | solution.py:589
  36.9 37.9 %collective-permute-start.8 = (bf16[96,3072]{1,0:T(8,128)(2,1)}, bf16[96,3072]{1,0:T(8,128)(2,1)}, u32[]{:S(2)}, u32[]{:S(2)}) collective-permute-start(bf16[96,3072]{1,0:T(8,128)(2,1)} %get-tuple-element.531), channel_id=1, source_target_pairs={{0,3},{1,2},{2,1},{3,0},{4,7},{5,6},{6,5},{7,4},{8,11},{9,10},{10,... | collective-permute-start | bytes 1769480 | tf_op jit(solution)/shard_map/ppermute | solution.py:589
  37.0 36.1 %collective-permute-start.9 = (bf16[96,3072]{1,0:T(8,128)(2,1)}, bf16[96,3072]{1,0:T(8,128)(2,1)}, u32[]{:S(2)}, u32[]{:S(2)}) collective-permute-start(bf16[96,3072]{1,0:T(8,128)(2,1)} %get-tuple-element.532), channel_id=1, source_target_pairs={{0,2},{1,3},{2,0},{3,1},{4,6},{5,7},{6,4},{7,5},{8,10},{9,11},{10,... | collective-permute-start | bytes 1769480 | tf_op jit(solution)/shard_map/ppermute | solution.py:589
  46.1 13.1 %collective-permute-start.10 = (bf16[192,1152]{1,0:T(8,128)(2,1)S(1)}, bf16[192,1152]{1,0:T(8,128)(2,1)S(1)}, u32[]{:S(2)}, u32[]{:S(2)}) collective-permute-start(bf16[192,1152]{1,0:T(8,128)(2,1)S(1)} %collective-permute-done.6.refs_2_), channel_id=1, source_target_pairs={{0,4},{4,8},{8,12},{12,0},{1,5},{5,9},{9,13},{13,1},{2,6},{6,10},{... | collective-permute-start | bytes 1327112 | tf_op jit(solution)/shard_map/ppermute | solution.py:597
  59.3 12.2 %collective-permute-start.11 = (bf16[192,1152]{1,0:T(8,128)(2,1)S(1)}, bf16[192,1152]{1,0:T(8,128)(2,1)}, u32[]{:S(2)}, u32[]{:S(2)}) collective-permute-start(bf16[192,1152]{1,0:T(8,128)(2,1)S(1)} %collective-permute-done.10.refs_4_), channel_id=1, source_target_pairs={{0,4},{4,8},{8,12},{12,0},{1,5},{5,9},{9,13},{13,1},{2,6},{6,10},{... | collective-permute-start | bytes 1327112 | tf_op jit(solution)/shard_map/ppermute | solution.py:597
  61.2 22.0 %collective-permute-start.17 = (bf16[192,1152]{1,0:T(8,128)(2,1)S(1)}, bf16[192,1152]{1,0:T(8,128)(2,1)}, u32[]{:S(2)}, u32[]{:S(2)}) collective-permute-start(bf16[192,1152]{1,0:T(8,128)(2,1)S(1)} %collective-permute-done.6.refs_2_), channel_id=1, source_target_pairs={{0,16},{16,0},{1,17},{17,1},{2,18},{18,2},{3,19},{19,3},{4,20},{20... | collective-permute-start | bytes 1327112 | tf_op jit(solution)/shard_map/ppermute | solution.py:601
  71.5 13.2 %collective-permute-start.16 = (bf16[192,1152]{1,0:T(8,128)(2,1)S(1)}, bf16[192,1152]{1,0:T(8,128)(2,1)}, u32[]{:S(2)}, u32[]{:S(2)}) collective-permute-start(bf16[192,1152]{1,0:T(8,128)(2,1)S(1)} %collective-permute-done.10.refs_4_), channel_id=1, source_target_pairs={{0,16},{16,0},{1,17},{17,1},{2,18},{18,2},{3,19},{19,3},{4,20},{20... | collective-permute-start | bytes 1327112 | tf_op jit(solution)/shard_map/ppermute | solution.py:601
  73.0 7.0 %collective-permute-start.14 = (bf16[96,1536]{1,0:T(8,128)(2,1)}, bf16[96,1536]{1,0:T(8,128)(2,1)S(1)}, u32[]{:S(2)}, u32[]{:S(2)}) collective-permute-start(bf16[96,1536]{1,0:T(8,128)(2,1)} %slice.297), channel_id=1, source_target_pairs={{0,2},{1,3},{2,0},{3,1},{4,6},{5,7},{6,4},{7,5},{8,10},{9,11},{10,... | collective-permute-start | bytes 884744 | tf_op jit(solution)/shard_map/ppermute | solution.py:589
  80.8 12.0 %collective-permute-start.19 = (bf16[192,1152]{1,0:T(8,128)(2,1)}, bf16[192,1152]{1,0:T(8,128)(2,1)S(1)}, u32[]{:S(2)}, u32[]{:S(2)}) collective-permute-start(bf16[192,1152]{1,0:T(8,128)(2,1)} %collective-permute-done.11.refs_6_), channel_id=1, source_target_pairs={{0,16},{16,0},{1,17},{17,1},{2,18},{18,2},{3,19},{19,3},{4,20},{20... | collective-permute-start | bytes 1327112 | tf_op jit(solution)/shard_map/ppermute | solution.py:601
  83.2 8.6 %collective-permute-start.15 = (bf16[96,1536]{1,0:T(8,128)(2,1)S(1)}, bf16[96,1536]{1,0:T(8,128)(2,1)}, u32[]{:S(2)}, u32[]{:S(2)}) collective-permute-start(bf16[96,1536]{1,0:T(8,128)(2,1)S(1)} %get-tuple-element.557), channel_id=1, source_target_pairs={{0,4},{4,8},{8,12},{12,0},{1,5},{5,9},{9,13},{13,1},{2,6},{6,10},{... | collective-permute-start | bytes 884744 | tf_op jit(solution)/shard_map/ppermute | solution.py:597
  92.8 275.0 %reduce-scatter.4.cloned.1.call-start = ((), (), s32[]{:S(2)}) async-start(), calls=%async_computation.4 | async-start | bytes 3932160 | tf_op jit(solution)/shard_map/reduce_scatter | solution.py:605
  92.8 35.3 %collective-permute-start.13 = (bf16[512,1536]{1,0:T(8,128)(2,1)S(1)}, bf16[512,1536]{1,0:T(8,128)(2,1)S(1)}, u32[]{:S(2)}, u32[]{:S(2)}) collective-permute-start(bf16[512,1536]{1,0:T(8,128)(2,1)S(1)} %fusion.4.left_ref.refs_0_), channel_id=1, source_target_pairs={{0,2},{1,3},{2,0},{3,1},{4,6},{5,7},{6,4},{7,5},{8,10},{9,11},{10,... | collective-permute-start | bytes 4718600 | tf_op jit(solution)/shard_map/ppermute | solution.py:589
  94.0 10.6 %collective-permute-start.18 = (bf16[96,1536]{1,0:T(8,128)(2,1)}, bf16[96,1536]{1,0:T(8,128)(2,1)S(1)}, u32[]{:S(2)}, u32[]{:S(2)}) collective-permute-start(bf16[96,1536]{1,0:T(8,128)(2,1)} %collective-permute-done.15.refs_2_), channel_id=1, source_target_pairs={{0,4},{4,8},{8,12},{12,0},{1,5},{5,9},{9,13},{13,1},{2,6},{6,10},{... | collective-permute-start | bytes 884744 | tf_op jit(solution)/shard_map/ppermute | solution.py:597
  94.0 13.8 %collective-permute-start.22 = (bf16[96,1536]{1,0:T(8,128)(2,1)}, bf16[96,1536]{1,0:T(8,128)(2,1)S(1)}, u32[]{:S(2)}, u32[]{:S(2)}) collective-permute-start(bf16[96,1536]{1,0:T(8,128)(2,1)} %collective-permute-done.15.refs_2_), channel_id=1, source_target_pairs={{0,16},{16,0},{1,17},{17,1},{2,18},{18,2},{3,19},{19,3},{4,20},{20... | collective-permute-start | bytes 884744 | tf_op jit(solution)/shard_map/ppermute | solution.py:601
  104.6 17.2 %collective-permute-start.21 = (bf16[96,1536]{1,0:T(8,128)(2,1)S(1)}, bf16[96,1536]{1,0:T(8,128)(2,1)S(1)}, u32[]{:S(2)}, u32[]{:S(2)}) collective-permute-start(bf16[96,1536]{1,0:T(8,128)(2,1)S(1)} %collective-permute-done.18.refs_4_), channel_id=1, source_target_pairs={{0,4},{4,8},{8,12},{12,0},{1,5},{5,9},{9,13},{13,1},{2,6},{6,10},{... | collective-permute-start | bytes 884744 | tf_op jit(solution)/shard_map/ppermute | solution.py:597
  104.6 17.2 %collective-permute-start.20 = (bf16[96,1536]{1,0:T(8,128)(2,1)S(1)}, bf16[96,1536]{1,0:T(8,128)(2,1)S(1)}, u32[]{:S(2)}, u32[]{:S(2)}) collective-permute-start(bf16[96,1536]{1,0:T(8,128)(2,1)S(1)} %collective-permute-done.18.refs_4_), channel_id=1, source_target_pairs={{0,16},{16,0},{1,17},{17,1},{2,18},{18,2},{3,19},{19,3},{4,20},{20... | collective-permute-start | bytes 884744 | tf_op jit(solution)/shard_map/ppermute | solution.py:601
  106.8 22.5 %collective-permute-start.25 = (f32[16,128]{1,0:T(8,128)S(1)}, f32[16,128]{1,0:T(8,128)S(1)}, u32[]{:S(2)}, u32[]{:S(2)}) collective-permute-start(f32[16,128]{1,0:T(8,128)S(1)} %pad_maximum_fusion.4), channel_id=1, source_target_pairs={{0,2},{1,3},{2,0},{3,1},{4,6},{5,7},{6,4},{7,5},{8,10},{9,11},{10,... | collective-permute-start | bytes 24584 | tf_op jit(solution)/shard_map/ppermute | solution.py:589
  108.5 32.7 %collective-permute-start.27 = (bf16[512,1536]{1,0:T(8,128)(2,1)S(1)}, bf16[512,1536]{1,0:T(8,128)(2,1)S(1)}, u32[]{:S(2)}, u32[]{:S(2)}) collective-permute-start(bf16[512,1536]{1,0:T(8,128)(2,1)S(1)} %fusion.4.left_ref.refs_0_), channel_id=1, source_target_pairs={{0,1},{1,0},{2,3},{3,2},{4,5},{5,4},{6,7},{7,6},{8,9},{9,8},{10,11... | collective-permute-start | bytes 4718600 | tf_op jit(solution)/shard_map/ppermute | solution.py:589
  129.3 34.6 %collective-permute-start.26 = (bf16[512,1536]{1,0:T(8,128)(2,1)}, bf16[512,1536]{1,0:T(8,128)(2,1)}, u32[]{:S(2)}, u32[]{:S(2)}) collective-permute-start(bf16[512,1536]{1,0:T(8,128)(2,1)} %refs_0_.3), channel_id=1, source_target_pairs={{0,2},{1,3},{2,0},{3,1},{4,6},{5,7},{6,4},{7,5},{8,10},{9,11},{10,... | collective-permute-start | bytes 4718600 | tf_op jit(solution)/shard_map/ppermute | solution.py:589
  131.8 32.1 %collective-permute-start.24 = (bf16[96,1536]{1,0:T(8,128)(2,1)}, bf16[96,1536]{1,0:T(8,128)(2,1)S(1)}, u32[]{:S(2)}, u32[]{:S(2)}) collective-permute-start(bf16[96,1536]{1,0:T(8,128)(2,1)} %copy-done.121), channel_id=1, source_target_pairs={{0,16},{16,0},{1,17},{17,1},{2,18},{18,2},{3,19},{19,3},{4,20},{20... | collective-permute-start | bytes 884744 | tf_op jit(solution)/shard_map/ppermute | solution.py:601
  166.0 20.1 %collective-permute-start.29 = (bf16[768,1536]{1,0:T(8,128)(2,1)S(1)}, bf16[768,1536]{1,0:T(8,128)(2,1)}, u32[]{:S(2)}, u32[]{:S(2)}) collective-permute-start(bf16[768,1536]{1,0:T(8,128)(2,1)S(1)} %bitcast.54), channel_id=1, source_target_pairs={{0,1},{1,0},{2,3},{3,2},{4,5},{5,4},{6,7},{7,6},{8,9},{9,8},{10,11... | collective-permute-start | bytes 7077896 | tf_op jit(solution)/shard_map/ppermute | solution.py:589
  166.1 8.7 %collective-permute-start.23 = (bf16[512,1536]{1,0:T(8,128)(2,1)S(1)}, bf16[512,1536]{1,0:T(8,128)(2,1)S(1)}, u32[]{:S(2)}, u32[]{:S(2)}) collective-permute-start(bf16[512,1536]{1,0:T(8,128)(2,1)S(1)} %copy-done.42), channel_id=1, source_target_pairs={{0,1},{1,0},{2,3},{3,2},{4,5},{5,4},{6,7},{7,6},{8,9},{9,8},{10,11... | collective-permute-start | bytes 4718600 | tf_op jit(solution)/shard_map/ppermute | solution.py:589
  166.6 18.8 %collective-permute-start.31 = (bf16[512,384]{1,0:T(8,128)(2,1)}, bf16[512,384]{1,0:T(8,128)(2,1)}, u32[]{:S(2)}, u32[]{:S(2)}) collective-permute-start(bf16[512,384]{1,0:T(8,128)(2,1)} %attend.5), channel_id=1, source_target_pairs={{0,1},{1,0},{2,3},{3,2},{4,5},{5,4},{6,7},{7,6},{8,9},{9,8},{10,11... | collective-permute-start | bytes 1179656 | tf_op jit(solution)/shard_map/ppermute | solution.py:589
  174.5 11.6 %collective-permute-start.30 = (bf16[512,384]{1,0:T(8,128)(2,1)S(1)}, bf16[512,384]{1,0:T(8,128)(2,1)}, u32[]{:S(2)}, u32[]{:S(2)}) collective-permute-start(bf16[512,384]{1,0:T(8,128)(2,1)S(1)} %attend.6), channel_id=1, source_target_pairs={{0,2},{1,3},{2,0},{3,1},{4,6},{5,7},{6,4},{7,5},{8,10},{9,11},{10,... | collective-permute-start | bytes 1179656 | tf_op jit(solution)/shard_map/ppermute | solution.py:589
  183.9 11.3 %collective-permute-start.28 = (bf16[512,384]{1,0:T(8,128)(2,1)S(1)}, bf16[512,384]{1,0:T(8,128)(2,1)}, u32[]{:S(2)}, u32[]{:S(2)}) collective-permute-start(bf16[512,384]{1,0:T(8,128)(2,1)S(1)} %attend.7), channel_id=1, source_target_pairs={{0,3},{1,2},{2,1},{3,0},{4,7},{5,6},{6,5},{7,4},{8,11},{9,10},{10,... | collective-permute-start | bytes 1179656 | tf_op jit(solution)/shard_map/ppermute | solution.py:589
  185.5 20.0 %collective-permute-start.33 = (bf16[512,1536]{1,0:T(8,128)(2,1)}, bf16[512,1536]{1,0:T(8,128)(2,1)}, u32[]{:S(2)}, u32[]{:S(2)}) collective-permute-start(bf16[512,1536]{1,0:T(8,128)(2,1)} %collective-permute-done.26.refs_2_), channel_id=1, source_target_pairs={{0,1},{1,0},{2,3},{3,2},{4,5},{5,4},{6,7},{7,6},{8,9},{9,8},{10,11... | collective-permute-start | bytes 4718600 | tf_op jit(solution)/shard_map/ppermute | solution.py:589
  185.8 19.7 %collective-permute-start.34 = (bf16[512,1536]{1,0:T(8,128)(2,1)}, bf16[512,1536]{1,0:T(8,128)(2,1)}, u32[]{:S(2)}, u32[]{:S(2)}) collective-permute-start(bf16[512,1536]{1,0:T(8,128)(2,1)} %refs_0_.3), channel_id=1, source_target_pairs={{0,1},{1,0},{2,3},{3,2},{4,5},{5,4},{6,7},{7,6},{8,9},{9,8},{10,11... | collective-permute-start | bytes 4718600 | tf_op jit(solution)/shard_map/ppermute | solution.py:589
  203.6 36.7 %collective-permute-start.32 = (bf16[512,1536]{1,0:T(8,128)(2,1)S(1)}, bf16[512,1536]{1,0:T(8,128)(2,1)S(1)}, u32[]{:S(2)}, u32[]{:S(2)}) collective-permute-start(bf16[512,1536]{1,0:T(8,128)(2,1)S(1)} %multiply_convert_fusion.refs_0_), channel_id=1, source_target_pairs={{0,2},{1,3},{2,0},{3,1},{4,6},{5,7},{6,4},{7,5},{8,10},{9,11},{10,... | collective-permute-start | bytes 4718600 | tf_op jit(solution)/shard_map/ppermute | solution.py:589
  205.3 36.8 %collective-permute-start.36 = (bf16[512,1536]{1,0:T(8,128)(2,1)S(1)}, bf16[512,1536]{1,0:T(8,128)(2,1)S(1)}, u32[]{:S(2)}, u32[]{:S(2)}) collective-permute-start(bf16[512,1536]{1,0:T(8,128)(2,1)S(1)} %multiply_convert_fusion.refs_0_), channel_id=1, source_target_pairs={{0,1},{1,0},{2,3},{3,2},{4,5},{5,4},{6,7},{7,6},{8,9},{9,8},{10,11... | collective-permute-start | bytes 4718600 | tf_op jit(solution)/shard_map/ppermute | solution.py:589
  240.3 50.3 %collective-permute-start.37 = (bf16[512,1536]{1,0:T(8,128)(2,1)}, bf16[512,1536]{1,0:T(8,128)(2,1)}, u32[]{:S(2)}, u32[]{:S(2)}) collective-permute-start(bf16[512,1536]{1,0:T(8,128)(2,1)} %pad_maximum_fusion.1.refs_0_), channel_id=1, source_target_pairs={{0,2},{1,3},{2,0},{3,1},{4,6},{5,7},{6,4},{7,5},{8,10},{9,11},{10,... | collective-permute-start | bytes 4718600 | tf_op jit(solution)/shard_map/ppermute | solution.py:589
  301.5 182.6 %reduce-scatter.6.cloned.1.call-start = ((), (), s32[]{:S(2)}) async-start(), calls=%async_computation.5 | async-start | bytes 7864320 | tf_op jit(solution)/shard_map/reduce_scatter | solution.py:605
  312.8 6.1 collective-permute-start.39
  328.9 38.9 %collective-permute-start.40 = (bf16[512,1536]{1,0:T(8,128)(2,1)}, bf16[512,1536]{1,0:T(8,128)(2,1)}, u32[]{:S(2)}, u32[]{:S(2)}) collective-permute-start(bf16[512,1536]{1,0:T(8,128)(2,1)} %back_product.14), channel_id=1, source_target_pairs={{0,2},{1,3},{2,0},{3,1},{4,6},{5,7},{6,4},{7,5},{8,10},{9,11},{10,... | collective-permute-start | bytes 4718600 | tf_op jit(solution)/shard_map/ppermute | solution.py:589
  367.8 201.5 %reduce-scatter.8.cloned.1.call-start = ((), (), s32[]{:S(2)}) async-start(), calls=%async_computation.6 | async-start | bytes 5898240 | tf_op jit(solution)/shard_map/reduce_scatter | solution.py:605
  368.1 12.4 %collective-permute-start.46 = (bf16[512,1536]{1,0:T(8,128)(2,1)}, bf16[512,1536]{1,0:T(8,128)(2,1)S(1)}, u32[]{:S(2)}, u32[]{:S(2)}) collective-permute-start(bf16[512,1536]{1,0:T(8,128)(2,1)} %collective-permute-done.37.refs_2_), channel_id=1, source_target_pairs={{0,1},{1,0},{2,3},{3,2},{4,5},{5,4},{6,7},{7,6},{8,9},{9,8},{10,11... | collective-permute-start | bytes 4718600 | tf_op jit(solution)/shard_map/ppermute | solution.py:589
  368.2 27.3 %collective-permute-start.44 = (bf16[512,1536]{1,0:T(8,128)(2,1)}, bf16[512,1536]{1,0:T(8,128)(2,1)S(1)}, u32[]{:S(2)}, u32[]{:S(2)}) collective-permute-start(bf16[512,1536]{1,0:T(8,128)(2,1)} %copy-done.92), channel_id=1, source_target_pairs={{0,1},{1,0},{2,3},{3,2},{4,5},{5,4},{6,7},{7,6},{8,9},{9,8},{10,11... | collective-permute-start | bytes 4718600 | tf_op jit(solution)/shard_map/ppermute | solution.py:589
  368.7 26.9 %collective-permute-start.45 = (bf16[512,1536]{1,0:T(8,128)(2,1)}, bf16[512,1536]{1,0:T(8,128)(2,1)S(1)}, u32[]{:S(2)}, u32[]{:S(2)}) collective-permute-start(bf16[512,1536]{1,0:T(8,128)(2,1)} %copy-done.93), channel_id=1, source_target_pairs={{0,1},{1,0},{2,3},{3,2},{4,5},{5,4},{6,7},{7,6},{8,9},{9,8},{10,11... | collective-permute-start | bytes 4718600 | tf_op jit(solution)/shard_map/ppermute | solution.py:589
  373.5 7.3 %collective-permute-start.47 = (bf16[512,1536]{1,0:T(8,128)(2,1)}, bf16[512,1536]{1,0:T(8,128)(2,1)S(1)}, u32[]{:S(2)}, u32[]{:S(2)}) collective-permute-start(bf16[512,1536]{1,0:T(8,128)(2,1)} %pad_maximum_fusion.1.refs_0_), channel_id=1, source_target_pairs={{0,1},{1,0},{2,3},{3,2},{4,5},{5,4},{6,7},{7,6},{8,9},{9,8},{10,11... | collective-permute-start | bytes 4718600 | tf_op jit(solution)/shard_map/ppermute | solution.py:589
  380.1 15.5 %collective-permute-start.43 = (bf16[512,384]{1,0:T(8,128)(2,1)S(1)}, bf16[512,384]{1,0:T(8,128)(2,1)S(1)}, u32[]{:S(2)}, u32[]{:S(2)}) collective-permute-start(bf16[512,384]{1,0:T(8,128)(2,1)S(1)} %get-tuple-element.1012), channel_id=1, source_target_pairs={{0,1},{1,0},{2,3},{3,2},{4,5},{5,4},{6,7},{7,6},{8,9},{9,8},{10,11... | collective-permute-start | bytes 1179656 | tf_op jit(solution)/shard_map/ppermute | solution.py:589
  380.5 27.3 %collective-permute-start.42 = (bf16[512,384]{1,0:T(8,128)(2,1)}, bf16[512,384]{1,0:T(8,128)(2,1)S(1)}, u32[]{:S(2)}, u32[]{:S(2)}) collective-permute-start(bf16[512,384]{1,0:T(8,128)(2,1)} %get-tuple-element.1011), channel_id=1, source_target_pairs={{0,2},{1,3},{2,0},{3,1},{4,6},{5,7},{6,4},{7,5},{8,10},{9,11},{10,... | collective-permute-start | bytes 1179656 | tf_op jit(solution)/shard_map/ppermute | solution.py:589
  380.8 26.9 %collective-permute-start.41 = (bf16[512,384]{1,0:T(8,128)(2,1)}, bf16[512,384]{1,0:T(8,128)(2,1)S(1)}, u32[]{:S(2)}, u32[]{:S(2)}) collective-permute-start(bf16[512,384]{1,0:T(8,128)(2,1)} %get-tuple-element.1010), channel_id=1, source_target_pairs={{0,3},{1,2},{2,1},{3,0},{4,7},{5,6},{6,5},{7,4},{8,11},{9,10},{10,... | collective-permute-start | bytes 1179656 | tf_op jit(solution)/shard_map/ppermute | solution.py:589
  408.6 14.1 %collective-permute-start.50 = (bf16[512,384]{1,0:T(8,128)(2,1)S(1)}, bf16[512,384]{1,0:T(8,128)(2,1)S(1)}, u32[]{:S(2)}, u32[]{:S(2)}) collective-permute-start(bf16[512,384]{1,0:T(8,128)(2,1)S(1)} %copy-done.149), channel_id=1, source_target_pairs={{0,2},{1,3},{2,0},{3,1},{4,6},{5,7},{6,4},{7,5},{8,10},{9,11},{10,... | collective-permute-start | bytes 1179656 | tf_op jit(solution)/shard_map/ppermute | solution.py:589
  409.1 19.2 %collective-permute-start.49 = (bf16[512,384]{1,0:T(8,128)(2,1)S(1)}, bf16[512,384]{1,0:T(8,128)(2,1)S(1)}, u32[]{:S(2)}, u32[]{:S(2)}) collective-permute-start(bf16[512,384]{1,0:T(8,128)(2,1)S(1)} %copy-done.148), channel_id=1, source_target_pairs={{0,3},{1,2},{2,1},{3,0},{4,7},{5,6},{6,5},{7,4},{8,11},{9,10},{10,... | collective-permute-start | bytes 1179656 | tf_op jit(solution)/shard_map/ppermute | solution.py:589
  410.6 17.8 %collective-permute-start.48 = (bf16[512,384]{1,0:T(8,128)(2,1)S(1)}, bf16[512,384]{1,0:T(8,128)(2,1)S(1)}, u32[]{:S(2)}, u32[]{:S(2)}) collective-permute-start(bf16[512,384]{1,0:T(8,128)(2,1)S(1)} %copy-done.147), channel_id=1, source_target_pairs={{0,1},{1,0},{2,3},{3,2},{4,5},{5,4},{6,7},{7,6},{8,9},{9,8},{10,11... | collective-permute-start | bytes 1179656 | tf_op jit(solution)/shard_map/ppermute | solution.py:589
  433.2 37.8 %collective-permute-start.51 = (bf16[512,1536]{1,0:T(8,128)(2,1)S(1)}, bf16[512,1536]{1,0:T(8,128)(2,1)}, u32[]{:S(2)}, u32[]{:S(2)}) collective-permute-start(bf16[512,1536]{1,0:T(8,128)(2,1)S(1)} %back_product.18), channel_id=1, source_target_pairs={{0,2},{1,3},{2,0},{3,1},{4,6},{5,7},{6,4},{7,5},{8,10},{9,11},{10,... | collective-permute-start | bytes 4718600 | tf_op jit(solution)/shard_map/ppermute | solution.py:589
  480.1 6.7 %collective-permute-start.53 = (bf16[512,1536]{1,0:T(8,128)(2,1)}, bf16[512,1536]{1,0:T(8,128)(2,1)}, u32[]{:S(2)}, u32[]{:S(2)}) collective-permute-start(bf16[512,1536]{1,0:T(8,128)(2,1)} %back_product.20), channel_id=1, source_target_pairs={{0,1},{1,0},{2,3},{3,2},{4,5},{5,4},{6,7},{7,6},{8,9},{9,8},{10,11... | collective-permute-start | bytes 4718600 | tf_op jit(solution)/shard_map/ppermute | solution.py:589
  483.9 9.7 %collective-permute-start.52 = (bf16[512,1536]{1,0:T(8,128)(2,1)}, bf16[512,1536]{1,0:T(8,128)(2,1)}, u32[]{:S(2)}, u32[]{:S(2)}) collective-permute-start(bf16[512,1536]{1,0:T(8,128)(2,1)} %back_product.21), channel_id=1, source_target_pairs={{0,1},{1,0},{2,3},{3,2},{4,5},{5,4},{6,7},{7,6},{8,9},{9,8},{10,11... | collective-permute-start | bytes 4718600 | tf_op jit(solution)/shard_map/ppermute | solution.py:589
  486.8 29.1 %collective-permute-start.54 = (bf16[96,3072]{1,0:T(8,128)(2,1)S(1)}, bf16[96,3072]{1,0:T(8,128)(2,1)S(1)}, u32[]{:S(2)}, u32[]{:S(2)}) collective-permute-start(bf16[96,3072]{1,0:T(8,128)(2,1)S(1)} %get-tuple-element.869), channel_id=1, source_target_pairs={{0,3},{1,2},{2,1},{3,0},{4,7},{5,6},{6,5},{7,4},{8,11},{9,10},{10,... | collective-permute-start | bytes 1769480 | tf_op jit(solution)/shard_map/ppermute | solution.py:589
  488.5 26.6 %collective-permute-start.55 = (bf16[96,3072]{1,0:T(8,128)(2,1)S(1)}, bf16[96,3072]{1,0:T(8,128)(2,1)S(1)}, u32[]{:S(2)}, u32[]{:S(2)}) collective-permute-start(bf16[96,3072]{1,0:T(8,128)(2,1)S(1)} %get-tuple-element.870), channel_id=1, source_target_pairs={{0,2},{1,3},{2,0},{3,1},{4,6},{5,7},{6,4},{7,5},{8,10},{9,11},{10,... | collective-permute-start | bytes 1769480 | tf_op jit(solution)/shard_map/ppermute | solution.py:589
  488.8 10.8 %collective-permute-start.56 = (bf16[96,3072]{1,0:T(8,128)(2,1)S(1)}, bf16[96,3072]{1,0:T(8,128)(2,1)S(1)}, u32[]{:S(2)}, u32[]{:S(2)}) collective-permute-start(bf16[96,3072]{1,0:T(8,128)(2,1)S(1)} %get-tuple-element.871), channel_id=1, source_target_pairs={{0,1},{1,0},{2,3},{3,2},{4,5},{5,4},{6,7},{7,6},{8,9},{9,8},{10,11... | collective-permute-start | bytes 1769480 | tf_op jit(solution)/shard_map/ppermute | solution.py:589
  516.7 43.2 %collective-permute-start.57 = (bf16[512,1536]{1,0:T(8,128)(2,1)}, bf16[512,1536]{1,0:T(8,128)(2,1)}, u32[]{:S(2)}, u32[]{:S(2)}) collective-permute-start(bf16[512,1536]{1,0:T(8,128)(2,1)} %back_product.22), channel_id=1, source_target_pairs={{0,2},{1,3},{2,0},{3,1},{4,6},{5,7},{6,4},{7,5},{8,10},{9,11},{10,... | collective-permute-start | bytes 4718600 | tf_op jit(solution)/shard_map/ppermute | solution.py:589
  540.8 5.7 collective-permute-start.59
  569.4 4.7 collective-permute-start.60
  572.3 15.7 %collective-permute-start.64 = (bf16[96,1536]{1,0:T(8,128)(2,1)S(1)}, bf16[96,1536]{1,0:T(8,128)(2,1)S(1)}, u32[]{:S(2)}, u32[]{:S(2)}) collective-permute-start(bf16[96,1536]{1,0:T(8,128)(2,1)S(1)} %get-tuple-element.932), channel_id=1, source_target_pairs={{0,3},{1,2},{2,1},{3,0},{4,7},{5,6},{6,5},{7,4},{8,11},{9,10},{10,... | collective-permute-start | bytes 884744 | tf_op jit(solution)/shard_map/ppermute | solution.py:589
  573.0 14.9 %collective-permute-start.65 = (bf16[96,1536]{1,0:T(8,128)(2,1)S(1)}, bf16[96,1536]{1,0:T(8,128)(2,1)S(1)}, u32[]{:S(2)}, u32[]{:S(2)}) collective-permute-start(bf16[96,1536]{1,0:T(8,128)(2,1)S(1)} %get-tuple-element.933), channel_id=1, source_target_pairs={{0,2},{1,3},{2,0},{3,1},{4,6},{5,7},{6,4},{7,5},{8,10},{9,11},{10,... | collective-permute-start | bytes 884744 | tf_op jit(solution)/shard_map/ppermute | solution.py:589
  573.9 10.0 %collective-permute-start.66 = (bf16[96,1536]{1,0:T(8,128)(2,1)S(1)}, bf16[96,1536]{1,0:T(8,128)(2,1)S(1)}, u32[]{:S(2)}, u32[]{:S(2)}) collective-permute-start(bf16[96,1536]{1,0:T(8,128)(2,1)S(1)} %get-tuple-element.934), channel_id=1, source_target_pairs={{0,1},{1,0},{2,3},{3,2},{4,5},{5,4},{6,7},{7,6},{8,9},{9,8},{10,11... | collective-permute-start | bytes 884744 | tf_op jit(solution)/shard_map/ppermute | solution.py:589
  579.2 4.7 collective-permute-start.63
  600.0 5.0 collective-permute-start.69
  (180 other events, 1997.0 us)
Sparse Core Ops, SparseCore 0:
  92.9 144.9 all-gather.1
  301.6 63.5 reduce-scatter.3
  368.0 113.4 reduce-scatter.5
  483.6 85.7 reduce-scatter.7

commit v4 on v3

--- a/solution.py
+++ b/solution.py
@@ -321,7 +321,7 @@
         out_specs=pl.BlockSpec((rows, width), lambda i: (i, place)),
         out_shape=jax.ShapeDtypeStruct((depth, columns), BF16),
         input_output_aliases={} if into is None else {2 * GROUP: 0},
-        compiler_params=pltpu.CompilerParams(vmem_limit_bytes=40 * 2**20),
+        compiler_params=pltpu.CompilerParams(vmem_limit_bytes=60 * 2**20),
         cost_estimate=pl.CostEstimate(
             flops=GROUP * length * depth * width // 32,
             bytes_accessed=GROUP * length * (depth + width) // 32,
@@ -378,7 +378,7 @@
         ],
         out_specs=[out_spec] * (3 * GROUP),
         out_shape=[low] * GROUP + [high] * (2 * GROUP),
-        compiler_params=pltpu.CompilerParams(vmem_limit_bytes=40 * 2**20),
+        compiler_params=pltpu.CompilerParams(vmem_limit_bytes=60 * 2**20),
         cost_estimate=pl.CostEstimate(flops=0, bytes_accessed=length * depth, transcendentals=0),
         name="raise_up",
     )(*mids, weight, weight)
@@ -410,7 +410,7 @@
         + [spec] * (2 * GROUP),
         out_specs=[spec] * (2 * GROUP),
         out_shape=[kind] * (2 * GROUP),
-        compiler_params=pltpu.CompilerParams(vmem_limit_bytes=40 * 2**20),
+        compiler_params=pltpu.CompilerParams(vmem_limit_bytes=60 * 2**20),
         cost_estimate=pl.CostEstimate(flops=0, bytes_accessed=length * depth, transcendentals=0),
         name="raise_back",
     )(*grads, weight, *gates, *ups)
@@ -779,12 +779,12 @@
     heads[0] = line.run(heads_of, qkv[0], 0)
     heads[1] = line.run(heads_of, qkv[1], 1)
     heads_beside = swap(heads[1], 1)
+    qkv[2] = line.run(project, normed_across, qkv_weight)
+    heads[2] = line.run(heads_of, qkv[2], 2)
+    heads_across = swap(heads[2], 2)
     cotangent_across = line(cotangent_across)
     out_mine = line(out_gather.finish())
     out_rest = swap(out_mine, 1)
-    qkv[2] = line.run(project, normed_across, qkv_weight)
-    heads[2] = line.run(heads_of, qkv[2], 2)
-    heads_across = swap(heads[2], 2)
     normed_opposite = line(normed_opposite)
     normed_all = [normed_low, normed_beside, normed_across, normed_opposite]
     qkv[3] = line.run(project, normed_opposite, qkv_weight)
@@ -849,8 +849,8 @@
     opposite_got = swap(lower(3), 1)
     beside_got = swap(lower(1), 1)
     opposite_got = line(opposite_got)
+    mid_sum = swap(lower(2, opposite_got), 2)
     beside_got = line(beside_got)
-    mid_sum = swap(lower(2, opposite_got), 2)
     up_partial = product(mid_all, grad_gate, 2 * FF_Q, 0)
     grad_mid_own = lower(0, beside_got, F32)
     up_partial = product(mid_all, grad_up, 2 * FF_Q, 1, up_partial)

time: 624 us -> 616 us (0.987)
  local copies, waits for them, and re-layouts: 85.6 us -> 67.1 us
  Pallas kernels: 254 us -> 271 us
    unnamed x341 -> x271, local copies, waits for them, and re-layouts: 80.9 us -> 62.4 us
    pallas_call x5, Pallas kernels: 40.9 us -> 54.5 us  [weight_product(): pl.pallas_call(weight_kernel, grid=(depth // rows,), in_specs=specs, out_...]
  transfers between devices with their start and end apart: 74 -> 74, of which waited for: 29 -> 28; matrix products, arithmetic and copies ran while one was open for 7% -> 7% of each run, Pallas kernels for 38% -> 40%
where the time goes in v4:
time: 616 us; the launch traced here: 610 us
  Pallas kernels  271 us (44%)
  waiting for transfers between devices  155 us (25%)
  local copies, waits for them, and re-layouts  67.1 us (11%)
  starting transfers between devices  55.6 us (9%)
  other arithmetic  36.1 us (6%)
  between operations  18.7 us (3%)
  matrix products  6.68 us (1%)
    ppermute x48, waiting for transfers between devices, swap(): return lax.ppermute(value, 'member', [(j, j ^ bits) for j in range(GROUP)])  71.3 us
    unnamed x271, local copies, waits for them, and re-layouts  62.4 us
    ppermute x6, waiting for transfers between devices, ring(): lax.ppermute(value, 'layer', [(z, (z + 1) % layers) for z in range(layers)])  57.6 us
    pallas_call x5, Pallas kernels, weight_product(): pl.pallas_call(weight_kernel, grid=(depth // rows,), in_specs=specs, out_...  54.5 us
    pallas_call x12, Pallas kernels, back_product(): pl.pallas_call(partial(back_kernel, pairs), grid=(width // tile,), in_spe...  49.8 us
    pallas_call x4, Pallas kernels, attend_back(): pl.pallas_call(attend_back_kernel, grid=(1,), in_specs=attention_specs(le...  47.4 us
    ppermute x48, starting transfers between devices, swap(): return lax.ppermute(value, 'member', [(j, j ^ bits) for j in range(GROUP)])  32.4 us
    pallas_call x1, Pallas kernels, raise_up(): pl.pallas_call(raise_kernel, grid=(count,), in_specs=[pl.BlockSpec((lengt...  19.2 us
  transfers between devices with their start and end apart: 74, of which 28 were waited for; matrix products, arithmetic and copies ran while one was open for 7% of the time, Pallas kernels for 40%

profile of v4, /device:TPU:0, one launch (start us, length us, event | category | flops | bytes accessed | tf_op | source)
XLA Modules:
  0.0 610.1 jit_solution(13129520490581837762)
XLA Ops:
  9.2 3.0 collective-permute-start.2
  24.6 6.1 collective-permute-done.1
  39.0 6.7 %collective-permute-done.6.refs_2_ = bf16[192,1152]{1,0:T(8,128)(2,1)S(1)} collective-permute-done((bf16[192,1152]{1,0:T(8,128)(2,1)S(1)}, bf16[192,1152]{1,0:T(8,128)(2,1)S(1)}, u32[]{:S(2)}, u32[]{:S(2)}) %collective-permute-start.6) | collective-permute-done | bytes 442400 | tf_op jit(solution)/shard_map/ppermute | solution.py:597
  46.7 12.6 %collective-permute-done.10.refs_4_ = bf16[192,1152]{1,0:T(8,128)(2,1)S(1)} collective-permute-done((bf16[192,1152]{1,0:T(8,128)(2,1)S(1)}, bf16[192,1152]{1,0:T(8,128)(2,1)S(1)}, u32[]{:S(2)}, u32[]{:S(2)}) %collective-permute-start.10) | collective-permute-done | bytes 442400 | tf_op jit(solution)/shard_map/ppermute | solution.py:597
  62.7 8.8 %collective-permute-done.11.refs_6_ = bf16[192,1152]{1,0:T(8,128)(2,1)} collective-permute-done((bf16[192,1152]{1,0:T(8,128)(2,1)S(1)}, bf16[192,1152]{1,0:T(8,128)(2,1)}, u32[]{:S(2)}, u32[]{:S(2)}) %collective-permute-start.11) | collective-permute-done | bytes 442400 | tf_op jit(solution)/shard_map/ppermute | solution.py:597
  84.7 7.1 %collective-permute-done.15.refs_2_ = bf16[96,1536]{1,0:T(8,128)(2,1)} collective-permute-done((bf16[96,1536]{1,0:T(8,128)(2,1)S(1)}, bf16[96,1536]{1,0:T(8,128)(2,1)}, u32[]{:S(2)}, u32[]{:S(2)}) %collective-permute-start.15) | collective-permute-done | bytes 294944 | tf_op jit(solution)/shard_map/ppermute | solution.py:597
  96.1 9.1 %collective-permute-done.18.refs_4_ = bf16[96,1536]{1,0:T(8,128)(2,1)S(1)} collective-permute-done((bf16[96,1536]{1,0:T(8,128)(2,1)}, bf16[96,1536]{1,0:T(8,128)(2,1)S(1)}, u32[]{:S(2)}, u32[]{:S(2)}) %collective-permute-start.18) | collective-permute-done | bytes 294944 | tf_op jit(solution)/shard_map/ppermute | solution.py:597
  109.1 13.3 %collective-permute-done.21.refs_6_ = bf16[96,1536]{1,0:T(8,128)(2,1)S(1)} collective-permute-done((bf16[96,1536]{1,0:T(8,128)(2,1)S(1)}, bf16[96,1536]{1,0:T(8,128)(2,1)S(1)}, u32[]{:S(2)}, u32[]{:S(2)}) %collective-permute-start.21) | collective-permute-done | bytes 294944 | tf_op jit(solution)/shard_map/ppermute | solution.py:597
  123.1 5.7 collective-permute-done.13.left_ref.refs_2_
  137.9 2.7 assemble.2
  140.7 3.4 project.4.qkv_ref
  144.2 5.0 project.5.qkv_ref
  149.2 4.3 attend.4
  153.6 5.1 attend.5
  158.7 3.4 project.6.qkv_ref
  162.1 4.3 attend.6
  172.1 4.7 collective-permute-done.23.left_ref.refs_3_
  176.7 3.6 project.7.qkv_ref
  180.4 4.3 attend.7
  188.0 6.8 %interleave.1 = bf16[1536,1536]{1,0:T(8,128)(2,1)} custom-call(s32[1]{0:T(128)} %bitcast.11.core_ref, bf16[768,1536]{1,0:T(8,128)(2,1)} %bitcast.55, bf16[768,1536]{1,0:T(8,128)(2,1)} %collective-permute-done.29.other_ref), custom_call_target="tpu_custom_call" | custom-call | bytes 9437184 | tf_op jit(solution)/shard_map/interleave/pallas_call | solution.py:466
  199.6 4.0 convert_add_fusion
  207.4 5.0 loss_gradients.1
  217.1 25.1 %collective-permute-done.32.refs_2_ = bf16[512,1536]{1,0:T(8,128)(2,1)S(1)} collective-permute-done((bf16[512,1536]{1,0:T(8,128)(2,1)S(1)}, bf16[512,1536]{1,0:T(8,128)(2,1)S(1)}, u32[]{:S(2)}, u32[]{:S(2)}) %collective-permute-start.32) | collective-permute-done | bytes 1572896 | tf_op jit(solution)/shard_map/ppermute | solution.py:589
  245.8 19.2 %raise_up.1 = (bf16[512,1024]{1,0:T(8,128)(2,1)}, bf16[512,1024]{1,0:T(8,128)(2,1)}, bf16[512,1024]{1,0:T(8,128)(2,1)}, bf16[512,1024]{1,0:T(8,128)(2,1)}, f32[5...) custom-call(bf16[512,1536]{1,0:T(8,128)(2,1)} %copy-done.103, ...), custom_call_target="tpu_custom_call" | custom-call | bytes 786432 | tf_op jit(solution)/shard_map/raise_up/pallas_call | solution.py:371
  265.0 16.1 %raise_back.1 = (bf16[512,1024]{1,0:T(8,128)(2,1)}, bf16[512,1024]{1,0:T(8,128)(2,1)}, bf16[512,1024]{1,0:T(8,128)(2,1)}, bf16[512,1024]{1,0:T(8,128)(2,1)}, bf1...) custom-call(bf16[512,1536]{1,0:T(8,128)(2,1)} %copy-done.22, ...), custom_call_target="tpu_custom_call" | custom-call | bytes 786432 | tf_op jit(solution)/shard_map/raise_back/pallas_call | solution.py:405
  281.1 11.6 %weight_product.5 = bf16[1536,1024]{1,0:T(8,128)(2,1)} custom-call(bf16[512,1536]{1,0:T(8,128)(2,1)} %copy-done.22, bf16[512,1536]{1,0:T(8,128)(2,1)} %copy-done.23, bf16[512,1536]{1,0:T(8,128)(2,1)} %copy-done.24, bf16[512,1536]{1,0:T(8,128)(2,1)} %copy-done.25, bf16[512,1024]{1,0:T(8,128)(2,1)} %get-tuple-element.822.refs_4_.refs_0_, ...), custom_call_target="tpu_custom_call" | custom-call | flops 100663296 | bytes 163840 | tf_op jit(solution)/shard_map/weight_product/pallas_call | solution.py:317
  294.2 3.7 copy-done
  297.9 4.4 back_product.12
  302.5 4.4 back_product.13
  307.3 6.7 %back_product.14 = bf16[512,1536]{1,0:T(8,128)(2,1)} custom-call(bf16[512,1024]{1,0:T(8,128)(2,1)S(1)} %copy-done.41, bf16[512,1024]{1,0:T(8,128)(2,1)S(1)} %copy-done.37, bf16[1536,3072]{1,0:T(8,128)(2,1)} %all-gather.2.cloned.1.call-done.refs_4_.refs_5_.refs_2_.refs_3_.refs_1_, ...), custom_call_target="tpu_custom_call" | custom-call | flops 100663296 | bytes 262144 | tf_op jit(solution)/shard_map/back_product/pallas_call | solution.py:283
  316.9 11.1 %weight_product.6.refs_8_ = bf16[1536,2048]{1,0:T(8,128)(2,1)} custom-call(bf16[512,1536]{1,0:T(8,128)(2,1)} %copy-done.103, bf16[512,1536]{1,0:T(8,128)(2,1)} %copy-done.105, bf16[512,1536]{1,0:T(8,128)(2,1)} %copy-done.104, bf16[512,1536]{1,0:T(8,128)(2,1)} %collective-permute-done.35.refs_3_, bf16[512,1024]{1,0:T(8,128)(2,1)} %get-tuple-element.740.refs_4_.refs_0_, ...), custom_call_target="tpu_custom_call" | custom-call | flops 100663296 | bytes 163840 | tf_op jit(solution)/shard_map/weight_product/pallas_call | solution.py:317
  331.9 5.8 back_product.15
  337.8 11.2 %weight_product.7 = bf16[1536,2048]{1,0:T(8,128)(2,1)} custom-call(bf16[512,1536]{1,0:T(8,128)(2,1)} %copy-done.103, bf16[512,1536]{1,0:T(8,128)(2,1)} %copy-done.105, bf16[512,1536]{1,0:T(8,128)(2,1)} %copy-done.104, bf16[512,1536]{1,0:T(8,128)(2,1)} %collective-permute-done.35.refs_3_, ...), custom_call_target="tpu_custom_call", output_to_operand_aliasing={{}: (8, {})} | custom-call | flops 100663296 | bytes 163840 | tf_op jit(solution)/shard_map/weight_product/pallas_call | solution.py:317
  349.0 3.7 copy-done.1
  362.3 3.4 multiply_reduce_fusion.1
  366.4 2.8 fusion.12
  376.1 11.7 %attend_back.4 = (bf16[512,1152]{1,0:T(8,128)(2,1)S(1)}, f32[8,128]{1,0:T(8,128)S(1)}) custom-call(f32[1]{0:T(128)} %bitcast.1.lam_ref, bf16[512,1152]{1,0:T(8,128)(2,1)S(1)} %copy-done.20, f32[8,128]{1,0:T(8,128)S(1)} %pad_maximum_fusion.5.marks_ref.refs_4_, f32[1,128]{1,0:T(1,128)S(1)} %copy-done.87, bf16[512,384]{1,0:T(8,128)(2,1)S(1)} %get-tuple-element.772.grad_ref), custom_call_target="tpu_custom_call" | custom-call | bytes 196608 | tf_op jit(solution)/shard_map/attend_back/pallas_call | solution.py:181
  388.9 12.0 %attend_back.5 = (bf16[512,1152]{1,0:T(8,128)(2,1)S(1)}, f32[8,128]{1,0:T(8,128)S(1)}) custom-call(f32[1]{0:T(128)} %bitcast.1.lam_ref, bf16[512,1152]{1,0:T(8,128)(2,1)S(1)} %copy-done.18, f32[8,128]{1,0:T(8,128)S(1)} %collective-permute-done.12.marks_ref.refs_5_, f32[1,128]{1,0:T(1,128)S(1)} %copy-done.87, ...), custom_call_target="tpu_custom_call" | custom-call | bytes 196608 | tf_op jit(solution)/shard_map/attend_back/pallas_call | solution.py:181
  404.2 11.9 %attend_back.6 = (bf16[512,1152]{1,0:T(8,128)(2,1)S(1)}, f32[8,128]{1,0:T(8,128)S(1)}) custom-call(f32[1]{0:T(128)} %bitcast.1.lam_ref, bf16[512,1152]{1,0:T(8,128)(2,1)S(1)} %copy-done.14, f32[16,128]{1,0:T(8,128)S(1)} %collective-permute-done.25.marks_ref.refs_6_.refs_7_, f32[1,128]{1,0:T(1,128)S(1)} %copy-done.87, ...), custom_call_target="tpu_custom_call" | custom-call | bytes 196608 | tf_op jit(solution)/shard_map/attend_back/pallas_call | solution.py:181
  417.1 4.9 collective-permute-done.49.refs_7_
  422.1 3.4 back_product.18
  425.6 11.7 %attend_back.7 = (bf16[512,1152]{1,0:T(8,128)(2,1)S(1)}, f32[8,128]{1,0:T(8,128)S(1)}) custom-call(f32[1]{0:T(128)} %bitcast.1.lam_ref, bf16[512,1152]{1,0:T(8,128)(2,1)S(1)} %copy-done.16, f32[16,128]{1,0:T(8,128)S(1)} %collective-permute-done.25.marks_ref.refs_6_.refs_7_, f32[1,128]{1,0:T(1,128)S(1)} %copy-done.87, ...), custom_call_target="tpu_custom_call" | custom-call | bytes 196608 | tf_op jit(solution)/shard_map/attend_back/pallas_call | solution.py:181
  439.0 7.4 %weight_product.8.refs_8_ = bf16[1536,1536]{1,0:T(8,128)(2,1)} custom-call(bf16[512,1536]{1,0:T(8,128)(2,1)} %pad_maximum_fusion.1.refs_0_, bf16[512,1536]{1,0:T(8,128)(2,1)} %copy-done.110, bf16[512,1536]{1,0:T(8,128)(2,1)} %collective-permute-done.37.refs_2_, bf16[512,1536]{1,0:T(8,128)(2,1)} %copy-done.109, bf16[512,384]{1,0:T(8,128)(2,1)} %get-tuple-element.1005.refs_4_, ...), custom_call_target="tpu_custom_call" | custom-call | flops 37748736 | bytes 122880 | tf_op jit(solution)/shard_map/weight_product/pallas_call | solution.py:317
  446.4 4.1 back_product.19
  452.1 13.2 %weight_product.9 = bf16[1536,1536]{1,0:T(8,128)(2,1)} custom-call(bf16[512,1536]{1,0:T(8,128)(2,1)} %copy-done.11, bf16[512,1536]{1,0:T(8,128)(2,1)} %collective-permute-done.27.left_ref.refs_1_, bf16[512,1536]{1,0:T(8,128)(2,1)} %copy-done.26, bf16[512,1536]{1,0:T(8,128)(2,1)} %copy-done.28, ...), custom_call_target="tpu_custom_call", output_to_operand_aliasing={{}: (8, {})} | custom-call | flops 113246208 | bytes 172032 | tf_op jit(solution)/shard_map/weight_product/pallas_call | solution.py:317
  465.4 5.5 add_convert_fusion
  470.9 3.5 back_product.20
  474.9 3.5 back_product.21
  483.3 4.8 back_product.22
  488.1 4.2 back_product.23
  494.8 14.7 %collective-permute-done.55.refs_2_ = bf16[96,3072]{1,0:T(8,128)(2,1)S(1)} collective-permute-done((bf16[96,3072]{1,0:T(8,128)(2,1)S(1)}, bf16[96,3072]{1,0:T(8,128)(2,1)S(1)}, u32[]{:S(2)}, u32[]{:S(2)}) %collective-permute-start.55) | collective-permute-done | bytes 589856 | tf_op jit(solution)/shard_map/ppermute | solution.py:589
  520.7 6.7 %merge.2 = (f32[96,12288]{1,0:T(8,128)}, f32[96,12288]{1,0:T(8,128)S(1)}, f32[8,96]{1,0:T(8,128)S(1)}) custom-call(s32[1]{0:T(128)} %bitcast.member_ref, bf16[96,3072]{1,0:T(8,128)(2,1)S(1)} %copy-done.49, bf16[96,3072]{1,0:T(8,128)(2,1)S(1)} %copy-done.69, bf16[96,3072]{1,0:T(8,128)(2,1)S(1)} %copy-done.67, bf16[96,3072]{1,0:T(8,128)(2,1)S(1)} %copy-done.65, ...), custom_call_target="tpu_custom_call" | custom-call | bytes 1179648 | tf_op jit(solution)/shard_map/merge/pallas_call | solution.py:502
  527.5 3.5 collective-permute-done.58.other_ref
  531.0 4.2 right_factor.2
  535.2 5.7 collective-permute-done.59.other_ref
  546.4 8.0 %update.2 = (f32[8,12288]{1,0:T(8,128)}, f32[96,12288]{1,0:T(8,128)}, f32[96,12288]{1,0:T(8,128)}, f32[96,12288]{1,0:T(8,128)}) custom-call(f32[8,96]{1,0:T(8,128)S(1)} %copy-done.93, bf16[8,12288]{1,0:T(8,128)(2,1)S(1)} %get-tuple-element.899.own_ref, bf16[8,12288]{1,0:T(8,128)(2,1)S(1)} %collective-permute-done.59.other_ref, f32[96,12288]{1,0:T(8,128)S(1)} %copy-done.10, ...), custom_call_target="tpu_custom_call" | custom-call | bytes 1179648 | tf_op jit(solution)/shard_map/update/pallas_call | solution.py:572
  557.1 4.0 reduce-scatter.8.cloned.1.call-done
  571.0 2.9 collective-permute-start.63
  575.6 4.1 collective-permute-done.65.refs_2_
  579.7 4.4 merge.3
  585.8 3.0 collective-permute-done.68.other_ref
  588.8 2.9 right_factor.3
  592.4 4.3 fusion.8
  596.7 4.8 update.3
  (460 shorter events, 158.1 us)
Async XLA Ops:
  7.2 238.6 %all-gather.2.cloned.1.call-start = ((), (), s32[]{:S(2)}) async-start(), calls=%async_computation.3 | async-start | bytes 10616832 | tf_op jit(solution)/shard_map/all_gather | solution.py:757
  13.8 6.2 %collective-permute-start.3 = (f32[8,128]{1,0:T(8,128)S(1)}, f32[8,128]{1,0:T(8,128)S(1)}, u32[]{:S(2)}, u32[]{:S(2)}) collective-permute-start(f32[8,128]{1,0:T(8,128)S(1)} %broadcast_add_fusion), channel_id=1, source_target_pairs={{0,4},{4,0},{8,12},{12,8},{1,5},{5,1},{9,13},{13,9},{2,6},{6,2},{1... | collective-permute-start | bytes 12296 | tf_op jit(solution)/shard_map/ppermute | solution.py:593
  18.1 12.5 %collective-permute-start = (bf16[96,1152]{1,0:T(8,128)(2,1)S(1)}, bf16[96,1152]{1,0:T(8,128)(2,1)S(1)}, u32[]{:S(2)}, u32[]{:S(2)}) collective-permute-start(bf16[96,1152]{1,0:T(8,128)(2,1)S(1)} %get-tuple-element.500), channel_id=1, source_target_pairs={{0,3},{1,2},{2,1},{3,0},{4,7},{5,6},{6,5},{7,4},{8,11},{9,10},{10,... | collective-permute-start | bytes 663560 | tf_op jit(solution)/shard_map/ppermute | solution.py:589
  18.2 12.5 %collective-permute-start.1 = (bf16[96,1152]{1,0:T(8,128)(2,1)S(1)}, bf16[96,1152]{1,0:T(8,128)(2,1)S(1)}, u32[]{:S(2)}, u32[]{:S(2)}) collective-permute-start(bf16[96,1152]{1,0:T(8,128)(2,1)S(1)} %get-tuple-element.501), channel_id=1, source_target_pairs={{0,2},{1,3},{2,0},{3,1},{4,6},{5,7},{6,4},{7,5},{8,10},{9,11},{10,... | collective-permute-start | bytes 663560 | tf_op jit(solution)/shard_map/ppermute | solution.py:589
  19.8 10.9 %collective-permute-start.5 = (bf16[96,1152]{1,0:T(8,128)(2,1)S(1)}, bf16[96,1152]{1,0:T(8,128)(2,1)S(1)}, u32[]{:S(2)}, u32[]{:S(2)}) collective-permute-start(bf16[96,1152]{1,0:T(8,128)(2,1)S(1)} %get-tuple-element.510), channel_id=1, source_target_pairs={{0,1},{1,0},{2,3},{3,2},{4,5},{5,4},{6,7},{7,6},{8,9},{9,8},{10,11... | collective-permute-start | bytes 663560 | tf_op jit(solution)/shard_map/ppermute | solution.py:589
  31.8 13.9 %collective-permute-start.6 = (bf16[192,1152]{1,0:T(8,128)(2,1)S(1)}, bf16[192,1152]{1,0:T(8,128)(2,1)S(1)}, u32[]{:S(2)}, u32[]{:S(2)}) collective-permute-start(bf16[192,1152]{1,0:T(8,128)(2,1)S(1)} %get-tuple-element.515), channel_id=1, source_target_pairs={{0,4},{4,8},{8,12},{12,0},{1,5},{5,9},{9,13},{13,1},{2,6},{6,10},{... | collective-permute-start | bytes 1327112 | tf_op jit(solution)/shard_map/ppermute | solution.py:597
  36.9 38.0 %collective-permute-start.7 = (bf16[96,3072]{1,0:T(8,128)(2,1)}, bf16[96,3072]{1,0:T(8,128)(2,1)}, u32[]{:S(2)}, u32[]{:S(2)}) collective-permute-start(bf16[96,3072]{1,0:T(8,128)(2,1)} %get-tuple-element.530), channel_id=1, source_target_pairs={{0,1},{1,0},{2,3},{3,2},{4,5},{5,4},{6,7},{7,6},{8,9},{9,8},{10,11... | collective-permute-start | bytes 1769480 | tf_op jit(solution)/shard_map/ppermute | solution.py:589
  36.9 37.9 %collective-permute-start.8 = (bf16[96,3072]{1,0:T(8,128)(2,1)}, bf16[96,3072]{1,0:T(8,128)(2,1)}, u32[]{:S(2)}, u32[]{:S(2)}) collective-permute-start(bf16[96,3072]{1,0:T(8,128)(2,1)} %get-tuple-element.531), channel_id=1, source_target_pairs={{0,3},{1,2},{2,1},{3,0},{4,7},{5,6},{6,5},{7,4},{8,11},{9,10},{10,... | collective-permute-start | bytes 1769480 | tf_op jit(solution)/shard_map/ppermute | solution.py:589
  37.0 36.1 %collective-permute-start.9 = (bf16[96,3072]{1,0:T(8,128)(2,1)}, bf16[96,3072]{1,0:T(8,128)(2,1)}, u32[]{:S(2)}, u32[]{:S(2)}) collective-permute-start(bf16[96,3072]{1,0:T(8,128)(2,1)} %get-tuple-element.532), channel_id=1, source_target_pairs={{0,2},{1,3},{2,0},{3,1},{4,6},{5,7},{6,4},{7,5},{8,10},{9,11},{10,... | collective-permute-start | bytes 1769480 | tf_op jit(solution)/shard_map/ppermute | solution.py:589
  46.1 13.1 %collective-permute-start.10 = (bf16[192,1152]{1,0:T(8,128)(2,1)S(1)}, bf16[192,1152]{1,0:T(8,128)(2,1)S(1)}, u32[]{:S(2)}, u32[]{:S(2)}) collective-permute-start(bf16[192,1152]{1,0:T(8,128)(2,1)S(1)} %collective-permute-done.6.refs_2_), channel_id=1, source_target_pairs={{0,4},{4,8},{8,12},{12,0},{1,5},{5,9},{9,13},{13,1},{2,6},{6,10},{... | collective-permute-start | bytes 1327112 | tf_op jit(solution)/shard_map/ppermute | solution.py:597
  59.3 12.2 %collective-permute-start.11 = (bf16[192,1152]{1,0:T(8,128)(2,1)S(1)}, bf16[192,1152]{1,0:T(8,128)(2,1)}, u32[]{:S(2)}, u32[]{:S(2)}) collective-permute-start(bf16[192,1152]{1,0:T(8,128)(2,1)S(1)} %collective-permute-done.10.refs_4_), channel_id=1, source_target_pairs={{0,4},{4,8},{8,12},{12,0},{1,5},{5,9},{9,13},{13,1},{2,6},{6,10},{... | collective-permute-start | bytes 1327112 | tf_op jit(solution)/shard_map/ppermute | solution.py:597
  61.2 22.0 %collective-permute-start.17 = (bf16[192,1152]{1,0:T(8,128)(2,1)S(1)}, bf16[192,1152]{1,0:T(8,128)(2,1)}, u32[]{:S(2)}, u32[]{:S(2)}) collective-permute-start(bf16[192,1152]{1,0:T(8,128)(2,1)S(1)} %collective-permute-done.6.refs_2_), channel_id=1, source_target_pairs={{0,16},{16,0},{1,17},{17,1},{2,18},{18,2},{3,19},{19,3},{4,20},{20... | collective-permute-start | bytes 1327112 | tf_op jit(solution)/shard_map/ppermute | solution.py:601
  71.5 13.2 %collective-permute-start.16 = (bf16[192,1152]{1,0:T(8,128)(2,1)S(1)}, bf16[192,1152]{1,0:T(8,128)(2,1)}, u32[]{:S(2)}, u32[]{:S(2)}) collective-permute-start(bf16[192,1152]{1,0:T(8,128)(2,1)S(1)} %collective-permute-done.10.refs_4_), channel_id=1, source_target_pairs={{0,16},{16,0},{1,17},{17,1},{2,18},{18,2},{3,19},{19,3},{4,20},{20... | collective-permute-start | bytes 1327112 | tf_op jit(solution)/shard_map/ppermute | solution.py:601
  73.0 7.0 %collective-permute-start.14 = (bf16[96,1536]{1,0:T(8,128)(2,1)}, bf16[96,1536]{1,0:T(8,128)(2,1)S(1)}, u32[]{:S(2)}, u32[]{:S(2)}) collective-permute-start(bf16[96,1536]{1,0:T(8,128)(2,1)} %slice.297), channel_id=1, source_target_pairs={{0,2},{1,3},{2,0},{3,1},{4,6},{5,7},{6,4},{7,5},{8,10},{9,11},{10,... | collective-permute-start | bytes 884744 | tf_op jit(solution)/shard_map/ppermute | solution.py:589
  80.8 12.0 %collective-permute-start.19 = (bf16[192,1152]{1,0:T(8,128)(2,1)}, bf16[192,1152]{1,0:T(8,128)(2,1)S(1)}, u32[]{:S(2)}, u32[]{:S(2)}) collective-permute-start(bf16[192,1152]{1,0:T(8,128)(2,1)} %collective-permute-done.11.refs_6_), channel_id=1, source_target_pairs={{0,16},{16,0},{1,17},{17,1},{2,18},{18,2},{3,19},{19,3},{4,20},{20... | collective-permute-start | bytes 1327112 | tf_op jit(solution)/shard_map/ppermute | solution.py:601
  83.2 8.6 %collective-permute-start.15 = (bf16[96,1536]{1,0:T(8,128)(2,1)S(1)}, bf16[96,1536]{1,0:T(8,128)(2,1)}, u32[]{:S(2)}, u32[]{:S(2)}) collective-permute-start(bf16[96,1536]{1,0:T(8,128)(2,1)S(1)} %get-tuple-element.557), channel_id=1, source_target_pairs={{0,4},{4,8},{8,12},{12,0},{1,5},{5,9},{9,13},{13,1},{2,6},{6,10},{... | collective-permute-start | bytes 884744 | tf_op jit(solution)/shard_map/ppermute | solution.py:597
  93.5 267.8 %reduce-scatter.4.cloned.1.call-start = ((), (), s32[]{:S(2)}) async-start(), calls=%async_computation.4 | async-start | bytes 3932160 | tf_op jit(solution)/shard_map/reduce_scatter | solution.py:605
  93.5 35.3 %collective-permute-start.13 = (bf16[512,1536]{1,0:T(8,128)(2,1)S(1)}, bf16[512,1536]{1,0:T(8,128)(2,1)S(1)}, u32[]{:S(2)}, u32[]{:S(2)}) collective-permute-start(bf16[512,1536]{1,0:T(8,128)(2,1)S(1)} %fusion.4.left_ref.refs_0_), channel_id=1, source_target_pairs={{0,2},{1,3},{2,0},{3,1},{4,6},{5,7},{6,4},{7,5},{8,10},{9,11},{10,... | collective-permute-start | bytes 4718600 | tf_op jit(solution)/shard_map/ppermute | solution.py:589
  94.6 10.6 %collective-permute-start.18 = (bf16[96,1536]{1,0:T(8,128)(2,1)}, bf16[96,1536]{1,0:T(8,128)(2,1)S(1)}, u32[]{:S(2)}, u32[]{:S(2)}) collective-permute-start(bf16[96,1536]{1,0:T(8,128)(2,1)} %collective-permute-done.15.refs_2_), channel_id=1, source_target_pairs={{0,4},{4,8},{8,12},{12,0},{1,5},{5,9},{9,13},{13,1},{2,6},{6,10},{... | collective-permute-start | bytes 884744 | tf_op jit(solution)/shard_map/ppermute | solution.py:597
  94.6 13.8 %collective-permute-start.22 = (bf16[96,1536]{1,0:T(8,128)(2,1)}, bf16[96,1536]{1,0:T(8,128)(2,1)S(1)}, u32[]{:S(2)}, u32[]{:S(2)}) collective-permute-start(bf16[96,1536]{1,0:T(8,128)(2,1)} %collective-permute-done.15.refs_2_), channel_id=1, source_target_pairs={{0,16},{16,0},{1,17},{17,1},{2,18},{18,2},{3,19},{19,3},{4,20},{20... | collective-permute-start | bytes 884744 | tf_op jit(solution)/shard_map/ppermute | solution.py:601
  105.2 17.2 %collective-permute-start.21 = (bf16[96,1536]{1,0:T(8,128)(2,1)S(1)}, bf16[96,1536]{1,0:T(8,128)(2,1)S(1)}, u32[]{:S(2)}, u32[]{:S(2)}) collective-permute-start(bf16[96,1536]{1,0:T(8,128)(2,1)S(1)} %collective-permute-done.18.refs_4_), channel_id=1, source_target_pairs={{0,4},{4,8},{8,12},{12,0},{1,5},{5,9},{9,13},{13,1},{2,6},{6,10},{... | collective-permute-start | bytes 884744 | tf_op jit(solution)/shard_map/ppermute | solution.py:597
  105.2 17.2 %collective-permute-start.20 = (bf16[96,1536]{1,0:T(8,128)(2,1)S(1)}, bf16[96,1536]{1,0:T(8,128)(2,1)S(1)}, u32[]{:S(2)}, u32[]{:S(2)}) collective-permute-start(bf16[96,1536]{1,0:T(8,128)(2,1)S(1)} %collective-permute-done.18.refs_4_), channel_id=1, source_target_pairs={{0,16},{16,0},{1,17},{17,1},{2,18},{18,2},{3,19},{19,3},{4,20},{20... | collective-permute-start | bytes 884744 | tf_op jit(solution)/shard_map/ppermute | solution.py:601
  107.4 21.5 %collective-permute-start.25 = (f32[16,128]{1,0:T(8,128)S(1)}, f32[16,128]{1,0:T(8,128)S(1)}, u32[]{:S(2)}, u32[]{:S(2)}) collective-permute-start(f32[16,128]{1,0:T(8,128)S(1)} %pad_maximum_fusion.4), channel_id=1, source_target_pairs={{0,2},{1,3},{2,0},{3,1},{4,6},{5,7},{6,4},{7,5},{8,10},{9,11},{10,... | collective-permute-start | bytes 24584 | tf_op jit(solution)/shard_map/ppermute | solution.py:589
  109.1 31.6 %collective-permute-start.27 = (bf16[512,1536]{1,0:T(8,128)(2,1)S(1)}, bf16[512,1536]{1,0:T(8,128)(2,1)}, u32[]{:S(2)}, u32[]{:S(2)}) collective-permute-start(bf16[512,1536]{1,0:T(8,128)(2,1)S(1)} %fusion.4.left_ref.refs_0_), channel_id=1, source_target_pairs={{0,1},{1,0},{2,3},{3,2},{4,5},{5,4},{6,7},{7,6},{8,9},{9,8},{10,11... | collective-permute-start | bytes 4718600 | tf_op jit(solution)/shard_map/ppermute | solution.py:589
  128.9 38.6 %collective-permute-start.26 = (bf16[512,1536]{1,0:T(8,128)(2,1)}, bf16[512,1536]{1,0:T(8,128)(2,1)}, u32[]{:S(2)}, u32[]{:S(2)}) collective-permute-start(bf16[512,1536]{1,0:T(8,128)(2,1)} %refs_0_.3), channel_id=1, source_target_pairs={{0,2},{1,3},{2,0},{3,1},{4,6},{5,7},{6,4},{7,5},{8,10},{9,11},{10,... | collective-permute-start | bytes 4718600 | tf_op jit(solution)/shard_map/ppermute | solution.py:589
  131.3 36.2 %collective-permute-start.24 = (bf16[96,1536]{1,0:T(8,128)(2,1)}, bf16[96,1536]{1,0:T(8,128)(2,1)S(1)}, u32[]{:S(2)}, u32[]{:S(2)}) collective-permute-start(bf16[96,1536]{1,0:T(8,128)(2,1)} %copy-done.81), channel_id=1, source_target_pairs={{0,16},{16,0},{1,17},{17,1},{2,18},{18,2},{3,19},{19,3},{4,20},{20... | collective-permute-start | bytes 884744 | tf_op jit(solution)/shard_map/ppermute | solution.py:601
  169.7 18.3 %collective-permute-start.29 = (bf16[768,1536]{1,0:T(8,128)(2,1)S(1)}, bf16[768,1536]{1,0:T(8,128)(2,1)}, u32[]{:S(2)}, u32[]{:S(2)}) collective-permute-start(bf16[768,1536]{1,0:T(8,128)(2,1)S(1)} %bitcast.54), channel_id=1, source_target_pairs={{0,1},{1,0},{2,3},{3,2},{4,5},{5,4},{6,7},{7,6},{8,9},{9,8},{10,11... | collective-permute-start | bytes 7077896 | tf_op jit(solution)/shard_map/ppermute | solution.py:589
  169.8 7.0 %collective-permute-start.23 = (bf16[512,1536]{1,0:T(8,128)(2,1)S(1)}, bf16[512,1536]{1,0:T(8,128)(2,1)S(1)}, u32[]{:S(2)}, u32[]{:S(2)}) collective-permute-start(bf16[512,1536]{1,0:T(8,128)(2,1)S(1)} %copy-done.27), channel_id=1, source_target_pairs={{0,1},{1,0},{2,3},{3,2},{4,5},{5,4},{6,7},{7,6},{8,9},{9,8},{10,11... | collective-permute-start | bytes 4718600 | tf_op jit(solution)/shard_map/ppermute | solution.py:589
  170.3 17.2 %collective-permute-start.31 = (bf16[512,384]{1,0:T(8,128)(2,1)}, bf16[512,384]{1,0:T(8,128)(2,1)}, u32[]{:S(2)}, u32[]{:S(2)}) collective-permute-start(bf16[512,384]{1,0:T(8,128)(2,1)} %attend.5), channel_id=1, source_target_pairs={{0,1},{1,0},{2,3},{3,2},{4,5},{5,4},{6,7},{7,6},{8,9},{9,8},{10,11... | collective-permute-start | bytes 1179656 | tf_op jit(solution)/shard_map/ppermute | solution.py:589
  170.4 17.2 %collective-permute-start.30 = (bf16[512,384]{1,0:T(8,128)(2,1)S(1)}, bf16[512,384]{1,0:T(8,128)(2,1)}, u32[]{:S(2)}, u32[]{:S(2)}) collective-permute-start(bf16[512,384]{1,0:T(8,128)(2,1)S(1)} %attend.6), channel_id=1, source_target_pairs={{0,2},{1,3},{2,0},{3,1},{4,6},{5,7},{6,4},{7,5},{8,10},{9,11},{10,... | collective-permute-start | bytes 1179656 | tf_op jit(solution)/shard_map/ppermute | solution.py:589
  185.8 11.1 %collective-permute-start.28 = (bf16[512,384]{1,0:T(8,128)(2,1)S(1)}, bf16[512,384]{1,0:T(8,128)(2,1)}, u32[]{:S(2)}, u32[]{:S(2)}) collective-permute-start(bf16[512,384]{1,0:T(8,128)(2,1)S(1)} %attend.7), channel_id=1, source_target_pairs={{0,3},{1,2},{2,1},{3,0},{4,7},{5,6},{6,5},{7,4},{8,11},{9,10},{10,... | collective-permute-start | bytes 1179656 | tf_op jit(solution)/shard_map/ppermute | solution.py:589
  187.5 19.9 %collective-permute-start.33 = (bf16[512,1536]{1,0:T(8,128)(2,1)}, bf16[512,1536]{1,0:T(8,128)(2,1)}, u32[]{:S(2)}, u32[]{:S(2)}) collective-permute-start(bf16[512,1536]{1,0:T(8,128)(2,1)} %collective-permute-done.26.refs_2_), channel_id=1, source_target_pairs={{0,1},{1,0},{2,3},{3,2},{4,5},{5,4},{6,7},{7,6},{8,9},{9,8},{10,11... | collective-permute-start | bytes 4718600 | tf_op jit(solution)/shard_map/ppermute | solution.py:589
  187.7 19.7 %collective-permute-start.34 = (bf16[512,1536]{1,0:T(8,128)(2,1)}, bf16[512,1536]{1,0:T(8,128)(2,1)}, u32[]{:S(2)}, u32[]{:S(2)}) collective-permute-start(bf16[512,1536]{1,0:T(8,128)(2,1)} %refs_0_.3), channel_id=1, source_target_pairs={{0,1},{1,0},{2,3},{3,2},{4,5},{5,4},{6,7},{7,6},{8,9},{9,8},{10,11... | collective-permute-start | bytes 4718600 | tf_op jit(solution)/shard_map/ppermute | solution.py:589
  205.4 36.9 %collective-permute-start.32 = (bf16[512,1536]{1,0:T(8,128)(2,1)S(1)}, bf16[512,1536]{1,0:T(8,128)(2,1)S(1)}, u32[]{:S(2)}, u32[]{:S(2)}) collective-permute-start(bf16[512,1536]{1,0:T(8,128)(2,1)S(1)} %multiply_convert_fusion.refs_0_), channel_id=1, source_target_pairs={{0,2},{1,3},{2,0},{3,1},{4,6},{5,7},{6,4},{7,5},{8,10},{9,11},{10,... | collective-permute-start | bytes 4718600 | tf_op jit(solution)/shard_map/ppermute | solution.py:589
  207.1 36.9 %collective-permute-start.36 = (bf16[512,1536]{1,0:T(8,128)(2,1)S(1)}, bf16[512,1536]{1,0:T(8,128)(2,1)S(1)}, u32[]{:S(2)}, u32[]{:S(2)}) collective-permute-start(bf16[512,1536]{1,0:T(8,128)(2,1)S(1)} %multiply_convert_fusion.refs_0_), channel_id=1, source_target_pairs={{0,1},{1,0},{2,3},{3,2},{4,5},{5,4},{6,7},{7,6},{8,9},{9,8},{10,11... | collective-permute-start | bytes 4718600 | tf_op jit(solution)/shard_map/ppermute | solution.py:589
  242.3 38.8 %collective-permute-start.37 = (bf16[512,1536]{1,0:T(8,128)(2,1)}, bf16[512,1536]{1,0:T(8,128)(2,1)}, u32[]{:S(2)}, u32[]{:S(2)}) collective-permute-start(bf16[512,1536]{1,0:T(8,128)(2,1)} %pad_maximum_fusion.1.refs_0_), channel_id=1, source_target_pairs={{0,2},{1,3},{2,0},{3,1},{4,6},{5,7},{6,4},{7,5},{8,10},{9,11},{10,... | collective-permute-start | bytes 4718600 | tf_op jit(solution)/shard_map/ppermute | solution.py:589
  292.7 185.7 %reduce-scatter.6.cloned.1.call-start = ((), (), s32[]{:S(2)}) async-start(), calls=%async_computation.5 | async-start | bytes 7864320 | tf_op jit(solution)/shard_map/reduce_scatter | solution.py:605
  302.3 5.0 collective-permute-start.39
  306.9 8.9 %collective-permute-start.38 = (bf16[512,1536]{1,0:T(8,128)(2,1)S(1)}, bf16[512,1536]{1,0:T(8,128)(2,1)S(1)}, u32[]{:S(2)}, u32[]{:S(2)}) collective-permute-start(bf16[512,1536]{1,0:T(8,128)(2,1)S(1)} %back_product.13), channel_id=1, source_target_pairs={{0,1},{1,0},{2,3},{3,2},{4,5},{5,4},{6,7},{7,6},{8,9},{9,8},{10,11... | collective-permute-start | bytes 4718600 | tf_op jit(solution)/shard_map/ppermute | solution.py:589
  314.0 47.3 %collective-permute-start.40 = (bf16[512,1536]{1,0:T(8,128)(2,1)}, bf16[512,1536]{1,0:T(8,128)(2,1)}, u32[]{:S(2)}, u32[]{:S(2)}) collective-permute-start(bf16[512,1536]{1,0:T(8,128)(2,1)} %back_product.14), channel_id=1, source_target_pairs={{0,2},{1,3},{2,0},{3,1},{4,6},{5,7},{6,4},{7,5},{8,10},{9,11},{10,... | collective-permute-start | bytes 4718600 | tf_op jit(solution)/shard_map/ppermute | solution.py:589
  361.4 199.7 %reduce-scatter.8.cloned.1.call-start = ((), (), s32[]{:S(2)}) async-start(), calls=%async_computation.6 | async-start | bytes 5898240 | tf_op jit(solution)/shard_map/reduce_scatter | solution.py:605
  361.6 11.8 %collective-permute-start.46 = (bf16[512,1536]{1,0:T(8,128)(2,1)}, bf16[512,1536]{1,0:T(8,128)(2,1)S(1)}, u32[]{:S(2)}, u32[]{:S(2)}) collective-permute-start(bf16[512,1536]{1,0:T(8,128)(2,1)} %collective-permute-done.37.refs_2_), channel_id=1, source_target_pairs={{0,1},{1,0},{2,3},{3,2},{4,5},{5,4},{6,7},{7,6},{8,9},{9,8},{10,11... | collective-permute-start | bytes 4718600 | tf_op jit(solution)/shard_map/ppermute | solution.py:589
  361.7 27.2 %collective-permute-start.44 = (bf16[512,1536]{1,0:T(8,128)(2,1)}, bf16[512,1536]{1,0:T(8,128)(2,1)S(1)}, u32[]{:S(2)}, u32[]{:S(2)}) collective-permute-start(bf16[512,1536]{1,0:T(8,128)(2,1)} %copy-done.57), channel_id=1, source_target_pairs={{0,1},{1,0},{2,3},{3,2},{4,5},{5,4},{6,7},{7,6},{8,9},{9,8},{10,11... | collective-permute-start | bytes 4718600 | tf_op jit(solution)/shard_map/ppermute | solution.py:589
  362.2 26.7 %collective-permute-start.45 = (bf16[512,1536]{1,0:T(8,128)(2,1)}, bf16[512,1536]{1,0:T(8,128)(2,1)S(1)}, u32[]{:S(2)}, u32[]{:S(2)}) collective-permute-start(bf16[512,1536]{1,0:T(8,128)(2,1)} %copy-done.58), channel_id=1, source_target_pairs={{0,1},{1,0},{2,3},{3,2},{4,5},{5,4},{6,7},{7,6},{8,9},{9,8},{10,11... | collective-permute-start | bytes 4718600 | tf_op jit(solution)/shard_map/ppermute | solution.py:589
  365.7 7.7 %collective-permute-start.47 = (bf16[512,1536]{1,0:T(8,128)(2,1)}, bf16[512,1536]{1,0:T(8,128)(2,1)S(1)}, u32[]{:S(2)}, u32[]{:S(2)}) collective-permute-start(bf16[512,1536]{1,0:T(8,128)(2,1)} %pad_maximum_fusion.1.refs_0_), channel_id=1, source_target_pairs={{0,1},{1,0},{2,3},{3,2},{4,5},{5,4},{6,7},{7,6},{8,9},{9,8},{10,11... | collective-permute-start | bytes 4718600 | tf_op jit(solution)/shard_map/ppermute | solution.py:589
  373.0 15.9 %collective-permute-start.43 = (bf16[512,384]{1,0:T(8,128)(2,1)}, bf16[512,384]{1,0:T(8,128)(2,1)S(1)}, u32[]{:S(2)}, u32[]{:S(2)}) collective-permute-start(bf16[512,384]{1,0:T(8,128)(2,1)} %get-tuple-element.1012), channel_id=1, source_target_pairs={{0,1},{1,0},{2,3},{3,2},{4,5},{5,4},{6,7},{7,6},{8,9},{9,8},{10,11... | collective-permute-start | bytes 1179656 | tf_op jit(solution)/shard_map/ppermute | solution.py:589
  373.4 28.7 %collective-permute-start.42 = (bf16[512,384]{1,0:T(8,128)(2,1)}, bf16[512,384]{1,0:T(8,128)(2,1)S(1)}, u32[]{:S(2)}, u32[]{:S(2)}) collective-permute-start(bf16[512,384]{1,0:T(8,128)(2,1)} %get-tuple-element.1011), channel_id=1, source_target_pairs={{0,2},{1,3},{2,0},{3,1},{4,6},{5,7},{6,4},{7,5},{8,10},{9,11},{10,... | collective-permute-start | bytes 1179656 | tf_op jit(solution)/shard_map/ppermute | solution.py:589
  373.4 28.6 %collective-permute-start.41 = (bf16[512,384]{1,0:T(8,128)(2,1)S(1)}, bf16[512,384]{1,0:T(8,128)(2,1)S(1)}, u32[]{:S(2)}, u32[]{:S(2)}) collective-permute-start(bf16[512,384]{1,0:T(8,128)(2,1)S(1)} %get-tuple-element.1010), channel_id=1, source_target_pairs={{0,3},{1,2},{2,1},{3,0},{4,7},{5,6},{6,5},{7,4},{8,11},{9,10},{10,... | collective-permute-start | bytes 1179656 | tf_op jit(solution)/shard_map/ppermute | solution.py:589
  402.1 15.1 %collective-permute-start.50 = (bf16[512,384]{1,0:T(8,128)(2,1)}, bf16[512,384]{1,0:T(8,128)(2,1)S(1)}, u32[]{:S(2)}, u32[]{:S(2)}) collective-permute-start(bf16[512,384]{1,0:T(8,128)(2,1)} %get-tuple-element.793), channel_id=1, source_target_pairs={{0,2},{1,3},{2,0},{3,1},{4,6},{5,7},{6,4},{7,5},{8,10},{9,11},{10,... | collective-permute-start | bytes 1179656 | tf_op jit(solution)/shard_map/ppermute | solution.py:589
  402.6 19.5 %collective-permute-start.49 = (bf16[512,384]{1,0:T(8,128)(2,1)}, bf16[512,384]{1,0:T(8,128)(2,1)S(1)}, u32[]{:S(2)}, u32[]{:S(2)}) collective-permute-start(bf16[512,384]{1,0:T(8,128)(2,1)} %get-tuple-element.792), channel_id=1, source_target_pairs={{0,3},{1,2},{2,1},{3,0},{4,7},{5,6},{6,5},{7,4},{8,11},{9,10},{10,... | collective-permute-start | bytes 1179656 | tf_op jit(solution)/shard_map/ppermute | solution.py:589
  404.0 18.0 %collective-permute-start.48 = (bf16[512,384]{1,0:T(8,128)(2,1)S(1)}, bf16[512,384]{1,0:T(8,128)(2,1)S(1)}, u32[]{:S(2)}, u32[]{:S(2)}) collective-permute-start(bf16[512,384]{1,0:T(8,128)(2,1)S(1)} %get-tuple-element.791), channel_id=1, source_target_pairs={{0,1},{1,0},{2,3},{3,2},{4,5},{5,4},{6,7},{7,6},{8,9},{9,8},{10,11... | collective-permute-start | bytes 1179656 | tf_op jit(solution)/shard_map/ppermute | solution.py:589
  425.6 39.8 %collective-permute-start.51 = (bf16[512,1536]{1,0:T(8,128)(2,1)}, bf16[512,1536]{1,0:T(8,128)(2,1)}, u32[]{:S(2)}, u32[]{:S(2)}) collective-permute-start(bf16[512,1536]{1,0:T(8,128)(2,1)} %back_product.18), channel_id=1, source_target_pairs={{0,2},{1,3},{2,0},{3,1},{4,6},{5,7},{6,4},{7,5},{8,10},{9,11},{10,... | collective-permute-start | bytes 4718600 | tf_op jit(solution)/shard_map/ppermute | solution.py:589
  474.4 6.7 %collective-permute-start.53 = (bf16[512,1536]{1,0:T(8,128)(2,1)}, bf16[512,1536]{1,0:T(8,128)(2,1)}, u32[]{:S(2)}, u32[]{:S(2)}) collective-permute-start(bf16[512,1536]{1,0:T(8,128)(2,1)} %back_product.20), channel_id=1, source_target_pairs={{0,1},{1,0},{2,3},{3,2},{4,5},{5,4},{6,7},{7,6},{8,9},{9,8},{10,11... | collective-permute-start | bytes 4718600 | tf_op jit(solution)/shard_map/ppermute | solution.py:589
  478.4 9.7 %collective-permute-start.52 = (bf16[512,1536]{1,0:T(8,128)(2,1)}, bf16[512,1536]{1,0:T(8,128)(2,1)}, u32[]{:S(2)}, u32[]{:S(2)}) collective-permute-start(bf16[512,1536]{1,0:T(8,128)(2,1)} %back_product.21), channel_id=1, source_target_pairs={{0,1},{1,0},{2,3},{3,2},{4,5},{5,4},{6,7},{7,6},{8,9},{9,8},{10,11... | collective-permute-start | bytes 4718600 | tf_op jit(solution)/shard_map/ppermute | solution.py:589
  481.1 29.2 %collective-permute-start.54 = (bf16[96,3072]{1,0:T(8,128)(2,1)S(1)}, bf16[96,3072]{1,0:T(8,128)(2,1)S(1)}, u32[]{:S(2)}, u32[]{:S(2)}) collective-permute-start(bf16[96,3072]{1,0:T(8,128)(2,1)S(1)} %get-tuple-element.869), channel_id=1, source_target_pairs={{0,3},{1,2},{2,1},{3,0},{4,7},{5,6},{6,5},{7,4},{8,11},{9,10},{10,... | collective-permute-start | bytes 1769480 | tf_op jit(solution)/shard_map/ppermute | solution.py:589
  482.9 26.5 %collective-permute-start.55 = (bf16[96,3072]{1,0:T(8,128)(2,1)S(1)}, bf16[96,3072]{1,0:T(8,128)(2,1)S(1)}, u32[]{:S(2)}, u32[]{:S(2)}) collective-permute-start(bf16[96,3072]{1,0:T(8,128)(2,1)S(1)} %get-tuple-element.870), channel_id=1, source_target_pairs={{0,2},{1,3},{2,0},{3,1},{4,6},{5,7},{6,4},{7,5},{8,10},{9,11},{10,... | collective-permute-start | bytes 1769480 | tf_op jit(solution)/shard_map/ppermute | solution.py:589
  483.2 10.7 %collective-permute-start.56 = (bf16[96,3072]{1,0:T(8,128)(2,1)S(1)}, bf16[96,3072]{1,0:T(8,128)(2,1)S(1)}, u32[]{:S(2)}, u32[]{:S(2)}) collective-permute-start(bf16[96,3072]{1,0:T(8,128)(2,1)S(1)} %get-tuple-element.871), channel_id=1, source_target_pairs={{0,1},{1,0},{2,3},{3,2},{4,5},{5,4},{6,7},{7,6},{8,9},{9,8},{10,11... | collective-permute-start | bytes 1769480 | tf_op jit(solution)/shard_map/ppermute | solution.py:589
  511.1 43.3 %collective-permute-start.57 = (bf16[512,1536]{1,0:T(8,128)(2,1)}, bf16[512,1536]{1,0:T(8,128)(2,1)}, u32[]{:S(2)}, u32[]{:S(2)}) collective-permute-start(bf16[512,1536]{1,0:T(8,128)(2,1)} %back_product.22), channel_id=1, source_target_pairs={{0,2},{1,3},{2,0},{3,1},{4,6},{5,7},{6,4},{7,5},{8,10},{9,11},{10,... | collective-permute-start | bytes 4718600 | tf_op jit(solution)/shard_map/ppermute | solution.py:589
  535.2 5.7 collective-permute-start.59
  561.2 4.7 collective-permute-start.60
  564.0 15.7 %collective-permute-start.64 = (bf16[96,1536]{1,0:T(8,128)(2,1)S(1)}, bf16[96,1536]{1,0:T(8,128)(2,1)S(1)}, u32[]{:S(2)}, u32[]{:S(2)}) collective-permute-start(bf16[96,1536]{1,0:T(8,128)(2,1)S(1)} %get-tuple-element.932), channel_id=1, source_target_pairs={{0,3},{1,2},{2,1},{3,0},{4,7},{5,6},{6,5},{7,4},{8,11},{9,10},{10,... | collective-permute-start | bytes 884744 | tf_op jit(solution)/shard_map/ppermute | solution.py:589
  564.8 14.9 %collective-permute-start.65 = (bf16[96,1536]{1,0:T(8,128)(2,1)S(1)}, bf16[96,1536]{1,0:T(8,128)(2,1)S(1)}, u32[]{:S(2)}, u32[]{:S(2)}) collective-permute-start(bf16[96,1536]{1,0:T(8,128)(2,1)S(1)} %get-tuple-element.933), channel_id=1, source_target_pairs={{0,2},{1,3},{2,0},{3,1},{4,6},{5,7},{6,4},{7,5},{8,10},{9,11},{10,... | collective-permute-start | bytes 884744 | tf_op jit(solution)/shard_map/ppermute | solution.py:589
  565.6 10.0 %collective-permute-start.66 = (bf16[96,1536]{1,0:T(8,128)(2,1)S(1)}, bf16[96,1536]{1,0:T(8,128)(2,1)S(1)}, u32[]{:S(2)}, u32[]{:S(2)}) collective-permute-start(bf16[96,1536]{1,0:T(8,128)(2,1)S(1)} %get-tuple-element.934), channel_id=1, source_target_pairs={{0,1},{1,0},{2,3},{3,2},{4,5},{5,4},{6,7},{7,6},{8,9},{9,8},{10,11... | collective-permute-start | bytes 884744 | tf_op jit(solution)/shard_map/ppermute | solution.py:589
  591.7 5.0 collective-permute-start.69
  (145 other events, 1546.5 us)
Sparse Core Ops, SparseCore 0:
  92.9 145.2 all-gather.1
  292.8 61.7 reduce-scatter.3
  361.5 111.6 reduce-scatter.5
  475.3 85.7 reduce-scatter.7

commit v5 on v4

--- a/solution.py
+++ b/solution.py
@@ -531,9 +531,10 @@
     right_ref[...] = dot(left_ref[...], merged_ref[...], precision=HIGHEST).astype(BF16)
 
 
-def right_factor(own, other, merged, tile=3072):
+def right_factor(own, other, merged, steps=4):
     rank, rows = own.shape
     total = merged.shape[1]
+    tile = total // steps
     small = pl.BlockSpec((rank, rows), lambda i: (0, 0))
     return pl.pallas_call(
         right_kernel,
@@ -562,9 +563,10 @@
     weight_out_ref[...] = weight_ref[...] - RATE_MATRIX * momentum
 
 
-def update(copies, ortho, own, other, merged, momentum, weight, tile=3072):
+def update(copies, ortho, own, other, merged, momentum, weight, steps=4):
     rank, rows = ortho.shape
     total = merged.shape[1]
+    tile = total // steps
     small = pl.BlockSpec((rank, rows), lambda i: (0, 0))
     low = pl.BlockSpec((rank, tile), lambda i: (0, i))
     wide = pl.BlockSpec((rows, tile), lambda i: (0, i))

time: 616 us -> 616 us (level)
  no operation moved by 1% of the time
where the time goes in v5:
time: 616 us; the launch traced here: 611 us
  Pallas kernels  271 us (44%)
  waiting for transfers between devices  155 us (25%)
  local copies, waits for them, and re-layouts  67.1 us (11%)
  starting transfers between devices  55.9 us (9%)
  other arithmetic  36.1 us (6%)
  between operations  18.7 us (3%)
  matrix products  6.67 us (1%)
    ppermute x48, waiting for transfers between devices, swap(): return lax.ppermute(value, 'member', [(j, j ^ bits) for j in range(GROUP)])  71.3 us
    unnamed x271, local copies, waits for them, and re-layouts  62.4 us
    ppermute x6, waiting for transfers between devices, ring(): lax.ppermute(value, 'layer', [(z, (z + 1) % layers) for z in range(layers)])  57.6 us
    pallas_call x5, Pallas kernels, weight_product(): pl.pallas_call(weight_kernel, grid=(depth // rows,), in_specs=specs, out_...  54.5 us
    pallas_call x12, Pallas kernels, back_product(): pl.pallas_call(partial(back_kernel, pairs), grid=(width // tile,), in_spe...  49.8 us
    pallas_call x4, Pallas kernels, attend_back(): pl.pallas_call(attend_back_kernel, grid=(1,), in_specs=attention_specs(le...  47.4 us
    ppermute x48, starting transfers between devices, swap(): return lax.ppermute(value, 'member', [(j, j ^ bits) for j in range(GROUP)])  32.3 us
    pallas_call x1, Pallas kernels, raise_up(): pl.pallas_call(raise_kernel, grid=(count,), in_specs=[pl.BlockSpec((lengt...  19.2 us
  transfers between devices with their start and end apart: 74, of which 28 were waited for; matrix products, arithmetic and copies ran while one was open for 7% of the time, Pallas kernels for 40%

profile of v5, /device:TPU:0, one launch (start us, length us, event | category | flops | bytes accessed | tf_op | source)
XLA Modules:
  0.0 610.6 jit_solution(255843149138745739)
XLA Ops:
  9.2 3.0 collective-permute-start.2
  24.6 6.1 collective-permute-done.1
  39.0 6.7 %collective-permute-done.6.refs_2_ = bf16[192,1152]{1,0:T(8,128)(2,1)S(1)} collective-permute-done((bf16[192,1152]{1,0:T(8,128)(2,1)S(1)}, bf16[192,1152]{1,0:T(8,128)(2,1)S(1)}, u32[]{:S(2)}, u32[]{:S(2)}) %collective-permute-start.6) | collective-permute-done | bytes 442400 | tf_op jit(solution)/shard_map/ppermute | solution.py:599
  46.7 12.6 %collective-permute-done.10.refs_4_ = bf16[192,1152]{1,0:T(8,128)(2,1)S(1)} collective-permute-done((bf16[192,1152]{1,0:T(8,128)(2,1)S(1)}, bf16[192,1152]{1,0:T(8,128)(2,1)S(1)}, u32[]{:S(2)}, u32[]{:S(2)}) %collective-permute-start.10) | collective-permute-done | bytes 442400 | tf_op jit(solution)/shard_map/ppermute | solution.py:599
  62.7 8.8 %collective-permute-done.11.refs_6_ = bf16[192,1152]{1,0:T(8,128)(2,1)} collective-permute-done((bf16[192,1152]{1,0:T(8,128)(2,1)S(1)}, bf16[192,1152]{1,0:T(8,128)(2,1)}, u32[]{:S(2)}, u32[]{:S(2)}) %collective-permute-start.11) | collective-permute-done | bytes 442400 | tf_op jit(solution)/shard_map/ppermute | solution.py:599
  84.7 7.1 %collective-permute-done.15.refs_2_ = bf16[96,1536]{1,0:T(8,128)(2,1)} collective-permute-done((bf16[96,1536]{1,0:T(8,128)(2,1)S(1)}, bf16[96,1536]{1,0:T(8,128)(2,1)}, u32[]{:S(2)}, u32[]{:S(2)}) %collective-permute-start.15) | collective-permute-done | bytes 294944 | tf_op jit(solution)/shard_map/ppermute | solution.py:599
  96.1 9.1 %collective-permute-done.18.refs_4_ = bf16[96,1536]{1,0:T(8,128)(2,1)S(1)} collective-permute-done((bf16[96,1536]{1,0:T(8,128)(2,1)}, bf16[96,1536]{1,0:T(8,128)(2,1)S(1)}, u32[]{:S(2)}, u32[]{:S(2)}) %collective-permute-start.18) | collective-permute-done | bytes 294944 | tf_op jit(solution)/shard_map/ppermute | solution.py:599
  109.1 13.3 %collective-permute-done.21.refs_6_ = bf16[96,1536]{1,0:T(8,128)(2,1)S(1)} collective-permute-done((bf16[96,1536]{1,0:T(8,128)(2,1)S(1)}, bf16[96,1536]{1,0:T(8,128)(2,1)S(1)}, u32[]{:S(2)}, u32[]{:S(2)}) %collective-permute-start.21) | collective-permute-done | bytes 294944 | tf_op jit(solution)/shard_map/ppermute | solution.py:599
  123.1 5.7 collective-permute-done.13.left_ref.refs_2_
  137.9 2.7 assemble.2
  140.7 3.4 project.4.qkv_ref
  144.2 5.0 project.5.qkv_ref
  149.2 4.3 attend.4
  153.6 5.1 attend.5
  158.7 3.4 project.6.qkv_ref
  162.1 4.3 attend.6
  172.1 4.7 collective-permute-done.23.left_ref.refs_3_
  176.7 3.6 project.7.qkv_ref
  180.4 4.3 attend.7
  188.0 6.8 %interleave.1 = bf16[1536,1536]{1,0:T(8,128)(2,1)} custom-call(s32[1]{0:T(128)} %bitcast.11.core_ref, bf16[768,1536]{1,0:T(8,128)(2,1)} %bitcast.55, bf16[768,1536]{1,0:T(8,128)(2,1)} %collective-permute-done.29.other_ref), custom_call_target="tpu_custom_call" | custom-call | bytes 9437184 | tf_op jit(solution)/shard_map/interleave/pallas_call | solution.py:466
  199.6 4.0 convert_add_fusion
  207.4 5.0 loss_gradients.1
  217.1 25.1 %collective-permute-done.32.refs_2_ = bf16[512,1536]{1,0:T(8,128)(2,1)S(1)} collective-permute-done((bf16[512,1536]{1,0:T(8,128)(2,1)S(1)}, bf16[512,1536]{1,0:T(8,128)(2,1)S(1)}, u32[]{:S(2)}, u32[]{:S(2)}) %collective-permute-start.32) | collective-permute-done | bytes 1572896 | tf_op jit(solution)/shard_map/ppermute | solution.py:591
  245.8 19.2 %raise_up.1 = (bf16[512,1024]{1,0:T(8,128)(2,1)}, bf16[512,1024]{1,0:T(8,128)(2,1)}, bf16[512,1024]{1,0:T(8,128)(2,1)}, bf16[512,1024]{1,0:T(8,128)(2,1)}, f32[5...) custom-call(bf16[512,1536]{1,0:T(8,128)(2,1)} %copy-done.103, ...), custom_call_target="tpu_custom_call" | custom-call | bytes 786432 | tf_op jit(solution)/shard_map/raise_up/pallas_call | solution.py:371
  265.0 16.1 %raise_back.1 = (bf16[512,1024]{1,0:T(8,128)(2,1)}, bf16[512,1024]{1,0:T(8,128)(2,1)}, bf16[512,1024]{1,0:T(8,128)(2,1)}, bf16[512,1024]{1,0:T(8,128)(2,1)}, bf1...) custom-call(bf16[512,1536]{1,0:T(8,128)(2,1)} %copy-done.22, ...), custom_call_target="tpu_custom_call" | custom-call | bytes 786432 | tf_op jit(solution)/shard_map/raise_back/pallas_call | solution.py:405
  281.1 11.6 %weight_product.5 = bf16[1536,1024]{1,0:T(8,128)(2,1)} custom-call(bf16[512,1536]{1,0:T(8,128)(2,1)} %copy-done.22, bf16[512,1536]{1,0:T(8,128)(2,1)} %copy-done.23, bf16[512,1536]{1,0:T(8,128)(2,1)} %copy-done.24, bf16[512,1536]{1,0:T(8,128)(2,1)} %copy-done.25, bf16[512,1024]{1,0:T(8,128)(2,1)} %get-tuple-element.822.refs_4_.refs_0_, ...), custom_call_target="tpu_custom_call" | custom-call | flops 100663296 | bytes 163840 | tf_op jit(solution)/shard_map/weight_product/pallas_call | solution.py:317
  294.2 3.7 copy-done
  297.9 4.4 back_product.12
  302.5 4.4 back_product.13
  307.3 6.7 %back_product.14 = bf16[512,1536]{1,0:T(8,128)(2,1)} custom-call(bf16[512,1024]{1,0:T(8,128)(2,1)S(1)} %copy-done.41, bf16[512,1024]{1,0:T(8,128)(2,1)S(1)} %copy-done.37, bf16[1536,3072]{1,0:T(8,128)(2,1)} %all-gather.2.cloned.1.call-done.refs_4_.refs_5_.refs_2_.refs_3_.refs_1_, ...), custom_call_target="tpu_custom_call" | custom-call | flops 100663296 | bytes 262144 | tf_op jit(solution)/shard_map/back_product/pallas_call | solution.py:283
  316.9 11.1 %weight_product.6.refs_8_ = bf16[1536,2048]{1,0:T(8,128)(2,1)} custom-call(bf16[512,1536]{1,0:T(8,128)(2,1)} %copy-done.103, bf16[512,1536]{1,0:T(8,128)(2,1)} %copy-done.105, bf16[512,1536]{1,0:T(8,128)(2,1)} %copy-done.104, bf16[512,1536]{1,0:T(8,128)(2,1)} %collective-permute-done.35.refs_3_, bf16[512,1024]{1,0:T(8,128)(2,1)} %get-tuple-element.740.refs_4_.refs_0_, ...), custom_call_target="tpu_custom_call" | custom-call | flops 100663296 | bytes 163840 | tf_op jit(solution)/shard_map/weight_product/pallas_call | solution.py:317
  331.9 5.8 back_product.15
  337.8 11.2 %weight_product.7 = bf16[1536,2048]{1,0:T(8,128)(2,1)} custom-call(bf16[512,1536]{1,0:T(8,128)(2,1)} %copy-done.103, bf16[512,1536]{1,0:T(8,128)(2,1)} %copy-done.105, bf16[512,1536]{1,0:T(8,128)(2,1)} %copy-done.104, bf16[512,1536]{1,0:T(8,128)(2,1)} %collective-permute-done.35.refs_3_, ...), custom_call_target="tpu_custom_call", output_to_operand_aliasing={{}: (8, {})} | custom-call | flops 100663296 | bytes 163840 | tf_op jit(solution)/shard_map/weight_product/pallas_call | solution.py:317
  348.9 3.7 copy-done.1
  362.3 3.4 multiply_reduce_fusion.1
  366.4 2.8 fusion.12
  376.1 11.7 %attend_back.4 = (bf16[512,1152]{1,0:T(8,128)(2,1)S(1)}, f32[8,128]{1,0:T(8,128)S(1)}) custom-call(f32[1]{0:T(128)} %bitcast.1.lam_ref, bf16[512,1152]{1,0:T(8,128)(2,1)S(1)} %copy-done.20, f32[8,128]{1,0:T(8,128)S(1)} %pad_maximum_fusion.5.marks_ref.refs_4_, f32[1,128]{1,0:T(1,128)S(1)} %copy-done.87, bf16[512,384]{1,0:T(8,128)(2,1)S(1)} %get-tuple-element.772.grad_ref), custom_call_target="tpu_custom_call" | custom-call | bytes 196608 | tf_op jit(solution)/shard_map/attend_back/pallas_call | solution.py:181
  388.9 12.0 %attend_back.5 = (bf16[512,1152]{1,0:T(8,128)(2,1)S(1)}, f32[8,128]{1,0:T(8,128)S(1)}) custom-call(f32[1]{0:T(128)} %bitcast.1.lam_ref, bf16[512,1152]{1,0:T(8,128)(2,1)S(1)} %copy-done.18, f32[8,128]{1,0:T(8,128)S(1)} %collective-permute-done.12.marks_ref.refs_5_, f32[1,128]{1,0:T(1,128)S(1)} %copy-done.87, ...), custom_call_target="tpu_custom_call" | custom-call | bytes 196608 | tf_op jit(solution)/shard_map/attend_back/pallas_call | solution.py:181
  404.2 11.9 %attend_back.6 = (bf16[512,1152]{1,0:T(8,128)(2,1)S(1)}, f32[8,128]{1,0:T(8,128)S(1)}) custom-call(f32[1]{0:T(128)} %bitcast.1.lam_ref, bf16[512,1152]{1,0:T(8,128)(2,1)S(1)} %copy-done.14, f32[16,128]{1,0:T(8,128)S(1)} %collective-permute-done.25.marks_ref.refs_6_.refs_7_, f32[1,128]{1,0:T(1,128)S(1)} %copy-done.87, ...), custom_call_target="tpu_custom_call" | custom-call | bytes 196608 | tf_op jit(solution)/shard_map/attend_back/pallas_call | solution.py:181
  417.1 4.9 collective-permute-done.49.refs_7_
  422.1 3.4 back_product.18
  425.6 11.7 %attend_back.7 = (bf16[512,1152]{1,0:T(8,128)(2,1)S(1)}, f32[8,128]{1,0:T(8,128)S(1)}) custom-call(f32[1]{0:T(128)} %bitcast.1.lam_ref, bf16[512,1152]{1,0:T(8,128)(2,1)S(1)} %copy-done.16, f32[16,128]{1,0:T(8,128)S(1)} %collective-permute-done.25.marks_ref.refs_6_.refs_7_, f32[1,128]{1,0:T(1,128)S(1)} %copy-done.87, ...), custom_call_target="tpu_custom_call" | custom-call | bytes 196608 | tf_op jit(solution)/shard_map/attend_back/pallas_call | solution.py:181
  439.0 7.4 %weight_product.8.refs_8_ = bf16[1536,1536]{1,0:T(8,128)(2,1)} custom-call(bf16[512,1536]{1,0:T(8,128)(2,1)} %pad_maximum_fusion.1.refs_0_, bf16[512,1536]{1,0:T(8,128)(2,1)} %copy-done.110, bf16[512,1536]{1,0:T(8,128)(2,1)} %collective-permute-done.37.refs_2_, bf16[512,1536]{1,0:T(8,128)(2,1)} %copy-done.109, bf16[512,384]{1,0:T(8,128)(2,1)} %get-tuple-element.1005.refs_4_, ...), custom_call_target="tpu_custom_call" | custom-call | flops 37748736 | bytes 122880 | tf_op jit(solution)/shard_map/weight_product/pallas_call | solution.py:317
  446.4 4.1 back_product.19
  452.1 13.2 %weight_product.9 = bf16[1536,1536]{1,0:T(8,128)(2,1)} custom-call(bf16[512,1536]{1,0:T(8,128)(2,1)} %copy-done.11, bf16[512,1536]{1,0:T(8,128)(2,1)} %collective-permute-done.27.left_ref.refs_1_, bf16[512,1536]{1,0:T(8,128)(2,1)} %copy-done.26, bf16[512,1536]{1,0:T(8,128)(2,1)} %copy-done.28, ...), custom_call_target="tpu_custom_call", output_to_operand_aliasing={{}: (8, {})} | custom-call | flops 113246208 | bytes 172032 | tf_op jit(solution)/shard_map/weight_product/pallas_call | solution.py:317
  465.4 5.5 add_convert_fusion
  470.9 3.5 back_product.20
  474.9 3.5 back_product.21
  483.2 4.8 back_product.22
  488.1 4.2 back_product.23
  494.8 14.7 %collective-permute-done.55.refs_2_ = bf16[96,3072]{1,0:T(8,128)(2,1)S(1)} collective-permute-done((bf16[96,3072]{1,0:T(8,128)(2,1)S(1)}, bf16[96,3072]{1,0:T(8,128)(2,1)S(1)}, u32[]{:S(2)}, u32[]{:S(2)}) %collective-permute-start.55) | collective-permute-done | bytes 589856 | tf_op jit(solution)/shard_map/ppermute | solution.py:591
  520.7 6.7 %merge.2 = (f32[96,12288]{1,0:T(8,128)}, f32[96,12288]{1,0:T(8,128)S(1)}, f32[8,96]{1,0:T(8,128)S(1)}) custom-call(s32[1]{0:T(128)} %bitcast.member_ref, bf16[96,3072]{1,0:T(8,128)(2,1)S(1)} %copy-done.49, bf16[96,3072]{1,0:T(8,128)(2,1)S(1)} %copy-done.69, bf16[96,3072]{1,0:T(8,128)(2,1)S(1)} %copy-done.67, bf16[96,3072]{1,0:T(8,128)(2,1)S(1)} %copy-done.65, ...), custom_call_target="tpu_custom_call" | custom-call | bytes 1179648 | tf_op jit(solution)/shard_map/merge/pallas_call | solution.py:502
  527.5 3.4 collective-permute-done.58.other_ref
  531.0 4.2 right_factor.2
  535.2 5.6 collective-permute-done.59.other_ref
  546.3 8.0 %update.2 = (f32[8,12288]{1,0:T(8,128)}, f32[96,12288]{1,0:T(8,128)}, f32[96,12288]{1,0:T(8,128)}, f32[96,12288]{1,0:T(8,128)}) custom-call(f32[8,96]{1,0:T(8,128)S(1)} %copy-done.93, bf16[8,12288]{1,0:T(8,128)(2,1)S(1)} %get-tuple-element.899.own_ref, bf16[8,12288]{1,0:T(8,128)(2,1)S(1)} %collective-permute-done.59.other_ref, f32[96,12288]{1,0:T(8,128)S(1)} %copy-done.10, ...), custom_call_target="tpu_custom_call" | custom-call | bytes 1179648 | tf_op jit(solution)/shard_map/update/pallas_call | solution.py:574
  557.0 4.1 reduce-scatter.8.cloned.1.call-done
  571.0 2.9 collective-permute-start.63
  575.6 4.1 collective-permute-done.65.refs_2_
  579.7 4.4 merge.3
  585.9 2.9 collective-permute-done.68.other_ref
  588.8 3.2 right_factor.3
  592.7 4.3 fusion.8
  597.0 5.0 update.3
  (460 shorter events, 158.4 us)
Async XLA Ops:
  7.2 238.6 %all-gather.2.cloned.1.call-start = ((), (), s32[]{:S(2)}) async-start(), calls=%async_computation.3 | async-start | bytes 10616832 | tf_op jit(solution)/shard_map/all_gather | solution.py:759
  13.8 6.2 %collective-permute-start.3 = (f32[8,128]{1,0:T(8,128)S(1)}, f32[8,128]{1,0:T(8,128)S(1)}, u32[]{:S(2)}, u32[]{:S(2)}) collective-permute-start(f32[8,128]{1,0:T(8,128)S(1)} %broadcast_add_fusion), channel_id=1, source_target_pairs={{0,4},{4,0},{8,12},{12,8},{1,5},{5,1},{9,13},{13,9},{2,6},{6,2},{1... | collective-permute-start | bytes 12296 | tf_op jit(solution)/shard_map/ppermute | solution.py:595
  18.1 12.5 %collective-permute-start = (bf16[96,1152]{1,0:T(8,128)(2,1)S(1)}, bf16[96,1152]{1,0:T(8,128)(2,1)S(1)}, u32[]{:S(2)}, u32[]{:S(2)}) collective-permute-start(bf16[96,1152]{1,0:T(8,128)(2,1)S(1)} %get-tuple-element.500), channel_id=1, source_target_pairs={{0,3},{1,2},{2,1},{3,0},{4,7},{5,6},{6,5},{7,4},{8,11},{9,10},{10,... | collective-permute-start | bytes 663560 | tf_op jit(solution)/shard_map/ppermute | solution.py:591
  18.2 12.5 %collective-permute-start.1 = (bf16[96,1152]{1,0:T(8,128)(2,1)S(1)}, bf16[96,1152]{1,0:T(8,128)(2,1)S(1)}, u32[]{:S(2)}, u32[]{:S(2)}) collective-permute-start(bf16[96,1152]{1,0:T(8,128)(2,1)S(1)} %get-tuple-element.501), channel_id=1, source_target_pairs={{0,2},{1,3},{2,0},{3,1},{4,6},{5,7},{6,4},{7,5},{8,10},{9,11},{10,... | collective-permute-start | bytes 663560 | tf_op jit(solution)/shard_map/ppermute | solution.py:591
  19.8 10.9 %collective-permute-start.5 = (bf16[96,1152]{1,0:T(8,128)(2,1)S(1)}, bf16[96,1152]{1,0:T(8,128)(2,1)S(1)}, u32[]{:S(2)}, u32[]{:S(2)}) collective-permute-start(bf16[96,1152]{1,0:T(8,128)(2,1)S(1)} %get-tuple-element.510), channel_id=1, source_target_pairs={{0,1},{1,0},{2,3},{3,2},{4,5},{5,4},{6,7},{7,6},{8,9},{9,8},{10,11... | collective-permute-start | bytes 663560 | tf_op jit(solution)/shard_map/ppermute | solution.py:591
  31.8 13.9 %collective-permute-start.6 = (bf16[192,1152]{1,0:T(8,128)(2,1)S(1)}, bf16[192,1152]{1,0:T(8,128)(2,1)S(1)}, u32[]{:S(2)}, u32[]{:S(2)}) collective-permute-start(bf16[192,1152]{1,0:T(8,128)(2,1)S(1)} %get-tuple-element.515), channel_id=1, source_target_pairs={{0,4},{4,8},{8,12},{12,0},{1,5},{5,9},{9,13},{13,1},{2,6},{6,10},{... | collective-permute-start | bytes 1327112 | tf_op jit(solution)/shard_map/ppermute | solution.py:599
  36.9 38.0 %collective-permute-start.7 = (bf16[96,3072]{1,0:T(8,128)(2,1)}, bf16[96,3072]{1,0:T(8,128)(2,1)}, u32[]{:S(2)}, u32[]{:S(2)}) collective-permute-start(bf16[96,3072]{1,0:T(8,128)(2,1)} %get-tuple-element.530), channel_id=1, source_target_pairs={{0,1},{1,0},{2,3},{3,2},{4,5},{5,4},{6,7},{7,6},{8,9},{9,8},{10,11... | collective-permute-start | bytes 1769480 | tf_op jit(solution)/shard_map/ppermute | solution.py:591
  36.9 37.9 %collective-permute-start.8 = (bf16[96,3072]{1,0:T(8,128)(2,1)}, bf16[96,3072]{1,0:T(8,128)(2,1)}, u32[]{:S(2)}, u32[]{:S(2)}) collective-permute-start(bf16[96,3072]{1,0:T(8,128)(2,1)} %get-tuple-element.531), channel_id=1, source_target_pairs={{0,3},{1,2},{2,1},{3,0},{4,7},{5,6},{6,5},{7,4},{8,11},{9,10},{10,... | collective-permute-start | bytes 1769480 | tf_op jit(solution)/shard_map/ppermute | solution.py:591
  37.0 36.1 %collective-permute-start.9 = (bf16[96,3072]{1,0:T(8,128)(2,1)}, bf16[96,3072]{1,0:T(8,128)(2,1)}, u32[]{:S(2)}, u32[]{:S(2)}) collective-permute-start(bf16[96,3072]{1,0:T(8,128)(2,1)} %get-tuple-element.532), channel_id=1, source_target_pairs={{0,2},{1,3},{2,0},{3,1},{4,6},{5,7},{6,4},{7,5},{8,10},{9,11},{10,... | collective-permute-start | bytes 1769480 | tf_op jit(solution)/shard_map/ppermute | solution.py:591
  46.1 13.1 %collective-permute-start.10 = (bf16[192,1152]{1,0:T(8,128)(2,1)S(1)}, bf16[192,1152]{1,0:T(8,128)(2,1)S(1)}, u32[]{:S(2)}, u32[]{:S(2)}) collective-permute-start(bf16[192,1152]{1,0:T(8,128)(2,1)S(1)} %collective-permute-done.6.refs_2_), channel_id=1, source_target_pairs={{0,4},{4,8},{8,12},{12,0},{1,5},{5,9},{9,13},{13,1},{2,6},{6,10},{... | collective-permute-start | bytes 1327112 | tf_op jit(solution)/shard_map/ppermute | solution.py:599
  59.3 12.2 %collective-permute-start.11 = (bf16[192,1152]{1,0:T(8,128)(2,1)S(1)}, bf16[192,1152]{1,0:T(8,128)(2,1)}, u32[]{:S(2)}, u32[]{:S(2)}) collective-permute-start(bf16[192,1152]{1,0:T(8,128)(2,1)S(1)} %collective-permute-done.10.refs_4_), channel_id=1, source_target_pairs={{0,4},{4,8},{8,12},{12,0},{1,5},{5,9},{9,13},{13,1},{2,6},{6,10},{... | collective-permute-start | bytes 1327112 | tf_op jit(solution)/shard_map/ppermute | solution.py:599
  61.2 22.0 %collective-permute-start.17 = (bf16[192,1152]{1,0:T(8,128)(2,1)S(1)}, bf16[192,1152]{1,0:T(8,128)(2,1)}, u32[]{:S(2)}, u32[]{:S(2)}) collective-permute-start(bf16[192,1152]{1,0:T(8,128)(2,1)S(1)} %collective-permute-done.6.refs_2_), channel_id=1, source_target_pairs={{0,16},{16,0},{1,17},{17,1},{2,18},{18,2},{3,19},{19,3},{4,20},{20... | collective-permute-start | bytes 1327112 | tf_op jit(solution)/shard_map/ppermute | solution.py:603
  71.5 13.2 %collective-permute-start.16 = (bf16[192,1152]{1,0:T(8,128)(2,1)S(1)}, bf16[192,1152]{1,0:T(8,128)(2,1)}, u32[]{:S(2)}, u32[]{:S(2)}) collective-permute-start(bf16[192,1152]{1,0:T(8,128)(2,1)S(1)} %collective-permute-done.10.refs_4_), channel_id=1, source_target_pairs={{0,16},{16,0},{1,17},{17,1},{2,18},{18,2},{3,19},{19,3},{4,20},{20... | collective-permute-start | bytes 1327112 | tf_op jit(solution)/shard_map/ppermute | solution.py:603
  73.0 7.0 %collective-permute-start.14 = (bf16[96,1536]{1,0:T(8,128)(2,1)}, bf16[96,1536]{1,0:T(8,128)(2,1)S(1)}, u32[]{:S(2)}, u32[]{:S(2)}) collective-permute-start(bf16[96,1536]{1,0:T(8,128)(2,1)} %slice.297), channel_id=1, source_target_pairs={{0,2},{1,3},{2,0},{3,1},{4,6},{5,7},{6,4},{7,5},{8,10},{9,11},{10,... | collective-permute-start | bytes 884744 | tf_op jit(solution)/shard_map/ppermute | solution.py:591
  80.8 12.0 %collective-permute-start.19 = (bf16[192,1152]{1,0:T(8,128)(2,1)}, bf16[192,1152]{1,0:T(8,128)(2,1)S(1)}, u32[]{:S(2)}, u32[]{:S(2)}) collective-permute-start(bf16[192,1152]{1,0:T(8,128)(2,1)} %collective-permute-done.11.refs_6_), channel_id=1, source_target_pairs={{0,16},{16,0},{1,17},{17,1},{2,18},{18,2},{3,19},{19,3},{4,20},{20... | collective-permute-start | bytes 1327112 | tf_op jit(solution)/shard_map/ppermute | solution.py:603
  83.2 8.6 %collective-permute-start.15 = (bf16[96,1536]{1,0:T(8,128)(2,1)S(1)}, bf16[96,1536]{1,0:T(8,128)(2,1)}, u32[]{:S(2)}, u32[]{:S(2)}) collective-permute-start(bf16[96,1536]{1,0:T(8,128)(2,1)S(1)} %get-tuple-element.557), channel_id=1, source_target_pairs={{0,4},{4,8},{8,12},{12,0},{1,5},{5,9},{9,13},{13,1},{2,6},{6,10},{... | collective-permute-start | bytes 884744 | tf_op jit(solution)/shard_map/ppermute | solution.py:599
  93.5 267.8 %reduce-scatter.4.cloned.1.call-start = ((), (), s32[]{:S(2)}) async-start(), calls=%async_computation.4 | async-start | bytes 3932160 | tf_op jit(solution)/shard_map/reduce_scatter | solution.py:607
  93.5 35.3 %collective-permute-start.13 = (bf16[512,1536]{1,0:T(8,128)(2,1)S(1)}, bf16[512,1536]{1,0:T(8,128)(2,1)S(1)}, u32[]{:S(2)}, u32[]{:S(2)}) collective-permute-start(bf16[512,1536]{1,0:T(8,128)(2,1)S(1)} %fusion.4.left_ref.refs_0_), channel_id=1, source_target_pairs={{0,2},{1,3},{2,0},{3,1},{4,6},{5,7},{6,4},{7,5},{8,10},{9,11},{10,... | collective-permute-start | bytes 4718600 | tf_op jit(solution)/shard_map/ppermute | solution.py:591
  94.6 10.6 %collective-permute-start.18 = (bf16[96,1536]{1,0:T(8,128)(2,1)}, bf16[96,1536]{1,0:T(8,128)(2,1)S(1)}, u32[]{:S(2)}, u32[]{:S(2)}) collective-permute-start(bf16[96,1536]{1,0:T(8,128)(2,1)} %collective-permute-done.15.refs_2_), channel_id=1, source_target_pairs={{0,4},{4,8},{8,12},{12,0},{1,5},{5,9},{9,13},{13,1},{2,6},{6,10},{... | collective-permute-start | bytes 884744 | tf_op jit(solution)/shard_map/ppermute | solution.py:599
  94.6 13.8 %collective-permute-start.22 = (bf16[96,1536]{1,0:T(8,128)(2,1)}, bf16[96,1536]{1,0:T(8,128)(2,1)S(1)}, u32[]{:S(2)}, u32[]{:S(2)}) collective-permute-start(bf16[96,1536]{1,0:T(8,128)(2,1)} %collective-permute-done.15.refs_2_), channel_id=1, source_target_pairs={{0,16},{16,0},{1,17},{17,1},{2,18},{18,2},{3,19},{19,3},{4,20},{20... | collective-permute-start | bytes 884744 | tf_op jit(solution)/shard_map/ppermute | solution.py:603
  105.2 17.2 %collective-permute-start.21 = (bf16[96,1536]{1,0:T(8,128)(2,1)S(1)}, bf16[96,1536]{1,0:T(8,128)(2,1)S(1)}, u32[]{:S(2)}, u32[]{:S(2)}) collective-permute-start(bf16[96,1536]{1,0:T(8,128)(2,1)S(1)} %collective-permute-done.18.refs_4_), channel_id=1, source_target_pairs={{0,4},{4,8},{8,12},{12,0},{1,5},{5,9},{9,13},{13,1},{2,6},{6,10},{... | collective-permute-start | bytes 884744 | tf_op jit(solution)/shard_map/ppermute | solution.py:599
  105.2 17.2 %collective-permute-start.20 = (bf16[96,1536]{1,0:T(8,128)(2,1)S(1)}, bf16[96,1536]{1,0:T(8,128)(2,1)S(1)}, u32[]{:S(2)}, u32[]{:S(2)}) collective-permute-start(bf16[96,1536]{1,0:T(8,128)(2,1)S(1)} %collective-permute-done.18.refs_4_), channel_id=1, source_target_pairs={{0,16},{16,0},{1,17},{17,1},{2,18},{18,2},{3,19},{19,3},{4,20},{20... | collective-permute-start | bytes 884744 | tf_op jit(solution)/shard_map/ppermute | solution.py:603
  107.4 21.5 %collective-permute-start.25 = (f32[16,128]{1,0:T(8,128)S(1)}, f32[16,128]{1,0:T(8,128)S(1)}, u32[]{:S(2)}, u32[]{:S(2)}) collective-permute-start(f32[16,128]{1,0:T(8,128)S(1)} %pad_maximum_fusion.4), channel_id=1, source_target_pairs={{0,2},{1,3},{2,0},{3,1},{4,6},{5,7},{6,4},{7,5},{8,10},{9,11},{10,... | collective-permute-start | bytes 24584 | tf_op jit(solution)/shard_map/ppermute | solution.py:591
  109.1 31.6 %collective-permute-start.27 = (bf16[512,1536]{1,0:T(8,128)(2,1)S(1)}, bf16[512,1536]{1,0:T(8,128)(2,1)}, u32[]{:S(2)}, u32[]{:S(2)}) collective-permute-start(bf16[512,1536]{1,0:T(8,128)(2,1)S(1)} %fusion.4.left_ref.refs_0_), channel_id=1, source_target_pairs={{0,1},{1,0},{2,3},{3,2},{4,5},{5,4},{6,7},{7,6},{8,9},{9,8},{10,11... | collective-permute-start | bytes 4718600 | tf_op jit(solution)/shard_map/ppermute | solution.py:591
  128.9 38.7 %collective-permute-start.26 = (bf16[512,1536]{1,0:T(8,128)(2,1)}, bf16[512,1536]{1,0:T(8,128)(2,1)}, u32[]{:S(2)}, u32[]{:S(2)}) collective-permute-start(bf16[512,1536]{1,0:T(8,128)(2,1)} %refs_0_.3), channel_id=1, source_target_pairs={{0,2},{1,3},{2,0},{3,1},{4,6},{5,7},{6,4},{7,5},{8,10},{9,11},{10,... | collective-permute-start | bytes 4718600 | tf_op jit(solution)/shard_map/ppermute | solution.py:591
  131.3 36.2 %collective-permute-start.24 = (bf16[96,1536]{1,0:T(8,128)(2,1)}, bf16[96,1536]{1,0:T(8,128)(2,1)S(1)}, u32[]{:S(2)}, u32[]{:S(2)}) collective-permute-start(bf16[96,1536]{1,0:T(8,128)(2,1)} %copy-done.81), channel_id=1, source_target_pairs={{0,16},{16,0},{1,17},{17,1},{2,18},{18,2},{3,19},{19,3},{4,20},{20... | collective-permute-start | bytes 884744 | tf_op jit(solution)/shard_map/ppermute | solution.py:603
  169.7 18.3 %collective-permute-start.29 = (bf16[768,1536]{1,0:T(8,128)(2,1)S(1)}, bf16[768,1536]{1,0:T(8,128)(2,1)}, u32[]{:S(2)}, u32[]{:S(2)}) collective-permute-start(bf16[768,1536]{1,0:T(8,128)(2,1)S(1)} %bitcast.54), channel_id=1, source_target_pairs={{0,1},{1,0},{2,3},{3,2},{4,5},{5,4},{6,7},{7,6},{8,9},{9,8},{10,11... | collective-permute-start | bytes 7077896 | tf_op jit(solution)/shard_map/ppermute | solution.py:591
  169.8 7.0 %collective-permute-start.23 = (bf16[512,1536]{1,0:T(8,128)(2,1)S(1)}, bf16[512,1536]{1,0:T(8,128)(2,1)S(1)}, u32[]{:S(2)}, u32[]{:S(2)}) collective-permute-start(bf16[512,1536]{1,0:T(8,128)(2,1)S(1)} %copy-done.27), channel_id=1, source_target_pairs={{0,1},{1,0},{2,3},{3,2},{4,5},{5,4},{6,7},{7,6},{8,9},{9,8},{10,11... | collective-permute-start | bytes 4718600 | tf_op jit(solution)/shard_map/ppermute | solution.py:591
  170.3 17.2 %collective-permute-start.31 = (bf16[512,384]{1,0:T(8,128)(2,1)}, bf16[512,384]{1,0:T(8,128)(2,1)}, u32[]{:S(2)}, u32[]{:S(2)}) collective-permute-start(bf16[512,384]{1,0:T(8,128)(2,1)} %attend.5), channel_id=1, source_target_pairs={{0,1},{1,0},{2,3},{3,2},{4,5},{5,4},{6,7},{7,6},{8,9},{9,8},{10,11... | collective-permute-start | bytes 1179656 | tf_op jit(solution)/shard_map/ppermute | solution.py:591
  170.4 17.2 %collective-permute-start.30 = (bf16[512,384]{1,0:T(8,128)(2,1)S(1)}, bf16[512,384]{1,0:T(8,128)(2,1)}, u32[]{:S(2)}, u32[]{:S(2)}) collective-permute-start(bf16[512,384]{1,0:T(8,128)(2,1)S(1)} %attend.6), channel_id=1, source_target_pairs={{0,2},{1,3},{2,0},{3,1},{4,6},{5,7},{6,4},{7,5},{8,10},{9,11},{10,... | collective-permute-start | bytes 1179656 | tf_op jit(solution)/shard_map/ppermute | solution.py:591
  185.8 11.1 %collective-permute-start.28 = (bf16[512,384]{1,0:T(8,128)(2,1)S(1)}, bf16[512,384]{1,0:T(8,128)(2,1)}, u32[]{:S(2)}, u32[]{:S(2)}) collective-permute-start(bf16[512,384]{1,0:T(8,128)(2,1)S(1)} %attend.7), channel_id=1, source_target_pairs={{0,3},{1,2},{2,1},{3,0},{4,7},{5,6},{6,5},{7,4},{8,11},{9,10},{10,... | collective-permute-start | bytes 1179656 | tf_op jit(solution)/shard_map/ppermute | solution.py:591
  187.5 19.9 %collective-permute-start.33 = (bf16[512,1536]{1,0:T(8,128)(2,1)}, bf16[512,1536]{1,0:T(8,128)(2,1)}, u32[]{:S(2)}, u32[]{:S(2)}) collective-permute-start(bf16[512,1536]{1,0:T(8,128)(2,1)} %collective-permute-done.26.refs_2_), channel_id=1, source_target_pairs={{0,1},{1,0},{2,3},{3,2},{4,5},{5,4},{6,7},{7,6},{8,9},{9,8},{10,11... | collective-permute-start | bytes 4718600 | tf_op jit(solution)/shard_map/ppermute | solution.py:591
  187.7 19.7 %collective-permute-start.34 = (bf16[512,1536]{1,0:T(8,128)(2,1)}, bf16[512,1536]{1,0:T(8,128)(2,1)}, u32[]{:S(2)}, u32[]{:S(2)}) collective-permute-start(bf16[512,1536]{1,0:T(8,128)(2,1)} %refs_0_.3), channel_id=1, source_target_pairs={{0,1},{1,0},{2,3},{3,2},{4,5},{5,4},{6,7},{7,6},{8,9},{9,8},{10,11... | collective-permute-start | bytes 4718600 | tf_op jit(solution)/shard_map/ppermute | solution.py:591
  205.4 36.9 %collective-permute-start.32 = (bf16[512,1536]{1,0:T(8,128)(2,1)S(1)}, bf16[512,1536]{1,0:T(8,128)(2,1)S(1)}, u32[]{:S(2)}, u32[]{:S(2)}) collective-permute-start(bf16[512,1536]{1,0:T(8,128)(2,1)S(1)} %multiply_convert_fusion.refs_0_), channel_id=1, source_target_pairs={{0,2},{1,3},{2,0},{3,1},{4,6},{5,7},{6,4},{7,5},{8,10},{9,11},{10,... | collective-permute-start | bytes 4718600 | tf_op jit(solution)/shard_map/ppermute | solution.py:591
  207.1 36.9 %collective-permute-start.36 = (bf16[512,1536]{1,0:T(8,128)(2,1)S(1)}, bf16[512,1536]{1,0:T(8,128)(2,1)S(1)}, u32[]{:S(2)}, u32[]{:S(2)}) collective-permute-start(bf16[512,1536]{1,0:T(8,128)(2,1)S(1)} %multiply_convert_fusion.refs_0_), channel_id=1, source_target_pairs={{0,1},{1,0},{2,3},{3,2},{4,5},{5,4},{6,7},{7,6},{8,9},{9,8},{10,11... | collective-permute-start | bytes 4718600 | tf_op jit(solution)/shard_map/ppermute | solution.py:591
  242.3 38.8 %collective-permute-start.37 = (bf16[512,1536]{1,0:T(8,128)(2,1)}, bf16[512,1536]{1,0:T(8,128)(2,1)}, u32[]{:S(2)}, u32[]{:S(2)}) collective-permute-start(bf16[512,1536]{1,0:T(8,128)(2,1)} %pad_maximum_fusion.1.refs_0_), channel_id=1, source_target_pairs={{0,2},{1,3},{2,0},{3,1},{4,6},{5,7},{6,4},{7,5},{8,10},{9,11},{10,... | collective-permute-start | bytes 4718600 | tf_op jit(solution)/shard_map/ppermute | solution.py:591
  292.7 185.7 %reduce-scatter.6.cloned.1.call-start = ((), (), s32[]{:S(2)}) async-start(), calls=%async_computation.5 | async-start | bytes 7864320 | tf_op jit(solution)/shard_map/reduce_scatter | solution.py:607
  302.3 5.0 collective-permute-start.39
  306.9 8.9 %collective-permute-start.38 = (bf16[512,1536]{1,0:T(8,128)(2,1)S(1)}, bf16[512,1536]{1,0:T(8,128)(2,1)S(1)}, u32[]{:S(2)}, u32[]{:S(2)}) collective-permute-start(bf16[512,1536]{1,0:T(8,128)(2,1)S(1)} %back_product.13), channel_id=1, source_target_pairs={{0,1},{1,0},{2,3},{3,2},{4,5},{5,4},{6,7},{7,6},{8,9},{9,8},{10,11... | collective-permute-start | bytes 4718600 | tf_op jit(solution)/shard_map/ppermute | solution.py:591
  314.0 47.3 %collective-permute-start.40 = (bf16[512,1536]{1,0:T(8,128)(2,1)}, bf16[512,1536]{1,0:T(8,128)(2,1)}, u32[]{:S(2)}, u32[]{:S(2)}) collective-permute-start(bf16[512,1536]{1,0:T(8,128)(2,1)} %back_product.14), channel_id=1, source_target_pairs={{0,2},{1,3},{2,0},{3,1},{4,6},{5,7},{6,4},{7,5},{8,10},{9,11},{10,... | collective-permute-start | bytes 4718600 | tf_op jit(solution)/shard_map/ppermute | solution.py:591
  361.4 199.7 %reduce-scatter.8.cloned.1.call-start = ((), (), s32[]{:S(2)}) async-start(), calls=%async_computation.6 | async-start | bytes 5898240 | tf_op jit(solution)/shard_map/reduce_scatter | solution.py:607
  361.6 11.7 %collective-permute-start.46 = (bf16[512,1536]{1,0:T(8,128)(2,1)}, bf16[512,1536]{1,0:T(8,128)(2,1)S(1)}, u32[]{:S(2)}, u32[]{:S(2)}) collective-permute-start(bf16[512,1536]{1,0:T(8,128)(2,1)} %collective-permute-done.37.refs_2_), channel_id=1, source_target_pairs={{0,1},{1,0},{2,3},{3,2},{4,5},{5,4},{6,7},{7,6},{8,9},{9,8},{10,11... | collective-permute-start | bytes 4718600 | tf_op jit(solution)/shard_map/ppermute | solution.py:591
  361.7 27.2 %collective-permute-start.44 = (bf16[512,1536]{1,0:T(8,128)(2,1)}, bf16[512,1536]{1,0:T(8,128)(2,1)S(1)}, u32[]{:S(2)}, u32[]{:S(2)}) collective-permute-start(bf16[512,1536]{1,0:T(8,128)(2,1)} %copy-done.57), channel_id=1, source_target_pairs={{0,1},{1,0},{2,3},{3,2},{4,5},{5,4},{6,7},{7,6},{8,9},{9,8},{10,11... | collective-permute-start | bytes 4718600 | tf_op jit(solution)/shard_map/ppermute | solution.py:591
  362.2 26.7 %collective-permute-start.45 = (bf16[512,1536]{1,0:T(8,128)(2,1)}, bf16[512,1536]{1,0:T(8,128)(2,1)S(1)}, u32[]{:S(2)}, u32[]{:S(2)}) collective-permute-start(bf16[512,1536]{1,0:T(8,128)(2,1)} %copy-done.58), channel_id=1, source_target_pairs={{0,1},{1,0},{2,3},{3,2},{4,5},{5,4},{6,7},{7,6},{8,9},{9,8},{10,11... | collective-permute-start | bytes 4718600 | tf_op jit(solution)/shard_map/ppermute | solution.py:591
  365.7 7.7 %collective-permute-start.47 = (bf16[512,1536]{1,0:T(8,128)(2,1)}, bf16[512,1536]{1,0:T(8,128)(2,1)S(1)}, u32[]{:S(2)}, u32[]{:S(2)}) collective-permute-start(bf16[512,1536]{1,0:T(8,128)(2,1)} %pad_maximum_fusion.1.refs_0_), channel_id=1, source_target_pairs={{0,1},{1,0},{2,3},{3,2},{4,5},{5,4},{6,7},{7,6},{8,9},{9,8},{10,11... | collective-permute-start | bytes 4718600 | tf_op jit(solution)/shard_map/ppermute | solution.py:591
  373.0 15.9 %collective-permute-start.43 = (bf16[512,384]{1,0:T(8,128)(2,1)}, bf16[512,384]{1,0:T(8,128)(2,1)S(1)}, u32[]{:S(2)}, u32[]{:S(2)}) collective-permute-start(bf16[512,384]{1,0:T(8,128)(2,1)} %get-tuple-element.1012), channel_id=1, source_target_pairs={{0,1},{1,0},{2,3},{3,2},{4,5},{5,4},{6,7},{7,6},{8,9},{9,8},{10,11... | collective-permute-start | bytes 1179656 | tf_op jit(solution)/shard_map/ppermute | solution.py:591
  373.4 28.7 %collective-permute-start.42 = (bf16[512,384]{1,0:T(8,128)(2,1)}, bf16[512,384]{1,0:T(8,128)(2,1)S(1)}, u32[]{:S(2)}, u32[]{:S(2)}) collective-permute-start(bf16[512,384]{1,0:T(8,128)(2,1)} %get-tuple-element.1011), channel_id=1, source_target_pairs={{0,2},{1,3},{2,0},{3,1},{4,6},{5,7},{6,4},{7,5},{8,10},{9,11},{10,... | collective-permute-start | bytes 1179656 | tf_op jit(solution)/shard_map/ppermute | solution.py:591
  373.4 28.7 %collective-permute-start.41 = (bf16[512,384]{1,0:T(8,128)(2,1)S(1)}, bf16[512,384]{1,0:T(8,128)(2,1)S(1)}, u32[]{:S(2)}, u32[]{:S(2)}) collective-permute-start(bf16[512,384]{1,0:T(8,128)(2,1)S(1)} %get-tuple-element.1010), channel_id=1, source_target_pairs={{0,3},{1,2},{2,1},{3,0},{4,7},{5,6},{6,5},{7,4},{8,11},{9,10},{10,... | collective-permute-start | bytes 1179656 | tf_op jit(solution)/shard_map/ppermute | solution.py:591
  402.0 15.1 %collective-permute-start.50 = (bf16[512,384]{1,0:T(8,128)(2,1)}, bf16[512,384]{1,0:T(8,128)(2,1)S(1)}, u32[]{:S(2)}, u32[]{:S(2)}) collective-permute-start(bf16[512,384]{1,0:T(8,128)(2,1)} %get-tuple-element.793), channel_id=1, source_target_pairs={{0,2},{1,3},{2,0},{3,1},{4,6},{5,7},{6,4},{7,5},{8,10},{9,11},{10,... | collective-permute-start | bytes 1179656 | tf_op jit(solution)/shard_map/ppermute | solution.py:591
  402.5 19.5 %collective-permute-start.49 = (bf16[512,384]{1,0:T(8,128)(2,1)}, bf16[512,384]{1,0:T(8,128)(2,1)S(1)}, u32[]{:S(2)}, u32[]{:S(2)}) collective-permute-start(bf16[512,384]{1,0:T(8,128)(2,1)} %get-tuple-element.792), channel_id=1, source_target_pairs={{0,3},{1,2},{2,1},{3,0},{4,7},{5,6},{6,5},{7,4},{8,11},{9,10},{10,... | collective-permute-start | bytes 1179656 | tf_op jit(solution)/shard_map/ppermute | solution.py:591
  404.0 18.0 %collective-permute-start.48 = (bf16[512,384]{1,0:T(8,128)(2,1)S(1)}, bf16[512,384]{1,0:T(8,128)(2,1)S(1)}, u32[]{:S(2)}, u32[]{:S(2)}) collective-permute-start(bf16[512,384]{1,0:T(8,128)(2,1)S(1)} %get-tuple-element.791), channel_id=1, source_target_pairs={{0,1},{1,0},{2,3},{3,2},{4,5},{5,4},{6,7},{7,6},{8,9},{9,8},{10,11... | collective-permute-start | bytes 1179656 | tf_op jit(solution)/shard_map/ppermute | solution.py:591
  425.5 39.8 %collective-permute-start.51 = (bf16[512,1536]{1,0:T(8,128)(2,1)}, bf16[512,1536]{1,0:T(8,128)(2,1)}, u32[]{:S(2)}, u32[]{:S(2)}) collective-permute-start(bf16[512,1536]{1,0:T(8,128)(2,1)} %back_product.18), channel_id=1, source_target_pairs={{0,2},{1,3},{2,0},{3,1},{4,6},{5,7},{6,4},{7,5},{8,10},{9,11},{10,... | collective-permute-start | bytes 4718600 | tf_op jit(solution)/shard_map/ppermute | solution.py:591
  474.4 6.7 %collective-permute-start.53 = (bf16[512,1536]{1,0:T(8,128)(2,1)}, bf16[512,1536]{1,0:T(8,128)(2,1)}, u32[]{:S(2)}, u32[]{:S(2)}) collective-permute-start(bf16[512,1536]{1,0:T(8,128)(2,1)} %back_product.20), channel_id=1, source_target_pairs={{0,1},{1,0},{2,3},{3,2},{4,5},{5,4},{6,7},{7,6},{8,9},{9,8},{10,11... | collective-permute-start | bytes 4718600 | tf_op jit(solution)/shard_map/ppermute | solution.py:591
  478.4 9.7 %collective-permute-start.52 = (bf16[512,1536]{1,0:T(8,128)(2,1)}, bf16[512,1536]{1,0:T(8,128)(2,1)}, u32[]{:S(2)}, u32[]{:S(2)}) collective-permute-start(bf16[512,1536]{1,0:T(8,128)(2,1)} %back_product.21), channel_id=1, source_target_pairs={{0,1},{1,0},{2,3},{3,2},{4,5},{5,4},{6,7},{7,6},{8,9},{9,8},{10,11... | collective-permute-start | bytes 4718600 | tf_op jit(solution)/shard_map/ppermute | solution.py:591
  481.1 29.2 %collective-permute-start.54 = (bf16[96,3072]{1,0:T(8,128)(2,1)S(1)}, bf16[96,3072]{1,0:T(8,128)(2,1)S(1)}, u32[]{:S(2)}, u32[]{:S(2)}) collective-permute-start(bf16[96,3072]{1,0:T(8,128)(2,1)S(1)} %get-tuple-element.869), channel_id=1, source_target_pairs={{0,3},{1,2},{2,1},{3,0},{4,7},{5,6},{6,5},{7,4},{8,11},{9,10},{10,... | collective-permute-start | bytes 1769480 | tf_op jit(solution)/shard_map/ppermute | solution.py:591
  482.9 26.5 %collective-permute-start.55 = (bf16[96,3072]{1,0:T(8,128)(2,1)S(1)}, bf16[96,3072]{1,0:T(8,128)(2,1)S(1)}, u32[]{:S(2)}, u32[]{:S(2)}) collective-permute-start(bf16[96,3072]{1,0:T(8,128)(2,1)S(1)} %get-tuple-element.870), channel_id=1, source_target_pairs={{0,2},{1,3},{2,0},{3,1},{4,6},{5,7},{6,4},{7,5},{8,10},{9,11},{10,... | collective-permute-start | bytes 1769480 | tf_op jit(solution)/shard_map/ppermute | solution.py:591
  483.2 10.7 %collective-permute-start.56 = (bf16[96,3072]{1,0:T(8,128)(2,1)S(1)}, bf16[96,3072]{1,0:T(8,128)(2,1)S(1)}, u32[]{:S(2)}, u32[]{:S(2)}) collective-permute-start(bf16[96,3072]{1,0:T(8,128)(2,1)S(1)} %get-tuple-element.871), channel_id=1, source_target_pairs={{0,1},{1,0},{2,3},{3,2},{4,5},{5,4},{6,7},{7,6},{8,9},{9,8},{10,11... | collective-permute-start | bytes 1769480 | tf_op jit(solution)/shard_map/ppermute | solution.py:591
  511.1 43.2 %collective-permute-start.57 = (bf16[512,1536]{1,0:T(8,128)(2,1)}, bf16[512,1536]{1,0:T(8,128)(2,1)}, u32[]{:S(2)}, u32[]{:S(2)}) collective-permute-start(bf16[512,1536]{1,0:T(8,128)(2,1)} %back_product.22), channel_id=1, source_target_pairs={{0,2},{1,3},{2,0},{3,1},{4,6},{5,7},{6,4},{7,5},{8,10},{9,11},{10,... | collective-permute-start | bytes 4718600 | tf_op jit(solution)/shard_map/ppermute | solution.py:591
  535.1 5.7 collective-permute-start.59
  561.2 4.8 collective-permute-start.60
  564.0 15.7 %collective-permute-start.64 = (bf16[96,1536]{1,0:T(8,128)(2,1)S(1)}, bf16[96,1536]{1,0:T(8,128)(2,1)S(1)}, u32[]{:S(2)}, u32[]{:S(2)}) collective-permute-start(bf16[96,1536]{1,0:T(8,128)(2,1)S(1)} %get-tuple-element.932), channel_id=1, source_target_pairs={{0,3},{1,2},{2,1},{3,0},{4,7},{5,6},{6,5},{7,4},{8,11},{9,10},{10,... | collective-permute-start | bytes 884744 | tf_op jit(solution)/shard_map/ppermute | solution.py:591
  564.7 14.9 %collective-permute-start.65 = (bf16[96,1536]{1,0:T(8,128)(2,1)S(1)}, bf16[96,1536]{1,0:T(8,128)(2,1)S(1)}, u32[]{:S(2)}, u32[]{:S(2)}) collective-permute-start(bf16[96,1536]{1,0:T(8,128)(2,1)S(1)} %get-tuple-element.933), channel_id=1, source_target_pairs={{0,2},{1,3},{2,0},{3,1},{4,6},{5,7},{6,4},{7,5},{8,10},{9,11},{10,... | collective-permute-start | bytes 884744 | tf_op jit(solution)/shard_map/ppermute | solution.py:591
  565.6 10.0 %collective-permute-start.66 = (bf16[96,1536]{1,0:T(8,128)(2,1)S(1)}, bf16[96,1536]{1,0:T(8,128)(2,1)S(1)}, u32[]{:S(2)}, u32[]{:S(2)}) collective-permute-start(bf16[96,1536]{1,0:T(8,128)(2,1)S(1)} %get-tuple-element.934), channel_id=1, source_target_pairs={{0,1},{1,0},{2,3},{3,2},{4,5},{5,4},{6,7},{7,6},{8,9},{9,8},{10,11... | collective-permute-start | bytes 884744 | tf_op jit(solution)/shard_map/ppermute | solution.py:591
  592.0 5.1 collective-permute-start.69
  (145 other events, 1547.1 us)
Sparse Core Ops, SparseCore 0:
  92.9 145.2 all-gather.1
  292.8 61.7 reduce-scatter.3
  361.5 111.6 reduce-scatter.5
  475.3 85.7 reduce-scatter.7
